TPU v7x, 32 devices: a whole 2x2x4 slice. The times are simulated.
32 devices in a mesh: grp: 4 (over z), sub: 8 (over y, x, core).
Axes of the slice: x: 2, y: 2, z: 4, core: 2. Of those that a mesh axis runs over, the one named last changes fastest.
Arguments:
- right_side: float32 [512, 512], P(('grp', 'sub')), may hold values from -8 to 8
- metric: float32 [512, 1536], P(('grp', 'sub')), may hold values from 0.3 to 3
- helmholtz: float32 [512, 512], P(('grp', 'sub')), may hold values from 0.5 to 2
- jacobi: float32 [512, 512], P(('grp', 'sub')), may hold values from 0.05 to 0.5
- pair_list: int32 [2, 32768], P(None, ('grp', 'sub')), may hold values from 0 to 8191
- shared_slots: int32 [32, 8, 128], P(('grp', 'sub')), may hold values from 0 to 8192, as said below
- face_points: int32 [2, 16384], P(None, ('grp', 'sub')), may hold values from 0 to 8191
- coarse_map: int32 [8, 512], P(None, ('grp', 'sub')), may hold values from 0 to 63
- coarse_inverse: float32 [4, 64, 64], P('grp'), as said below
Outputs:
- solution: float32 [512, 512], P(('grp', 'sub'))
- residual: float32 [512, 512], P(('grp', 'sub'))
Inputs may be any that keep to these rules, and one draw needn't show every extreme that they name: `shared_slots`: entries equal to 8192 mark empty slots; the slot of device a for peer b in one group is filled exactly when the slot of b for a at the same position is; a device's slots for itself are empty; filled slots come first in each row. `coarse_inverse`: each group's matrix is symmetric and positive definite.
All inputs are finite; a program needn't handle non-finite values.
Results may differ from a plain program's by a relative error of at most 0.0003.
Values sent between devices are 32-bit elements; how exact they have to be, the bound alone decides.
No kernel may reach another device: no remote copies, remote signals or barrier semaphores. Data moves between devices by JAX's collectives and lax.ppermute only.
A program may use at most 64 MiB of HBM per device.

v0:
```python
import jax
import jax.numpy as jnp
import numpy as np
from jax import lax
from jax.sharding import PartitionSpec as P

ITERS = 2
NC = 64


def extended(cells, sides, width):
    for axis, dim in sides:
        count = lax.axis_size(axis)
        ends = count - 1
        head = lax.slice_in_dim(cells, 0, width, axis=dim)
        tail = lax.slice_in_dim(cells, cells.shape[dim] - width, cells.shape[dim], axis=dim)
        cells = jnp.concatenate(
            [
                lax.ppermute(tail, axis, [(i, (i + 1) % count) for i in range(ends)]),
                cells,
                lax.ppermute(head, axis, [((i + 1) % count, i) for i in range(ends)]),
            ],
            axis=dim,
        )
    return cells


def tables():
    order_index = np.arange(8)
    colloc = np.cos(np.pi * order_index / 7.0)
    end_weights = (
        np.where((order_index == 0) | (order_index == 7), 2.0, 1.0) * (-1.0) ** order_index
    )
    spacing = colloc[:, None] - colloc[None, :] + np.eye(8)
    raw_matrix = np.outer(end_weights, 1.0 / end_weights) / spacing
    off_part = raw_matrix * (1.0 - np.eye(8))
    derivative = 0.25 * (off_part - np.eye(8) * off_part.sum(axis=1)[:, None])
    along_first = np.kron(derivative, np.eye(64)).T
    along_inner = np.concatenate(
        [np.kron(derivative, np.eye(8)).T, np.kron(np.eye(8), derivative).T], axis=1
    )
    point_index = np.arange(512)
    corner_index = np.arange(8)
    sign_first = 1.0 - 2.0 * (corner_index >> 2 & 1)
    sign_second = 1.0 - 2.0 * (corner_index >> 1 & 1)
    sign_third = 1.0 - 2.0 * (corner_index & 1)
    node_first = colloc[point_index // 64][:, None]
    node_second = colloc[point_index // 8 % 8][:, None]
    node_third = colloc[point_index % 8][:, None]
    corner = (
        0.5
        * (1.0 + sign_first[None, :] * node_first)
        * (0.5 * (1.0 + sign_second[None, :] * node_second))
        * (0.5 * (1.0 + sign_third[None, :] * node_third))
    )
    return (
        jnp.asarray(along_first, jnp.float32),
        jnp.asarray(along_inner, jnp.float32),
        jnp.asarray(corner, jnp.float32),
    )


def residual_product(resid, smoothed):
    return lax.psum(jnp.sum(resid * smoothed), ("grp", "sub"))


def body(
    right_side,
    metric,
    helmholtz,
    jacobi,
    pair_list,
    shared_slots,
    face_points,
    coarse_map,
    coarse_inverse,
):
    highest = lax.Precision.HIGHEST
    along_first, along_inner, corner = tables()
    elements = right_side.shape[0]
    points = elements * right_side.shape[1]
    slots = shared_slots[0]

    def assemble(field):
        flat = field.reshape(-1)
        total = (
            flat.at[pair_list[0]].add(flat[pair_list[1]]).at[pair_list[1]].add(flat[pair_list[0]])
        )
        padded = jnp.concatenate([flat, jnp.zeros((1,), jnp.float32)])
        sent = padded[slots]
        received = lax.all_to_all(sent, "sub", split_axis=0, concat_axis=0, tiled=True)
        total = (
            jnp.concatenate([total, jnp.zeros((1,), jnp.float32)]).at[slots].add(received)[:points]
        )
        face_values = flat[face_points]
        rim = extended(face_values, (("grp", 0),), 1)
        total = total.at[face_points[0]].add(rim[0]).at[face_points[1]].add(rim[3])
        return total.reshape(field.shape)

    onehot = (coarse_map.reshape(-1)[:, None] == jnp.arange(NC, dtype=jnp.int32)[None, :]).astype(
        jnp.float32
    )

    def precondition(resid):
        vertex = jnp.dot(resid, corner, precision=highest)
        partial_coarse = jnp.dot(vertex.T.reshape(-1), onehot, precision=highest)
        coarse = lax.psum(partial_coarse, "sub")
        solved = jnp.dot(coarse_inverse[0], coarse, precision=highest)
        at_vertex = jnp.dot(onehot, solved, precision=highest).reshape(8, -1)
        return jacobi * resid + jnp.dot(at_vertex.T, corner.T, precision=highest)

    solution = jnp.zeros_like(right_side)
    residual = right_side
    smoothed = precondition(residual)
    direction = smoothed
    rz_now = residual_product(residual, smoothed)
    for iteration in range(ITERS):
        summed = assemble(direction)
        grad_first = jnp.dot(summed, along_first, precision=highest)
        inner = jnp.dot(summed.reshape(elements * 8, 64), along_inner, precision=highest)
        grad_second = inner[:, :64].reshape(elements, 512)
        grad_third = inner[:, 64:].reshape(elements, 512)
        flux_first = metric[:, :512] * grad_first
        flux_second = (metric[:, 512:1024] * grad_second).reshape(elements * 8, 64)
        flux_third = (metric[:, 1024:] * grad_third).reshape(elements * 8, 64)
        back = jnp.dot(flux_first, along_first.T, precision=highest)
        fluxes = jnp.concatenate([flux_second, flux_third], axis=1)
        back = back + jnp.dot(fluxes, along_inner.T, precision=highest).reshape(elements, 512)
        image = assemble(back) + helmholtz * direction
        alpha = rz_now / lax.psum(jnp.sum(direction * image), ("grp", "sub"))
        solution = solution + alpha * direction
        residual = residual - alpha * image
        if iteration + 1 < ITERS:
            smoothed = precondition(residual)
            rz_new = residual_product(residual, smoothed)
            direction = smoothed + rz_new / rz_now * direction
            rz_now = rz_new
    return (solution, residual)


def solution(mesh):
    in_specs = (
        P(("grp", "sub"), None),
        P(("grp", "sub"), None),
        P(("grp", "sub"), None),
        P(("grp", "sub"), None),
        P(None, ("grp", "sub")),
        P(("grp", "sub"), None, None),
        P(None, ("grp", "sub")),
        P(None, ("grp", "sub")),
        P("grp", None, None),
    )
    out_specs = (P(("grp", "sub"), None), P(("grp", "sub"), None))
    return jax.shard_map(body, mesh=mesh, in_specs=in_specs, out_specs=out_specs, check_vma=False)
```

profile of v0, /device:TPU:0, one launch (start us, length us, event | category | flops | bytes accessed | tf_op | source)
XLA Modules:
  0.0 433.0 jit_solution(17682091301607332374)
XLA Ops:
  0.7 0.8 eq.15
  1.5 1.5 fusion.18
  3.3 15.1 %psum.42 = f32[64]{0:T(128)S(1)} all-reduce(f32[64]{0:T(128)S(1)} %convolution_bitcast_fusion.5), channel_id=1, replica_groups=mesh['grp'=4,'sub'=8] {'sub'}, use_global_device_ids=true, to_apply=%region_0.0 | all-reduce | flops 64 | bytes 512 | tf_op jit(solution)/shard_map/psum | solution.py:107
  19.7 0.7 copy-done.10
  20.4 10.5 %gather_fusion.2 = f32[1024]{0:T(1024)} fusion(f32[8193]{0:T(1024)S(1)} %pad_maximum_fusion.6, s32[1024]{0:T(1024)S(1)} %broadcast_clamp_fusion), kind=kCustom, calls=%fused_computation.2 | custom fusion | bytes 12288 | tf_op jit(solution)/shard_map/gather | solution.py:90
  31.0 3.4 all-to-all-start
  34.5 6.2 %gather_fusion.3 = f32[1024]{0:T(1024)S(1)} fusion(f32[8192]{0:T(1024)S(1)} %bitcast.115, s32[1024]{0:T(1024)S(1)} %broadcast_clamp_fusion.1), kind=kCustom, calls=%fused_computation.3 | custom fusion | bytes 12288 | tf_op jit(solution)/shard_map/gather | solution.py:95
  40.6 3.5 collective-permute-start
  44.2 1.3 collective-permute-start.1
  45.5 6.2 %gather_fusion = f32[1024]{0:T(1024)S(1)} fusion(f32[8192]{0:T(1024)S(1)} %bitcast.116, s32[1024]{0:T(1024)S(1)} %broadcast_clamp_fusion.3), kind=kCustom, calls=%fused_computation | custom fusion | bytes 12288 | tf_op jit(solution)/shard_map/gather | solution.py:87
  51.7 6.2 %gather_fusion.1 = f32[1024]{0:T(1024)S(1)} fusion(f32[8192]{0:T(1024)S(1)} %bitcast.117, s32[1024]{0:T(1024)S(1)} %broadcast_clamp_fusion.2), kind=kCustom, calls=%fused_computation.1 | custom fusion | bytes 12288 | tf_op jit(solution)/shard_map/gather | solution.py:87
  57.9 6.1 %scatter_fusion = f32[8192]{0:T(1024)S(1)} fusion(f32[8192]{0:T(1024)S(1)} %bitcast.118, s32[1024]{0:T(1024)S(1)} %bitcast.142, f32[1024]{0:T(1024)S(1)} %gather_fusion), kind=kCustom, calls=%fused_computation.16 | custom fusion | flops 1024 | bytes 16384 | tf_op jit(solution)/shard_map/scatter-add | solution.py:87
  64.0 6.1 %scatter_fusion.1 = f32[8192]{0:T(1024)S(1)} fusion(f32[8192]{0:T(1024)S(1)} %scatter_fusion, s32[1024]{0:T(1024)S(1)} %bitcast.137, f32[1024]{0:T(1024)S(1)} %gather_fusion.1), kind=kCustom, calls=%fused_computation.17 | custom fusion | flops 1024 | bytes 16384 | tf_op jit(solution)/shard_map/scatter-add | solution.py:87
  70.1 6.7 %scatter_fusion.2 = f32[8193]{0:T(1024)S(1)} fusion(f32[8193]{0:T(1024)S(1)} %pad_maximum_fusion.7, s32[1024]{0:T(1024)S(1)} %fusion.8, f32[1024]{0:T(1024)S(1)} %bitcast.154), kind=kCustom, calls=%fused_computation.18 | custom fusion | flops 1024 | bytes 16384 | tf_op jit(solution)/shard_map/scatter-add | solution.py:93
  76.9 3.4 scatter_fusion.3
  80.3 3.6 scatter_fusion.4
  84.8 0.7 copy-done.9
  86.7 0.6 convolution_multiply_fusion.1
  87.3 1.0 fusion.1
  88.3 6.2 %gather_fusion.4 = f32[1024]{0:T(1024)S(1)} fusion(f32[8192]{0:T(1024)S(1)} %bitcast.125, s32[1024]{0:T(1024)S(1)} %broadcast_clamp_fusion.3), kind=kCustom, calls=%fused_computation.4 | custom fusion | bytes 12288 | tf_op jit(solution)/shard_map/gather | solution.py:87
  94.5 6.2 %gather_fusion.5 = f32[1024]{0:T(1024)S(1)} fusion(f32[8192]{0:T(1024)S(1)} %bitcast.126, s32[1024]{0:T(1024)S(1)} %broadcast_clamp_fusion.2), kind=kCustom, calls=%fused_computation.5 | custom fusion | bytes 12288 | tf_op jit(solution)/shard_map/gather | solution.py:87
  100.6 6.2 %gather_fusion.7 = f32[1024]{0:T(1024)S(1)} fusion(f32[8192]{0:T(1024)S(1)} %bitcast.127, s32[1024]{0:T(1024)S(1)} %broadcast_clamp_fusion.1), kind=kCustom, calls=%fused_computation.7 | custom fusion | bytes 12288 | tf_op jit(solution)/shard_map/gather | solution.py:95
  106.8 10.5 %gather_fusion.6 = f32[1024]{0:T(1024)} fusion(f32[8193]{0:T(1024)S(1)} %pad_maximum_fusion.4, s32[1024]{0:T(1024)S(1)} %broadcast_clamp_fusion), kind=kCustom, calls=%fused_computation.6 | custom fusion | bytes 12288 | tf_op jit(solution)/shard_map/gather | solution.py:90
  117.3 6.1 %scatter_fusion.5 = f32[8192]{0:T(1024)S(1)} fusion(f32[8192]{0:T(1024)S(1)} %bitcast.128, s32[1024]{0:T(1024)S(1)} %bitcast.143, f32[1024]{0:T(1024)S(1)} %gather_fusion.4), kind=kCustom, calls=%fused_computation.21 | custom fusion | flops 1024 | bytes 16384 | tf_op jit(solution)/shard_map/scatter-add | solution.py:87
  123.4 6.1 %scatter_fusion.6 = f32[8192]{0:T(1024)S(1)} fusion(f32[8192]{0:T(1024)S(1)} %scatter_fusion.5, s32[1024]{0:T(1024)S(1)} %bitcast.138, f32[1024]{0:T(1024)S(1)} %gather_fusion.5), kind=kCustom, calls=%fused_computation.22 | custom fusion | flops 1024 | bytes 16384 | tf_op jit(solution)/shard_map/scatter-add | solution.py:87
  129.5 4.4 %all-to-all-start.1 = ((f32[8,1,128]{2,1,0:T(1,128)}), f32[8,1,128]{2,1,0:T(1,128)S(1)}, u32[]{:S(2)}, u32[]{:S(2)}) async-start(f32[8,1,128]{2,1,0:T(1,128)} %bitcast.22), calls=%async_computation.1 | async-start | bytes 8192 | tf_op jit(solution)/shard_map/all_to_all | solution.py:91
  133.9 4.3 %collective-permute-start.2 = (f32[1,512]{1,0:T(1,128)S(1)}, f32[1,512]{1,0:T(1,128)S(1)}, u32[]{:S(2)}, u32[]{:S(2)}) collective-permute-start(f32[1,512]{1,0:T(1,128)S(1)} %bitcast.173), channel_id=1, source_target_pairs={{0,8},{8,16},{16,24},{1,9},{9,17},{17,25},{2,10},{10,18},{18,26},{... | collective-permute-start | bytes 6152 | tf_op jit(solution)/shard_map/ppermute | solution.py:19
  138.3 1.3 collective-permute-start.3
  139.6 6.7 %scatter_fusion.7 = f32[8193]{0:T(1024)S(1)} fusion(f32[8193]{0:T(1024)S(1)} %pad_maximum_fusion.5, s32[1024]{0:T(1024)S(1)} %fusion.8, f32[1024]{0:T(1024)S(1)} %bitcast.156), kind=kCustom, calls=%fused_computation.23 | custom fusion | flops 1024 | bytes 16384 | tf_op jit(solution)/shard_map/scatter-add | solution.py:93
  146.3 3.4 scatter_fusion.8
  149.7 3.4 scatter_fusion.9
  153.1 0.7 copy-done.4
  154.5 43.2 %all-reduce = (f32[]{:T(128)}, f32[]{:T(128)}) all-reduce(f32[]{:T(128)} %get-tuple-element.3, f32[]{:T(128)} %get-tuple-element.2), channel_id=1, replica_groups=mesh['grp'=4,'sub'=8] {'grp','sub'}, use_global_device_ids=true, to_apply=%region_2.0 | all-reduce | flops 2 | bytes 16 | tf_op jit(solution)/shard_map/psum | solution.py:64
  199.9 12.9 %psum.45 = f32[64]{0:T(128)S(1)} all-reduce(f32[64]{0:T(128)S(1)} %convolution_bitcast_fusion.2), channel_id=1, replica_groups=mesh['grp'=4,'sub'=8] {'sub'}, use_global_device_ids=true, to_apply=%region_15.0 | all-reduce | flops 64 | bytes 512 | tf_op jit(solution)/shard_map/psum | solution.py:107
  213.3 1.0 multiply_reduce_fusion.1
  214.3 39.0 %psum.46 = f32[]{:T(128)} all-reduce(f32[]{:T(128)} %get-tuple-element.28), channel_id=1, replica_groups=mesh['grp'=4,'sub'=8] {'grp','sub'}, use_global_device_ids=true, to_apply=%region_17.0 | all-reduce | flops 1 | bytes 8 | tf_op jit(solution)/shard_map/psum | solution.py:64
  254.7 6.2 %gather_fusion.8 = f32[1024]{0:T(1024)S(1)} fusion(f32[8192]{0:T(1024)S(1)} %bitcast.130, s32[1024]{0:T(1024)S(1)} %broadcast_clamp_fusion.3), kind=kCustom, calls=%fused_computation.8 | custom fusion | bytes 12288 | tf_op jit(solution)/shard_map/gather | solution.py:87
  260.9 6.2 %gather_fusion.9 = f32[1024]{0:T(1024)S(1)} fusion(f32[8192]{0:T(1024)S(1)} %bitcast.131, s32[1024]{0:T(1024)S(1)} %broadcast_clamp_fusion.2), kind=kCustom, calls=%fused_computation.9 | custom fusion | bytes 12288 | tf_op jit(solution)/shard_map/gather | solution.py:87
  267.1 6.2 %gather_fusion.11 = f32[1024]{0:T(1024)S(1)} fusion(f32[8192]{0:T(1024)S(1)} %bitcast.132, s32[1024]{0:T(1024)S(1)} %broadcast_clamp_fusion.1), kind=kCustom, calls=%fused_computation.11 | custom fusion | bytes 12288 | tf_op jit(solution)/shard_map/gather | solution.py:95
  273.2 10.5 %gather_fusion.10 = f32[1024]{0:T(1024)} fusion(f32[8193]{0:T(1024)S(1)} %pad_maximum_fusion.2, s32[1024]{0:T(1024)S(1)} %broadcast_clamp_fusion), kind=kCustom, calls=%fused_computation.10 | custom fusion | bytes 12288 | tf_op jit(solution)/shard_map/gather | solution.py:90
  283.8 6.1 %scatter_fusion.10 = f32[8192]{0:T(1024)S(1)} fusion(f32[8192]{0:T(1024)S(1)} %bitcast.133, s32[1024]{0:T(1024)S(1)} %bitcast.144, f32[1024]{0:T(1024)S(1)} %gather_fusion.8), kind=kCustom, calls=%fused_computation.26 | custom fusion | flops 1024 | bytes 16384 | tf_op jit(solution)/shard_map/scatter-add | solution.py:87
  289.9 6.1 %scatter_fusion.11 = f32[8192]{0:T(1024)S(1)} fusion(f32[8192]{0:T(1024)S(1)} %scatter_fusion.10, s32[1024]{0:T(1024)S(1)} %bitcast.139, f32[1024]{0:T(1024)S(1)} %gather_fusion.9), kind=kCustom, calls=%fused_computation.27 | custom fusion | flops 1024 | bytes 16384 | tf_op jit(solution)/shard_map/scatter-add | solution.py:87
  296.0 4.7 %all-to-all-start.2 = ((f32[8,1,128]{2,1,0:T(1,128)}), f32[8,1,128]{2,1,0:T(1,128)S(1)}, u32[]{:S(2)}, u32[]{:S(2)}) async-start(f32[8,1,128]{2,1,0:T(1,128)} %bitcast.33), calls=%async_computation.2 | async-start | bytes 8192 | tf_op jit(solution)/shard_map/all_to_all | solution.py:91
  300.7 3.0 collective-permute-start.4
  303.7 1.3 collective-permute-start.5
  305.3 6.7 %scatter_fusion.12 = f32[8193]{0:T(1024)S(1)} fusion(f32[8193]{0:T(1024)S(1)} %pad_maximum_fusion.3, s32[1024]{0:T(1024)S(1)} %fusion.8, f32[1024]{0:T(1024)S(1)} %bitcast.157), kind=kCustom, calls=%fused_computation.28 | custom fusion | flops 1024 | bytes 16384 | tf_op jit(solution)/shard_map/scatter-add | solution.py:93
  312.0 3.4 scatter_fusion.13
  315.4 3.4 scatter_fusion.14
  320.4 0.6 convolution_multiply_fusion
  321.0 1.0 fusion
  322.0 6.2 %gather_fusion.12 = f32[1024]{0:T(1024)S(1)} fusion(f32[8192]{0:T(1024)S(1)} %bitcast.120, s32[1024]{0:T(1024)S(1)} %broadcast_clamp_fusion.3), kind=kCustom, calls=%fused_computation.12 | custom fusion | bytes 12288 | tf_op jit(solution)/shard_map/gather | solution.py:87
  328.2 6.2 %gather_fusion.13 = f32[1024]{0:T(1024)S(1)} fusion(f32[8192]{0:T(1024)S(1)} %bitcast.121, s32[1024]{0:T(1024)S(1)} %broadcast_clamp_fusion.2), kind=kCustom, calls=%fused_computation.13 | custom fusion | bytes 12288 | tf_op jit(solution)/shard_map/gather | solution.py:87
  334.3 6.2 %gather_fusion.15 = f32[1024]{0:T(1024)S(1)} fusion(f32[8192]{0:T(1024)S(1)} %bitcast.122, s32[1024]{0:T(1024)S(1)} %broadcast_clamp_fusion.1), kind=kCustom, calls=%fused_computation.15 | custom fusion | bytes 12288 | tf_op jit(solution)/shard_map/gather | solution.py:95
  340.5 10.5 %gather_fusion.14 = f32[1024]{0:T(1024)} fusion(f32[8193]{0:T(1024)S(1)} %pad_maximum_fusion, s32[1024]{0:T(1024)S(1)} %broadcast_clamp_fusion), kind=kCustom, calls=%fused_computation.14 | custom fusion | bytes 12288 | tf_op jit(solution)/shard_map/gather | solution.py:90
  351.0 6.3 %scatter_fusion.15 = f32[8192]{0:T(1024)S(1)} fusion(f32[8192]{0:T(1024)S(1)} %bitcast.123, s32[1024]{0:T(1024)S(1)} %bitcast.145, f32[1024]{0:T(1024)S(1)} %gather_fusion.12), kind=kCustom, calls=%fused_computation.31 | custom fusion | flops 1024 | bytes 16384 | tf_op jit(solution)/shard_map/scatter-add | solution.py:87
  357.4 6.1 %scatter_fusion.16 = f32[8192]{0:T(1024)S(1)} fusion(f32[8192]{0:T(1024)S(1)} %scatter_fusion.15, s32[1024]{0:T(1024)S(1)} %bitcast.140, f32[1024]{0:T(1024)S(1)} %gather_fusion.13), kind=kCustom, calls=%fused_computation.32 | custom fusion | flops 1024 | bytes 16384 | tf_op jit(solution)/shard_map/scatter-add | solution.py:87
  363.5 4.3 all-to-all-start.3
  367.8 4.3 %collective-permute-start.6 = (f32[1,512]{1,0:T(1,128)S(1)}, f32[1,512]{1,0:T(1,128)S(1)}, u32[]{:S(2)}, u32[]{:S(2)}) collective-permute-start(f32[1,512]{1,0:T(1,128)S(1)} %bitcast.172), channel_id=1, source_target_pairs={{0,8},{8,16},{16,24},{1,9},{9,17},{17,25},{2,10},{10,18},{18,26},{... | collective-permute-start | bytes 6152 | tf_op jit(solution)/shard_map/ppermute | solution.py:19
  372.1 1.3 collective-permute-start.7
  373.4 6.7 %scatter_fusion.17 = f32[8193]{0:T(1024)S(1)} fusion(f32[8193]{0:T(1024)S(1)} %pad_maximum_fusion.1, s32[1024]{0:T(1024)S(1)} %fusion.8, f32[1024]{0:T(1024)S(1)} %bitcast.155), kind=kCustom, calls=%fused_computation.33 | custom fusion | flops 1024 | bytes 16384 | tf_op jit(solution)/shard_map/scatter-add | solution.py:93
  380.2 3.4 scatter_fusion.18
  383.6 3.4 scatter_fusion.19
  387.6 43.0 %psum.47 = f32[]{:T(128)} all-reduce(f32[]{:T(128)} %multiply_reduce_fusion), channel_id=1, replica_groups=mesh['grp'=4,'sub'=8] {'grp','sub'}, use_global_device_ids=true, to_apply=%region_29.0 | all-reduce | flops 1 | bytes 8 | tf_op jit(solution)/shard_map/psum | solution.py:130
  431.9 0.6 multiply_subtract_fusion
  (112 shorter events, 8.2 us)
Async XLA Ops:
  0.6 17.8 %copy-start = (f32[1,64,64]{2,1,0:T(8,128)S(1)}, f32[1,64,64]{2,1,0:T(8,128)}, u32[]{:S(2)}) copy-start(f32[1,64,64]{2,1,0:T(8,128)} %param.20) | copy-start | bytes 49156
  0.6 18.2 %copy-start.2 = (f32[512,8]{1,0:T(8,128)S(1)}, f32[512,8]{1,0:T(8,128)}, u32[]{:S(2)}) copy-start(f32[512,8]{1,0:T(8,128)} %constant.5.clone) | copy-start | bytes 49156
  18.5 0.8 copy-start.3
  18.5 0.8 copy-start.6
  19.7 0.7 copy-start.10
  31.0 3.5 copy-start.11
  31.0 39.2 %all-to-all-start = ((f32[8,1,128]{2,1,0:T(1,128)}), f32[8,1,128]{2,1,0:T(1,128)S(1)}, u32[]{:S(2)}, u32[]{:S(2)}) async-start(f32[8,1,128]{2,1,0:T(1,128)} %bitcast.12), calls=%async_computation | async-start | bytes 8192 | tf_op jit(solution)/shard_map/all_to_all | solution.py:91
  40.6 4.8 %copy-start.12 = (s32[2,1024]{1,0:T(2,128)S(1)}, s32[2,1024]{1,0:T(2,128)}, u32[]{:S(2)}) copy-start(s32[2,1024]{1,0:T(2,128)} %param.16) | copy-start | bytes 24580
  40.6 36.2 %collective-permute-start = (f32[1,512]{1,0:T(1,128)S(1)}, f32[1,512]{1,0:T(1,128)S(1)}, u32[]{:S(2)}, u32[]{:S(2)}) collective-permute-start(f32[1,512]{1,0:T(1,128)S(1)} %bitcast.169), channel_id=1, source_target_pairs={{0,8},{8,16},{16,24},{1,9},{9,17},{17,25},{2,10},{10,18},{18,26},{... | collective-permute-start | bytes 6152 | tf_op jit(solution)/shard_map/ppermute | solution.py:19
  44.2 36.1 %collective-permute-start.1 = (f32[1,512]{1,0:T(1,128)S(1)}, f32[1,512]{1,0:T(1,128)S(1)}, u32[]{:S(2)}, u32[]{:S(2)}) collective-permute-start(f32[1,512]{1,0:T(1,128)S(1)} %bitcast.167), channel_id=1, source_target_pairs={{8,0},{16,8},{24,16},{9,1},{17,9},{25,17},{10,2},{18,10},{26,18},{... | collective-permute-start | bytes 6152 | tf_op jit(solution)/shard_map/ppermute | solution.py:21
  80.3 3.7 copy-start.8
  80.3 4.4 %copy-start.5 = (f32[16,1536]{1,0:T(8,128)S(1)}, f32[16,1536]{1,0:T(8,128)}, u32[]{:S(2)}) copy-start(f32[16,1536]{1,0:T(8,128)} %param.13) | copy-start | bytes 294916
  83.8 2.8 copy-start.1
  84.7 0.8 copy-start.9
  85.5 0.8 copy-start.7
  129.5 10.0 %all-to-all-start.1 = ((f32[8,1,128]{2,1,0:T(1,128)}), f32[8,1,128]{2,1,0:T(1,128)S(1)}, u32[]{:S(2)}, u32[]{:S(2)}) async-start(f32[8,1,128]{2,1,0:T(1,128)} %bitcast.22), calls=%async_computation.1 | async-start | bytes 8192 | tf_op jit(solution)/shard_map/all_to_all | solution.py:91
  133.9 12.4 %collective-permute-start.2 = (f32[1,512]{1,0:T(1,128)S(1)}, f32[1,512]{1,0:T(1,128)S(1)}, u32[]{:S(2)}, u32[]{:S(2)}) collective-permute-start(f32[1,512]{1,0:T(1,128)S(1)} %bitcast.173), channel_id=1, source_target_pairs={{0,8},{8,16},{16,24},{1,9},{9,17},{17,25},{2,10},{10,18},{18,26},{... | collective-permute-start | bytes 6152 | tf_op jit(solution)/shard_map/ppermute | solution.py:19
  138.3 11.4 %collective-permute-start.3 = (f32[1,512]{1,0:T(1,128)S(1)}, f32[1,512]{1,0:T(1,128)S(1)}, u32[]{:S(2)}, u32[]{:S(2)}) collective-permute-start(f32[1,512]{1,0:T(1,128)S(1)} %bitcast.170), channel_id=1, source_target_pairs={{8,0},{16,8},{24,16},{9,1},{17,9},{25,17},{10,2},{18,10},{26,18},{... | collective-permute-start | bytes 6152 | tf_op jit(solution)/shard_map/ppermute | solution.py:21
  153.1 0.8 copy-start.4
  296.0 9.3 %all-to-all-start.2 = ((f32[8,1,128]{2,1,0:T(1,128)}), f32[8,1,128]{2,1,0:T(1,128)S(1)}, u32[]{:S(2)}, u32[]{:S(2)}) async-start(f32[8,1,128]{2,1,0:T(1,128)} %bitcast.33), calls=%async_computation.2 | async-start | bytes 8192 | tf_op jit(solution)/shard_map/all_to_all | solution.py:91
  300.7 11.3 %collective-permute-start.4 = (f32[1,512]{1,0:T(1,128)S(1)}, f32[1,512]{1,0:T(1,128)S(1)}, u32[]{:S(2)}, u32[]{:S(2)}) collective-permute-start(f32[1,512]{1,0:T(1,128)S(1)} %bitcast.174), channel_id=1, source_target_pairs={{0,8},{8,16},{16,24},{1,9},{9,17},{17,25},{2,10},{10,18},{18,26},{... | collective-permute-start | bytes 6152 | tf_op jit(solution)/shard_map/ppermute | solution.py:19
  303.7 11.7 %collective-permute-start.5 = (f32[1,512]{1,0:T(1,128)S(1)}, f32[1,512]{1,0:T(1,128)S(1)}, u32[]{:S(2)}, u32[]{:S(2)}) collective-permute-start(f32[1,512]{1,0:T(1,128)S(1)} %bitcast.171), channel_id=1, source_target_pairs={{8,0},{16,8},{24,16},{9,1},{17,9},{25,17},{10,2},{18,10},{26,18},{... | collective-permute-start | bytes 6152 | tf_op jit(solution)/shard_map/ppermute | solution.py:21
  363.5 9.9 %all-to-all-start.3 = ((f32[8,1,128]{2,1,0:T(1,128)}), f32[8,1,128]{2,1,0:T(1,128)S(1)}, u32[]{:S(2)}, u32[]{:S(2)}) async-start(f32[8,1,128]{2,1,0:T(1,128)} %bitcast.39), calls=%async_computation.3 | async-start | bytes 8192 | tf_op jit(solution)/shard_map/all_to_all | solution.py:91
  367.8 12.4 %collective-permute-start.6 = (f32[1,512]{1,0:T(1,128)S(1)}, f32[1,512]{1,0:T(1,128)S(1)}, u32[]{:S(2)}, u32[]{:S(2)}) collective-permute-start(f32[1,512]{1,0:T(1,128)S(1)} %bitcast.172), channel_id=1, source_target_pairs={{0,8},{8,16},{16,24},{1,9},{9,17},{17,25},{2,10},{10,18},{18,26},{... | collective-permute-start | bytes 6152 | tf_op jit(solution)/shard_map/ppermute | solution.py:19
  372.1 11.4 %collective-permute-start.7 = (f32[1,512]{1,0:T(1,128)S(1)}, f32[1,512]{1,0:T(1,128)S(1)}, u32[]{:S(2)}, u32[]{:S(2)}) collective-permute-start(f32[1,512]{1,0:T(1,128)S(1)} %bitcast.168), channel_id=1, source_target_pairs={{8,0},{16,8},{24,16},{9,1},{17,9},{25,17},{10,2},{18,10},{26,18},{... | collective-permute-start | bytes 6152 | tf_op jit(solution)/shard_map/ppermute | solution.py:21
where the time goes:
time: 440 us; the launch traced here: 433 us
  blocking collectives  153 us (35%)
  local copies, waits for them, and re-layouts  122 us (28%)
  other arithmetic  105 us (24%)
  starting transfers between devices  37.1 us (8%)
  matrix products  9.32 us (2%)
  between operations  6.08 us (1%)
    psum x2, blocking collectives, residual_product(): return lax.psum(jnp.sum(resid * smoothed), ('grp', 'sub'))  82.2 us
    scatter-add x8, other arithmetic, assemble(): flat.at[pair_list[0]].add(flat[pair_list[1]]).at[pair_list[1]]  49.1 us
    psum x1, blocking collectives, body(): alpha = rz_now / lax.psum(jnp.sum(direction * image), ('grp', 'sub'))  43 us
    gather x4, local copies, waits for them, and re-layouts, assemble(): sent = padded[slots]  42.2 us
    psum x2, blocking collectives, precondition(): coarse = lax.psum(partial_coarse, 'sub')  28 us
    scatter-add x8, other arithmetic, assemble(): total = total.at[face_points[0]].add(rim[0]).at[face_points[1]].add(rim[3])  27.2 us
    scatter-add x4, other arithmetic, assemble(): jnp.concatenate([total, jnp.zeros((1,), jnp.float32)]).at[slots]  26.8 us
    gather x4, local copies, waits for them, and re-layouts, assemble(): face_values = flat[face_points]  24.6 us
  transfers between devices with their start and end apart: 12, of which 1 were waited for; matrix products, arithmetic and copies ran while one was open for 16% of the time, Pallas kernels for 0%

commit v1 on v0

v1 whole, which is shorter than its diff:
```python
import jax
import jax.numpy as jnp
import ml_dtypes
import numpy as np
from jax import lax
from jax.experimental import pallas as pl
from jax.experimental.pallas import tpu as pltpu
from jax.sharding import PartitionSpec as P

NC = 64
POINTS = 512
LANES = 128
STEP = 256
F32 = jnp.float32
BF16 = jnp.bfloat16
NT = (((1,), (1,)), ((), ()))


def split_constant(array):
    high = array.astype(ml_dtypes.bfloat16)
    low = (array - high.astype(np.float64)).astype(ml_dtypes.bfloat16)
    return high, low


def tables(elements):
    order_index = np.arange(8)
    colloc = np.cos(np.pi * order_index / 7.0)
    end_weights = (
        np.where((order_index == 0) | (order_index == 7), 2.0, 1.0) * (-1.0) ** order_index
    )
    spacing = colloc[:, None] - colloc[None, :] + np.eye(8)
    raw_matrix = np.outer(end_weights, 1.0 / end_weights) / spacing
    off_part = raw_matrix * (1.0 - np.eye(8))
    derivative = 0.25 * (off_part - np.eye(8) * off_part.sum(axis=1)[:, None])
    along_inner = np.concatenate(
        [np.kron(np.eye(2), np.kron(derivative, np.eye(8))).T, np.kron(np.eye(16), derivative).T],
        axis=1,
    )
    high, low = split_constant(along_inner)
    inner = np.concatenate([high, high, low], axis=0)
    inner_back = np.concatenate([high.T, high.T, low.T], axis=0)

    half = np.arange(LANES) // 64

    def first_rows(matrix):
        rows = []
        for to in range(4):
            for at in range(4):
                rows.append(matrix[2 * to + half, 2 * at + half])
                rows.append(matrix[2 * to + half, 2 * at + 1 - half])
        return np.stack(rows).astype(np.float32)

    point_index = np.arange(POINTS)
    corner_index = np.arange(8)
    sign_first = 1.0 - 2.0 * (corner_index >> 2 & 1)
    sign_second = 1.0 - 2.0 * (corner_index >> 1 & 1)
    sign_third = 1.0 - 2.0 * (corner_index & 1)
    node_first = colloc[point_index // 64][:, None]
    node_second = colloc[point_index // 8 % 8][:, None]
    node_third = colloc[point_index % 8][:, None]
    corner = (
        0.5
        * (1.0 + sign_first[None, :] * node_first)
        * (0.5 * (1.0 + sign_second[None, :] * node_second))
        * (0.5 * (1.0 + sign_third[None, :] * node_third))
    )
    corner_high, corner_low = split_constant(np.repeat(corner.T, elements, axis=0))
    spread = np.tile(np.eye(elements), (1, 8)).astype(np.float32)
    return {
        "inner": inner,
        "inner_back": inner_back,
        "first": first_rows(derivative),
        "first_back": first_rows(derivative.T),
        "corner_high": corner_high,
        "corner_low": corner_low,
        "spread": spread,
    }


def split(value):
    high = value.astype(BF16)
    return high, (value - high.astype(F32)).astype(BF16)


def rows_of(wide):
    return jnp.concatenate([wide[:, LANES * c : LANES * (c + 1)] for c in range(4)], axis=0)


def wide_of(rows):
    elements = rows.shape[0] // 4
    return jnp.concatenate([rows[c * elements : (c + 1) * elements] for c in range(4)], axis=1)


def locate(points, elements):
    element = points >> 9
    chunk = (points >> 7) & 3
    row = jnp.where(points < elements * POINTS, chunk * elements + element, 4 * elements)
    return row, points & (LANES - 1)


def one_hot(index, count):
    steps = lax.broadcasted_iota(jnp.int32, (count, index.shape[1]), 0)
    return steps == index


def gather(field, chunks):
    high, low = split(field)
    both = jnp.concatenate([high, low], axis=1)
    out = []
    for row, lane in chunks:
        lanes = one_hot(lane, LANES).astype(F32).astype(BF16)
        picked = jnp.dot(
            both, jnp.concatenate([lanes, lanes], axis=0), preferred_element_type=F32
        )
        out.append(
            jnp.sum(
                jnp.where(one_hot(row, field.shape[0]), picked, 0.0), axis=0, keepdims=True
            )
        )
    return out


def scatter(rows, chunks, values):
    total = jnp.zeros((2 * rows, LANES), F32)
    for (row, lane), value in zip(chunks, values):
        lanes = one_hot(lane, LANES).astype(F32).astype(BF16)
        high, low = split(jnp.where(one_hot(row, rows), value, 0.0))
        total = total + lax.dot_general(
            jnp.concatenate([high, low], axis=0), lanes, NT, preferred_element_type=F32
        )
    return total[:rows] + total[rows:]


def chunked(row, lane):
    return [
        (row[:, at : at + STEP], lane[:, at : at + STEP]) for at in range(0, row.shape[1], STEP)
    ]


def cut(row):
    return [row[:, at : at + STEP] for at in range(0, row.shape[1], STEP)]


def index_chunks(pair_ref, slot_ref, face_ref, elements):
    pair_row, pair_lane = locate(pair_ref[...], elements)
    slot_row, slot_lane = locate(slot_ref[0], elements)
    face_row, face_lane = locate(face_ref[...], elements)
    pairs = chunked(pair_row[0:1], pair_lane[0:1]) + chunked(pair_row[1:2], pair_lane[1:2])
    slots = []
    for at in range(0, slot_row.shape[0], 2):
        slots.append(
            tuple(
                jnp.concatenate([part[at : at + 1], part[at + 1 : at + 2]], axis=1)
                for part in (slot_row, slot_lane)
            )
        )
    faces = chunked(face_row[0:1], face_lane[0:1]) + chunked(face_row[1:2], face_lane[1:2])
    return pairs, slots, faces


def gather_all(field, refs, outs):
    pair_ref, slot_ref, face_ref = refs
    local_ref, sent_ref, down_ref, up_ref = outs
    pairs, slots, faces = index_chunks(pair_ref, slot_ref, face_ref, field.shape[0] // 4)
    values = gather(field, pairs + slots + faces)
    count = pair_ref.shape[1] // STEP
    for k in range(count):
        local_ref[0:1, k * STEP : (k + 1) * STEP] = values[k]
        local_ref[1:2, k * STEP : (k + 1) * STEP] = values[count + k]
    values = values[2 * count :]
    for k in range(len(slots)):
        sent_ref[2 * k : 2 * k + 1, 0:LANES] = values[k][:, :LANES]
        sent_ref[2 * k + 1 : 2 * k + 2, 0:LANES] = values[k][:, LANES:]
    values = values[len(slots) :]
    count = face_ref.shape[1] // STEP
    for k in range(count):
        down_ref[0:1, k * STEP : (k + 1) * STEP] = values[k]
        up_ref[0:1, k * STEP : (k + 1) * STEP] = values[count + k]


def assembled(field, refs, local, received, below, above):
    pair_ref, slot_ref, face_ref = refs
    pairs, slots, faces = index_chunks(pair_ref, slot_ref, face_ref, field.shape[0] // 4)
    values = cut(local[1:2]) + cut(local[0:1])
    for at in range(0, received.shape[0], 2):
        values.append(jnp.concatenate([received[at : at + 1], received[at + 1 : at + 2]], axis=1))
    values = values + cut(below) + cut(above)
    return field + scatter(field.shape[0], pairs + slots + faces, values)


def along_first(field, table_ref):
    elements = field.shape[0] // 4
    turned = pltpu.roll(field, 64, axis=1)
    out = []
    for to in range(4):
        total = None
        for at in range(4):
            place = 2 * (4 * to + at)
            rows = slice(at * elements, (at + 1) * elements)
            term = (
                table_ref[place : place + 1, :] * field[rows]
                + table_ref[place + 1 : place + 2, :] * turned[rows]
            )
            total = term if total is None else total + term
        out.append(total)
    return jnp.concatenate(out, axis=0)


def stiffness(field, metric_ref, first_ref, first_back_ref, inner_ref, inner_back_ref):
    metric = [rows_of(metric_ref[:, POINTS * d : POINTS * (d + 1)]) for d in range(3)]
    grad_first = along_first(field, first_ref)
    high, low = split(field)
    inner = jnp.dot(
        jnp.concatenate([high, low, high], axis=1), inner_ref[...], preferred_element_type=F32
    )
    flux_first = metric[0] * grad_first
    flux = jnp.concatenate([metric[1], metric[2]], axis=1) * inner
    high, low = split(flux)
    back = along_first(flux_first, first_back_ref) + jnp.dot(
        jnp.concatenate([high, low, high], axis=1), inner_back_ref[...], preferred_element_type=F32
    )
    energy = flux * inner
    return back, flux_first * grad_first + energy[:, :LANES] + energy[:, LANES:]


def vertex_map(map_ref, spread_ref):
    wide = jnp.dot(
        map_ref[...].astype(F32),
        spread_ref[...],
        precision=lax.Precision.HIGHEST,
        preferred_element_type=F32,
    )
    corners, width = wide.shape
    own = lax.broadcasted_iota(jnp.int32, wide.shape, 0) == (
        lax.broadcasted_iota(jnp.int32, wide.shape, 1) // (width // corners)
    )
    flat = jnp.sum(jnp.where(own, wide, 0.0), axis=0, keepdims=True)
    flat = (flat + 0.5).astype(jnp.int32)
    return jnp.where(one_hot(flat, NC), 1.0, 0.0)


def own_element(elements, width):
    shape = (elements, width)
    return lax.broadcasted_iota(jnp.int32, shape, 0) == (
        lax.broadcasted_iota(jnp.int32, shape, 1) % elements
    )


def coarse_part(wide, vertices, corner_high_ref, corner_low_ref):
    elements = wide.shape[0]
    high, low = split(wide)
    both = lax.dot_general(
        jnp.concatenate([high, low], axis=0), corner_high_ref[...], NT, preferred_element_type=F32
    )
    inner = (
        both[:elements]
        + both[elements:]
        + lax.dot_general(high, corner_low_ref[...], NT, preferred_element_type=F32)
    )
    inner = jnp.where(own_element(elements, inner.shape[1]), inner, 0.0)
    flat = jnp.sum(inner, axis=0, keepdims=True)
    return lax.dot_general(
        jnp.broadcast_to(flat, (8, flat.shape[1])),
        vertices,
        NT,
        precision=lax.Precision.HIGHEST,
        preferred_element_type=F32,
    )[0:1]


def prolonged(coarse, inverse_ref, vertices, elements, corner_high_ref, corner_low_ref):
    solved = jnp.sum(inverse_ref[0] * coarse, axis=1, keepdims=True)
    flat = jnp.sum(vertices * solved, axis=0, keepdims=True)
    spread = jnp.where(own_element(elements, flat.shape[1]), flat, 0.0)
    high, low = split(spread)
    both = jnp.dot(
        jnp.concatenate([high, low], axis=0), corner_high_ref[...], preferred_element_type=F32
    )
    return (
        both[:elements]
        + both[elements:]
        + jnp.dot(high, corner_low_ref[...], preferred_element_type=F32)
    )


def total_of(array):
    return jnp.sum(jnp.sum(array, axis=0, keepdims=True), axis=1, keepdims=True)


def packed(values):
    lane = lax.broadcasted_iota(jnp.int32, (1, LANES), 1)
    out = jnp.zeros((1, LANES), F32)
    for k, value in enumerate(values):
        out = jnp.where(lane == k, value, out)
    return out


def unpacked(row, count):
    lane = lax.broadcasted_iota(jnp.int32, row.shape, 1)
    return [
        jnp.sum(jnp.where(lane == k, row, 0.0), axis=1, keepdims=True) for k in range(count)
    ]


def first_kernel(right_ref, map_ref, spread_ref, high_ref, low_ref, sent_ref):
    vertices = vertex_map(map_ref, spread_ref)
    part = coarse_part(right_ref[...], vertices, high_ref, low_ref)
    sent_ref[...] = jnp.broadcast_to(part, sent_ref.shape)


def smooth_kernel(
    right_ref, jacobi_ref, coarse_ref, inverse_ref, map_ref, spread_ref, high_ref, low_ref,
    pair_ref, slot_ref, face_ref,
    smoothed_ref, total_ref, dots_ref, local_ref, sent_ref, down_ref, up_ref,
):
    vertices = vertex_map(map_ref, spread_ref)
    coarse = jnp.sum(coarse_ref[...], axis=0, keepdims=True)
    total_ref[...] = coarse
    resid = right_ref[...]
    smoothed = jacobi_ref[...] * resid + prolonged(
        coarse, inverse_ref, vertices, resid.shape[0], high_ref, low_ref
    )
    dots_ref[...] = packed([total_of(resid * smoothed)])
    field = rows_of(smoothed)
    smoothed_ref[...] = field
    gather_all(field, (pair_ref, slot_ref, face_ref), (local_ref, sent_ref, down_ref, up_ref))


def apply_kernel(
    field_ref, dots_in_ref, local_in_ref, received_ref, below_ref, above_ref,
    metric_ref, helmholtz_ref, first_ref, first_back_ref, inner_ref, inner_back_ref,
    pair_ref, slot_ref, face_ref,
    back_ref, local_ref, sent_ref, down_ref, up_ref,
):
    refs = (pair_ref, slot_ref, face_ref)
    field = field_ref[...]
    summed = assembled(
        field, refs, local_in_ref[...], received_ref[...], below_ref[...], above_ref[...]
    )
    back, energy = stiffness(
        summed, metric_ref, first_ref, first_back_ref, inner_ref, inner_back_ref
    )
    energy = energy + rows_of(helmholtz_ref[...]) * field * field
    dots = dots_in_ref[...]
    lane = lax.broadcasted_iota(jnp.int32, dots.shape, 1)
    dots = jnp.where(lane == 7, total_of(energy), dots)
    back_ref[...] = back
    gather_all(back, refs, (local_ref, sent_ref, down_ref, up_ref))
    sent_ref[:, LANES:] = jnp.broadcast_to(dots, (sent_ref.shape[0], LANES))


def image_of(field_ref, back_ref, local_in_ref, received_ref, below_ref, above_ref, helmholtz_ref, refs):
    summed = assembled(
        back_ref[...],
        refs,
        local_in_ref[...],
        received_ref[:, :LANES],
        below_ref[...],
        above_ref[...],
    )
    return summed + rows_of(helmholtz_ref[...]) * field_ref[...]


def image_kernel(
    field_ref, back_ref, local_in_ref, received_ref, below_ref, above_ref,
    helmholtz_ref, map_ref, spread_ref, high_ref, low_ref,
    pair_ref, slot_ref, face_ref,
    image_ref, sent_ref, dots_ref,
):
    image = image_of(
        field_ref, back_ref, local_in_ref, received_ref, below_ref, above_ref, helmholtz_ref,
        (pair_ref, slot_ref, face_ref),
    )
    image_ref[...] = image
    vertices = vertex_map(map_ref, spread_ref)
    part = coarse_part(wide_of(image), vertices, high_ref, low_ref)
    sent_ref[...] = jnp.broadcast_to(part, sent_ref.shape)
    dots = jnp.sum(received_ref[:, LANES:], axis=0, keepdims=True)
    dots_ref[...] = jnp.broadcast_to(dots, dots_ref.shape)


def second_kernel(
    right_ref, image_ref, jacobi_ref, dots_in_ref, total_ref, coarse_ref, inverse_ref,
    map_ref, spread_ref, high_ref, low_ref,
    pair_ref, slot_ref, face_ref,
    smoothed_ref, resid_ref, scalars_ref, dots_ref, local_ref, sent_ref, down_ref, up_ref,
):
    dots = jnp.sum(dots_in_ref[...], axis=0, keepdims=True)
    scalars_ref[...] = dots
    values = unpacked(dots, 8)
    alpha = values[0] / values[7]
    vertices = vertex_map(map_ref, spread_ref)
    coarse = total_ref[...] - alpha * jnp.sum(coarse_ref[...], axis=0, keepdims=True)
    image = image_ref[...]
    resid = rows_of(right_ref[...]) - alpha * image
    resid_ref[...] = resid
    elements = right_ref.shape[0]
    field = rows_of(jacobi_ref[...]) * resid + rows_of(
        prolonged(coarse, inverse_ref, vertices, elements, high_ref, low_ref)
    )
    smoothed_ref[...] = field
    dots_ref[...] = packed([total_of(resid * field), total_of(image * field)])
    gather_all(field, (pair_ref, slot_ref, face_ref), (local_ref, sent_ref, down_ref, up_ref))


def last_image_kernel(
    field_ref, back_ref, local_in_ref, received_ref, below_ref, above_ref,
    helmholtz_ref, pair_ref, slot_ref, face_ref,
    image_ref, dots_ref,
):
    image_ref[...] = image_of(
        field_ref, back_ref, local_in_ref, received_ref, below_ref, above_ref, helmholtz_ref,
        (pair_ref, slot_ref, face_ref),
    )
    dots = jnp.sum(received_ref[:, LANES:], axis=0, keepdims=True)
    dots_ref[...] = jnp.broadcast_to(dots, dots_ref.shape)


def final_kernel(
    old_ref, field_ref, resid_ref, old_image_ref, image_ref, scalars_ref, dots_ref,
    solution_ref, residual_ref,
):
    before = unpacked(scalars_ref[...], 8)
    now = unpacked(jnp.sum(dots_ref[...], axis=0, keepdims=True), 8)
    alpha = before[0] / before[7]
    beta = now[0] / before[0]
    curved = now[7] + beta * (2.0 * now[1] + beta * before[7])
    step = now[0] / curved
    old = old_ref[...]
    direction = field_ref[...] + beta * old
    solution_ref[...] = wide_of(alpha * old + step * direction)
    image = image_ref[...] + beta * old_image_ref[...]
    residual_ref[...] = wide_of(resid_ref[...] - step * image)


def call(kernel, outs, *args):
    return pl.pallas_call(
        kernel,
        out_shape=[jax.ShapeDtypeStruct(shape, F32) for shape in outs],
        in_specs=[pl.BlockSpec(memory_space=pltpu.VMEM)] * len(args),
        out_specs=[pl.BlockSpec(memory_space=pltpu.VMEM)] * len(outs),
        compiler_params=pltpu.CompilerParams(vmem_limit_bytes=24 * 1024 * 1024),
    )(*args)


def swap(array, axis):
    return lax.all_to_all(array, axis, split_axis=0, concat_axis=0, tiled=True)


def body(
    right_side,
    metric,
    helmholtz,
    jacobi,
    pair_list,
    shared_slots,
    face_points,
    coarse_map,
    coarse_inverse,
):
    elements = right_side.shape[0]
    peers = lax.axis_size("sub")
    groups = lax.axis_size("grp")
    t = {name: jnp.asarray(value) for name, value in tables(elements).items()}
    field = (4 * elements, LANES)
    local = pair_list.shape
    face = (1, face_points.shape[1])
    points = (pair_list, shared_slots, face_points)
    corners = (coarse_map, t["spread"], t["corner_high"], t["corner_low"])
    derivatives = (t["first"], t["first_back"], t["inner"], t["inner_back"])
    ups = [(g, g + 1) for g in range(groups - 1)]
    downs = [(g + 1, g) for g in range(groups - 1)]

    def exchange(sent, down, up):
        below = lax.ppermute(up, "grp", ups)
        above = lax.ppermute(down, "grp", downs)
        return swap(sent, "sub"), below, above

    (sent,) = call(first_kernel, [(peers, NC)], right_side, *corners)
    coarse = swap(sent, "sub")
    smoothed, total, dots, near, sent, down, up = call(
        smooth_kernel,
        [field, (1, NC), (1, LANES), local, (peers, LANES), face, face],
        right_side, jacobi, coarse, coarse_inverse, *corners, *points,
    )
    received, below, above = exchange(sent, down, up)
    apply_outs = [field, local, (peers, 2 * LANES), face, face]
    back, near, sent, down, up = call(
        apply_kernel, apply_outs,
        smoothed, dots, near, received, below, above, metric, helmholtz, *derivatives, *points,
    )
    received, below, above = exchange(sent, down, up)
    image, sent, dots = call(
        image_kernel,
        [field, (peers, NC), (groups, LANES)],
        smoothed, back, near, received, below, above, helmholtz, *corners, *points,
    )
    coarse = swap(sent, "sub")
    dots = swap(dots, "grp")
    second, resid, scalars, dots, near, sent, down, up = call(
        second_kernel,
        [field, field, (1, LANES), (1, LANES), local, (peers, LANES), face, face],
        right_side, image, jacobi, dots, total, coarse, coarse_inverse, *corners, *points,
    )
    received, below, above = exchange(sent, down, up)
    back, near, sent, down, up = call(
        apply_kernel, apply_outs,
        second, dots, near, received, below, above, metric, helmholtz, *derivatives, *points,
    )
    received, below, above = exchange(sent, down, up)
    second_image, dots = call(
        last_image_kernel,
        [field, (groups, LANES)],
        second, back, near, received, below, above, helmholtz, *points,
    )
    dots = swap(dots, "grp")
    return tuple(
        call(
            final_kernel,
            [right_side.shape, right_side.shape],
            smoothed, second, resid, image, second_image, scalars, dots,
        )
    )


def solution(mesh):
    in_specs = (
        P(("grp", "sub"), None),
        P(("grp", "sub"), None),
        P(("grp", "sub"), None),
        P(("grp", "sub"), None),
        P(None, ("grp", "sub")),
        P(("grp", "sub"), None, None),
        P(None, ("grp", "sub")),
        P(None, ("grp", "sub")),
        P("grp", None, None),
    )
    out_specs = (P(("grp", "sub"), None), P(("grp", "sub"), None))
    return jax.shard_map(body, mesh=mesh, in_specs=in_specs, out_specs=out_specs, check_vma=False)
```

time: 440 us -> 99.1 us (0.23); the launches traced: 433 us -> 98.2 us
  blocking collectives: 153 us -> 34.5 us
  local copies, waits for them, and re-layouts: 122 us -> 5.24 us
  other arithmetic: 105 us -> 0 us
  waiting for transfers between devices: 0.28 us -> 16.7 us
  matrix products: 9.32 us -> 0 us
  Pallas kernels: 0 us -> 8.95 us
  starting transfers between devices: 37.1 us -> 31.9 us
  between operations: 6.08 us -> 0.94 us
    psum x5 -> x0, blocking collectives: 153 us -> none  [the longest x2 82.2 us: residual_product(): return lax.psum(jnp.sum(resid * smoothed), ('grp', 'sub'))]
    gather x16 -> x0, local copies, waits for them, and re-layouts: 116 us -> none  [the longest x4 42.2 us: assemble(): sent = padded[slots]]
    scatter-add x20 -> x0, other arithmetic: 103 us -> none  [the longest x8 49.1 us: assemble(): flat.at[pair_list[0]].add(flat[pair_list[1]]).at[pair_list[1]]]
    all_to_all x0 -> x4, blocking collectives: none -> 34.5 us  [swap(): return lax.all_to_all(array, axis, split_axis=0, concat_axis=0, tiled=True)]
    ppermute x8, waiting for transfers between devices: 0.02 us -> 15.7 us  [the longest x4 15.7 us: exchange(): above = lax.ppermute(down, 'grp', downs)]
    dot_general x20 -> x0, matrix products: 9.32 us -> none  [the longest x2 2.05 us: precondition(): vertex = jnp.dot(resid, corner, precision=highest)]
    pallas_call x0 -> x8, Pallas kernels: none -> 8.95 us  [call(): pl.pallas_call(kernel, out_shape=[jax.ShapeDtypeStruct(shape, F32) for sh...]
  transfers between devices with their start and end apart: 12 -> 12, of which waited for: 1 -> 5; matrix products, arithmetic and copies ran while one was open for 16% -> 0% of each run, Pallas kernels for 0% -> 0%
where the time goes in v1:
time: 99.1 us; the launch traced here: 98.2 us
  blocking collectives  34.5 us (35%)
  starting transfers between devices  31.9 us (32%)
  waiting for transfers between devices  16.7 us (17%)
  Pallas kernels  8.95 us (9%)
  local copies, waits for them, and re-layouts  5.24 us (5%)
    all_to_all x4, blocking collectives, swap(): return lax.all_to_all(array, axis, split_axis=0, concat_axis=0, tiled=True)  34.5 us
    ppermute x4, waiting for transfers between devices, exchange(): above = lax.ppermute(down, 'grp', downs)  15.7 us
    all_to_all x4, starting transfers between devices, swap(): return lax.all_to_all(array, axis, split_axis=0, concat_axis=0, tiled=True)  14.8 us
    ppermute x4, starting transfers between devices, exchange(): below = lax.ppermute(up, 'grp', ups)  11.9 us
    pallas_call x8, Pallas kernels, call(): pl.pallas_call(kernel, out_shape=[jax.ShapeDtypeStruct(shape, F32) for sh...  8.95 us
    ppermute x4, starting transfers between devices, exchange(): above = lax.ppermute(down, 'grp', downs)  5.17 us
    unnamed x42, local copies, waits for them, and re-layouts  4.03 us
  transfers between devices with their start and end apart: 12, of which 5 were waited for; matrix products, arithmetic and copies ran while one was open for 0% of the time, Pallas kernels for 0%

profile of v1, /device:TPU:0, one launch (start us, length us, event | category | flops | bytes accessed | tf_op | source)
XLA Modules:
  0.0 98.2 jit_solution(7970183728110086270)
XLA Ops:
  0.6 0.0 copy-start.15
  0.6 0.7 copy-done.15
  1.3 0.9 copy-done
  2.2 0.9 copy-done.2
  3.1 0.8 copy-done.9
  3.9 0.7 copy-done.16
  4.6 0.0 copy-start.14
  4.6 0.0 copy-start.7
  4.6 0.0 copy-start.18
  4.6 0.0 copy-start.19
  4.6 0.4 shard_map.167
  5.1 9.8 %all_to_all.88 = f32[8,1,64]{2,1,0:T(1,128)S(1)} all-to-all(f32[8,1,64]{2,1,0:T(1,128)S(1)} %bitcast.37), channel_id=1, replica_groups=mesh['grp'=4,'sub'=8] {'sub'}, dimensions={0} | all-to-all | bytes 4096 | tf_op jit(solution)/shard_map/all_to_all | solution.py:447
  14.9 0.0 copy-done.8
  14.9 0.0 copy-done.11
  14.9 0.0 copy-done.12
  14.9 0.0 copy-done.13
  14.9 0.0 copy-done.14
  14.9 0.0 copy-start.4
  14.9 0.0 copy-start.5
  14.9 1.4 %shard_map.168 = (f32[64,128]{1,0:T(8,128)S(1)}, f32[1,64]{1,0:T(1,128)S(1)}, f32[1,128]{1,0:T(1,128)S(1)}, f32[2,1024]{1,0:T(2,128)S(1)}, f32[8,128]{1,0:T(8,12...) custom-call(f32[16,512]{1,0:T(8,128)S(1)} %copy-done.9, f32[16,512]{1,0:T(8,128)S(1)} %copy-done.13, ...), custom_call_target="tpu_custom_call" | custom-call | tf_op jit(solution)/shard_map/pallas_call | solution.py:437
  16.4 3.3 %all-to-all-start.1 = ((f32[8,1,128]{2,1,0:T(1,128)}), f32[8,1,128]{2,1,0:T(1,128)S(1)}, u32[]{:S(2)}, u32[]{:S(2)}) async-start(f32[8,1,128]{2,1,0:T(1,128)} %bitcast.4), calls=%async_computation.1 | async-start | bytes 8192 | tf_op jit(solution)/shard_map/all_to_all | solution.py:447
  19.7 3.5 %collective-permute-start = (f32[1,512]{1,0:T(1,128)S(1)}, f32[1,512]{1,0:T(1,128)S(1)}, u32[]{:S(2)}, u32[]{:S(2)}) collective-permute-start(f32[1,512]{1,0:T(1,128)S(1)} %get-tuple-element.36), channel_id=1, source_target_pairs={{0,8},{8,16},{16,24},{1,9},{9,17},{17,25},{2,10},{10,18},{18,26},{... | collective-permute-start | bytes 6152 | tf_op jit(solution)/shard_map/ppermute | solution.py:475
  23.2 1.3 %collective-permute-start.1 = (f32[1,512]{1,0:T(1,128)S(1)}, f32[1,512]{1,0:T(1,128)S(1)}, u32[]{:S(2)}, u32[]{:S(2)}) collective-permute-start(f32[1,512]{1,0:T(1,128)S(1)} %get-tuple-element.37), channel_id=1, source_target_pairs={{8,0},{16,8},{24,16},{9,1},{17,9},{25,17},{10,2},{18,10},{26,18},{... | collective-permute-start | bytes 6152 | tf_op jit(solution)/shard_map/ppermute | solution.py:476
  24.5 0.0 collective-permute-done.below_ref
  24.5 4.2 %collective-permute-done.1.above_ref = f32[1,512]{1,0:T(1,128)S(1)} collective-permute-done((f32[1,512]{1,0:T(1,128)S(1)}, f32[1,512]{1,0:T(1,128)S(1)}, u32[]{:S(2)}, u32[]{:S(2)}) %collective-permute-start.1) | collective-permute-done | bytes 2080 | tf_op jit(solution)/shard_map/ppermute | solution.py:476
  28.7 0.0 all-to-all-done.1
  28.7 0.0 copy-done.7
  28.7 0.0 copy-done.18
  28.7 0.0 copy-done.19
  28.7 0.0 copy-done.6
  28.7 0.0 copy-start.1
  28.7 0.0 copy-start.3
  28.8 1.6 %shard_map.169 = (f32[64,128]{1,0:T(8,128)S(1)}, f32[2,1024]{1,0:T(2,128)S(1)}, f32[8,256]{1,0:T(8,128)S(1)}, f32[1,512]{1,0:T(1,128)S(1)}, f32[1,512]{1,0:T(1,128)S(1)}) custom-call(f32[64,128]{1,0:T(8,128)S(1)} %get-tuple-element.32.field_ref.old_ref, f32[1,128]{1,0:T(1,128)S(1)} %get-tuple-element.33.dots_in_ref, ...), custom_call_target="tpu_custom_call" | custom-call | tf_op jit(solution)/shard_map/pallas_call | solution.py:437
  30.3 0.6 copy.20
  30.9 4.1 %all-to-all-start.2 = ((f32[8,1,256]{2,1,0:T(1,128)}), f32[8,1,256]{2,1,0:T(1,128)S(1)}, u32[]{:S(2)}, u32[]{:S(2)}) async-start(f32[8,1,256]{2,1,0:T(1,128)} %copy.20), calls=%async_computation.2 | async-start | bytes 16384 | tf_op jit(solution)/shard_map/all_to_all | solution.py:447
  35.0 3.5 %collective-permute-start.2 = (f32[1,512]{1,0:T(1,128)S(1)}, f32[1,512]{1,0:T(1,128)S(1)}, u32[]{:S(2)}, u32[]{:S(2)}) collective-permute-start(f32[1,512]{1,0:T(1,128)S(1)} %get-tuple-element.41), channel_id=1, source_target_pairs={{0,8},{8,16},{16,24},{1,9},{9,17},{17,25},{2,10},{10,18},{18,26},{... | collective-permute-start | bytes 6152 | tf_op jit(solution)/shard_map/ppermute | solution.py:475
  38.5 1.3 %collective-permute-start.3 = (f32[1,512]{1,0:T(1,128)S(1)}, f32[1,512]{1,0:T(1,128)S(1)}, u32[]{:S(2)}, u32[]{:S(2)}) collective-permute-start(f32[1,512]{1,0:T(1,128)S(1)} %get-tuple-element.42), channel_id=1, source_target_pairs={{8,0},{16,8},{24,16},{9,1},{17,9},{25,17},{10,2},{18,10},{26,18},{... | collective-permute-start | bytes 6152 | tf_op jit(solution)/shard_map/ppermute | solution.py:476
  39.8 0.0 all-to-all-done.2
  39.8 0.0 copy-start.17
  39.8 0.0 collective-permute-done.2.below_ref
  39.9 4.1 %collective-permute-done.3.above_ref = f32[1,512]{1,0:T(1,128)S(1)} collective-permute-done((f32[1,512]{1,0:T(1,128)S(1)}, f32[1,512]{1,0:T(1,128)S(1)}, u32[]{:S(2)}, u32[]{:S(2)}) %collective-permute-start.3) | collective-permute-done | bytes 2080 | tf_op jit(solution)/shard_map/ppermute | solution.py:476
  44.0 0.0 copy-done.17
  44.0 0.0 copy-start.10
  44.0 1.1 %shard_map.170 = (f32[64,128]{1,0:T(8,128)S(1)}, f32[8,64]{1,0:T(8,128)S(1)}, f32[4,128]{1,0:T(4,128)S(1)}) custom-call(f32[64,128]{1,0:T(8,128)S(1)} %get-tuple-element.32.field_ref.old_ref, f32[64,128]{1,0:T(8,128)S(1)} %get-tuple-element.38.back_ref, f32[2,1024]{1,0:T(2,128)S(1)} %get-tuple-element.39.local_in_ref, f32[8,256]{1,0:T(8,128)S(1)} %bitcast.32, ...), custom_call_target="tpu_custom_call" | custom-call | tf_op jit(solution)/shard_map/pallas_call | solution.py:437
  45.1 8.7 %all_to_all.89 = f32[8,1,64]{2,1,0:T(1,128)S(1)} all-to-all(f32[8,1,64]{2,1,0:T(1,128)S(1)} %bitcast.43), channel_id=1, replica_groups=mesh['grp'=4,'sub'=8] {'sub'}, dimensions={0} | all-to-all | bytes 4096 | tf_op jit(solution)/shard_map/all_to_all | solution.py:447
  53.8 8.2 %all_to_all.90 = f32[4,1,128]{2,1,0:T(1,128)S(1)} all-to-all(f32[4,1,128]{2,1,0:T(1,128)S(1)} %bitcast.44), channel_id=1, replica_groups=mesh['grp'=4,'sub'=8] {'grp'}, dimensions={0} | all-to-all | bytes 4096 | tf_op jit(solution)/shard_map/all_to_all | solution.py:447
  61.9 1.5 %shard_map.171 = (f32[64,128]{1,0:T(8,128)S(1)}, f32[64,128]{1,0:T(8,128)S(1)}, f32[1,128]{1,0:T(1,128)S(1)}, f32[1,128]{1,0:T(1,128)S(1)}, f32[2,1024]{1,0:T(2,...) custom-call(f32[16,512]{1,0:T(8,128)S(1)} %copy-done.10, ...), custom_call_target="tpu_custom_call" | custom-call | tf_op jit(solution)/shard_map/pallas_call | solution.py:437
  63.4 3.3 %all-to-all-start.5 = ((f32[8,1,128]{2,1,0:T(1,128)}), f32[8,1,128]{2,1,0:T(1,128)S(1)}, u32[]{:S(2)}, u32[]{:S(2)}) async-start(f32[8,1,128]{2,1,0:T(1,128)} %bitcast.14), calls=%async_computation.5 | async-start | bytes 8192 | tf_op jit(solution)/shard_map/all_to_all | solution.py:447
  66.7 2.5 %collective-permute-start.4 = (f32[1,512]{1,0:T(1,128)S(1)}, f32[1,512]{1,0:T(1,128)S(1)}, u32[]{:S(2)}, u32[]{:S(2)}) collective-permute-start(f32[1,512]{1,0:T(1,128)S(1)} %get-tuple-element.52), channel_id=1, source_target_pairs={{0,8},{8,16},{16,24},{1,9},{9,17},{17,25},{2,10},{10,18},{18,26},{... | collective-permute-start | bytes 6152 | tf_op jit(solution)/shard_map/ppermute | solution.py:475
  69.3 1.3 %collective-permute-start.5 = (f32[1,512]{1,0:T(1,128)S(1)}, f32[1,512]{1,0:T(1,128)S(1)}, u32[]{:S(2)}, u32[]{:S(2)}) collective-permute-start(f32[1,512]{1,0:T(1,128)S(1)} %get-tuple-element.53), channel_id=1, source_target_pairs={{8,0},{16,8},{24,16},{9,1},{17,9},{25,17},{10,2},{18,10},{26,18},{... | collective-permute-start | bytes 6152 | tf_op jit(solution)/shard_map/ppermute | solution.py:476
  70.6 0.0 collective-permute-done.4.below_ref
  70.6 4.2 %collective-permute-done.5.above_ref = f32[1,512]{1,0:T(1,128)S(1)} collective-permute-done((f32[1,512]{1,0:T(1,128)S(1)}, f32[1,512]{1,0:T(1,128)S(1)}, u32[]{:S(2)}, u32[]{:S(2)}) %collective-permute-start.5) | collective-permute-done | bytes 2080 | tf_op jit(solution)/shard_map/ppermute | solution.py:476
  74.7 0.0 all-to-all-done.5
  74.7 1.6 %shard_map.172 = (f32[64,128]{1,0:T(8,128)S(1)}, f32[2,1024]{1,0:T(2,128)S(1)}, f32[8,256]{1,0:T(8,128)S(1)}, f32[1,512]{1,0:T(1,128)S(1)}, f32[1,512]{1,0:T(1,128)S(1)}) custom-call(f32[64,128]{1,0:T(8,128)S(1)} %get-tuple-element.47.field_ref, f32[1,128]{1,0:T(1,128)S(1)} %get-tuple-element.49.dots_in_ref, f32[2,1024]{1,0:T(2,128)S(1)} %get-tuple-element.50.local_in_ref, ...), custom_call_target="tpu_custom_call" | custom-call | tf_op jit(solution)/shard_map/pallas_call | solution.py:437
  76.3 0.6 copy.24
  76.9 4.1 %all-to-all-start.6 = ((f32[8,1,256]{2,1,0:T(1,128)}), f32[8,1,256]{2,1,0:T(1,128)S(1)}, u32[]{:S(2)}, u32[]{:S(2)}) async-start(f32[8,1,256]{2,1,0:T(1,128)} %copy.24), calls=%async_computation.6 | async-start | bytes 16384 | tf_op jit(solution)/shard_map/all_to_all | solution.py:447
  81.0 2.5 %collective-permute-start.6 = (f32[1,512]{1,0:T(1,128)S(1)}, f32[1,512]{1,0:T(1,128)S(1)}, u32[]{:S(2)}, u32[]{:S(2)}) collective-permute-start(f32[1,512]{1,0:T(1,128)S(1)} %get-tuple-element.57), channel_id=1, source_target_pairs={{0,8},{8,16},{16,24},{1,9},{9,17},{17,25},{2,10},{10,18},{18,26},{... | collective-permute-start | bytes 6152 | tf_op jit(solution)/shard_map/ppermute | solution.py:475
  83.5 1.3 %collective-permute-start.7 = (f32[1,512]{1,0:T(1,128)S(1)}, f32[1,512]{1,0:T(1,128)S(1)}, u32[]{:S(2)}, u32[]{:S(2)}) collective-permute-start(f32[1,512]{1,0:T(1,128)S(1)} %get-tuple-element.58), channel_id=1, source_target_pairs={{8,0},{16,8},{24,16},{9,1},{17,9},{25,17},{10,2},{18,10},{26,18},{... | collective-permute-start | bytes 6152 | tf_op jit(solution)/shard_map/ppermute | solution.py:476
  84.8 0.9 all-to-all-done.6
  85.7 0.0 collective-permute-done.6.below_ref
  85.7 3.2 %collective-permute-done.7.above_ref = f32[1,512]{1,0:T(1,128)S(1)} collective-permute-done((f32[1,512]{1,0:T(1,128)S(1)}, f32[1,512]{1,0:T(1,128)S(1)}, u32[]{:S(2)}, u32[]{:S(2)}) %collective-permute-start.7) | collective-permute-done | bytes 2080 | tf_op jit(solution)/shard_map/ppermute | solution.py:476
  88.9 0.7 shard_map.173
  89.6 7.9 %all_to_all.91 = f32[4,1,128]{2,1,0:T(1,128)S(1)} all-to-all(f32[4,1,128]{2,1,0:T(1,128)S(1)} %bitcast.45), channel_id=1, replica_groups=mesh['grp'=4,'sub'=8] {'grp'}, dimensions={0} | all-to-all | bytes 4096 | tf_op jit(solution)/shard_map/all_to_all | solution.py:447
  97.5 0.7 shard_map.174
  (16 shorter events, 0.0 us)
Async XLA Ops:
  0.6 0.7 copy-start.15
  1.3 0.9 copy-start
  2.2 0.9 copy-start.2
  3.1 0.8 copy-start.9
  3.9 0.7 copy-start.16
  4.6 10.3 %copy-start.8 = (s32[2,1024]{1,0:T(2,128)S(1)}, s32[2,1024]{1,0:T(2,128)}, u32[]{:S(2)}) copy-start(s32[2,1024]{1,0:T(2,128)} %pair_ref.11) | copy-start | bytes 24580
  4.6 10.3 %copy-start.11 = (s32[1,8,128]{2,1,0:T(8,128)S(1)}, s32[1,8,128]{2,1,0:T(8,128)}, u32[]{:S(2)}) copy-start(s32[1,8,128]{2,1,0:T(8,128)} %slot_ref.11) | copy-start | bytes 12292
  4.6 10.3 %copy-start.12 = (s32[2,512]{1,0:T(2,128)S(1)}, s32[2,512]{1,0:T(2,128)}, u32[]{:S(2)}) copy-start(s32[2,512]{1,0:T(2,128)} %face_ref.11) | copy-start | bytes 12292
  4.6 10.3 %copy-start.13 = (f32[16,512]{1,0:T(8,128)S(1)}, f32[16,512]{1,0:T(8,128)}, u32[]{:S(2)}) copy-start(f32[16,512]{1,0:T(8,128)} %jacobi_ref.3) | copy-start | bytes 98308
  4.6 10.3 %copy-start.14 = (f32[1,64,64]{2,1,0:T(8,128)S(1)}, f32[1,64,64]{2,1,0:T(8,128)}, u32[]{:S(2)}) copy-start(f32[1,64,64]{2,1,0:T(8,128)} %inverse_ref.3) | copy-start | bytes 49156
  4.6 24.1 %copy-start.7 = (f32[16,1536]{1,0:T(8,128)S(1)}, f32[16,1536]{1,0:T(8,128)}, u32[]{:S(2)}) copy-start(f32[16,1536]{1,0:T(8,128)} %metric_ref.3) | copy-start | bytes 294916
  4.6 24.1 %copy-start.18 = (f32[32,128]{1,0:T(8,128)S(1)}, f32[32,128]{1,0:T(8,128)}, u32[]{:S(2)}) copy-start(f32[32,128]{1,0:T(8,128)} %constant.17.clone.first_back_ref) | copy-start | bytes 49156
  4.6 24.1 %copy-start.19 = (f32[32,128]{1,0:T(8,128)S(1)}, f32[32,128]{1,0:T(8,128)}, u32[]{:S(2)}) copy-start(f32[32,128]{1,0:T(8,128)} %constant.16.clone.first_ref) | copy-start | bytes 49156
  5.1 23.6 %copy-start.6 = (f32[16,512]{1,0:T(8,128)S(1)}, f32[16,512]{1,0:T(8,128)}, u32[]{:S(2)}) copy-start(f32[16,512]{1,0:T(8,128)} %helmholtz_ref.7) | copy-start | bytes 98308
  14.9 13.8 %copy-start.4 = (bf16[768,128]{1,0:T(8,128)(2,1)S(1)}, bf16[768,128]{1,0:T(8,128)(2,1)}, u32[]{:S(2)}) copy-start(bf16[768,128]{1,0:T(8,128)(2,1)} %constant.15.clone.inner_back_ref) | copy-start | bytes 589828
  14.9 13.8 %copy-start.5 = (bf16[384,256]{1,0:T(8,128)(2,1)S(1)}, bf16[384,256]{1,0:T(8,128)(2,1)}, u32[]{:S(2)}) copy-start(bf16[384,256]{1,0:T(8,128)(2,1)} %constant.14.clone.inner_ref) | copy-start | bytes 589828
  16.4 12.3 %all-to-all-start.1 = ((f32[8,1,128]{2,1,0:T(1,128)}), f32[8,1,128]{2,1,0:T(1,128)S(1)}, u32[]{:S(2)}, u32[]{:S(2)}) async-start(f32[8,1,128]{2,1,0:T(1,128)} %bitcast.4), calls=%async_computation.1 | async-start | bytes 8192 | tf_op jit(solution)/shard_map/all_to_all | solution.py:447
  19.7 4.8 %collective-permute-start = (f32[1,512]{1,0:T(1,128)S(1)}, f32[1,512]{1,0:T(1,128)S(1)}, u32[]{:S(2)}, u32[]{:S(2)}) collective-permute-start(f32[1,512]{1,0:T(1,128)S(1)} %get-tuple-element.36), channel_id=1, source_target_pairs={{0,8},{8,16},{16,24},{1,9},{9,17},{17,25},{2,10},{10,18},{18,26},{... | collective-permute-start | bytes 6152 | tf_op jit(solution)/shard_map/ppermute | solution.py:475
  23.2 5.5 %collective-permute-start.1 = (f32[1,512]{1,0:T(1,128)S(1)}, f32[1,512]{1,0:T(1,128)S(1)}, u32[]{:S(2)}, u32[]{:S(2)}) collective-permute-start(f32[1,512]{1,0:T(1,128)S(1)} %get-tuple-element.37), channel_id=1, source_target_pairs={{8,0},{16,8},{24,16},{9,1},{17,9},{25,17},{10,2},{18,10},{26,18},{... | collective-permute-start | bytes 6152 | tf_op jit(solution)/shard_map/ppermute | solution.py:476
  28.7 15.3 %copy-start.1 = (bf16[128,512]{1,0:T(8,128)(2,1)S(1)}, bf16[128,512]{1,0:T(8,128)(2,1)}, u32[]{:S(2)}) copy-start(bf16[128,512]{1,0:T(8,128)(2,1)} %constant.19.clone.low_ref) | copy-start | bytes 393220
  28.7 15.3 %copy-start.3 = (bf16[128,512]{1,0:T(8,128)(2,1)S(1)}, bf16[128,512]{1,0:T(8,128)(2,1)}, u32[]{:S(2)}) copy-start(bf16[128,512]{1,0:T(8,128)(2,1)} %constant.18.clone.high_ref) | copy-start | bytes 393220
  30.9 8.9 %all-to-all-start.2 = ((f32[8,1,256]{2,1,0:T(1,128)}), f32[8,1,256]{2,1,0:T(1,128)S(1)}, u32[]{:S(2)}, u32[]{:S(2)}) async-start(f32[8,1,256]{2,1,0:T(1,128)} %copy.20), calls=%async_computation.2 | async-start | bytes 16384 | tf_op jit(solution)/shard_map/all_to_all | solution.py:447
  35.0 4.8 %collective-permute-start.2 = (f32[1,512]{1,0:T(1,128)S(1)}, f32[1,512]{1,0:T(1,128)S(1)}, u32[]{:S(2)}, u32[]{:S(2)}) collective-permute-start(f32[1,512]{1,0:T(1,128)S(1)} %get-tuple-element.41), channel_id=1, source_target_pairs={{0,8},{8,16},{16,24},{1,9},{9,17},{17,25},{2,10},{10,18},{18,26},{... | collective-permute-start | bytes 6152 | tf_op jit(solution)/shard_map/ppermute | solution.py:475
  38.5 5.5 %collective-permute-start.3 = (f32[1,512]{1,0:T(1,128)S(1)}, f32[1,512]{1,0:T(1,128)S(1)}, u32[]{:S(2)}, u32[]{:S(2)}) collective-permute-start(f32[1,512]{1,0:T(1,128)S(1)} %get-tuple-element.42), channel_id=1, source_target_pairs={{8,0},{16,8},{24,16},{9,1},{17,9},{25,17},{10,2},{18,10},{26,18},{... | collective-permute-start | bytes 6152 | tf_op jit(solution)/shard_map/ppermute | solution.py:476
  39.8 4.2 %copy-start.17 = (s32[8,16]{1,0:T(8,128)S(1)}, s32[8,16]{1,0:T(8,128)}, u32[]{:S(2)}) copy-start(s32[8,16]{1,0:T(8,128)} %map_ref.7) | copy-start | bytes 1540
  44.0 17.9 %copy-start.10 = (f32[16,512]{1,0:T(8,128)S(1)}, f32[16,512]{1,0:T(8,128)}, u32[]{:S(2)}) copy-start(f32[16,512]{1,0:T(8,128)} %right_ref.5) | copy-start | bytes 98308
  63.4 11.3 %all-to-all-start.5 = ((f32[8,1,128]{2,1,0:T(1,128)}), f32[8,1,128]{2,1,0:T(1,128)S(1)}, u32[]{:S(2)}, u32[]{:S(2)}) async-start(f32[8,1,128]{2,1,0:T(1,128)} %bitcast.14), calls=%async_computation.5 | async-start | bytes 8192 | tf_op jit(solution)/shard_map/all_to_all | solution.py:447
  66.7 3.8 %collective-permute-start.4 = (f32[1,512]{1,0:T(1,128)S(1)}, f32[1,512]{1,0:T(1,128)S(1)}, u32[]{:S(2)}, u32[]{:S(2)}) collective-permute-start(f32[1,512]{1,0:T(1,128)S(1)} %get-tuple-element.52), channel_id=1, source_target_pairs={{0,8},{8,16},{16,24},{1,9},{9,17},{17,25},{2,10},{10,18},{18,26},{... | collective-permute-start | bytes 6152 | tf_op jit(solution)/shard_map/ppermute | solution.py:475
  69.3 5.5 %collective-permute-start.5 = (f32[1,512]{1,0:T(1,128)S(1)}, f32[1,512]{1,0:T(1,128)S(1)}, u32[]{:S(2)}, u32[]{:S(2)}) collective-permute-start(f32[1,512]{1,0:T(1,128)S(1)} %get-tuple-element.53), channel_id=1, source_target_pairs={{8,0},{16,8},{24,16},{9,1},{17,9},{25,17},{10,2},{18,10},{26,18},{... | collective-permute-start | bytes 6152 | tf_op jit(solution)/shard_map/ppermute | solution.py:476
  76.9 8.8 %all-to-all-start.6 = ((f32[8,1,256]{2,1,0:T(1,128)}), f32[8,1,256]{2,1,0:T(1,128)S(1)}, u32[]{:S(2)}, u32[]{:S(2)}) async-start(f32[8,1,256]{2,1,0:T(1,128)} %copy.24), calls=%async_computation.6 | async-start | bytes 16384 | tf_op jit(solution)/shard_map/all_to_all | solution.py:447
  81.0 4.7 %collective-permute-start.6 = (f32[1,512]{1,0:T(1,128)S(1)}, f32[1,512]{1,0:T(1,128)S(1)}, u32[]{:S(2)}, u32[]{:S(2)}) collective-permute-start(f32[1,512]{1,0:T(1,128)S(1)} %get-tuple-element.57), channel_id=1, source_target_pairs={{0,8},{8,16},{16,24},{1,9},{9,17},{17,25},{2,10},{10,18},{18,26},{... | collective-permute-start | bytes 6152 | tf_op jit(solution)/shard_map/ppermute | solution.py:475
  83.5 5.5 %collective-permute-start.7 = (f32[1,512]{1,0:T(1,128)S(1)}, f32[1,512]{1,0:T(1,128)S(1)}, u32[]{:S(2)}, u32[]{:S(2)}) collective-permute-start(f32[1,512]{1,0:T(1,128)S(1)} %get-tuple-element.58), channel_id=1, source_target_pairs={{8,0},{16,8},{24,16},{9,1},{17,9},{25,17},{10,2},{18,10},{26,18},{... | collective-permute-start | bytes 6152 | tf_op jit(solution)/shard_map/ppermute | solution.py:476

commit v2 on v1

--- a/solution.py
+++ b/solution.py
@@ -11,6 +11,8 @@
 POINTS = 512
 LANES = 128
 STEP = 256
+FACE_ROWS = 4
+ROWS = FACE_ROWS + 1
 F32 = jnp.float32
 BF16 = jnp.bfloat16
 NT = (((1,), (1,)), ((), ()))
@@ -158,9 +160,18 @@
     return pairs, slots, faces
 
 
-def gather_all(field, refs, outs):
+def halves(wide):
+    return [wide[:, at : at + LANES] for at in range(0, wide.shape[1], LANES)]
+
+
+def own_group(devices, peers, away=0):
+    shape = (devices, LANES)
+    return lax.broadcasted_iota(jnp.int32, shape, 0) // peers - lax.axis_index("grp") == away
+
+
+def gather_all(field, refs, outs, extra):
     pair_ref, slot_ref, face_ref = refs
-    local_ref, sent_ref, down_ref, up_ref = outs
+    local_ref, sent_ref = outs
     pairs, slots, faces = index_chunks(pair_ref, slot_ref, face_ref, field.shape[0] // 4)
     values = gather(field, pairs + slots + faces)
     count = pair_ref.shape[1] // STEP
@@ -168,23 +179,49 @@
         local_ref[0:1, k * STEP : (k + 1) * STEP] = values[k]
         local_ref[1:2, k * STEP : (k + 1) * STEP] = values[count + k]
     values = values[2 * count :]
-    for k in range(len(slots)):
-        sent_ref[2 * k : 2 * k + 1, 0:LANES] = values[k][:, :LANES]
-        sent_ref[2 * k + 1 : 2 * k + 2, 0:LANES] = values[k][:, LANES:]
+    peers = slot_ref.shape[1]
+    devices = sent_ref.shape[0] // ROWS
+    shared = jnp.concatenate([row for pair in values[: len(slots)] for row in halves(pair)], axis=0)
+    shared = jnp.concatenate([shared] * (devices // peers), axis=0)
     values = values[len(slots) :]
     count = face_ref.shape[1] // STEP
-    for k in range(count):
-        down_ref[0:1, k * STEP : (k + 1) * STEP] = values[k]
-        up_ref[0:1, k * STEP : (k + 1) * STEP] = values[count + k]
-
-
-def assembled(field, refs, local, received, below, above):
+    down = [row for pair in values[:count] for row in halves(pair)]
+    up = [row for pair in values[count:] for row in halves(pair)]
+    above = own_group(devices, peers, 1)
+    for r in range(FACE_ROWS):
+        rows = jnp.where(above, up[r], down[r])
+        if r == 0:
+            rows = jnp.where(own_group(devices, peers), shared, rows)
+        sent_ref[pl.ds(r, devices, ROWS), :] = rows
+    sent_ref[pl.ds(FACE_ROWS, devices, ROWS), :] = jnp.broadcast_to(extra, (devices, LANES))
+
+
+def terms(received_ref):
+    devices = received_ref.shape[0] // ROWS
+    return jnp.sum(received_ref[pl.ds(FACE_ROWS, devices, ROWS), :], axis=0, keepdims=True)
+
+
+def assembled(field, refs, local, received_ref):
     pair_ref, slot_ref, face_ref = refs
     pairs, slots, faces = index_chunks(pair_ref, slot_ref, face_ref, field.shape[0] // 4)
     values = cut(local[1:2]) + cut(local[0:1])
-    for at in range(0, received.shape[0], 2):
-        values.append(jnp.concatenate([received[at : at + 1], received[at + 1 : at + 2]], axis=1))
-    values = values + cut(below) + cut(above)
+    peers = slot_ref.shape[1]
+    devices = received_ref.shape[0] // ROWS
+    rows = [received_ref[pl.ds(r, devices, ROWS), :] for r in range(FACE_ROWS)]
+    mine = jnp.where(own_group(devices, peers), rows[0], 0.0)
+    shared = mine[:peers]
+    for g in range(1, devices // peers):
+        shared = shared + mine[g * peers : (g + 1) * peers]
+    for at in range(0, peers, 2):
+        values.append(jnp.concatenate([shared[at : at + 1], shared[at + 1 : at + 2]], axis=1))
+    place = lax.broadcasted_iota(jnp.int32, (devices, LANES), 0)
+    here = lax.axis_index("grp") * peers + lax.axis_index("sub")
+    for away in (-peers, peers):
+        side = [
+            jnp.sum(jnp.where(place - here == away, part, 0.0), axis=0, keepdims=True)
+            for part in rows
+        ]
+        values = values + cut(jnp.concatenate(side, axis=1))
     return field + scatter(field.shape[0], pairs + slots + faces, values)
 
 
@@ -311,32 +348,29 @@
 def smooth_kernel(
     right_ref, jacobi_ref, coarse_ref, inverse_ref, map_ref, spread_ref, high_ref, low_ref,
     pair_ref, slot_ref, face_ref,
-    smoothed_ref, total_ref, dots_ref, local_ref, sent_ref, down_ref, up_ref,
+    smoothed_ref, dots_ref, local_ref, sent_ref,
 ):
     vertices = vertex_map(map_ref, spread_ref)
     coarse = jnp.sum(coarse_ref[...], axis=0, keepdims=True)
-    total_ref[...] = coarse
     resid = right_ref[...]
     smoothed = jacobi_ref[...] * resid + prolonged(
         coarse, inverse_ref, vertices, resid.shape[0], high_ref, low_ref
     )
-    dots_ref[...] = packed([total_of(resid * smoothed)])
+    dots = packed([total_of(resid * smoothed)])
+    dots_ref[...] = dots
     field = rows_of(smoothed)
     smoothed_ref[...] = field
-    gather_all(field, (pair_ref, slot_ref, face_ref), (local_ref, sent_ref, down_ref, up_ref))
+    gather_all(field, (pair_ref, slot_ref, face_ref), (local_ref, sent_ref), dots)
 
 
 def apply_kernel(
-    field_ref, dots_in_ref, local_in_ref, received_ref, below_ref, above_ref,
-    metric_ref, helmholtz_ref, first_ref, first_back_ref, inner_ref, inner_back_ref,
+    field_ref, dots_in_ref, local_in_ref, received_ref, metric_ref, helmholtz_ref, first_ref, first_back_ref, inner_ref, inner_back_ref,
     pair_ref, slot_ref, face_ref,
-    back_ref, local_ref, sent_ref, down_ref, up_ref,
+    back_ref, local_ref, sent_ref,
 ):
     refs = (pair_ref, slot_ref, face_ref)
     field = field_ref[...]
-    summed = assembled(
-        field, refs, local_in_ref[...], received_ref[...], below_ref[...], above_ref[...]
-    )
+    summed = assembled(field, refs, local_in_ref[...], received_ref)
     back, energy = stiffness(
         summed, metric_ref, first_ref, first_back_ref, inner_ref, inner_back_ref
     )
@@ -345,83 +379,62 @@
     lane = lax.broadcasted_iota(jnp.int32, dots.shape, 1)
     dots = jnp.where(lane == 7, total_of(energy), dots)
     back_ref[...] = back
-    gather_all(back, refs, (local_ref, sent_ref, down_ref, up_ref))
-    sent_ref[:, LANES:] = jnp.broadcast_to(dots, (sent_ref.shape[0], LANES))
-
-
-def image_of(field_ref, back_ref, local_in_ref, received_ref, below_ref, above_ref, helmholtz_ref, refs):
-    summed = assembled(
-        back_ref[...],
-        refs,
-        local_in_ref[...],
-        received_ref[:, :LANES],
-        below_ref[...],
-        above_ref[...],
-    )
+    gather_all(back, refs, (local_ref, sent_ref), dots)
+
+
+def image_of(field_ref, back_ref, local_in_ref, received_ref, helmholtz_ref, refs):
+    summed = assembled(back_ref[...], refs, local_in_ref[...], received_ref)
     return summed + rows_of(helmholtz_ref[...]) * field_ref[...]
 
 
 def image_kernel(
-    field_ref, back_ref, local_in_ref, received_ref, below_ref, above_ref,
-    helmholtz_ref, map_ref, spread_ref, high_ref, low_ref,
-    pair_ref, slot_ref, face_ref,
-    image_ref, sent_ref, dots_ref,
-):
-    image = image_of(
-        field_ref, back_ref, local_in_ref, received_ref, below_ref, above_ref, helmholtz_ref,
-        (pair_ref, slot_ref, face_ref),
-    )
-    image_ref[...] = image
-    vertices = vertex_map(map_ref, spread_ref)
-    part = coarse_part(wide_of(image), vertices, high_ref, low_ref)
-    sent_ref[...] = jnp.broadcast_to(part, sent_ref.shape)
-    dots = jnp.sum(received_ref[:, LANES:], axis=0, keepdims=True)
-    dots_ref[...] = jnp.broadcast_to(dots, dots_ref.shape)
-
-
-def second_kernel(
-    right_ref, image_ref, jacobi_ref, dots_in_ref, total_ref, coarse_ref, inverse_ref,
+    right_ref, field_ref, back_ref, local_in_ref, received_ref, helmholtz_ref,
     map_ref, spread_ref, high_ref, low_ref,
     pair_ref, slot_ref, face_ref,
-    smoothed_ref, resid_ref, scalars_ref, dots_ref, local_ref, sent_ref, down_ref, up_ref,
+    image_ref, resid_ref, scalars_ref, sent_ref,
 ):
-    dots = jnp.sum(dots_in_ref[...], axis=0, keepdims=True)
+    dots = terms(received_ref)
     scalars_ref[...] = dots
     values = unpacked(dots, 8)
     alpha = values[0] / values[7]
-    vertices = vertex_map(map_ref, spread_ref)
-    coarse = total_ref[...] - alpha * jnp.sum(coarse_ref[...], axis=0, keepdims=True)
-    image = image_ref[...]
+    image = image_of(
+        field_ref, back_ref, local_in_ref, received_ref, helmholtz_ref,
+        (pair_ref, slot_ref, face_ref),
+    )
+    image_ref[...] = image
     resid = rows_of(right_ref[...]) - alpha * image
     resid_ref[...] = resid
-    elements = right_ref.shape[0]
+    vertices = vertex_map(map_ref, spread_ref)
+    part = coarse_part(wide_of(resid), vertices, high_ref, low_ref)
+    sent_ref[...] = jnp.broadcast_to(part, sent_ref.shape)
+
+
+def second_kernel(
+    resid_ref, image_ref, jacobi_ref, coarse_ref, inverse_ref,
+    map_ref, spread_ref, high_ref, low_ref,
+    pair_ref, slot_ref, face_ref,
+    smoothed_ref, dots_ref, local_ref, sent_ref,
+):
+    vertices = vertex_map(map_ref, spread_ref)
+    coarse = jnp.sum(coarse_ref[...], axis=0, keepdims=True)
+    resid = resid_ref[...]
+    elements = jacobi_ref.shape[0]
     field = rows_of(jacobi_ref[...]) * resid + rows_of(
         prolonged(coarse, inverse_ref, vertices, elements, high_ref, low_ref)
     )
     smoothed_ref[...] = field
-    dots_ref[...] = packed([total_of(resid * field), total_of(image * field)])
-    gather_all(field, (pair_ref, slot_ref, face_ref), (local_ref, sent_ref, down_ref, up_ref))
-
-
-def last_image_kernel(
-    field_ref, back_ref, local_in_ref, received_ref, below_ref, above_ref,
-    helmholtz_ref, pair_ref, slot_ref, face_ref,
-    image_ref, dots_ref,
-):
-    image_ref[...] = image_of(
-        field_ref, back_ref, local_in_ref, received_ref, below_ref, above_ref, helmholtz_ref,
-        (pair_ref, slot_ref, face_ref),
-    )
-    dots = jnp.sum(received_ref[:, LANES:], axis=0, keepdims=True)
-    dots_ref[...] = jnp.broadcast_to(dots, dots_ref.shape)
+    dots = packed([total_of(resid * field), total_of(image_ref[...] * field)])
+    dots_ref[...] = dots
+    gather_all(field, (pair_ref, slot_ref, face_ref), (local_ref, sent_ref), dots)
 
 
 def final_kernel(
-    old_ref, field_ref, resid_ref, old_image_ref, image_ref, scalars_ref, dots_ref,
+    old_ref, field_ref, resid_ref, old_image_ref, scalars_ref,
+    back_ref, local_in_ref, received_ref, helmholtz_ref, pair_ref, slot_ref, face_ref,
     solution_ref, residual_ref,
 ):
     before = unpacked(scalars_ref[...], 8)
-    now = unpacked(jnp.sum(dots_ref[...], axis=0, keepdims=True), 8)
+    now = unpacked(terms(received_ref), 8)
     alpha = before[0] / before[7]
     beta = now[0] / before[0]
     curved = now[7] + beta * (2.0 * now[1] + beta * before[7])
@@ -429,7 +442,11 @@
     old = old_ref[...]
     direction = field_ref[...] + beta * old
     solution_ref[...] = wide_of(alpha * old + step * direction)
-    image = image_ref[...] + beta * old_image_ref[...]
+    image = image_of(
+        field_ref, back_ref, local_in_ref, received_ref, helmholtz_ref,
+        (pair_ref, slot_ref, face_ref),
+    )
+    image = image + beta * old_image_ref[...]
     residual_ref[...] = wide_of(resid_ref[...] - step * image)
 
 
@@ -464,61 +481,51 @@
     t = {name: jnp.asarray(value) for name, value in tables(elements).items()}
     field = (4 * elements, LANES)
     local = pair_list.shape
-    face = (1, face_points.shape[1])
+    sent_rows = (groups * peers * ROWS, LANES)
     points = (pair_list, shared_slots, face_points)
     corners = (coarse_map, t["spread"], t["corner_high"], t["corner_low"])
     derivatives = (t["first"], t["first_back"], t["inner"], t["inner_back"])
-    ups = [(g, g + 1) for g in range(groups - 1)]
-    downs = [(g + 1, g) for g in range(groups - 1)]
-
-    def exchange(sent, down, up):
-        below = lax.ppermute(up, "grp", ups)
-        above = lax.ppermute(down, "grp", downs)
-        return swap(sent, "sub"), below, above
+
+    def exchange(sent):
+        rows = sent.reshape(groups * peers, 1, ROWS * LANES)
+        return swap(rows, ("grp", "sub")).reshape(sent_rows)
 
     (sent,) = call(first_kernel, [(peers, NC)], right_side, *corners)
     coarse = swap(sent, "sub")
-    smoothed, total, dots, near, sent, down, up = call(
+    smoothed, dots, near, sent = call(
         smooth_kernel,
-        [field, (1, NC), (1, LANES), local, (peers, LANES), face, face],
+        [field, (1, LANES), local, sent_rows],
         right_side, jacobi, coarse, coarse_inverse, *corners, *points,
     )
-    received, below, above = exchange(sent, down, up)
-    apply_outs = [field, local, (peers, 2 * LANES), face, face]
-    back, near, sent, down, up = call(
+    received = exchange(sent)
+    apply_outs = [field, local, sent_rows]
+    back, near, sent = call(
         apply_kernel, apply_outs,
-        smoothed, dots, near, received, below, above, metric, helmholtz, *derivatives, *points,
-    )
-    received, below, above = exchange(sent, down, up)
-    image, sent, dots = call(
+        smoothed, dots, near, received, metric, helmholtz, *derivatives, *points,
+    )
+    received = exchange(sent)
+    image, resid, scalars, sent = call(
         image_kernel,
-        [field, (peers, NC), (groups, LANES)],
-        smoothed, back, near, received, below, above, helmholtz, *corners, *points,
+        [field, field, (1, LANES), (peers, NC)],
+        right_side, smoothed, back, near, received, helmholtz, *corners, *points,
     )
     coarse = swap(sent, "sub")
-    dots = swap(dots, "grp")
-    second, resid, scalars, dots, near, sent, down, up = call(
+    second, dots, near, sent = call(
         second_kernel,
-        [field, field, (1, LANES), (1, LANES), local, (peers, LANES), face, face],
-        right_side, image, jacobi, dots, total, coarse, coarse_inverse, *corners, *points,
-    )
-    received, below, above = exchange(sent, down, up)
-    back, near, sent, down, up = call(
+        [field, (1, LANES), local, sent_rows],
+        resid, image, jacobi, coarse, coarse_inverse, *corners, *points,
+    )
+    received = exchange(sent)
+    back, near, sent = call(
         apply_kernel, apply_outs,
-        second, dots, near, received, below, above, metric, helmholtz, *derivatives, *points,
-    )
-    received, below, above = exchange(sent, down, up)
-    second_image, dots = call(
-        last_image_kernel,
-        [field, (groups, LANES)],
-        second, back, near, received, below, above, helmholtz, *points,
-    )
-    dots = swap(dots, "grp")
+        second, dots, near, received, metric, helmholtz, *derivatives, *points,
+    )
+    received = exchange(sent)
     return tuple(
         call(
             final_kernel,
             [right_side.shape, right_side.shape],
-            smoothed, second, resid, image, second_image, scalars, dots,
+            smoothed, second, resid, image, scalars, back, near, received, helmholtz, *points,
         )
     )
 

time: 99.1 us -> 69.6 us (0.70)
  starting transfers between devices: 31.9 us -> 0 us
  blocking collectives: 34.5 us -> 56.2 us
  waiting for transfers between devices: 16.7 us -> 0 us
  local copies, waits for them, and re-layouts: 5.24 us -> 4.02 us
    all_to_all x4 -> x6, blocking collectives: 34.5 us -> 56.2 us  [swap(): return lax.all_to_all(array, axis, split_axis=0, concat_axis=0, tiled=True)]
    ppermute x8 -> x0, starting transfers between devices: 17.1 us -> none  [the longest x4 11.9 us: exchange(): below = lax.ppermute(up, 'grp', ups)]
    ppermute x8 -> x0, waiting for transfers between devices: 15.7 us -> none  [the longest x4 15.7 us: exchange(): above = lax.ppermute(down, 'grp', downs)]
    all_to_all x4 -> x0, starting transfers between devices: 14.8 us -> none  [swap(): return lax.all_to_all(array, axis, split_axis=0, concat_axis=0, tiled=True)]
    all_to_all x2 -> x0, local copies, waits for them, and re-layouts: 1.22 us -> none  [swap(): return lax.all_to_all(array, axis, split_axis=0, concat_axis=0, tiled=True)]
    pallas_call x8 -> x7, Pallas kernels: 8.95 us -> 8.04 us  [call(): pl.pallas_call(kernel, out_shape=[jax.ShapeDtypeStruct(shape, F32) for sh...]
    unnamed x42 -> x38, local copies, waits for them, and re-layouts: 4.03 us -> 4.02 us
  transfers between devices with their start and end apart: 12 -> 0, of which waited for: 5 -> 0; matrix products, arithmetic and copies ran while one was open for 0% -> 0% of each run, Pallas kernels for 0% -> 0%
where the time goes in v2:
time: 69.6 us; the launch traced here: 69.1 us
  blocking collectives  56.2 us (81%)
  Pallas kernels  8.04 us (12%)
  local copies, waits for them, and re-layouts  4.02 us (6%)
  between operations  0.81 us (1%)
    all_to_all x6, blocking collectives, swap(): return lax.all_to_all(array, axis, split_axis=0, concat_axis=0, tiled=True)  56.2 us
    pallas_call x7, Pallas kernels, call(): pl.pallas_call(kernel, out_shape=[jax.ShapeDtypeStruct(shape, F32) for sh...  8.04 us
    unnamed x38, local copies, waits for them, and re-layouts  4.02 us

profile of v2, /device:TPU:0, one launch (start us, length us, event | category | flops | bytes accessed | tf_op | source)
XLA Modules:
  0.0 69.1 jit_solution(10880970705314183524)
XLA Ops:
  0.6 0.0 copy-start.13
  0.6 0.7 copy-done.13
  1.3 0.0 copy-start
  1.3 0.9 %copy-done = bf16[128,512]{1,0:T(8,128)(2,1)S(1)} copy-done((bf16[128,512]{1,0:T(8,128)(2,1)S(1)}, bf16[128,512]{1,0:T(8,128)(2,1)}, u32[]{:S(2)}) %copy-start) | copy-done | bytes 131096
  2.2 0.0 copy-start.2
  2.2 0.9 %copy-done.2 = bf16[128,512]{1,0:T(8,128)(2,1)S(1)} copy-done((bf16[128,512]{1,0:T(8,128)(2,1)S(1)}, bf16[128,512]{1,0:T(8,128)(2,1)}, u32[]{:S(2)}) %copy-start.2) | copy-done | bytes 131096
  3.1 0.0 copy-start.9
  3.1 0.8 %copy-done.9 = f32[16,512]{1,0:T(8,128)S(1)} copy-done((f32[16,512]{1,0:T(8,128)S(1)}, f32[16,512]{1,0:T(8,128)}, u32[]{:S(2)}) %copy-start.9) | copy-done | bytes 32792
  3.9 0.0 copy-start.16
  3.9 0.7 copy-done.16
  4.6 0.0 copy-start.11
  4.6 0.0 copy-start.12
  4.6 0.0 copy-start.14
  4.6 0.0 copy-start.15
  4.6 0.4 shard_map.167
  5.0 0.0 copy-start.8
  5.0 9.8 %all_to_all.42 = f32[8,1,64]{2,1,0:T(1,128)S(1)} all-to-all(f32[8,1,64]{2,1,0:T(1,128)S(1)} %bitcast.25), channel_id=1, replica_groups=mesh['grp'=4,'sub'=8] {'sub'}, dimensions={0} | all-to-all | bytes 4096 | tf_op jit(solution)/shard_map/all_to_all | solution.py:464
  14.8 0.0 copy-done.11
  14.8 0.0 copy-done.12
  14.8 0.0 copy-done.14
  14.8 0.0 copy-done.15
  14.8 0.0 copy-done.8
  14.9 0.0 copy-start.4
  14.9 0.0 copy-start.5
  14.9 0.9 %shard_map.168 = (f32[64,128]{1,0:T(8,128)S(1)}, f32[1,128]{1,0:T(1,128)S(1)}, f32[2,1024]{1,0:T(2,128)S(1)}, f32[160,128]{1,0:T(8,128)S(1)}) custom-call(f32[16,512]{1,0:T(8,128)S(1)} %copy-done.9, f32[16,512]{1,0:T(8,128)S(1)} %copy-done.14, f32[8,64]{1,0:T(8,128)S(1)} %bitcast.24, f32[1,64,64]{2,1,0:T(8,128)S(1)} %copy-done.15, s32[8,16]{1,0:T(8,128)S(1)} %copy-done.16, ...), custom_call_target="tpu_custom_call" | custom-call | tf_op jit(solution)/shard_map/pallas_call | solution.py:454
  15.8 0.0 copy-start.7
  15.8 0.0 copy-start.6
  15.9 0.0 copy-start.17
  15.9 0.0 copy-start.18
  15.9 11.4 %all_to_all.43 = f32[32,1,640]{2,1,0:T(1,128)S(1)} all-to-all(f32[32,1,640]{2,1,0:T(1,128)S(1)} %bitcast.23), channel_id=1, replica_groups=mesh['grp'=4,'sub'=8] {'grp','sub'}, dimensions={0} | all-to-all | bytes 163840 | tf_op jit(solution)/shard_map/all_to_all | solution.py:464
  27.3 0.0 copy-done.4
  27.3 0.0 copy-done.5
  27.3 0.0 copy-done.7
  27.3 0.0 copy-done.6
  27.3 0.0 copy-done.17
  27.3 0.0 copy-done.18
  27.3 0.0 copy-start.3
  27.3 1.6 %shard_map.169 = (f32[64,128]{1,0:T(8,128)S(1)}, f32[2,1024]{1,0:T(2,128)S(1)}, f32[160,128]{1,0:T(8,128)S(1)}) custom-call(f32[64,128]{1,0:T(8,128)S(1)} %get-tuple-element.20.field_ref.old_ref, f32[1,128]{1,0:T(1,128)S(1)} %get-tuple-element.21.dots_in_ref, f32[2,1024]{1,0:T(2,128)S(1)} %get-tuple-element.22.local_in_ref, f32[160,128]{1,0:T(8,128)S(1)} %bitcast.18, ...), custom_call_target="tpu_custom_call" | custom-call | tf_op jit(solution)/shard_map/pallas_call | solution.py:454
  28.9 0.0 copy-start.1
  29.0 0.0 copy-start.10
  29.0 9.4 %all_to_all.44 = f32[32,1,640]{2,1,0:T(1,128)S(1)} all-to-all(f32[32,1,640]{2,1,0:T(1,128)S(1)} %bitcast.22), channel_id=1, replica_groups=mesh['grp'=4,'sub'=8] {'grp','sub'}, dimensions={0} | all-to-all | bytes 163840 | tf_op jit(solution)/shard_map/all_to_all | solution.py:464
  38.4 0.0 copy-done.3
  38.4 0.0 copy-done.1
  38.4 0.0 copy-done.10
  38.4 1.1 %shard_map.170 = (f32[64,128]{1,0:T(8,128)S(1)}, f32[64,128]{1,0:T(8,128)S(1)}, f32[1,128]{1,0:T(1,128)S(1)}, f32[8,64]{1,0:T(8,128)S(1)}) custom-call(f32[16,512]{1,0:T(8,128)S(1)} %copy-done.10, f32[64,128]{1,0:T(8,128)S(1)} %get-tuple-element.20.field_ref.old_ref, f32[64,128]{1,0:T(8,128)S(1)} %get-tuple-element.24.back_ref, ...), custom_call_target="tpu_custom_call" | custom-call | tf_op jit(solution)/shard_map/pallas_call | solution.py:454
  39.5 7.0 %all_to_all.45 = f32[8,1,64]{2,1,0:T(1,128)S(1)} all-to-all(f32[8,1,64]{2,1,0:T(1,128)S(1)} %bitcast.27), channel_id=1, replica_groups=mesh['grp'=4,'sub'=8] {'sub'}, dimensions={0} | all-to-all | bytes 4096 | tf_op jit(solution)/shard_map/all_to_all | solution.py:464
  46.6 0.9 %shard_map.171 = (f32[64,128]{1,0:T(8,128)S(1)}, f32[1,128]{1,0:T(1,128)S(1)}, f32[2,1024]{1,0:T(2,128)S(1)}, f32[160,128]{1,0:T(8,128)S(1)}) custom-call(f32[64,128]{1,0:T(8,128)S(1)} %get-tuple-element.27.resid_ref, f32[64,128]{1,0:T(8,128)S(1)} %get-tuple-element.28.image_ref.old_image_ref, f32[16,512]{1,0:T(8,128)S(1)} %copy-done.14, ...), custom_call_target="tpu_custom_call" | custom-call | tf_op jit(solution)/shard_map/pallas_call | solution.py:454
  47.5 9.3 %all_to_all.46 = f32[32,1,640]{2,1,0:T(1,128)S(1)} all-to-all(f32[32,1,640]{2,1,0:T(1,128)S(1)} %bitcast.21), channel_id=1, replica_groups=mesh['grp'=4,'sub'=8] {'grp','sub'}, dimensions={0} | all-to-all | bytes 163840 | tf_op jit(solution)/shard_map/all_to_all | solution.py:464
  56.8 1.6 %shard_map.172 = (f32[64,128]{1,0:T(8,128)S(1)}, f32[2,1024]{1,0:T(2,128)S(1)}, f32[160,128]{1,0:T(8,128)S(1)}) custom-call(f32[64,128]{1,0:T(8,128)S(1)} %get-tuple-element.30.field_ref, f32[1,128]{1,0:T(1,128)S(1)} %get-tuple-element.32.dots_in_ref, f32[2,1024]{1,0:T(2,128)S(1)} %get-tuple-element.33.local_in_ref, f32[160,128]{1,0:T(8,128)S(1)} %bitcast.16, ...), custom_call_target="tpu_custom_call" | custom-call | tf_op jit(solution)/shard_map/pallas_call | solution.py:454
  58.5 9.3 %all_to_all.47 = f32[32,1,640]{2,1,0:T(1,128)S(1)} all-to-all(f32[32,1,640]{2,1,0:T(1,128)S(1)} %bitcast.20), channel_id=1, replica_groups=mesh['grp'=4,'sub'=8] {'grp','sub'}, dimensions={0} | all-to-all | bytes 163840 | tf_op jit(solution)/shard_map/all_to_all | solution.py:464
  67.8 1.3 %shard_map.173 = (f32[16,512]{1,0:T(8,128)}, f32[16,512]{1,0:T(8,128)}) custom-call(f32[64,128]{1,0:T(8,128)S(1)} %get-tuple-element.20.field_ref.old_ref, f32[64,128]{1,0:T(8,128)S(1)} %get-tuple-element.30.field_ref, f32[64,128]{1,0:T(8,128)S(1)} %get-tuple-element.27.resid_ref, f32[64,128]{1,0:T(8,128)S(1)} %get-tuple-element.28.image_ref.old_image_ref, ...), custom_call_target="tpu_custom_call" | custom-call | tf_op jit(solution)/shard_map/pallas_call | solution.py:454
Async XLA Ops:
  0.6 0.7 %copy-start.13 = (f32[16,128]{1,0:T(8,128)S(1)}, f32[16,128]{1,0:T(8,128)}, u32[]{:S(2)}) copy-start(f32[16,128]{1,0:T(8,128)} %constant.20.clone.spread_ref) | copy-start | bytes 24580
  1.3 0.9 %copy-start = (bf16[128,512]{1,0:T(8,128)(2,1)S(1)}, bf16[128,512]{1,0:T(8,128)(2,1)}, u32[]{:S(2)}) copy-start(bf16[128,512]{1,0:T(8,128)(2,1)} %constant.19.clone.low_ref) | copy-start | bytes 393220
  2.2 0.9 %copy-start.2 = (bf16[128,512]{1,0:T(8,128)(2,1)S(1)}, bf16[128,512]{1,0:T(8,128)(2,1)}, u32[]{:S(2)}) copy-start(bf16[128,512]{1,0:T(8,128)(2,1)} %constant.18.clone.high_ref) | copy-start | bytes 393220
  3.1 0.8 %copy-start.9 = (f32[16,512]{1,0:T(8,128)S(1)}, f32[16,512]{1,0:T(8,128)}, u32[]{:S(2)}) copy-start(f32[16,512]{1,0:T(8,128)} %right_ref.5) | copy-start | bytes 98308
  3.9 0.7 copy-start.16
  4.6 10.2 %copy-start.11 = (s32[1,8,128]{2,1,0:T(8,128)S(1)}, s32[1,8,128]{2,1,0:T(8,128)}, u32[]{:S(2)}) copy-start(s32[1,8,128]{2,1,0:T(8,128)} %slot_ref.11) | copy-start | bytes 12292
  4.6 10.2 %copy-start.12 = (s32[2,512]{1,0:T(2,128)S(1)}, s32[2,512]{1,0:T(2,128)}, u32[]{:S(2)}) copy-start(s32[2,512]{1,0:T(2,128)} %face_ref.11) | copy-start | bytes 12292
  4.6 10.2 %copy-start.14 = (f32[16,512]{1,0:T(8,128)S(1)}, f32[16,512]{1,0:T(8,128)}, u32[]{:S(2)}) copy-start(f32[16,512]{1,0:T(8,128)} %jacobi_ref.3) | copy-start | bytes 98308
  4.6 10.2 %copy-start.15 = (f32[1,64,64]{2,1,0:T(8,128)S(1)}, f32[1,64,64]{2,1,0:T(8,128)}, u32[]{:S(2)}) copy-start(f32[1,64,64]{2,1,0:T(8,128)} %inverse_ref.3) | copy-start | bytes 49156
  5.0 9.8 %copy-start.8 = (s32[2,1024]{1,0:T(2,128)S(1)}, s32[2,1024]{1,0:T(2,128)}, u32[]{:S(2)}) copy-start(s32[2,1024]{1,0:T(2,128)} %pair_ref.11) | copy-start | bytes 24580
  14.9 12.4 %copy-start.4 = (bf16[768,128]{1,0:T(8,128)(2,1)S(1)}, bf16[768,128]{1,0:T(8,128)(2,1)}, u32[]{:S(2)}) copy-start(bf16[768,128]{1,0:T(8,128)(2,1)} %constant.15.clone.inner_back_ref) | copy-start | bytes 589828
  14.9 12.4 %copy-start.5 = (bf16[384,256]{1,0:T(8,128)(2,1)S(1)}, bf16[384,256]{1,0:T(8,128)(2,1)}, u32[]{:S(2)}) copy-start(bf16[384,256]{1,0:T(8,128)(2,1)} %constant.14.clone.inner_ref) | copy-start | bytes 589828
  15.8 11.4 %copy-start.7 = (f32[16,1536]{1,0:T(8,128)S(1)}, f32[16,1536]{1,0:T(8,128)}, u32[]{:S(2)}) copy-start(f32[16,1536]{1,0:T(8,128)} %metric_ref.3) | copy-start | bytes 294916
  15.8 11.4 %copy-start.6 = (f32[16,512]{1,0:T(8,128)S(1)}, f32[16,512]{1,0:T(8,128)}, u32[]{:S(2)}) copy-start(f32[16,512]{1,0:T(8,128)} %helmholtz_ref.7) | copy-start | bytes 98308
  15.9 11.4 %copy-start.17 = (f32[32,128]{1,0:T(8,128)S(1)}, f32[32,128]{1,0:T(8,128)}, u32[]{:S(2)}) copy-start(f32[32,128]{1,0:T(8,128)} %constant.17.clone.first_back_ref) | copy-start | bytes 49156
  15.9 11.4 %copy-start.18 = (f32[32,128]{1,0:T(8,128)S(1)}, f32[32,128]{1,0:T(8,128)}, u32[]{:S(2)}) copy-start(f32[32,128]{1,0:T(8,128)} %constant.16.clone.first_ref) | copy-start | bytes 49156
  27.3 11.1 %copy-start.3 = (bf16[128,512]{1,0:T(8,128)(2,1)S(1)}, bf16[128,512]{1,0:T(8,128)(2,1)}, u32[]{:S(2)}) copy-start(bf16[128,512]{1,0:T(8,128)(2,1)} %constant.18.clone.high_ref) | copy-start | bytes 393220
  28.9 9.5 %copy-start.1 = (bf16[128,512]{1,0:T(8,128)(2,1)S(1)}, bf16[128,512]{1,0:T(8,128)(2,1)}, u32[]{:S(2)}) copy-start(bf16[128,512]{1,0:T(8,128)(2,1)} %constant.19.clone.low_ref) | copy-start | bytes 393220
  29.0 9.5 %copy-start.10 = (f32[16,512]{1,0:T(8,128)S(1)}, f32[16,512]{1,0:T(8,128)}, u32[]{:S(2)}) copy-start(f32[16,512]{1,0:T(8,128)} %right_ref.5) | copy-start | bytes 98308

commit v3 on v2

v3 whole, which is shorter than its diff:
```python
import jax
import jax.numpy as jnp
import ml_dtypes
import numpy as np
from jax import lax
from jax.experimental import pallas as pl
from jax.experimental.pallas import tpu as pltpu
from jax.sharding import PartitionSpec as P

NC = 64
POINTS = 512
LANES = 128
STEP = 256
FACE_ROWS = 4
ROWS = FACE_ROWS + 1
FIRST_ROWS = ROWS + 1 + FACE_ROWS
F32 = jnp.float32
BF16 = jnp.bfloat16
NT = (((1,), (1,)), ((), ()))


def split_constant(array):
    high = array.astype(ml_dtypes.bfloat16)
    low = (array - high.astype(np.float64)).astype(ml_dtypes.bfloat16)
    return high, low


def tables():
    order_index = np.arange(8)
    colloc = np.cos(np.pi * order_index / 7.0)
    end_weights = (
        np.where((order_index == 0) | (order_index == 7), 2.0, 1.0) * (-1.0) ** order_index
    )
    spacing = colloc[:, None] - colloc[None, :] + np.eye(8)
    raw_matrix = np.outer(end_weights, 1.0 / end_weights) / spacing
    off_part = raw_matrix * (1.0 - np.eye(8))
    derivative = 0.25 * (off_part - np.eye(8) * off_part.sum(axis=1)[:, None])
    along_inner = np.concatenate(
        [np.kron(np.eye(2), np.kron(derivative, np.eye(8))).T, np.kron(np.eye(16), derivative).T],
        axis=1,
    )
    high, low = split_constant(along_inner)
    inner = np.concatenate([high, high, low], axis=0)
    inner_back = np.concatenate([high.T, high.T, low.T], axis=0)

    half = np.arange(LANES) // 64

    def first_rows(matrix):
        rows = []
        for to in range(4):
            for at in range(4):
                rows.append(matrix[2 * to + half, 2 * at + half])
                rows.append(matrix[2 * to + half, 2 * at + 1 - half])
        return np.stack(rows).astype(np.float32)

    return {
        "inner": inner,
        "inner_back": inner_back,
        "first": first_rows(derivative),
        "first_back": first_rows(derivative.T),
    }


def split(value):
    high = value.astype(BF16)
    return high, (value - high.astype(F32)).astype(BF16)


def rows_of(wide):
    return jnp.concatenate([wide[:, LANES * c : LANES * (c + 1)] for c in range(4)], axis=0)


def wide_of(rows):
    elements = rows.shape[0] // 4
    return jnp.concatenate([rows[c * elements : (c + 1) * elements] for c in range(4)], axis=1)


def locate(points, elements):
    element = points >> 9
    chunk = (points >> 7) & 3
    row = jnp.where(points < elements * POINTS, chunk * elements + element, 4 * elements)
    return row, points & (LANES - 1)


def one_hot(index, count):
    steps = lax.broadcasted_iota(jnp.int32, (count, index.shape[1]), 0)
    return steps == index


def gather(field, chunks):
    high, low = split(field)
    both = jnp.concatenate([high, low], axis=1)
    out = []
    for row, lane in chunks:
        lanes = one_hot(lane, LANES).astype(F32).astype(BF16)
        picked = jnp.dot(
            both, jnp.concatenate([lanes, lanes], axis=0), preferred_element_type=F32
        )
        out.append(
            jnp.sum(
                jnp.where(one_hot(row, field.shape[0]), picked, 0.0), axis=0, keepdims=True
            )
        )
    return out


def scatter(rows, chunks, values):
    total = jnp.zeros((2 * rows, LANES), F32)
    for (row, lane), value in zip(chunks, values):
        lanes = one_hot(lane, LANES).astype(F32).astype(BF16)
        high, low = split(jnp.where(one_hot(row, rows), value, 0.0))
        total = total + lax.dot_general(
            jnp.concatenate([high, low], axis=0), lanes, NT, preferred_element_type=F32
        )
    return total[:rows] + total[rows:]


def chunked(row, lane):
    return [
        (row[:, at : at + STEP], lane[:, at : at + STEP]) for at in range(0, row.shape[1], STEP)
    ]


def cut(row):
    return [row[:, at : at + STEP] for at in range(0, row.shape[1], STEP)]


def pair_chunks(pair_ref, elements):
    row, lane = locate(pair_ref[...], elements)
    return chunked(row[0:1], lane[0:1]) + chunked(row[1:2], lane[1:2])


def far_chunks(slots, faces, elements):
    row, lane = locate(slots, elements)
    chunks = []
    for at in range(0, row.shape[0], 2):
        chunks.append(
            tuple(
                jnp.concatenate([part[at : at + 1], part[at + 1 : at + 2]], axis=1)
                for part in (row, lane)
            )
        )
    row, lane = locate(faces, elements)
    return chunks + chunked(row[0:1], lane[0:1]) + chunked(row[1:2], lane[1:2])


def halves(wide):
    return [wide[:, at : at + LANES] for at in range(0, wide.shape[1], LANES)]


def own_group(devices, peers, away=0):
    shape = (devices, LANES)
    return lax.broadcasted_iota(jnp.int32, shape, 0) // peers - lax.axis_index("grp") == away


def send(sent_ref, count, first, shared, down, up):
    devices = sent_ref.shape[0] // count
    peers = shared.shape[0]
    above = own_group(devices, peers, 1)
    shared = jnp.concatenate([shared] * (devices // peers), axis=0)
    for r in range(FACE_ROWS):
        rows = jnp.where(above, up[r], down[r])
        if r == 0:
            rows = jnp.where(own_group(devices, peers), shared, rows)
        sent_ref[pl.ds(first + r, devices, count), :] = rows


def send_same(sent_ref, count, at, row):
    devices = sent_ref.shape[0] // count
    sent_ref[pl.ds(at, devices, count), :] = jnp.broadcast_to(row, (devices, LANES))


def send_values(sent_ref, count, values, peers):
    shared = jnp.concatenate([row for pair in values[: peers // 2] for row in halves(pair)], axis=0)
    faces = [row for pair in values[peers // 2 :] for row in halves(pair)]
    send(sent_ref, count, 0, shared, faces[:FACE_ROWS], faces[FACE_ROWS:])


def get(received_ref, count, first, peers):
    devices = received_ref.shape[0] // count
    rows = [received_ref[pl.ds(first + r, devices, count), :] for r in range(FACE_ROWS)]
    mine = jnp.where(own_group(devices, peers), rows[0], 0.0)
    shared = mine[:peers]
    for g in range(1, devices // peers):
        shared = shared + mine[g * peers : (g + 1) * peers]
    return (shared, *[get_sides(rows, peers, away) for away in (-1, 1)])


def get_sides(rows, peers, away):
    here = lax.axis_index("grp") * peers + lax.axis_index("sub")
    source = lax.broadcasted_iota(jnp.int32, rows[0].shape, 0) - here == away * peers
    return jnp.concatenate(
        [jnp.sum(jnp.where(source, part, 0.0), axis=0, keepdims=True) for part in rows], axis=1
    )


def get_terms(received_ref, count):
    devices = received_ref.shape[0] // count
    return received_ref[pl.ds(FACE_ROWS, devices, count), :]


def far_values(shared, below, above):
    values = []
    for at in range(0, shared.shape[0], 2):
        values.append(jnp.concatenate([shared[at : at + 1], shared[at + 1 : at + 2]], axis=1))
    return values + cut(below) + cut(above)


def swapped(values):
    count = len(values) // 2
    return values[count:] + values[:count]


def along_first(field, table_ref):
    elements = field.shape[0] // 4
    turned = pltpu.roll(field, 64, axis=1)
    out = []
    for to in range(4):
        total = None
        for at in range(4):
            place = 2 * (4 * to + at)
            rows = slice(at * elements, (at + 1) * elements)
            term = (
                table_ref[place : place + 1, :] * field[rows]
                + table_ref[place + 1 : place + 2, :] * turned[rows]
            )
            total = term if total is None else total + term
        out.append(total)
    return jnp.concatenate(out, axis=0)


def stiffness(field, metric_ref, first_ref, first_back_ref, inner_ref, inner_back_ref):
    metric = [rows_of(metric_ref[:, POINTS * d : POINTS * (d + 1)]) for d in range(3)]
    grad_first = along_first(field, first_ref)
    high, low = split(field)
    inner = jnp.dot(
        jnp.concatenate([high, low, high], axis=1), inner_ref[...], preferred_element_type=F32
    )
    flux_first = metric[0] * grad_first
    flux = jnp.concatenate([metric[1], metric[2]], axis=1) * inner
    high, low = split(flux)
    back = along_first(flux_first, first_back_ref) + jnp.dot(
        jnp.concatenate([high, low, high], axis=1), inner_back_ref[...], preferred_element_type=F32
    )
    energy = flux * inner
    return back, flux_first * grad_first + energy[:, :LANES] + energy[:, LANES:]


def factors(points):
    nodes = 0.5 * (1.0 + np.cos(np.pi * np.arange(8) / 7.0))
    out = []
    for shift in (6, 3, 0):
        index = (points >> shift) & 7
        near = jnp.full(points.shape, nodes[7], F32)
        far = jnp.full(points.shape, nodes[0], F32)
        for m in range(7):
            near = jnp.where(index == m, float(nodes[m]), near)
            far = jnp.where(index == m, float(nodes[7 - m]), far)
        out.append((near, far))
    return out


def corners(points):
    first, second, third = factors(points)
    return [
        first[q >> 2 & 1] * (second[q >> 1 & 1] * third[q & 1]) for q in range(8)
    ]


def own_corners():
    return corners(lax.broadcasted_iota(jnp.int32, (1, POINTS), 1))


def flat_map(mapped):
    elements = mapped.shape[1]
    width = 8 * elements
    own = own_element(elements, width)
    place = lax.broadcasted_iota(jnp.int32, (8, width), 1) // elements
    spread = jnp.where(own, 1.0, 0.0).astype(BF16)
    wide = jnp.dot(mapped.astype(F32).astype(BF16), spread, preferred_element_type=F32)
    keep = lax.broadcasted_iota(jnp.int32, (8, width), 0) == place
    return jnp.sum(jnp.where(keep, wide, 0.0), axis=0, keepdims=True)


def one_vertex(flat):
    return jnp.where(one_hot(whole(flat), NC), 1.0, 0.0)


def whole(values):
    return (values + 0.5).astype(jnp.int32)


def own_element(elements, width):
    shape = (elements, width)
    return lax.broadcasted_iota(jnp.int32, shape, 0) == (
        lax.broadcasted_iota(jnp.int32, shape, 1) % elements
    )


def own_place(elements, q):
    shape = (elements, 8 * elements)
    lane = lax.broadcasted_iota(jnp.int32, shape, 1)
    return lane == lax.broadcasted_iota(jnp.int32, shape, 0) + q * elements


def coarse_part(field, vertices, inverse):
    elements = field.shape[0] // 4
    flat = jnp.zeros((elements, 8 * elements), F32)
    for q, corner in enumerate(own_corners()):
        inner = None
        for c in range(4):
            term = field[c * elements : (c + 1) * elements] * corner[:, c * LANES : (c + 1) * LANES]
            inner = term if inner is None else inner + term
        flat = jnp.where(own_place(elements, q), jnp.sum(inner, axis=1, keepdims=True), flat)
    flat = jnp.sum(flat, axis=0, keepdims=True)
    part = jnp.sum(vertices * flat, axis=1, keepdims=True)
    part = jnp.sum(inverse * part, axis=0, keepdims=True)
    return jnp.concatenate([part, jnp.zeros((1, LANES - NC), F32)], axis=1)


def column(row):
    shape = (NC, LANES)
    keep = lax.broadcasted_iota(jnp.int32, shape, 0) == lax.broadcasted_iota(jnp.int32, shape, 1)
    return jnp.sum(jnp.where(keep, row, 0.0), axis=1, keepdims=True)


def get_solved(received_ref, count, peers):
    rows = get_terms(received_ref, count)
    return [
        column(
            jnp.sum(
                jnp.where(own_group(rows.shape[0], peers, away), rows, 0.0), axis=0, keepdims=True
            )
        )
        for away in (0, -1, 1)
    ]


def prolonged(solved, vertices, elements):
    flat = jnp.sum(vertices * solved, axis=0, keepdims=True)
    out = [None] * 4
    for q, corner in enumerate(own_corners()):
        value = jnp.sum(jnp.where(own_place(elements, q), flat, 0.0), axis=1, keepdims=True)
        for c in range(4):
            term = value * corner[:, c * LANES : (c + 1) * LANES]
            out[c] = term if out[c] is None else out[c] + term
    return jnp.concatenate(out, axis=0)


def prolong_at(points, vertices, elements):
    mine = lax.broadcasted_iota(jnp.int32, (elements, points.shape[1]), 0) == points >> 9
    weights = jnp.concatenate([jnp.where(mine, corner, 0.0) for corner in corners(points)], axis=0)
    high, low = split(weights)
    both = jnp.dot(
        vertices.astype(BF16),
        jnp.concatenate([high, low], axis=1),
        preferred_element_type=F32,
    )
    return both[:, : points.shape[1]] + both[:, points.shape[1] :]


def total_of(array):
    return jnp.sum(jnp.sum(array, axis=0, keepdims=True), axis=1, keepdims=True)


def packed(values):
    lane = lax.broadcasted_iota(jnp.int32, (1, LANES), 1)
    out = jnp.zeros((1, LANES), F32)
    for k, value in enumerate(values):
        out = jnp.where(lane == k, value, out)
    return out


def unpacked(row, count):
    lane = lax.broadcasted_iota(jnp.int32, row.shape, 1)
    return [
        jnp.sum(jnp.where(lane == k, row, 0.0), axis=1, keepdims=True) for k in range(count)
    ]


def first_kernel(
    right_hbm, jacobi_hbm, inverse_hbm, map_hbm, slot_hbm, face_hbm,
    sent_ref,
    right_ref, jacobi_ref, inverse_ref, map_ref, slot_ref, face_ref, sems,
):
    copies = []
    for k, (source, target) in enumerate(
        (
            (face_hbm, face_ref),
            (slot_hbm, slot_ref),
            (right_hbm, right_ref),
            (jacobi_hbm, jacobi_ref),
            (map_hbm, map_ref),
            (inverse_hbm, inverse_ref),
        )
    ):
        copy = pltpu.make_async_copy(source, target, sems.at[k])
        copy.start()
        copies.append(copy)
    for copy in copies:
        copy.wait()
    elements = right_ref.shape[0]
    peers = slot_ref.shape[1]
    resid = rows_of(right_ref[...])
    flat = flat_map(map_ref[...])
    part = coarse_part(resid, one_vertex(flat), inverse_ref[0])
    smoothed = rows_of(jacobi_ref[...]) * resid
    values = gather(smoothed, far_chunks(slot_ref[0], face_ref[...], elements))
    send_values(sent_ref, FIRST_ROWS, values, peers)
    send_same(sent_ref, FIRST_ROWS, FACE_ROWS, part)
    send_same(sent_ref, FIRST_ROWS, ROWS, flat)
    faces = face_ref[...].astype(F32)
    send(
        sent_ref, FIRST_ROWS, ROWS + 1, slot_ref[0].astype(F32),
        halves(faces[0:1]), halves(faces[1:2]),
    )


def static_of(received_ref, peers, elements):
    shared, below, above = get(received_ref, FIRST_ROWS, ROWS + 1, peers)
    devices = received_ref.shape[0] // FIRST_ROWS
    maps = received_ref[pl.ds(ROWS, devices, FIRST_ROWS), :]
    mine = jnp.where(own_group(devices, peers), maps, 0.0)
    own = mine[:peers]
    for g in range(1, devices // peers):
        own = own + mine[g * peers : (g + 1) * peers]
    out = []
    for b in range(peers):
        out.append(
            prolong_at(whole(shared[b : b + 1]), one_vertex(own[b : b + 1]), elements)
        )
    for points, away in ((below, -1), (above, 1)):
        flat = get_sides([maps], peers, away)
        out.append(prolong_at(whole(points), one_vertex(flat), elements))
    return jnp.concatenate(out, axis=1)


def apply(
    smoothed, count, received_ref, weights, solved, metric_ref, helmholtz_ref, derivatives, points,
    dots, back_ref, local_ref, sent_ref,
):
    pair_ref, slot_ref, face_ref = points
    elements = smoothed.shape[0] // 4
    peers = slot_ref.shape[1]
    pairs = pair_chunks(pair_ref, elements)
    far = far_chunks(slot_ref[0], face_ref[...], elements)
    shared, below, above = get(received_ref, count, 0, peers)
    ends = (0, peers * LANES, peers * LANES + below.shape[1], weights.shape[1])
    coarse = [
        jnp.sum(weights[:, ends[k] : ends[k + 1]] * solved[k], axis=0, keepdims=True)
        for k in range(3)
    ]
    shared = shared + jnp.concatenate(halves(coarse[0]), axis=0)
    values = swapped(gather(smoothed, pairs))
    values = values + far_values(shared, below + coarse[1], above + coarse[2])
    summed = smoothed + scatter(smoothed.shape[0], pairs + far, values)
    back, energy = stiffness(summed, metric_ref, *derivatives)
    energy = energy + rows_of(helmholtz_ref[...]) * smoothed * smoothed
    back_ref[...] = back
    values = gather(back, pairs + far)
    near = swapped(values[: len(pairs)])
    for k, value in enumerate(near):
        local_ref[0:1, k * STEP : (k + 1) * STEP] = value
    send_values(sent_ref, ROWS, values[len(pairs) :], peers)
    send_same(sent_ref, ROWS, FACE_ROWS, packed(dots + [total_of(energy)]))


def image_of(field_ref, back_ref, local_ref, received_ref, helmholtz_ref, points):
    pair_ref, slot_ref, face_ref = points
    elements = field_ref.shape[0] // 4
    chunks = pair_chunks(pair_ref, elements) + far_chunks(slot_ref[0], face_ref[...], elements)
    values = cut(local_ref[...]) + far_values(*get(received_ref, ROWS, 0, slot_ref.shape[1]))
    summed = back_ref[...] + scatter(field_ref.shape[0], chunks, values)
    return summed + rows_of(helmholtz_ref[...]) * field_ref[...]


def start_kernel(
    received_ref, right_ref, jacobi_ref, metric_ref, helmholtz_ref, map_ref,
    pair_ref, slot_ref, face_ref, first_ref, first_back_ref, inner_ref, inner_back_ref,
    smoothed_ref, weights_ref, back_ref, local_ref, sent_ref,
):
    elements = right_ref.shape[0]
    peers = slot_ref.shape[1]
    solved = get_solved(received_ref, FIRST_ROWS, peers)
    resid = rows_of(right_ref[...])
    vertices = one_vertex(flat_map(map_ref[...]))
    smoothed = rows_of(jacobi_ref[...]) * resid + prolonged(solved[0], vertices, elements)
    smoothed_ref[...] = smoothed
    weights = static_of(received_ref, peers, elements)
    weights_ref[...] = weights
    apply(
        smoothed, FIRST_ROWS, received_ref, weights, solved, metric_ref, helmholtz_ref,
        (first_ref, first_back_ref, inner_ref, inner_back_ref), (pair_ref, slot_ref, face_ref),
        [total_of(resid * smoothed)], back_ref, local_ref, sent_ref,
    )


def middle_kernel(
    received_ref, right_ref, jacobi_ref, helmholtz_ref, map_ref, inverse_ref,
    smoothed_ref, back_ref, local_ref, pair_ref, slot_ref, face_ref,
    image_ref, resid_ref, scalars_ref, sent_ref,
):
    elements = right_ref.shape[0]
    points = (pair_ref, slot_ref, face_ref)
    dots = jnp.sum(get_terms(received_ref, ROWS), axis=0, keepdims=True)
    scalars_ref[...] = dots
    values = unpacked(dots, 2)
    alpha = values[0] / values[1]
    image = image_of(smoothed_ref, back_ref, local_ref, received_ref, helmholtz_ref, points)
    image_ref[...] = image
    resid = rows_of(right_ref[...]) - alpha * image
    resid_ref[...] = resid
    part = coarse_part(resid, one_vertex(flat_map(map_ref[...])), inverse_ref[0])
    values = gather(
        rows_of(jacobi_ref[...]) * resid, far_chunks(slot_ref[0], face_ref[...], elements)
    )
    send_values(sent_ref, ROWS, values, slot_ref.shape[1])
    send_same(sent_ref, ROWS, FACE_ROWS, part)


def second_kernel(
    received_ref, resid_ref, image_ref, weights_ref, jacobi_ref, metric_ref, helmholtz_ref, map_ref,
    pair_ref, slot_ref, face_ref, first_ref, first_back_ref, inner_ref, inner_back_ref,
    smoothed_ref, back_ref, local_ref, sent_ref,
):
    elements = jacobi_ref.shape[0]
    solved = get_solved(received_ref, ROWS, slot_ref.shape[1])
    resid = resid_ref[...]
    vertices = one_vertex(flat_map(map_ref[...]))
    smoothed = rows_of(jacobi_ref[...]) * resid + prolonged(solved[0], vertices, elements)
    smoothed_ref[...] = smoothed
    apply(
        smoothed, ROWS, received_ref, weights_ref[...], solved, metric_ref, helmholtz_ref,
        (first_ref, first_back_ref, inner_ref, inner_back_ref), (pair_ref, slot_ref, face_ref),
        [total_of(resid * smoothed), total_of(image_ref[...] * smoothed)],
        back_ref, local_ref, sent_ref,
    )


def final_kernel(
    received_ref, old_ref, field_ref, resid_ref, old_image_ref, scalars_ref,
    back_ref, local_ref, helmholtz_ref, pair_ref, slot_ref, face_ref,
    solution_ref, residual_ref,
):
    before = unpacked(scalars_ref[...], 2)
    now = unpacked(jnp.sum(get_terms(received_ref, ROWS), axis=0, keepdims=True), 3)
    alpha = before[0] / before[1]
    beta = now[0] / before[0]
    curved = now[2] + beta * (2.0 * now[1] + beta * before[1])
    step = now[0] / curved
    old = old_ref[...]
    direction = field_ref[...] + beta * old
    solution_ref[...] = wide_of(alpha * old + step * direction)
    image = image_of(
        field_ref, back_ref, local_ref, received_ref, helmholtz_ref, (pair_ref, slot_ref, face_ref)
    )
    image = image + beta * old_image_ref[...]
    residual_ref[...] = wide_of(resid_ref[...] - step * image)


def call(kernel, outs, *args, copied=False):
    space = pl.ANY if copied else pltpu.VMEM
    scratch = [pltpu.VMEM(arg.shape, arg.dtype) for arg in args] if copied else []
    return pl.pallas_call(
        kernel,
        out_shape=[jax.ShapeDtypeStruct(shape, F32) for shape in outs],
        in_specs=[pl.BlockSpec(memory_space=space)] * len(args),
        out_specs=[pl.BlockSpec(memory_space=pltpu.VMEM)] * len(outs),
        scratch_shapes=scratch + ([pltpu.SemaphoreType.DMA((len(args),))] if copied else []),
        compiler_params=pltpu.CompilerParams(vmem_limit_bytes=(60 if copied else 24) * 1024 * 1024),
    )(*args)


def body(
    right_side,
    metric,
    helmholtz,
    jacobi,
    pair_list,
    shared_slots,
    face_points,
    coarse_map,
    coarse_inverse,
):
    peers = lax.axis_size("sub")
    groups = lax.axis_size("grp")
    t = {name: jnp.asarray(value) for name, value in tables().items()}
    field = (4 * right_side.shape[0], LANES)
    local = (1, pair_list.shape[0] * pair_list.shape[1])
    weights_shape = (NC, peers * LANES + face_points.shape[0] * face_points.shape[1])
    sent_rows = (groups * peers * ROWS, LANES)
    points = (pair_list, shared_slots, face_points)
    derivatives = (t["first"], t["first_back"], t["inner"], t["inner_back"])

    def exchange(sent):
        rows = sent.reshape(groups * peers, 1, -1)
        return lax.all_to_all(rows, ("grp", "sub"), 0, 0, tiled=True).reshape(sent.shape)

    (sent,) = call(
        first_kernel, [(groups * peers * FIRST_ROWS, LANES)],
        right_side, jacobi, coarse_inverse, coarse_map, shared_slots, face_points, copied=True,
    )
    smoothed, weights, back, near, sent = call(
        start_kernel, [field, weights_shape, field, local, sent_rows],
        exchange(sent), right_side, jacobi, metric, helmholtz, coarse_map, *points, *derivatives,
    )
    image, resid, scalars, sent = call(
        middle_kernel, [field, field, (1, LANES), sent_rows],
        exchange(sent), right_side, jacobi, helmholtz, coarse_map, coarse_inverse,
        smoothed, back, near, *points,
    )
    second, back, near, sent = call(
        second_kernel, [field, field, local, sent_rows],
        exchange(sent), resid, image, weights, jacobi, metric, helmholtz, coarse_map,
        *points, *derivatives,
    )
    return tuple(
        call(
            final_kernel, [right_side.shape, right_side.shape],
            exchange(sent), smoothed, second, resid, image, scalars, back, near, helmholtz, *points,
        )
    )


def solution(mesh):
    in_specs = (
        P(("grp", "sub"), None),
        P(("grp", "sub"), None),
        P(("grp", "sub"), None),
        P(("grp", "sub"), None),
        P(None, ("grp", "sub")),
        P(("grp", "sub"), None, None),
        P(None, ("grp", "sub")),
        P(None, ("grp", "sub")),
        P("grp", None, None),
    )
    out_specs = (P(("grp", "sub"), None), P(("grp", "sub"), None))
    return jax.shard_map(body, mesh=mesh, in_specs=in_specs, out_specs=out_specs, check_vma=False)
```

time: 69.6 us -> 56.9 us (0.82)
  blocking collectives: 56.2 us -> 44.2 us
  local copies, waits for them, and re-layouts: 4.02 us -> 2.87 us
    all_to_all x6 -> x4, blocking collectives: 56.2 us -> 44.2 us  [exchange(): lax.all_to_all(rows, ('grp', 'sub'), 0, 0, tiled=True).reshape(sent.shape)]
    unnamed x38 -> x30, local copies, waits for them, and re-layouts: 4.02 us -> 2.87 us
    pallas_call x7 -> x5, Pallas kernels: 8.04 us -> 8.53 us  [call(): pl.pallas_call(kernel, out_shape=[jax.ShapeDtypeStruct(shape, F32) for sh...]
where the time goes in v3:
time: 56.9 us; the launch traced here: 56.4 us
  blocking collectives  44.2 us (78%)
  Pallas kernels  8.53 us (15%)
  local copies, waits for them, and re-layouts  2.87 us (5%)
  between operations  0.81 us (1%)
    all_to_all x4, blocking collectives, exchange(): lax.all_to_all(rows, ('grp', 'sub'), 0, 0, tiled=True).reshape(sent.shape)  44.2 us
    pallas_call x5, Pallas kernels, call(): pl.pallas_call(kernel, out_shape=[jax.ShapeDtypeStruct(shape, F32) for sh...  8.53 us
    unnamed x30, local copies, waits for them, and re-layouts  2.87 us

profile of v3, /device:TPU:0, one launch (start us, length us, event | category | flops | bytes accessed | tf_op | source)
XLA Modules:
  0.0 56.4 jit_solution(866731680452689584)
XLA Ops:
  0.6 0.0 copy-start.1
  0.6 0.0 copy-start.4
  0.7 2.0 %shard_map.140 = f32[320,128]{1,0:T(8,128)} custom-call(f32[16,512]{1,0:T(8,128)} %right_ref.3, f32[16,512]{1,0:T(8,128)} %jacobi_ref.5, f32[1,64,64]{2,1,0:T(8,128)} %inverse_ref.1, s32[8,16]{1,0:T(8,128)} %map_ref.5, s32[1,8,128]{2,1,0:T(8,128)} %slot_ref.7, s32[2,512]{1,0:T(2,128)} %face_ref.7), custom_call_target="tpu_custom_call" | custom-call | tf_op jit(solution)/shard_map/pallas_call | solution.py:564
  2.7 0.0 copy-start
  2.7 0.0 copy-start.2
  2.7 0.0 copy-start.3
  2.7 0.0 copy-start.5
  2.7 0.0 copy-start.6
  2.8 0.0 copy-start.8
  2.8 15.9 %all_to_all.20 = f32[32,1,1280]{2,1,0:T(1,128)S(1)} all-to-all(f32[32,1,1280]{2,1,0:T(1,128)} %bitcast.15), channel_id=1, replica_groups=mesh['grp'=4,'sub'=8] {'grp','sub'}, dimensions={0} | all-to-all | bytes 327680 | tf_op jit(solution)/shard_map/all_to_all | solution.py:597
  18.7 0.0 copy-done.1
  18.7 0.0 copy-done.4
  18.7 0.0 copy-done
  18.7 0.0 copy-done.2
  18.7 0.0 copy-done.3
  18.7 0.0 copy-done.5
  18.7 0.0 copy-done.6
  18.7 0.0 copy-done.8
  18.7 0.0 copy-start.9
  18.7 0.7 %copy-done.9 = s32[2,512]{1,0:T(2,128)S(1)} copy-done((s32[2,512]{1,0:T(2,128)S(1)}, s32[2,512]{1,0:T(2,128)}, u32[]{:S(2)}) %copy-start.9) | copy-done | bytes 4120
  19.4 0.0 copy-start.10
  19.4 0.7 %copy-done.10 = s32[8,16]{1,0:T(8,128)S(1)} copy-done((s32[8,16]{1,0:T(8,128)S(1)}, s32[8,16]{1,0:T(8,128)}, u32[]{:S(2)}) %copy-start.10) | copy-done | bytes 536
  20.1 0.0 copy-start.11
  20.1 0.7 %copy-done.11 = f32[32,128]{1,0:T(8,128)S(1)} copy-done((f32[32,128]{1,0:T(8,128)S(1)}, f32[32,128]{1,0:T(8,128)}, u32[]{:S(2)}) %copy-start.11) | copy-done | bytes 16408
  20.8 0.0 copy-start.13
  20.8 0.7 %copy-done.13 = f32[32,128]{1,0:T(8,128)S(1)} copy-done((f32[32,128]{1,0:T(8,128)S(1)}, f32[32,128]{1,0:T(8,128)}, u32[]{:S(2)}) %copy-start.13) | copy-done | bytes 16408
  21.5 2.2 %shard_map.141 = (f32[64,128]{1,0:T(8,128)S(1)}, f32[64,2048]{1,0:T(8,128)S(1)}, f32[64,128]{1,0:T(8,128)S(1)}, f32[1,2048]{1,0:T(1,128)S(1)}, f32[160,128]{1,0:T(8,128)S(1)}) custom-call(f32[320,128]{1,0:T(8,128)S(1)} %bitcast.8, f32[16,512]{1,0:T(8,128)S(1)} %copy-done.5, f32[16,512]{1,0:T(8,128)S(1)} %copy-done.2, f32[16,1536]{1,0:T(8,128)S(1)} %copy-done.4, ...), custom_call_target="tpu_custom_call" | custom-call | tf_op jit(solution)/shard_map/pallas_call | solution.py:564
  23.8 0.0 copy-start.7
  23.8 9.7 %all_to_all.21 = f32[32,1,640]{2,1,0:T(1,128)S(1)} all-to-all(f32[32,1,640]{2,1,0:T(1,128)S(1)} %bitcast.14), channel_id=1, replica_groups=mesh['grp'=4,'sub'=8] {'grp','sub'}, dimensions={0} | all-to-all | bytes 163840 | tf_op jit(solution)/shard_map/all_to_all | solution.py:597
  33.5 0.0 copy-done.7
  33.5 1.1 %shard_map.142 = (f32[64,128]{1,0:T(8,128)S(1)}, f32[64,128]{1,0:T(8,128)S(1)}, f32[1,128]{1,0:T(1,128)S(1)}, f32[160,128]{1,0:T(8,128)S(1)}) custom-call(f32[160,128]{1,0:T(8,128)S(1)} %bitcast.11, f32[16,512]{1,0:T(8,128)S(1)} %copy-done.5, f32[16,512]{1,0:T(8,128)S(1)} %copy-done.2, f32[16,512]{1,0:T(8,128)S(1)} %copy-done.3, s32[8,16]{1,0:T(8,128)S(1)} %copy-done.10, ...), custom_call_target="tpu_custom_call" | custom-call | tf_op jit(solution)/shard_map/pallas_call | solution.py:564
  34.6 0.0 copy-start.12
  34.6 0.0 copy-start.14
  34.6 9.3 %all_to_all.22 = f32[32,1,640]{2,1,0:T(1,128)S(1)} all-to-all(f32[32,1,640]{2,1,0:T(1,128)S(1)} %bitcast.13), channel_id=1, replica_groups=mesh['grp'=4,'sub'=8] {'grp','sub'}, dimensions={0} | all-to-all | bytes 163840 | tf_op jit(solution)/shard_map/all_to_all | solution.py:597
  43.9 0.0 copy-done.12
  43.9 0.0 copy-done.14
  43.9 1.9 %shard_map.143 = (f32[64,128]{1,0:T(8,128)S(1)}, f32[64,128]{1,0:T(8,128)S(1)}, f32[1,2048]{1,0:T(1,128)S(1)}, f32[160,128]{1,0:T(8,128)S(1)}) custom-call(f32[160,128]{1,0:T(8,128)S(1)} %bitcast.9, f32[64,128]{1,0:T(8,128)S(1)} %get-tuple-element.20.resid_ref, f32[64,128]{1,0:T(8,128)S(1)} %get-tuple-element.21.image_ref.old_image_ref, ...), custom_call_target="tpu_custom_call" | custom-call | tf_op jit(solution)/shard_map/pallas_call | solution.py:564
  45.8 9.3 %all_to_all.23 = f32[32,1,640]{2,1,0:T(1,128)S(1)} all-to-all(f32[32,1,640]{2,1,0:T(1,128)S(1)} %bitcast.12), channel_id=1, replica_groups=mesh['grp'=4,'sub'=8] {'grp','sub'}, dimensions={0} | all-to-all | bytes 163840 | tf_op jit(solution)/shard_map/all_to_all | solution.py:597
  55.1 1.3 %shard_map.144 = (f32[16,512]{1,0:T(8,128)}, f32[16,512]{1,0:T(8,128)}) custom-call(f32[160,128]{1,0:T(8,128)S(1)} %bitcast.10, f32[64,128]{1,0:T(8,128)S(1)} %get-tuple-element.16.smoothed_ref.old_ref, f32[64,128]{1,0:T(8,128)S(1)} %get-tuple-element.24.field_ref, f32[64,128]{1,0:T(8,128)S(1)} %get-tuple-element.20.resid_ref, ...), custom_call_target="tpu_custom_call" | custom-call | tf_op jit(solution)/shard_map/pallas_call | solution.py:564
Async XLA Ops:
  0.6 18.0 %copy-start.1 = (bf16[384,256]{1,0:T(8,128)(2,1)S(1)}, bf16[384,256]{1,0:T(8,128)(2,1)}, u32[]{:S(2)}) copy-start(bf16[384,256]{1,0:T(8,128)(2,1)} %constant.8.clone.inner_ref) | copy-start | bytes 589828
  0.6 18.0 %copy-start.4 = (f32[16,1536]{1,0:T(8,128)S(1)}, f32[16,1536]{1,0:T(8,128)}, u32[]{:S(2)}) copy-start(f32[16,1536]{1,0:T(8,128)} %metric_ref.3) | copy-start | bytes 294916
  2.7 16.0 %copy-start = (bf16[768,128]{1,0:T(8,128)(2,1)S(1)}, bf16[768,128]{1,0:T(8,128)(2,1)}, u32[]{:S(2)}) copy-start(bf16[768,128]{1,0:T(8,128)(2,1)} %constant.9.clone.inner_back_ref) | copy-start | bytes 589828
  2.7 16.0 %copy-start.2 = (f32[16,512]{1,0:T(8,128)S(1)}, f32[16,512]{1,0:T(8,128)}, u32[]{:S(2)}) copy-start(f32[16,512]{1,0:T(8,128)} %jacobi_ref.5) | copy-start | bytes 98308
  2.7 16.0 %copy-start.3 = (f32[16,512]{1,0:T(8,128)S(1)}, f32[16,512]{1,0:T(8,128)}, u32[]{:S(2)}) copy-start(f32[16,512]{1,0:T(8,128)} %helmholtz_ref.7) | copy-start | bytes 98308
  2.7 16.0 %copy-start.5 = (f32[16,512]{1,0:T(8,128)S(1)}, f32[16,512]{1,0:T(8,128)}, u32[]{:S(2)}) copy-start(f32[16,512]{1,0:T(8,128)} %right_ref.3) | copy-start | bytes 98308
  2.7 16.0 %copy-start.6 = (s32[2,1024]{1,0:T(2,128)S(1)}, s32[2,1024]{1,0:T(2,128)}, u32[]{:S(2)}) copy-start(s32[2,1024]{1,0:T(2,128)} %pair_ref.7) | copy-start | bytes 24580
  2.8 16.0 %copy-start.8 = (s32[1,8,128]{2,1,0:T(8,128)S(1)}, s32[1,8,128]{2,1,0:T(8,128)}, u32[]{:S(2)}) copy-start(s32[1,8,128]{2,1,0:T(8,128)} %slot_ref.7) | copy-start | bytes 12292
  18.7 0.7 %copy-start.9 = (s32[2,512]{1,0:T(2,128)S(1)}, s32[2,512]{1,0:T(2,128)}, u32[]{:S(2)}) copy-start(s32[2,512]{1,0:T(2,128)} %face_ref.7) | copy-start | bytes 12292
  19.4 0.7 %copy-start.10 = (s32[8,16]{1,0:T(8,128)S(1)}, s32[8,16]{1,0:T(8,128)}, u32[]{:S(2)}) copy-start(s32[8,16]{1,0:T(8,128)} %map_ref.5) | copy-start | bytes 1540
  20.1 0.7 %copy-start.11 = (f32[32,128]{1,0:T(8,128)S(1)}, f32[32,128]{1,0:T(8,128)}, u32[]{:S(2)}) copy-start(f32[32,128]{1,0:T(8,128)} %constant.11.clone.first_back_ref) | copy-start | bytes 49156
  20.8 0.7 %copy-start.13 = (f32[32,128]{1,0:T(8,128)S(1)}, f32[32,128]{1,0:T(8,128)}, u32[]{:S(2)}) copy-start(f32[32,128]{1,0:T(8,128)} %constant.10.clone.first_ref) | copy-start | bytes 49156
  23.8 9.7 %copy-start.7 = (f32[1,64,64]{2,1,0:T(8,128)S(1)}, f32[1,64,64]{2,1,0:T(8,128)}, u32[]{:S(2)}) copy-start(f32[1,64,64]{2,1,0:T(8,128)} %inverse_ref.1) | copy-start | bytes 49156
  34.6 9.3 %copy-start.12 = (f32[32,128]{1,0:T(8,128)S(1)}, f32[32,128]{1,0:T(8,128)}, u32[]{:S(2)}) copy-start(f32[32,128]{1,0:T(8,128)} %constant.11.clone.first_back_ref) | copy-start | bytes 49156
  34.6 9.3 %copy-start.14 = (f32[32,128]{1,0:T(8,128)S(1)}, f32[32,128]{1,0:T(8,128)}, u32[]{:S(2)}) copy-start(f32[32,128]{1,0:T(8,128)} %constant.10.clone.first_ref) | copy-start | bytes 49156

commit v4 on v3

v4 whole, which is shorter than its diff:
```python
import jax
import jax.numpy as jnp
import ml_dtypes
import numpy as np
from jax import lax
from jax.experimental import pallas as pl
from jax.experimental.pallas import tpu as pltpu
from jax.sharding import PartitionSpec as P

NC = 64
POINTS = 512
LANES = 128
STEP = 256
FACE_ROWS = 4
ROWS = 2
FIRST_ROWS = 4
F32 = jnp.float32
BF16 = jnp.bfloat16
NT = (((1,), (1,)), ((), ()))


def split_constant(array):
    high = array.astype(ml_dtypes.bfloat16)
    low = (array - high.astype(np.float64)).astype(ml_dtypes.bfloat16)
    return high, low


def tables():
    order_index = np.arange(8)
    colloc = np.cos(np.pi * order_index / 7.0)
    end_weights = (
        np.where((order_index == 0) | (order_index == 7), 2.0, 1.0) * (-1.0) ** order_index
    )
    spacing = colloc[:, None] - colloc[None, :] + np.eye(8)
    raw_matrix = np.outer(end_weights, 1.0 / end_weights) / spacing
    off_part = raw_matrix * (1.0 - np.eye(8))
    derivative = 0.25 * (off_part - np.eye(8) * off_part.sum(axis=1)[:, None])
    along_inner = np.concatenate(
        [np.kron(np.eye(2), np.kron(derivative, np.eye(8))).T, np.kron(np.eye(16), derivative).T],
        axis=1,
    )
    high, low = split_constant(along_inner)
    inner = np.concatenate([high, low], axis=0)

    half = np.arange(LANES) // 64

    def first_rows(matrix):
        rows = []
        for to in range(4):
            for at in range(4):
                rows.append(matrix[2 * to + half, 2 * at + half])
                rows.append(matrix[2 * to + half, 2 * at + 1 - half])
        return np.stack(rows).astype(np.float32)

    return {
        "inner": inner,
        "first": np.concatenate([first_rows(derivative), first_rows(derivative.T)], axis=0),
    }


def split(value):
    high = value.astype(BF16)
    return high, (value - high.astype(F32)).astype(BF16)


def rows_of(wide):
    return jnp.concatenate([wide[:, LANES * c : LANES * (c + 1)] for c in range(4)], axis=0)


def wide_of(rows):
    elements = rows.shape[0] // 4
    return jnp.concatenate([rows[c * elements : (c + 1) * elements] for c in range(4)], axis=1)


def locate(points, elements):
    element = points >> 9
    chunk = (points >> 7) & 3
    row = jnp.where(points < elements * POINTS, chunk * elements + element, 4 * elements)
    return row, points & (LANES - 1)


def one_hot(index, count):
    steps = lax.broadcasted_iota(jnp.int32, (count, index.shape[1]), 0)
    return steps == index


def gather(field, chunks):
    high, low = split(field)
    both = jnp.concatenate([high, low], axis=1)
    out = []
    for row, lane in chunks:
        lanes = one_hot(lane, LANES).astype(F32).astype(BF16)
        picked = jnp.dot(
            both, jnp.concatenate([lanes, lanes], axis=0), preferred_element_type=F32
        )
        out.append(
            jnp.sum(
                jnp.where(one_hot(row, field.shape[0]), picked, 0.0), axis=0, keepdims=True
            )
        )
    return out


def scatter(rows, chunks, values):
    total = jnp.zeros((2 * rows, LANES), F32)
    for (row, lane), value in zip(chunks, values):
        lanes = one_hot(lane, LANES).astype(F32).astype(BF16)
        high, low = split(jnp.where(one_hot(row, rows), value, 0.0))
        total = total + lax.dot_general(
            jnp.concatenate([high, low], axis=0), lanes, NT, preferred_element_type=F32
        )
    return total[:rows] + total[rows:]


def chunked(row, lane):
    return [
        (row[:, at : at + STEP], lane[:, at : at + STEP]) for at in range(0, row.shape[1], STEP)
    ]


def cut(row):
    return [row[:, at : at + STEP] for at in range(0, row.shape[1], STEP)]


def pair_chunks(pair_ref, elements):
    row, lane = locate(pair_ref[...], elements)
    return chunked(row[0:1], lane[0:1]) + chunked(row[1:2], lane[1:2])


def joined(rows):
    return [
        jnp.concatenate([rows[at : at + 1], rows[at + 1 : at + 2]], axis=1)
        for at in range(0, rows.shape[0], 2)
    ]


def far_chunks(points, elements):
    row, lane = locate(points, elements)
    return list(zip(joined(row), joined(lane)))


def halves(wide):
    return [wide[:, at : at + LANES] for at in range(0, wide.shape[1], LANES)]


def own_group(devices, peers, away=0):
    shape = (devices, LANES)
    return lax.broadcasted_iota(jnp.int32, shape, 0) // peers - lax.axis_index("grp") == away


def send_shared(sent_ref, count, at, shared):
    devices = sent_ref.shape[0] // count
    copies = devices // shared.shape[0]
    sent_ref[pl.ds(at, devices, count), :] = jnp.concatenate([shared] * copies, axis=0)


def send_same(sent_ref, count, at, row):
    devices = sent_ref.shape[0] // count
    sent_ref[pl.ds(at, devices, count), :] = jnp.broadcast_to(row, (devices, LANES))


def send_values(sent_ref, faces_ref, count, values, peers):
    rows = jnp.concatenate([row for pair in values for row in halves(pair)], axis=0)
    send_shared(sent_ref, count, 0, rows[:peers])
    faces_ref[0 : 2 * FACE_ROWS, :] = rows[peers:]


def get(received_ref, count, at):
    return received_ref[pl.ds(at, received_ref.shape[0] // count, count), :]


def get_shared(received_ref, count, at, peers):
    rows = get(received_ref, count, at)
    mine = jnp.where(own_group(rows.shape[0], peers), rows, 0.0)
    shared = mine[:peers]
    for g in range(1, rows.shape[0] // peers):
        shared = shared + mine[g * peers : (g + 1) * peers]
    return shared


def get_row(rows, peers, away):
    here = lax.axis_index("grp") * peers + lax.axis_index("sub")
    source = lax.broadcasted_iota(jnp.int32, rows.shape, 0) - here == away * peers
    return jnp.sum(jnp.where(source, rows, 0.0), axis=0, keepdims=True)


def get_faces(gathered_ref, at, groups):
    count = gathered_ref.shape[0] // groups
    group = lax.axis_index("grp")
    below, above = 0.0, 0.0
    for g in range(groups):
        rows = gathered_ref[g * count + at : g * count + at + 2 * FACE_ROWS, :]
        below = below + jnp.where(group == g + 1, rows[FACE_ROWS:], 0.0)
        above = above + jnp.where(group == g - 1, rows[:FACE_ROWS], 0.0)
    return jnp.concatenate([below, above], axis=0)


def swapped(values):
    count = len(values) // 2
    return values[count:] + values[:count]


def along_first(field, table_ref, base):
    elements = field.shape[0] // 4
    turned = pltpu.roll(field, 64, axis=1)
    out = []
    for to in range(4):
        total = None
        for at in range(4):
            place = base + 2 * (4 * to + at)
            rows = slice(at * elements, (at + 1) * elements)
            term = (
                table_ref[place : place + 1, :] * field[rows]
                + table_ref[place + 1 : place + 2, :] * turned[rows]
            )
            total = term if total is None else total + term
        out.append(total)
    return jnp.concatenate(out, axis=0)


def stiffness(field, metric_ref, first_ref, inner_ref):
    metric = [rows_of(metric_ref[:, POINTS * d : POINTS * (d + 1)]) for d in range(3)]
    count = field.shape[0]
    grad_first = along_first(field, first_ref, 0)
    high, low = split(field)
    both = jnp.dot(
        jnp.concatenate([high, low], axis=0), inner_ref[:LANES], preferred_element_type=F32
    )
    inner = both[:count] + both[count:]
    inner = inner + jnp.dot(high, inner_ref[LANES:], preferred_element_type=F32)
    flux_first = metric[0] * grad_first
    flux = jnp.concatenate([metric[1], metric[2]], axis=1) * inner
    high, low = split(flux)
    both = lax.dot_general(
        jnp.concatenate([high, low], axis=0), inner_ref[:LANES], NT, preferred_element_type=F32
    )
    back = both[:count] + both[count:]
    back = back + lax.dot_general(high, inner_ref[LANES:], NT, preferred_element_type=F32)
    back = back + along_first(flux_first, first_ref, 32)
    energy = flux * inner
    return back, flux_first * grad_first + energy[:, :LANES] + energy[:, LANES:]


def factors(points):
    nodes = 0.5 * (1.0 + np.cos(np.pi * np.arange(8) / 7.0))
    out = []
    for shift in (6, 3, 0):
        index = (points >> shift) & 7
        near = jnp.full(points.shape, nodes[7], F32)
        far = jnp.full(points.shape, nodes[0], F32)
        for m in range(7):
            near = jnp.where(index == m, float(nodes[m]), near)
            far = jnp.where(index == m, float(nodes[7 - m]), far)
        out.append((near, far))
    return out


def corners(points):
    first, second, third = factors(points)
    return [
        first[q >> 2 & 1] * (second[q >> 1 & 1] * third[q & 1]) for q in range(8)
    ]


def own_corners():
    return corners(lax.broadcasted_iota(jnp.int32, (1, POINTS), 1))


def flat_map(mapped):
    elements = mapped.shape[1]
    width = 8 * elements
    own = own_element(elements, width)
    place = lax.broadcasted_iota(jnp.int32, (8, width), 1) // elements
    spread = jnp.where(own, 1.0, 0.0).astype(BF16)
    wide = jnp.dot(mapped.astype(F32).astype(BF16), spread, preferred_element_type=F32)
    keep = lax.broadcasted_iota(jnp.int32, (8, width), 0) == place
    return jnp.sum(jnp.where(keep, wide, 0.0), axis=0, keepdims=True)


def one_vertex(flat):
    return jnp.where(one_hot(whole(flat), NC), 1.0, 0.0)


def whole(values):
    return (values + 0.5).astype(jnp.int32)


def own_element(elements, width):
    shape = (elements, width)
    return lax.broadcasted_iota(jnp.int32, shape, 0) == (
        lax.broadcasted_iota(jnp.int32, shape, 1) % elements
    )


def own_place(elements, q):
    shape = (elements, 8 * elements)
    lane = lax.broadcasted_iota(jnp.int32, shape, 1)
    return lane == lax.broadcasted_iota(jnp.int32, shape, 0) + q * elements


def coarse_part(field, vertices, inverse):
    elements = field.shape[0] // 4
    flat = jnp.zeros((elements, 8 * elements), F32)
    for q, corner in enumerate(own_corners()):
        inner = None
        for c in range(4):
            term = field[c * elements : (c + 1) * elements] * corner[:, c * LANES : (c + 1) * LANES]
            inner = term if inner is None else inner + term
        flat = jnp.where(own_place(elements, q), jnp.sum(inner, axis=1, keepdims=True), flat)
    flat = jnp.sum(flat, axis=0, keepdims=True)
    part = jnp.sum(vertices * flat, axis=1, keepdims=True)
    part = jnp.sum(inverse * part, axis=0, keepdims=True)
    return jnp.concatenate([part, jnp.zeros((1, LANES - NC), F32)], axis=1)


def column(row):
    shape = (NC, LANES)
    keep = lax.broadcasted_iota(jnp.int32, shape, 0) == lax.broadcasted_iota(jnp.int32, shape, 1)
    return jnp.sum(jnp.where(keep, row, 0.0), axis=1, keepdims=True)


def get_solved(received_ref, count, peers):
    rows = get(received_ref, count, 1)
    return [
        column(
            jnp.sum(
                jnp.where(own_group(rows.shape[0], peers, away), rows, 0.0), axis=0, keepdims=True
            )
        )
        for away in (0, -1, 1)
    ]


def prolonged(solved, vertices, elements):
    flat = jnp.sum(vertices * solved, axis=0, keepdims=True)
    out = [None] * 4
    for q, corner in enumerate(own_corners()):
        value = jnp.sum(jnp.where(own_place(elements, q), flat, 0.0), axis=1, keepdims=True)
        for c in range(4):
            term = value * corner[:, c * LANES : (c + 1) * LANES]
            out[c] = term if out[c] is None else out[c] + term
    return jnp.concatenate(out, axis=0)


def prolong_at(points, vertices, elements):
    mine = lax.broadcasted_iota(jnp.int32, (elements, points.shape[1]), 0) == points >> 9
    weights = jnp.concatenate([jnp.where(mine, corner, 0.0) for corner in corners(points)], axis=0)
    high, low = split(weights)
    both = jnp.dot(
        vertices.astype(BF16),
        jnp.concatenate([high, low], axis=1),
        preferred_element_type=F32,
    )
    return both[:, : points.shape[1]] + both[:, points.shape[1] :]


def total_of(array):
    return jnp.sum(jnp.sum(array, axis=0, keepdims=True), axis=1, keepdims=True)


def packed(values):
    lane = lax.broadcasted_iota(jnp.int32, (1, LANES), 1)
    out = jnp.zeros((1, LANES), F32)
    for k, value in enumerate(values):
        out = jnp.where(lane == k, value, out)
    return out


def unpacked(row, count):
    lane = lax.broadcasted_iota(jnp.int32, row.shape, 1)
    return [
        jnp.sum(jnp.where(lane == k, row, 0.0), axis=1, keepdims=True) for k in range(count)
    ]


def first_kernel(
    right_hbm, jacobi_hbm, inverse_hbm, map_hbm, slot_hbm, face_hbm,
    sent_ref, faces_ref, fields_ref, points_ref,
    right_ref, jacobi_ref, inverse_ref, map_ref, slot_ref, face_ref, sems,
):
    copies = []
    for k, (source, target) in enumerate(
        (
            (face_hbm, face_ref),
            (slot_hbm, slot_ref),
            (right_hbm, right_ref),
            (jacobi_hbm, jacobi_ref),
            (map_hbm, map_ref),
            (inverse_hbm, inverse_ref),
        )
    ):
        copy = pltpu.make_async_copy(source, target, sems.at[k])
        copy.start()
        copies.append(copy)
    for copy in copies:
        copy.wait()
    elements = right_ref.shape[0]
    peers = slot_ref.shape[1]
    faces = face_ref[...]
    faces = jnp.concatenate(halves(faces[0:1]) + halves(faces[1:2]), axis=0)
    points = jnp.concatenate([slot_ref[0], faces], axis=0)
    points_ref[...] = points
    resid = rows_of(right_ref[...])
    flat = flat_map(map_ref[...])
    smoothed = rows_of(jacobi_ref[...]) * resid
    fields_ref[0 : 4 * elements, :] = resid
    fields_ref[4 * elements : 8 * elements, :] = smoothed
    fields_ref[8 * elements :, :] = jnp.broadcast_to(flat, (8, LANES))
    part = coarse_part(resid, one_vertex(flat), inverse_ref[0])
    values = gather(smoothed, far_chunks(points, elements))
    send_values(sent_ref, faces_ref, FIRST_ROWS, values, peers)
    send_same(sent_ref, FIRST_ROWS, 1, part)
    send_same(sent_ref, FIRST_ROWS, 2, flat)
    points = points.astype(F32)
    send_shared(sent_ref, FIRST_ROWS, 3, points[:peers])
    faces_ref[2 * FACE_ROWS :, :] = points[peers:]


def static_of(received_ref, gathered_ref, peers, elements):
    maps = get(received_ref, FIRST_ROWS, 2)
    own = get_shared(received_ref, FIRST_ROWS, 2, peers)
    shared = whole(get_shared(received_ref, FIRST_ROWS, 3, peers))
    out = [
        prolong_at(shared[b : b + 1], one_vertex(own[b : b + 1]), elements) for b in range(peers)
    ]
    faces = whole(get_faces(gathered_ref, 2 * FACE_ROWS, maps.shape[0] // peers))
    faces = joined(faces)
    for k, points in enumerate(faces):
        away = -1 if k < len(faces) // 2 else 1
        out.append(prolong_at(points, one_vertex(get_row(maps, peers, away)), elements))
    return jnp.concatenate(out, axis=1)


def get_far(received_ref, gathered_ref, count, peers):
    groups = received_ref.shape[0] // (count * peers)
    return jnp.concatenate(
        [get_shared(received_ref, count, 0, peers), get_faces(gathered_ref, 0, groups)], axis=0
    )


def apply(
    smoothed, count, received_ref, gathered_ref, weights, solved, metric_ref, helmholtz_ref,
    first_ref, inner_ref, pair_ref, points_ref, dots, back_ref, local_ref, sent_ref, faces_ref,
):
    elements = smoothed.shape[0] // 4
    peers = points_ref.shape[0] - 2 * FACE_ROWS
    pairs = pair_chunks(pair_ref, elements)
    far = far_chunks(points_ref[...], elements)
    ends = [LANES * k for k in (0, peers, peers + FACE_ROWS, peers + 2 * FACE_ROWS)]
    coarse = []
    for k in range(3):
        coarse += halves(
            jnp.sum(weights[:, ends[k] : ends[k + 1]] * solved[k], axis=0, keepdims=True)
        )
    incoming = get_far(received_ref, gathered_ref, count, peers) + jnp.concatenate(coarse, axis=0)
    values = swapped(gather(smoothed, pairs)) + joined(incoming)
    summed = smoothed + scatter(smoothed.shape[0], pairs + far, values)
    back, energy = stiffness(summed, metric_ref, first_ref, inner_ref)
    energy = energy + rows_of(helmholtz_ref[...]) * smoothed * smoothed
    back_ref[...] = back
    values = gather(back, pairs + far)
    near = swapped(values[: len(pairs)])
    for k, value in enumerate(near):
        local_ref[0:1, k * STEP : (k + 1) * STEP] = value
    send_values(sent_ref, faces_ref, ROWS, values[len(pairs) :], peers)
    send_same(sent_ref, ROWS, 1, packed(dots + [total_of(energy)]))


def image_of(
    field_ref, back_ref, local_ref, received_ref, gathered_ref, helmholtz_ref, pair_ref, points_ref
):
    elements = field_ref.shape[0] // 4
    peers = points_ref.shape[0] - 2 * FACE_ROWS
    chunks = pair_chunks(pair_ref, elements) + far_chunks(points_ref[...], elements)
    values = cut(local_ref[...]) + joined(get_far(received_ref, gathered_ref, ROWS, peers))
    summed = back_ref[...] + scatter(field_ref.shape[0], chunks, values)
    return summed + rows_of(helmholtz_ref[...]) * field_ref[...]


def start_kernel(
    received_ref, gathered_ref, fields_ref, points_ref, pair_ref, metric_ref, helmholtz_ref,
    first_ref, inner_ref,
    smoothed_ref, weights_ref, back_ref, local_ref, sent_ref, faces_ref,
):
    elements = helmholtz_ref.shape[0]
    peers = points_ref.shape[0] - 2 * FACE_ROWS
    solved = get_solved(received_ref, FIRST_ROWS, peers)
    resid = fields_ref[0 : 4 * elements, :]
    vertices = one_vertex(fields_ref[8 * elements : 8 * elements + 1, :])
    smoothed = fields_ref[4 * elements : 8 * elements, :]
    smoothed = smoothed + prolonged(solved[0], vertices, elements)
    smoothed_ref[...] = smoothed
    weights = static_of(received_ref, gathered_ref, peers, elements)
    weights_ref[...] = weights
    apply(
        smoothed, FIRST_ROWS, received_ref, gathered_ref, weights, solved, metric_ref,
        helmholtz_ref, first_ref, inner_ref, pair_ref, points_ref,
        [total_of(resid * smoothed)], back_ref, local_ref, sent_ref, faces_ref,
    )


def middle_kernel(
    received_ref, gathered_ref, fields_ref, points_ref, pair_ref, jacobi_ref, helmholtz_ref,
    inverse_ref, smoothed_ref, back_ref, local_ref,
    image_ref, resid_ref, scalars_ref, sent_ref, faces_ref,
):
    elements = helmholtz_ref.shape[0]
    peers = points_ref.shape[0] - 2 * FACE_ROWS
    dots = jnp.sum(get(received_ref, ROWS, 1), axis=0, keepdims=True)
    scalars_ref[...] = dots
    values = unpacked(dots, 2)
    alpha = values[0] / values[1]
    image = image_of(
        smoothed_ref, back_ref, local_ref, received_ref, gathered_ref, helmholtz_ref, pair_ref,
        points_ref,
    )
    image_ref[...] = image
    resid = fields_ref[0 : 4 * elements, :] - alpha * image
    resid_ref[...] = resid
    vertices = one_vertex(fields_ref[8 * elements : 8 * elements + 1, :])
    part = coarse_part(resid, vertices, inverse_ref[0])
    values = gather(rows_of(jacobi_ref[...]) * resid, far_chunks(points_ref[...], elements))
    send_values(sent_ref, faces_ref, ROWS, values, peers)
    send_same(sent_ref, ROWS, 1, part)


def second_kernel(
    received_ref, gathered_ref, fields_ref, points_ref, pair_ref, resid_ref, image_ref,
    weights_ref, jacobi_ref, metric_ref, helmholtz_ref, first_ref, inner_ref,
    smoothed_ref, back_ref, local_ref, sent_ref, faces_ref,
):
    elements = helmholtz_ref.shape[0]
    peers = points_ref.shape[0] - 2 * FACE_ROWS
    solved = get_solved(received_ref, ROWS, peers)
    resid = resid_ref[...]
    vertices = one_vertex(fields_ref[8 * elements : 8 * elements + 1, :])
    smoothed = rows_of(jacobi_ref[...]) * resid + prolonged(solved[0], vertices, elements)
    smoothed_ref[...] = smoothed
    apply(
        smoothed, ROWS, received_ref, gathered_ref, weights_ref[...], solved, metric_ref,
        helmholtz_ref, first_ref, inner_ref, pair_ref, points_ref,
        [total_of(resid * smoothed), total_of(image_ref[...] * smoothed)],
        back_ref, local_ref, sent_ref, faces_ref,
    )


def final_kernel(
    received_ref, gathered_ref, points_ref, pair_ref, old_ref, field_ref, resid_ref, old_image_ref,
    scalars_ref, back_ref, local_ref, helmholtz_ref,
    solution_ref, residual_ref,
):
    before = unpacked(scalars_ref[...], 2)
    now = unpacked(jnp.sum(get(received_ref, ROWS, 1), axis=0, keepdims=True), 3)
    alpha = before[0] / before[1]
    beta = now[0] / before[0]
    curved = now[2] + beta * (2.0 * now[1] + beta * before[1])
    step = now[0] / curved
    old = old_ref[...]
    direction = field_ref[...] + beta * old
    solution_ref[...] = wide_of(alpha * old + step * direction)
    image = image_of(
        field_ref, back_ref, local_ref, received_ref, gathered_ref, helmholtz_ref, pair_ref,
        points_ref,
    )
    image = image + beta * old_image_ref[...]
    residual_ref[...] = wide_of(resid_ref[...] - step * image)


def call(kernel, outs, *args, copied=False):
    space = pl.ANY if copied else pltpu.VMEM
    scratch = [pltpu.VMEM(arg.shape, arg.dtype) for arg in args] if copied else []
    return pl.pallas_call(
        kernel,
        out_shape=[jax.ShapeDtypeStruct(*out) if isinstance(out[0], tuple) else jax.ShapeDtypeStruct(out, F32) for out in outs],
        in_specs=[pl.BlockSpec(memory_space=space)] * len(args),
        out_specs=[pl.BlockSpec(memory_space=pltpu.VMEM)] * len(outs),
        scratch_shapes=scratch + ([pltpu.SemaphoreType.DMA((len(args),))] if copied else []),
        compiler_params=pltpu.CompilerParams(vmem_limit_bytes=(60 if copied else 24) * 1024 * 1024),
    )(*args)


def body(
    right_side,
    metric,
    helmholtz,
    jacobi,
    pair_list,
    shared_slots,
    face_points,
    coarse_map,
    coarse_inverse,
):
    peers = lax.axis_size("sub")
    groups = lax.axis_size("grp")
    t = {name: jnp.asarray(value) for name, value in tables().items()}
    elements = right_side.shape[0]
    field = (4 * elements, LANES)
    local = (1, pair_list.shape[0] * pair_list.shape[1])
    points_shape = (peers + 2 * FACE_ROWS, LANES)
    outs = [(groups * peers * ROWS, LANES), (2 * FACE_ROWS, LANES)]

    def exchange(sent, faces):
        gathered = lax.all_gather(faces, "grp", axis=0, tiled=True)
        rows = sent.reshape(groups * peers, 1, -1)
        received = lax.all_to_all(rows, ("grp", "sub"), 0, 0, tiled=True)
        return received.reshape(sent.shape), gathered

    sent, faces, fields, points = call(
        first_kernel,
        [
            (groups * peers * FIRST_ROWS, LANES),
            (4 * FACE_ROWS, LANES),
            (8 * elements + 8, LANES),
            (points_shape, jnp.int32),
        ],
        right_side, jacobi, coarse_inverse, coarse_map, shared_slots, face_points, copied=True,
    )
    smoothed, weights, back, near, sent, faces = call(
        start_kernel,
        [field, (NC, points_shape[0] * LANES), field, local, *outs],
        *exchange(sent, faces), fields, points, pair_list, metric, helmholtz,
        t["first"], t["inner"],
    )
    image, resid, scalars, sent, faces = call(
        middle_kernel, [field, field, (1, LANES), *outs],
        *exchange(sent, faces), fields, points, pair_list, jacobi, helmholtz, coarse_inverse,
        smoothed, back, near,
    )
    second, back, near, sent, faces = call(
        second_kernel, [field, field, local, *outs],
        *exchange(sent, faces), fields, points, pair_list, resid, image, weights, jacobi,
        metric, helmholtz, t["first"], t["inner"],
    )
    return tuple(
        call(
            final_kernel, [right_side.shape, right_side.shape],
            *exchange(sent, faces), points, pair_list, smoothed, second, resid, image, scalars,
            back, near, helmholtz,
        )
    )


def solution(mesh):
    in_specs = (
        P(("grp", "sub"), None),
        P(("grp", "sub"), None),
        P(("grp", "sub"), None),
        P(("grp", "sub"), None),
        P(None, ("grp", "sub")),
        P(("grp", "sub"), None, None),
        P(None, ("grp", "sub")),
        P(None, ("grp", "sub")),
        P("grp", None, None),
    )
    out_specs = (P(("grp", "sub"), None), P(("grp", "sub"), None))
    return jax.shard_map(body, mesh=mesh, in_specs=in_specs, out_specs=out_specs, check_vma=False)
```

time: 56.9 us -> 89.9 us (1.58)
  starting transfers between devices: 0 us -> 23.9 us
  blocking collectives: 44.2 us -> 53.8 us
  local copies, waits for them, and re-layouts: 2.87 us -> 0.94 us
  Pallas kernels: 8.53 us -> 9.98 us
    all_gather x0 -> x4, blocking collectives: none -> 53.8 us  [exchange(): gathered = lax.all_gather(faces, 'grp', axis=0, tiled=True)]
    all_to_all x4 -> x0, blocking collectives: 44.2 us -> none  [exchange(): lax.all_to_all(rows, ('grp', 'sub'), 0, 0, tiled=True).reshape(sent.shape)]
    all_to_all x0 -> x4, starting transfers between devices: none -> 23.9 us  [exchange(): received = lax.all_to_all(rows, ('grp', 'sub'), 0, 0, tiled=True)]
    unnamed x30 -> x22, local copies, waits for them, and re-layouts: 2.87 us -> 0.94 us
    pallas_call x5, Pallas kernels: 8.53 us -> 9.98 us  [call(): pl.pallas_call(kernel, out_shape=[jax.ShapeDtypeStruct(*out) if isinstanc...]
  transfers between devices with their start and end apart: 0 -> 4, of which waited for: 0 -> 0; matrix products, arithmetic and copies ran while one was open for 0% -> 0% of each run, Pallas kernels for 0% -> 0%
where the time goes in v4:
time: 89.9 us; the launch traced here: 89.4 us
  blocking collectives  53.8 us (60%)
  starting transfers between devices  23.9 us (27%)
  Pallas kernels  9.98 us (11%)
  local copies, waits for them, and re-layouts  0.94 us (1%)
    all_gather x4, blocking collectives, exchange(): gathered = lax.all_gather(faces, 'grp', axis=0, tiled=True)  53.8 us
    all_to_all x4, starting transfers between devices, exchange(): received = lax.all_to_all(rows, ('grp', 'sub'), 0, 0, tiled=True)  23.9 us
    pallas_call x5, Pallas kernels, call(): pl.pallas_call(kernel, out_shape=[jax.ShapeDtypeStruct(*out) if isinstanc...  9.98 us
  transfers between devices with their start and end apart: 4, of which 0 were waited for; matrix products, arithmetic and copies ran while one was open for 0% of the time, Pallas kernels for 0%

profile of v4, /device:TPU:0, one launch (start us, length us, event | category | flops | bytes accessed | tf_op | source)
XLA Modules:
  0.0 89.4 jit_solution(17644400832147788801)
XLA Ops:
  0.6 0.0 copy-start.2
  0.6 2.0 %shard_map.122 = (f32[128,128]{1,0:T(8,128)}, f32[16,128]{1,0:T(8,128)}, f32[136,128]{1,0:T(8,128)}, s32[16,128]{1,0:T(8,128)}) custom-call(f32[16,512]{1,0:T(8,128)} %right_hbm.1, f32[16,512]{1,0:T(8,128)} %jacobi_ref.3, f32[1,64,64]{2,1,0:T(8,128)} %inverse_ref.1, s32[8,16]{1,0:T(8,128)} %map_hbm.1, s32[1,8,128]{2,1,0:T(8,128)} %slot_hbm.1, s32[2,512]{1,0:T(2,128)} %face_hbm.1), custom_call_target="tpu_custom_call" | custom-call | tf_op jit(solution)/shard_map/pallas_call | solution.py:572
  2.6 0.0 copy-start.10
  2.7 0.0 copy-start
  2.7 0.0 copy-start.8
  2.7 0.0 copy-start.9
  2.7 7.3 %all-to-all-start = ((f32[32,1,512]{2,1,0:T(1,128)}), f32[32,1,512]{2,1,0:T(1,128)S(1)}, u32[]{:S(2)}, u32[]{:S(2)}) async-start(f32[32,1,512]{2,1,0:T(1,128)} %bitcast.12), calls=%async_computation | async-start | bytes 131072 | tf_op jit(solution)/shard_map/all_to_all | solution.py:605
  10.0 0.0 copy-start.1
  10.0 0.0 copy-done.10
  10.0 0.0 copy-start.7
  10.0 13.4 %all_gather.12.gathered_ref = f32[64,128]{1,0:T(8,128)S(1)} all-gather(f32[16,128]{1,0:T(8,128)S(1)} %copy-done.10), channel_id=1, replica_groups=mesh['grp'=4,'sub'=8] {'grp'}, dimensions={0}, use_global_device_ids=true | all-gather | bytes 40960 | tf_op jit(solution)/shard_map/all_gather | solution.py:603
  23.5 0.0 all-to-all-done
  23.5 0.0 copy-done.2
  23.5 0.0 copy-done
  23.5 0.0 copy-done.8
  23.5 0.0 copy-done.9
  23.5 0.0 copy-done.1
  23.5 0.0 copy-done.7
  23.5 0.0 copy-start.3
  23.5 0.9 copy-done.3
  24.4 2.6 %shard_map.123 = (f32[64,128]{1,0:T(8,128)S(1)}, f32[64,2048]{1,0:T(8,128)S(1)}, f32[64,128]{1,0:T(8,128)S(1)}, f32[1,2048]{1,0:T(1,128)S(1)}, f32[64,128]{1,0:T(8,128)}, /*index=5*/f32[8,128]{1,0:T(8,128)S(1)}) custom-call(f32[128,128]{1,0:T(8,128)S(1)} %bitcast.8, f32[64,128]{1,0:T(8,128)S(1)} %all_gather.12.gathered_ref, f32[136,128]{1,0:T(8,128)S(1)} %copy-done, ...), custom_call_target="tpu_custom_call" | custom-call | tf_op jit(solution)/shard_map/pallas_call | solution.py:572
  27.1 0.0 copy-start.5
  27.1 0.0 copy-start.6
  27.1 5.5 %all-to-all-start.1 = ((f32[32,1,256]{2,1,0:T(1,128)}), f32[32,1,256]{2,1,0:T(1,128)S(1)}, u32[]{:S(2)}, u32[]{:S(2)}) async-start(f32[32,1,256]{2,1,0:T(1,128)} %bitcast.2), calls=%async_computation.1 | async-start | bytes 65536 | tf_op jit(solution)/shard_map/all_to_all | solution.py:605
  32.6 13.4 %all_gather.13.gathered_ref = f32[32,128]{1,0:T(8,128)S(1)} all-gather(f32[8,128]{1,0:T(8,128)S(1)} %get-tuple-element.27), channel_id=1, replica_groups=mesh['grp'=4,'sub'=8] {'grp'}, dimensions={0}, use_global_device_ids=true | all-gather | bytes 20480 | tf_op jit(solution)/shard_map/all_gather | solution.py:603
  46.0 0.0 all-to-all-done.1
  46.0 0.0 copy-done.5
  46.1 0.0 copy-done.6
  46.1 1.6 %shard_map.124 = (f32[64,128]{1,0:T(8,128)S(1)}, f32[64,128]{1,0:T(8,128)S(1)}, f32[1,128]{1,0:T(1,128)S(1)}, f32[64,128]{1,0:T(8,128)}, f32[8,128]{1,0:T(8,128)S(1)}) custom-call(f32[64,128]{1,0:T(8,128)S(1)} %bitcast.11, f32[32,128]{1,0:T(8,128)S(1)} %all_gather.13.gathered_ref, f32[136,128]{1,0:T(8,128)S(1)} %copy-done, s32[16,128]{1,0:T(8,128)S(1)} %copy-done.8, ...), custom_call_target="tpu_custom_call" | custom-call | tf_op jit(solution)/shard_map/pallas_call | solution.py:572
  47.7 0.0 copy-start.4
  47.7 5.5 %all-to-all-start.2 = ((f32[32,1,256]{2,1,0:T(1,128)}), f32[32,1,256]{2,1,0:T(1,128)S(1)}, u32[]{:S(2)}, u32[]{:S(2)}) async-start(f32[32,1,256]{2,1,0:T(1,128)} %bitcast.4), calls=%async_computation.2 | async-start | bytes 65536 | tf_op jit(solution)/shard_map/all_to_all | solution.py:605
  53.2 13.4 %all_gather.14.gathered_ref = f32[32,128]{1,0:T(8,128)S(1)} all-gather(f32[8,128]{1,0:T(8,128)S(1)} %get-tuple-element.32), channel_id=1, replica_groups=mesh['grp'=4,'sub'=8] {'grp'}, dimensions={0}, use_global_device_ids=true | all-gather | bytes 20480 | tf_op jit(solution)/shard_map/all_gather | solution.py:603
  66.7 0.0 all-to-all-done.2
  66.7 0.0 copy-done.4
  66.7 2.4 %shard_map.125 = (f32[64,128]{1,0:T(8,128)S(1)}, f32[64,128]{1,0:T(8,128)S(1)}, f32[1,2048]{1,0:T(1,128)S(1)}, f32[64,128]{1,0:T(8,128)}, f32[8,128]{1,0:T(8,128)S(1)}) custom-call(f32[64,128]{1,0:T(8,128)S(1)} %bitcast.10, f32[32,128]{1,0:T(8,128)S(1)} %all_gather.14.gathered_ref, f32[136,128]{1,0:T(8,128)S(1)} %copy-done, s32[16,128]{1,0:T(8,128)S(1)} %copy-done.8, ...), custom_call_target="tpu_custom_call" | custom-call | tf_op jit(solution)/shard_map/pallas_call | solution.py:572
  69.1 5.5 %all-to-all-start.3 = ((f32[32,1,256]{2,1,0:T(1,128)}), f32[32,1,256]{2,1,0:T(1,128)S(1)}, u32[]{:S(2)}, u32[]{:S(2)}) async-start(f32[32,1,256]{2,1,0:T(1,128)} %bitcast.6), calls=%async_computation.3 | async-start | bytes 65536 | tf_op jit(solution)/shard_map/all_to_all | solution.py:605
  74.6 13.4 %all_gather.15.gathered_ref = f32[32,128]{1,0:T(8,128)S(1)} all-gather(f32[8,128]{1,0:T(8,128)S(1)} %get-tuple-element.37), channel_id=1, replica_groups=mesh['grp'=4,'sub'=8] {'grp'}, dimensions={0}, use_global_device_ids=true | all-gather | bytes 20480 | tf_op jit(solution)/shard_map/all_gather | solution.py:603
  88.0 0.0 all-to-all-done.3
  88.0 1.3 %shard_map.126 = (f32[16,512]{1,0:T(8,128)}, f32[16,512]{1,0:T(8,128)}) custom-call(f32[64,128]{1,0:T(8,128)S(1)} %bitcast.9, f32[32,128]{1,0:T(8,128)S(1)} %all_gather.15.gathered_ref, s32[16,128]{1,0:T(8,128)S(1)} %copy-done.8, s32[2,1024]{1,0:T(2,128)S(1)} %copy-done.7, f32[64,128]{1,0:T(8,128)S(1)} %get-tuple-element.28.smoothed_ref.old_ref, ...), custom_call_target="tpu_custom_call" | custom-call | tf_op jit(solution)/shard_map/pallas_call | solution.py:572
Async XLA Ops:
  0.6 22.8 %copy-start.2 = (bf16[256,256]{1,0:T(8,128)(2,1)S(1)}, bf16[256,256]{1,0:T(8,128)(2,1)}, u32[]{:S(2)}) copy-start(bf16[256,256]{1,0:T(8,128)(2,1)} %constant.4.clone.inner_ref) | copy-start | bytes 393220
  2.6 7.4 %copy-start.10 = (f32[16,128]{1,0:T(8,128)S(1)}, f32[16,128]{1,0:T(8,128)}, u32[]{:S(2)}) copy-start(f32[16,128]{1,0:T(8,128)} %get-tuple-element.23) | copy-start | bytes 24580
  2.7 20.8 %copy-start = (f32[136,128]{1,0:T(8,128)S(1)}, f32[136,128]{1,0:T(8,128)}, u32[]{:S(2)}) copy-start(f32[136,128]{1,0:T(8,128)} %get-tuple-element.24.fields_ref) | copy-start | bytes 208900
  2.7 20.8 %copy-start.8 = (s32[16,128]{1,0:T(8,128)S(1)}, s32[16,128]{1,0:T(8,128)}, u32[]{:S(2)}) copy-start(s32[16,128]{1,0:T(8,128)} %get-tuple-element.25.points_ref) | copy-start | bytes 24580
  2.7 20.8 %copy-start.9 = (f32[64,128]{1,0:T(8,128)S(1)}, f32[64,128]{1,0:T(8,128)}, u32[]{:S(2)}) copy-start(f32[64,128]{1,0:T(8,128)} %constant.5.clone.first_ref) | copy-start | bytes 98308
  2.7 20.8 %all-to-all-start = ((f32[32,1,512]{2,1,0:T(1,128)}), f32[32,1,512]{2,1,0:T(1,128)S(1)}, u32[]{:S(2)}, u32[]{:S(2)}) async-start(f32[32,1,512]{2,1,0:T(1,128)} %bitcast.12), calls=%async_computation | async-start | bytes 131072 | tf_op jit(solution)/shard_map/all_to_all | solution.py:605
  10.0 13.5 %copy-start.1 = (f32[16,512]{1,0:T(8,128)S(1)}, f32[16,512]{1,0:T(8,128)}, u32[]{:S(2)}) copy-start(f32[16,512]{1,0:T(8,128)} %helmholtz_ref.7) | copy-start | bytes 98308
  10.0 13.5 %copy-start.7 = (s32[2,1024]{1,0:T(2,128)S(1)}, s32[2,1024]{1,0:T(2,128)}, u32[]{:S(2)}) copy-start(s32[2,1024]{1,0:T(2,128)} %pair_ref.7) | copy-start | bytes 24580
  23.5 0.9 %copy-start.3 = (f32[16,1536]{1,0:T(8,128)S(1)}, f32[16,1536]{1,0:T(8,128)}, u32[]{:S(2)}) copy-start(f32[16,1536]{1,0:T(8,128)} %metric_ref.3) | copy-start | bytes 294916
  27.1 19.0 %copy-start.5 = (f32[16,512]{1,0:T(8,128)S(1)}, f32[16,512]{1,0:T(8,128)}, u32[]{:S(2)}) copy-start(f32[16,512]{1,0:T(8,128)} %jacobi_ref.3) | copy-start | bytes 98308
  27.1 19.0 %copy-start.6 = (f32[1,64,64]{2,1,0:T(8,128)S(1)}, f32[1,64,64]{2,1,0:T(8,128)}, u32[]{:S(2)}) copy-start(f32[1,64,64]{2,1,0:T(8,128)} %inverse_ref.1) | copy-start | bytes 49156
  27.1 19.0 %all-to-all-start.1 = ((f32[32,1,256]{2,1,0:T(1,128)}), f32[32,1,256]{2,1,0:T(1,128)S(1)}, u32[]{:S(2)}, u32[]{:S(2)}) async-start(f32[32,1,256]{2,1,0:T(1,128)} %bitcast.2), calls=%async_computation.1 | async-start | bytes 65536 | tf_op jit(solution)/shard_map/all_to_all | solution.py:605
  47.7 19.0 %copy-start.4 = (f32[16,1536]{1,0:T(8,128)S(1)}, f32[16,1536]{1,0:T(8,128)}, u32[]{:S(2)}) copy-start(f32[16,1536]{1,0:T(8,128)} %metric_ref.3) | copy-start | bytes 294916
  47.7 19.0 %all-to-all-start.2 = ((f32[32,1,256]{2,1,0:T(1,128)}), f32[32,1,256]{2,1,0:T(1,128)S(1)}, u32[]{:S(2)}, u32[]{:S(2)}) async-start(f32[32,1,256]{2,1,0:T(1,128)} %bitcast.4), calls=%async_computation.2 | async-start | bytes 65536 | tf_op jit(solution)/shard_map/all_to_all | solution.py:605
  69.1 19.0 %all-to-all-start.3 = ((f32[32,1,256]{2,1,0:T(1,128)}), f32[32,1,256]{2,1,0:T(1,128)S(1)}, u32[]{:S(2)}, u32[]{:S(2)}) async-start(f32[32,1,256]{2,1,0:T(1,128)} %bitcast.6), calls=%async_computation.3 | async-start | bytes 65536 | tf_op jit(solution)/shard_map/all_to_all | solution.py:605

commit v5 on v4

--- a/solution.py
+++ b/solution.py
@@ -12,8 +12,9 @@
 LANES = 128
 STEP = 256
 FACE_ROWS = 4
-ROWS = 2
-FIRST_ROWS = 4
+ROWS = 8
+FIRST_ROWS = 16
+TERMS = FACE_ROWS
 F32 = jnp.float32
 BF16 = jnp.bfloat16
 NT = (((1,), (1,)), ((), ()))
@@ -148,10 +149,17 @@
     return lax.broadcasted_iota(jnp.int32, shape, 0) // peers - lax.axis_index("grp") == away
 
 
-def send_shared(sent_ref, count, at, shared):
+def send_rows(sent_ref, count, at, rows, peers):
     devices = sent_ref.shape[0] // count
-    copies = devices // shared.shape[0]
-    sent_ref[pl.ds(at, devices, count), :] = jnp.concatenate([shared] * copies, axis=0)
+    above = own_group(devices, peers, 1)
+    shared = jnp.concatenate([rows[:peers]] * (devices // peers), axis=0)
+    for r in range(FACE_ROWS):
+        down = rows[peers + r : peers + r + 1]
+        up = rows[peers + FACE_ROWS + r : peers + FACE_ROWS + r + 1]
+        out = jnp.where(above, up, down)
+        if r == 0:
+            out = jnp.where(own_group(devices, peers), shared, out)
+        sent_ref[pl.ds(at + r, devices, count), :] = out
 
 
 def send_same(sent_ref, count, at, row):
@@ -159,18 +167,16 @@
     sent_ref[pl.ds(at, devices, count), :] = jnp.broadcast_to(row, (devices, LANES))
 
 
-def send_values(sent_ref, faces_ref, count, values, peers):
+def send_values(sent_ref, count, values, peers):
     rows = jnp.concatenate([row for pair in values for row in halves(pair)], axis=0)
-    send_shared(sent_ref, count, 0, rows[:peers])
-    faces_ref[0 : 2 * FACE_ROWS, :] = rows[peers:]
+    send_rows(sent_ref, count, 0, rows, peers)
 
 
 def get(received_ref, count, at):
     return received_ref[pl.ds(at, received_ref.shape[0] // count, count), :]
 
 
-def get_shared(received_ref, count, at, peers):
-    rows = get(received_ref, count, at)
+def get_shared(rows, peers):
     mine = jnp.where(own_group(rows.shape[0], peers), rows, 0.0)
     shared = mine[:peers]
     for g in range(1, rows.shape[0] // peers):
@@ -184,15 +190,10 @@
     return jnp.sum(jnp.where(source, rows, 0.0), axis=0, keepdims=True)
 
 
-def get_faces(gathered_ref, at, groups):
-    count = gathered_ref.shape[0] // groups
-    group = lax.axis_index("grp")
-    below, above = 0.0, 0.0
-    for g in range(groups):
-        rows = gathered_ref[g * count + at : g * count + at + 2 * FACE_ROWS, :]
-        below = below + jnp.where(group == g + 1, rows[FACE_ROWS:], 0.0)
-        above = above + jnp.where(group == g - 1, rows[:FACE_ROWS], 0.0)
-    return jnp.concatenate([below, above], axis=0)
+def get_rows(received_ref, count, at, peers):
+    rows = [get(received_ref, count, at + r) for r in range(FACE_ROWS)]
+    faces = [get_row(part, peers, away) for away in (-1, 1) for part in rows]
+    return jnp.concatenate([get_shared(rows[0], peers)] + faces, axis=0)
 
 
 def swapped(values):
@@ -320,7 +321,7 @@
 
 
 def get_solved(received_ref, count, peers):
-    rows = get(received_ref, count, 1)
+    rows = get(received_ref, count, TERMS)
     return [
         column(
             jnp.sum(
@@ -375,7 +376,7 @@
 
 def first_kernel(
     right_hbm, jacobi_hbm, inverse_hbm, map_hbm, slot_hbm, face_hbm,
-    sent_ref, faces_ref, fields_ref, points_ref,
+    sent_ref, fields_ref, points_ref,
     right_ref, jacobi_ref, inverse_ref, map_ref, slot_ref, face_ref, sems,
 ):
     copies = []
@@ -408,39 +409,28 @@
     fields_ref[8 * elements :, :] = jnp.broadcast_to(flat, (8, LANES))
     part = coarse_part(resid, one_vertex(flat), inverse_ref[0])
     values = gather(smoothed, far_chunks(points, elements))
-    send_values(sent_ref, faces_ref, FIRST_ROWS, values, peers)
-    send_same(sent_ref, FIRST_ROWS, 1, part)
-    send_same(sent_ref, FIRST_ROWS, 2, flat)
-    points = points.astype(F32)
-    send_shared(sent_ref, FIRST_ROWS, 3, points[:peers])
-    faces_ref[2 * FACE_ROWS :, :] = points[peers:]
-
-
-def static_of(received_ref, gathered_ref, peers, elements):
-    maps = get(received_ref, FIRST_ROWS, 2)
-    own = get_shared(received_ref, FIRST_ROWS, 2, peers)
-    shared = whole(get_shared(received_ref, FIRST_ROWS, 3, peers))
+    send_values(sent_ref, FIRST_ROWS, values, peers)
+    send_same(sent_ref, FIRST_ROWS, TERMS, part)
+    send_same(sent_ref, FIRST_ROWS, TERMS + 1, flat)
+    send_rows(sent_ref, FIRST_ROWS, TERMS + 2, points.astype(F32), peers)
+
+
+def static_of(received_ref, peers, elements):
+    maps = get(received_ref, FIRST_ROWS, TERMS + 1)
+    own = get_shared(maps, peers)
+    points = whole(get_rows(received_ref, FIRST_ROWS, TERMS + 2, peers))
     out = [
-        prolong_at(shared[b : b + 1], one_vertex(own[b : b + 1]), elements) for b in range(peers)
+        prolong_at(points[b : b + 1], one_vertex(own[b : b + 1]), elements) for b in range(peers)
     ]
-    faces = whole(get_faces(gathered_ref, 2 * FACE_ROWS, maps.shape[0] // peers))
-    faces = joined(faces)
-    for k, points in enumerate(faces):
-        away = -1 if k < len(faces) // 2 else 1
-        out.append(prolong_at(points, one_vertex(get_row(maps, peers, away)), elements))
+    for k, pair in enumerate(joined(points[peers:])):
+        away = -1 if 2 * k < FACE_ROWS else 1
+        out.append(prolong_at(pair, one_vertex(get_row(maps, peers, away)), elements))
     return jnp.concatenate(out, axis=1)
 
 
-def get_far(received_ref, gathered_ref, count, peers):
-    groups = received_ref.shape[0] // (count * peers)
-    return jnp.concatenate(
-        [get_shared(received_ref, count, 0, peers), get_faces(gathered_ref, 0, groups)], axis=0
-    )
-
-
 def apply(
-    smoothed, count, received_ref, gathered_ref, weights, solved, metric_ref, helmholtz_ref,
-    first_ref, inner_ref, pair_ref, points_ref, dots, back_ref, local_ref, sent_ref, faces_ref,
+    smoothed, count, received_ref, weights, solved, metric_ref, helmholtz_ref,
+    first_ref, inner_ref, pair_ref, points_ref, dots, back_ref, local_ref, sent_ref,
 ):
     elements = smoothed.shape[0] // 4
     peers = points_ref.shape[0] - 2 * FACE_ROWS
@@ -452,7 +442,7 @@
         coarse += halves(
             jnp.sum(weights[:, ends[k] : ends[k + 1]] * solved[k], axis=0, keepdims=True)
         )
-    incoming = get_far(received_ref, gathered_ref, count, peers) + jnp.concatenate(coarse, axis=0)
+    incoming = get_rows(received_ref, count, 0, peers) + jnp.concatenate(coarse, axis=0)
     values = swapped(gather(smoothed, pairs)) + joined(incoming)
     summed = smoothed + scatter(smoothed.shape[0], pairs + far, values)
     back, energy = stiffness(summed, metric_ref, first_ref, inner_ref)
@@ -462,25 +452,25 @@
     near = swapped(values[: len(pairs)])
     for k, value in enumerate(near):
         local_ref[0:1, k * STEP : (k + 1) * STEP] = value
-    send_values(sent_ref, faces_ref, ROWS, values[len(pairs) :], peers)
-    send_same(sent_ref, ROWS, 1, packed(dots + [total_of(energy)]))
+    send_values(sent_ref, ROWS, values[len(pairs) :], peers)
+    send_same(sent_ref, ROWS, TERMS, packed(dots + [total_of(energy)]))
 
 
 def image_of(
-    field_ref, back_ref, local_ref, received_ref, gathered_ref, helmholtz_ref, pair_ref, points_ref
+    field_ref, back_ref, local_ref, received_ref, helmholtz_ref, pair_ref, points_ref
 ):
     elements = field_ref.shape[0] // 4
     peers = points_ref.shape[0] - 2 * FACE_ROWS
     chunks = pair_chunks(pair_ref, elements) + far_chunks(points_ref[...], elements)
-    values = cut(local_ref[...]) + joined(get_far(received_ref, gathered_ref, ROWS, peers))
+    values = cut(local_ref[...]) + joined(get_rows(received_ref, ROWS, 0, peers))
     summed = back_ref[...] + scatter(field_ref.shape[0], chunks, values)
     return summed + rows_of(helmholtz_ref[...]) * field_ref[...]
 
 
 def start_kernel(
-    received_ref, gathered_ref, fields_ref, points_ref, pair_ref, metric_ref, helmholtz_ref,
+    received_ref, fields_ref, points_ref, pair_ref, metric_ref, helmholtz_ref,
     first_ref, inner_ref,
-    smoothed_ref, weights_ref, back_ref, local_ref, sent_ref, faces_ref,
+    smoothed_ref, weights_ref, back_ref, local_ref, sent_ref,
 ):
     elements = helmholtz_ref.shape[0]
     peers = points_ref.shape[0] - 2 * FACE_ROWS
@@ -490,28 +480,28 @@
     smoothed = fields_ref[4 * elements : 8 * elements, :]
     smoothed = smoothed + prolonged(solved[0], vertices, elements)
     smoothed_ref[...] = smoothed
-    weights = static_of(received_ref, gathered_ref, peers, elements)
+    weights = static_of(received_ref, peers, elements)
     weights_ref[...] = weights
     apply(
-        smoothed, FIRST_ROWS, received_ref, gathered_ref, weights, solved, metric_ref,
+        smoothed, FIRST_ROWS, received_ref, weights, solved, metric_ref,
         helmholtz_ref, first_ref, inner_ref, pair_ref, points_ref,
-        [total_of(resid * smoothed)], back_ref, local_ref, sent_ref, faces_ref,
+        [total_of(resid * smoothed)], back_ref, local_ref, sent_ref,
     )
 
 
 def middle_kernel(
-    received_ref, gathered_ref, fields_ref, points_ref, pair_ref, jacobi_ref, helmholtz_ref,
+    received_ref, fields_ref, points_ref, pair_ref, jacobi_ref, helmholtz_ref,
     inverse_ref, smoothed_ref, back_ref, local_ref,
-    image_ref, resid_ref, scalars_ref, sent_ref, faces_ref,
+    image_ref, resid_ref, scalars_ref, sent_ref,
 ):
     elements = helmholtz_ref.shape[0]
     peers = points_ref.shape[0] - 2 * FACE_ROWS
-    dots = jnp.sum(get(received_ref, ROWS, 1), axis=0, keepdims=True)
+    dots = jnp.sum(get(received_ref, ROWS, TERMS), axis=0, keepdims=True)
     scalars_ref[...] = dots
     values = unpacked(dots, 2)
     alpha = values[0] / values[1]
     image = image_of(
-        smoothed_ref, back_ref, local_ref, received_ref, gathered_ref, helmholtz_ref, pair_ref,
+        smoothed_ref, back_ref, local_ref, received_ref, helmholtz_ref, pair_ref,
         points_ref,
     )
     image_ref[...] = image
@@ -520,14 +510,14 @@
     vertices = one_vertex(fields_ref[8 * elements : 8 * elements + 1, :])
     part = coarse_part(resid, vertices, inverse_ref[0])
     values = gather(rows_of(jacobi_ref[...]) * resid, far_chunks(points_ref[...], elements))
-    send_values(sent_ref, faces_ref, ROWS, values, peers)
-    send_same(sent_ref, ROWS, 1, part)
+    send_values(sent_ref, ROWS, values, peers)
+    send_same(sent_ref, ROWS, TERMS, part)
 
 
 def second_kernel(
-    received_ref, gathered_ref, fields_ref, points_ref, pair_ref, resid_ref, image_ref,
+    received_ref, fields_ref, points_ref, pair_ref, resid_ref, image_ref,
     weights_ref, jacobi_ref, metric_ref, helmholtz_ref, first_ref, inner_ref,
-    smoothed_ref, back_ref, local_ref, sent_ref, faces_ref,
+    smoothed_ref, back_ref, local_ref, sent_ref,
 ):
     elements = helmholtz_ref.shape[0]
     peers = points_ref.shape[0] - 2 * FACE_ROWS
@@ -537,20 +527,20 @@
     smoothed = rows_of(jacobi_ref[...]) * resid + prolonged(solved[0], vertices, elements)
     smoothed_ref[...] = smoothed
     apply(
-        smoothed, ROWS, received_ref, gathered_ref, weights_ref[...], solved, metric_ref,
+        smoothed, ROWS, received_ref, weights_ref[...], solved, metric_ref,
         helmholtz_ref, first_ref, inner_ref, pair_ref, points_ref,
         [total_of(resid * smoothed), total_of(image_ref[...] * smoothed)],
-        back_ref, local_ref, sent_ref, faces_ref,
+        back_ref, local_ref, sent_ref,
     )
 
 
 def final_kernel(
-    received_ref, gathered_ref, points_ref, pair_ref, old_ref, field_ref, resid_ref, old_image_ref,
+    received_ref, points_ref, pair_ref, old_ref, field_ref, resid_ref, old_image_ref,
     scalars_ref, back_ref, local_ref, helmholtz_ref,
     solution_ref, residual_ref,
 ):
     before = unpacked(scalars_ref[...], 2)
-    now = unpacked(jnp.sum(get(received_ref, ROWS, 1), axis=0, keepdims=True), 3)
+    now = unpacked(jnp.sum(get(received_ref, ROWS, TERMS), axis=0, keepdims=True), 3)
     alpha = before[0] / before[1]
     beta = now[0] / before[0]
     curved = now[2] + beta * (2.0 * now[1] + beta * before[1])
@@ -559,7 +549,7 @@
     direction = field_ref[...] + beta * old
     solution_ref[...] = wide_of(alpha * old + step * direction)
     image = image_of(
-        field_ref, back_ref, local_ref, received_ref, gathered_ref, helmholtz_ref, pair_ref,
+        field_ref, back_ref, local_ref, received_ref, helmholtz_ref, pair_ref,
         points_ref,
     )
     image = image + beta * old_image_ref[...]
@@ -571,7 +561,9 @@
     scratch = [pltpu.VMEM(arg.shape, arg.dtype) for arg in args] if copied else []
     return pl.pallas_call(
         kernel,
-        out_shape=[jax.ShapeDtypeStruct(*out) if isinstance(out[0], tuple) else jax.ShapeDtypeStruct(out, F32) for out in outs],
+        out_shape=[
+            jax.ShapeDtypeStruct(*(out if isinstance(out[0], tuple) else (out, F32))) for out in outs
+        ],
         in_specs=[pl.BlockSpec(memory_space=space)] * len(args),
         out_specs=[pl.BlockSpec(memory_space=pltpu.VMEM)] * len(outs),
         scratch_shapes=scratch + ([pltpu.SemaphoreType.DMA((len(args),))] if copied else []),
@@ -597,44 +589,41 @@
     field = (4 * elements, LANES)
     local = (1, pair_list.shape[0] * pair_list.shape[1])
     points_shape = (peers + 2 * FACE_ROWS, LANES)
-    outs = [(groups * peers * ROWS, LANES), (2 * FACE_ROWS, LANES)]
-
-    def exchange(sent, faces):
-        gathered = lax.all_gather(faces, "grp", axis=0, tiled=True)
-        rows = sent.reshape(groups * peers, 1, -1)
-        received = lax.all_to_all(rows, ("grp", "sub"), 0, 0, tiled=True)
-        return received.reshape(sent.shape), gathered
-
-    sent, faces, fields, points = call(
+    sent_shape = (groups * peers * ROWS, LANES)
+
+    def exchange(sent):
+        rows = sent.reshape(groups * peers, -1, LANES)
+        return lax.all_to_all(rows, ("grp", "sub"), 0, 0, tiled=True).reshape(sent.shape)
+
+    sent, fields, points = call(
         first_kernel,
         [
             (groups * peers * FIRST_ROWS, LANES),
-            (4 * FACE_ROWS, LANES),
             (8 * elements + 8, LANES),
             (points_shape, jnp.int32),
         ],
         right_side, jacobi, coarse_inverse, coarse_map, shared_slots, face_points, copied=True,
     )
-    smoothed, weights, back, near, sent, faces = call(
+    smoothed, weights, back, near, sent = call(
         start_kernel,
-        [field, (NC, points_shape[0] * LANES), field, local, *outs],
-        *exchange(sent, faces), fields, points, pair_list, metric, helmholtz,
+        [field, (NC, points_shape[0] * LANES), field, local, sent_shape],
+        exchange(sent), fields, points, pair_list, metric, helmholtz,
         t["first"], t["inner"],
     )
-    image, resid, scalars, sent, faces = call(
-        middle_kernel, [field, field, (1, LANES), *outs],
-        *exchange(sent, faces), fields, points, pair_list, jacobi, helmholtz, coarse_inverse,
+    image, resid, scalars, sent = call(
+        middle_kernel, [field, field, (1, LANES), sent_shape],
+        exchange(sent), fields, points, pair_list, jacobi, helmholtz, coarse_inverse,
         smoothed, back, near,
     )
-    second, back, near, sent, faces = call(
-        second_kernel, [field, field, local, *outs],
-        *exchange(sent, faces), fields, points, pair_list, resid, image, weights, jacobi,
+    second, back, near, sent = call(
+        second_kernel, [field, field, local, sent_shape],
+        exchange(sent), fields, points, pair_list, resid, image, weights, jacobi,
         metric, helmholtz, t["first"], t["inner"],
     )
     return tuple(
         call(
             final_kernel, [right_side.shape, right_side.shape],
-            *exchange(sent, faces), points, pair_list, smoothed, second, resid, image, scalars,
+            exchange(sent), points, pair_list, smoothed, second, resid, image, scalars,
             back, near, helmholtz,
         )
     )

time: 89.9 us -> 58.1 us (0.65)
  starting transfers between devices: 23.9 us -> 0 us
  blocking collectives: 53.8 us -> 48.4 us
  Pallas kernels: 9.98 us -> 8.51 us
    all_gather x4 -> x0, blocking collectives: 53.8 us -> none  [exchange(): gathered = lax.all_gather(faces, 'grp', axis=0, tiled=True)]
    all_to_all x0 -> x4, blocking collectives: none -> 48.4 us  [exchange(): lax.all_to_all(rows, ('grp', 'sub'), 0, 0, tiled=True).reshape(sent.shape)]
    all_to_all x4 -> x0, starting transfers between devices: 23.9 us -> none  [exchange(): received = lax.all_to_all(rows, ('grp', 'sub'), 0, 0, tiled=True)]
    pallas_call x5, Pallas kernels: 9.98 us -> 8.51 us  [call(): pl.pallas_call(kernel, out_shape=[jax.ShapeDtypeStruct(*(out if isinstanc...]
  transfers between devices with their start and end apart: 4 -> 0, of which waited for: 0 -> 0; matrix products, arithmetic and copies ran while one was open for 0% -> 0% of each run, Pallas kernels for 0% -> 0%
where the time goes in v5:
time: 58.1 us; the launch traced here: 57.7 us
  blocking collectives  48.4 us (83%)
  Pallas kernels  8.51 us (15%)
  between operations  0.77 us (1%)
    all_to_all x4, blocking collectives, exchange(): lax.all_to_all(rows, ('grp', 'sub'), 0, 0, tiled=True).reshape(sent.shape)  48.4 us
    pallas_call x5, Pallas kernels, call(): pl.pallas_call(kernel, out_shape=[jax.ShapeDtypeStruct(*(out if isinstanc...  8.51 us

profile of v5, /device:TPU:0, one launch (start us, length us, event | category | flops | bytes accessed | tf_op | source)
XLA Modules:
  0.0 57.7 jit_solution(10190184684796490809)
XLA Ops:
  0.6 2.1 %shard_map.122 = (f32[512,128]{1,0:T(8,128)}, f32[136,128]{1,0:T(8,128)}, s32[16,128]{1,0:T(8,128)}) custom-call(f32[16,512]{1,0:T(8,128)} %right_hbm.1, f32[16,512]{1,0:T(8,128)} %jacobi_ref.3, f32[1,64,64]{2,1,0:T(8,128)} %inverse_ref.1, s32[8,16]{1,0:T(8,128)} %map_hbm.1, s32[1,8,128]{2,1,0:T(8,128)} %slot_hbm.1, s32[2,512]{1,0:T(2,128)} %face_hbm.1), custom_call_target="tpu_custom_call" | custom-call | tf_op jit(solution)/shard_map/pallas_call | solution.py:562
  2.7 0.0 copy-start
  2.7 0.0 copy-start.1
  2.7 0.0 copy-start.2
  2.7 0.0 copy-start.3
  2.8 0.0 copy-start.5
  2.8 0.0 copy-start.6
  2.8 0.0 copy-start.8
  2.8 17.9 %all_to_all.20 = f32[32,16,128]{2,1,0:T(8,128)S(1)} all-to-all(f32[32,16,128]{2,1,0:T(8,128)} %bitcast.15), channel_id=1, replica_groups=mesh['grp'=4,'sub'=8] {'grp','sub'}, dimensions={0} | all-to-all | bytes 524288 | tf_op jit(solution)/shard_map/all_to_all | solution.py:596
  20.7 0.0 copy-done
  20.7 0.0 copy-done.1
  20.7 0.0 copy-done.2
  20.7 0.0 copy-done.3
  20.7 0.0 copy-done.5
  20.7 0.0 copy-done.6
  20.7 0.0 copy-done.8
  20.8 2.2 %shard_map.123 = (f32[64,128]{1,0:T(8,128)S(1)}, f32[64,2048]{1,0:T(8,128)S(1)}, f32[64,128]{1,0:T(8,128)S(1)}, f32[1,2048]{1,0:T(1,128)S(1)}, f32[256,128]{1,0:T(8,128)S(1)}) custom-call(f32[512,128]{1,0:T(8,128)S(1)} %bitcast.8, f32[136,128]{1,0:T(8,128)S(1)} %copy-done, s32[16,128]{1,0:T(8,128)S(1)} %copy-done.6, s32[2,1024]{1,0:T(2,128)S(1)} %copy-done.5, ...), custom_call_target="tpu_custom_call" | custom-call | tf_op jit(solution)/shard_map/pallas_call | solution.py:562
  22.9 0.0 copy-start.4
  23.0 0.0 copy-start.7
  23.0 10.4 %all_to_all.21 = f32[32,8,128]{2,1,0:T(8,128)S(1)} all-to-all(f32[32,8,128]{2,1,0:T(8,128)S(1)} %bitcast.14), channel_id=1, replica_groups=mesh['grp'=4,'sub'=8] {'grp','sub'}, dimensions={0} | all-to-all | bytes 262144 | tf_op jit(solution)/shard_map/all_to_all | solution.py:596
  33.4 0.0 copy-done.4
  33.4 0.0 copy-done.7
  33.4 1.1 %shard_map.124 = (f32[64,128]{1,0:T(8,128)S(1)}, f32[64,128]{1,0:T(8,128)S(1)}, f32[1,128]{1,0:T(1,128)S(1)}, f32[256,128]{1,0:T(8,128)S(1)}) custom-call(f32[256,128]{1,0:T(8,128)S(1)} %bitcast.10, f32[136,128]{1,0:T(8,128)S(1)} %copy-done, s32[16,128]{1,0:T(8,128)S(1)} %copy-done.6, s32[2,1024]{1,0:T(2,128)S(1)} %copy-done.5, f32[16,512]{1,0:T(8,128)S(1)} %copy-done.4, ...), custom_call_target="tpu_custom_call" | custom-call | tf_op jit(solution)/shard_map/pallas_call | solution.py:562
  34.5 10.0 %all_to_all.22 = f32[32,8,128]{2,1,0:T(8,128)S(1)} all-to-all(f32[32,8,128]{2,1,0:T(8,128)S(1)} %bitcast.13), channel_id=1, replica_groups=mesh['grp'=4,'sub'=8] {'grp','sub'}, dimensions={0} | all-to-all | bytes 262144 | tf_op jit(solution)/shard_map/all_to_all | solution.py:596
  44.5 1.9 %shard_map.125 = (f32[64,128]{1,0:T(8,128)S(1)}, f32[64,128]{1,0:T(8,128)S(1)}, f32[1,2048]{1,0:T(1,128)S(1)}, f32[256,128]{1,0:T(8,128)S(1)}) custom-call(f32[256,128]{1,0:T(8,128)S(1)} %bitcast.9, f32[136,128]{1,0:T(8,128)S(1)} %copy-done, s32[16,128]{1,0:T(8,128)S(1)} %copy-done.6, s32[2,1024]{1,0:T(2,128)S(1)} %copy-done.5, ...), custom_call_target="tpu_custom_call" | custom-call | tf_op jit(solution)/shard_map/pallas_call | solution.py:562
  46.4 10.0 %all_to_all.23 = f32[32,8,128]{2,1,0:T(8,128)S(1)} all-to-all(f32[32,8,128]{2,1,0:T(8,128)S(1)} %bitcast.12), channel_id=1, replica_groups=mesh['grp'=4,'sub'=8] {'grp','sub'}, dimensions={0} | all-to-all | bytes 262144 | tf_op jit(solution)/shard_map/all_to_all | solution.py:596
  56.4 1.3 %shard_map.126 = (f32[16,512]{1,0:T(8,128)}, f32[16,512]{1,0:T(8,128)}) custom-call(f32[256,128]{1,0:T(8,128)S(1)} %bitcast.11, s32[16,128]{1,0:T(8,128)S(1)} %copy-done.6, s32[2,1024]{1,0:T(2,128)S(1)} %copy-done.5, f32[64,128]{1,0:T(8,128)S(1)} %get-tuple-element.22.smoothed_ref.old_ref, f32[64,128]{1,0:T(8,128)S(1)} %get-tuple-element.30.field_ref, ...), custom_call_target="tpu_custom_call" | custom-call | tf_op jit(solution)/shard_map/pallas_call | solution.py:562
Async XLA Ops:
  2.7 18.0 %copy-start = (f32[136,128]{1,0:T(8,128)S(1)}, f32[136,128]{1,0:T(8,128)}, u32[]{:S(2)}) copy-start(f32[136,128]{1,0:T(8,128)} %get-tuple-element.19.fields_ref) | copy-start | bytes 208900
  2.7 18.0 %copy-start.1 = (bf16[256,256]{1,0:T(8,128)(2,1)S(1)}, bf16[256,256]{1,0:T(8,128)(2,1)}, u32[]{:S(2)}) copy-start(bf16[256,256]{1,0:T(8,128)(2,1)} %constant.4.clone.inner_ref) | copy-start | bytes 393220
  2.7 18.0 %copy-start.2 = (f32[16,512]{1,0:T(8,128)S(1)}, f32[16,512]{1,0:T(8,128)}, u32[]{:S(2)}) copy-start(f32[16,512]{1,0:T(8,128)} %helmholtz_ref.7) | copy-start | bytes 98308
  2.7 18.0 %copy-start.3 = (f32[16,1536]{1,0:T(8,128)S(1)}, f32[16,1536]{1,0:T(8,128)}, u32[]{:S(2)}) copy-start(f32[16,1536]{1,0:T(8,128)} %metric_ref.3) | copy-start | bytes 294916
  2.8 18.0 %copy-start.5 = (s32[2,1024]{1,0:T(2,128)S(1)}, s32[2,1024]{1,0:T(2,128)}, u32[]{:S(2)}) copy-start(s32[2,1024]{1,0:T(2,128)} %pair_ref.7) | copy-start | bytes 24580
  2.8 18.0 %copy-start.6 = (s32[16,128]{1,0:T(8,128)S(1)}, s32[16,128]{1,0:T(8,128)}, u32[]{:S(2)}) copy-start(s32[16,128]{1,0:T(8,128)} %get-tuple-element.20.points_ref) | copy-start | bytes 24580
  2.8 18.0 %copy-start.8 = (f32[64,128]{1,0:T(8,128)S(1)}, f32[64,128]{1,0:T(8,128)}, u32[]{:S(2)}) copy-start(f32[64,128]{1,0:T(8,128)} %constant.5.clone.first_ref) | copy-start | bytes 98308
  22.9 10.5 %copy-start.4 = (f32[16,512]{1,0:T(8,128)S(1)}, f32[16,512]{1,0:T(8,128)}, u32[]{:S(2)}) copy-start(f32[16,512]{1,0:T(8,128)} %jacobi_ref.3) | copy-start | bytes 98308
  23.0 10.5 %copy-start.7 = (f32[1,64,64]{2,1,0:T(8,128)S(1)}, f32[1,64,64]{2,1,0:T(8,128)}, u32[]{:S(2)}) copy-start(f32[1,64,64]{2,1,0:T(8,128)} %inverse_ref.1) | copy-start | bytes 49156

commit v6 on v5

--- a/solution.py
+++ b/solution.py
@@ -12,8 +12,8 @@
 LANES = 128
 STEP = 256
 FACE_ROWS = 4
-ROWS = 8
-FIRST_ROWS = 16
+ROWS = 5
+FIRST_ROWS = 10
 TERMS = FACE_ROWS
 F32 = jnp.float32
 BF16 = jnp.bfloat16
@@ -85,12 +85,18 @@
     return steps == index
 
 
+def lane_hot(lane):
+    steps = lax.broadcasted_iota(jnp.int32, (LANES, lane.shape[1]), 0).astype(F32).astype(BF16)
+    one = jnp.ones(steps.shape, BF16)
+    return jnp.where(steps == lane.astype(F32).astype(BF16), one, jnp.zeros_like(one))
+
+
 def gather(field, chunks):
     high, low = split(field)
     both = jnp.concatenate([high, low], axis=1)
     out = []
     for row, lane in chunks:
-        lanes = one_hot(lane, LANES).astype(F32).astype(BF16)
+        lanes = lane_hot(lane)
         picked = jnp.dot(
             both, jnp.concatenate([lanes, lanes], axis=0), preferred_element_type=F32
         )
@@ -105,10 +111,11 @@
 def scatter(rows, chunks, values):
     total = jnp.zeros((2 * rows, LANES), F32)
     for (row, lane), value in zip(chunks, values):
-        lanes = one_hot(lane, LANES).astype(F32).astype(BF16)
-        high, low = split(jnp.where(one_hot(row, rows), value, 0.0))
+        steps = lax.broadcasted_iota(jnp.int32, (rows, row.shape[1]), 0).astype(F32).astype(BF16)
+        mine = steps == row.astype(F32).astype(BF16)
+        parts = [jnp.where(mine, part, jnp.zeros_like(steps)) for part in split(value)]
         total = total + lax.dot_general(
-            jnp.concatenate([high, low], axis=0), lanes, NT, preferred_element_type=F32
+            jnp.concatenate(parts, axis=0), lane_hot(lane), NT, preferred_element_type=F32
         )
     return total[:rows] + total[rows:]
 
@@ -559,6 +566,8 @@
 def call(kernel, outs, *args, copied=False):
     space = pl.ANY if copied else pltpu.VMEM
     scratch = [pltpu.VMEM(arg.shape, arg.dtype) for arg in args] if copied else []
+    if copied:
+        args = [pltpu.with_memory_space_constraint(arg, pltpu.HBM) for arg in args]
     return pl.pallas_call(
         kernel,
         out_shape=[
@@ -567,7 +576,7 @@
         in_specs=[pl.BlockSpec(memory_space=space)] * len(args),
         out_specs=[pl.BlockSpec(memory_space=pltpu.VMEM)] * len(outs),
         scratch_shapes=scratch + ([pltpu.SemaphoreType.DMA((len(args),))] if copied else []),
-        compiler_params=pltpu.CompilerParams(vmem_limit_bytes=(60 if copied else 24) * 1024 * 1024),
+        compiler_params=pltpu.CompilerParams(vmem_limit_bytes=24 * 1024 * 1024),
     )(*args)
 
 
@@ -592,7 +601,7 @@
     sent_shape = (groups * peers * ROWS, LANES)
 
     def exchange(sent):
-        rows = sent.reshape(groups * peers, -1, LANES)
+        rows = sent.reshape(groups * peers, 1, -1)
         return lax.all_to_all(rows, ("grp", "sub"), 0, 0, tiled=True).reshape(sent.shape)
 
     sent, fields, points = call(

time: 58.1 us -> 51.8 us (0.89)
  blocking collectives: 48.4 us -> 44 us
  Pallas kernels: 8.51 us -> 6.69 us
    all_to_all x4, blocking collectives: 48.4 us -> 44 us  [exchange(): lax.all_to_all(rows, ('grp', 'sub'), 0, 0, tiled=True).reshape(sent.shape)]
    pallas_call x5, Pallas kernels: 8.51 us -> 6.69 us  [call(): pl.pallas_call(kernel, out_shape=[jax.ShapeDtypeStruct(*(out if isinstanc...]
where the time goes in v6:
time: 51.8 us; the launch traced here: 51.5 us
  blocking collectives  44 us (85%)
  Pallas kernels  6.69 us (13%)
  between operations  0.74 us (1%)
    all_to_all x4, blocking collectives, exchange(): lax.all_to_all(rows, ('grp', 'sub'), 0, 0, tiled=True).reshape(sent.shape)  44 us
    pallas_call x5, Pallas kernels, call(): pl.pallas_call(kernel, out_shape=[jax.ShapeDtypeStruct(*(out if isinstanc...  6.69 us

profile of v6, /device:TPU:0, one launch (start us, length us, event | category | flops | bytes accessed | tf_op | source)
XLA Modules:
  0.0 51.5 jit_solution(1151110749212520919)
XLA Ops:
  0.6 1.3 %shard_map.122 = (f32[320,128]{1,0:T(8,128)S(1)}, f32[136,128]{1,0:T(8,128)S(1)}, s32[16,128]{1,0:T(8,128)S(1)}) custom-call(f32[16,512]{1,0:T(8,128)} %right_hbm.1, f32[16,512]{1,0:T(8,128)} %jacobi_ref.3, f32[1,64,64]{2,1,0:T(8,128)} %inverse_ref.1, s32[8,16]{1,0:T(8,128)} %map_hbm.1, s32[1,8,128]{2,1,0:T(8,128)} %slot_hbm.1, s32[2,512]{1,0:T(2,128)} %face_hbm.1), custom_call_target="tpu_custom_call" | custom-call | tf_op jit(solution)/shard_map/pallas_call | solution.py:571
  1.9 0.0 copy-start
  1.9 0.0 copy-start.1
  1.9 0.0 copy-start.2
  1.9 0.0 copy-start.4
  2.0 0.0 copy-start.5
  2.0 15.7 %all_to_all.20 = f32[32,1,1280]{2,1,0:T(1,128)S(1)} all-to-all(f32[32,1,1280]{2,1,0:T(1,128)S(1)} %bitcast.12), channel_id=1, replica_groups=mesh['grp'=4,'sub'=8] {'grp','sub'}, dimensions={0} | all-to-all | bytes 327680 | tf_op jit(solution)/shard_map/all_to_all | solution.py:605
  17.6 0.0 copy-done
  17.7 0.0 copy-done.1
  17.7 0.0 copy-done.2
  17.7 0.0 copy-done.4
  17.7 0.0 copy-done.5
  17.7 1.9 %shard_map.123 = (f32[64,128]{1,0:T(8,128)S(1)}, f32[64,2048]{1,0:T(8,128)S(1)}, f32[64,128]{1,0:T(8,128)S(1)}, f32[1,2048]{1,0:T(1,128)S(1)}, f32[160,128]{1,0:T(8,128)S(1)}) custom-call(f32[320,128]{1,0:T(8,128)S(1)} %bitcast.8, f32[136,128]{1,0:T(8,128)S(1)} %get-tuple-element.19.fields_ref, s32[16,128]{1,0:T(8,128)S(1)} %get-tuple-element.20.points_ref, ...), custom_call_target="tpu_custom_call" | custom-call | tf_op jit(solution)/shard_map/pallas_call | solution.py:571
  19.6 0.0 copy-start.3
  19.6 0.0 copy-start.6
  19.7 9.7 %all_to_all.21 = f32[32,1,640]{2,1,0:T(1,128)S(1)} all-to-all(f32[32,1,640]{2,1,0:T(1,128)S(1)} %bitcast.15), channel_id=1, replica_groups=mesh['grp'=4,'sub'=8] {'grp','sub'}, dimensions={0} | all-to-all | bytes 163840 | tf_op jit(solution)/shard_map/all_to_all | solution.py:605
  29.4 0.0 copy-done.3
  29.4 0.0 copy-done.6
  29.4 0.7 %shard_map.124 = (f32[64,128]{1,0:T(8,128)S(1)}, f32[64,128]{1,0:T(8,128)S(1)}, f32[1,128]{1,0:T(1,128)S(1)}, f32[160,128]{1,0:T(8,128)S(1)}) custom-call(f32[160,128]{1,0:T(8,128)S(1)} %bitcast.11, f32[136,128]{1,0:T(8,128)S(1)} %get-tuple-element.19.fields_ref, s32[16,128]{1,0:T(8,128)S(1)} %get-tuple-element.20.points_ref, s32[2,1024]{1,0:T(2,128)S(1)} %copy-done.4, ...), custom_call_target="tpu_custom_call" | custom-call | tf_op jit(solution)/shard_map/pallas_call | solution.py:571
  30.1 9.3 %all_to_all.22 = f32[32,1,640]{2,1,0:T(1,128)S(1)} all-to-all(f32[32,1,640]{2,1,0:T(1,128)S(1)} %bitcast.14), channel_id=1, replica_groups=mesh['grp'=4,'sub'=8] {'grp','sub'}, dimensions={0} | all-to-all | bytes 163840 | tf_op jit(solution)/shard_map/all_to_all | solution.py:605
  39.4 1.7 %shard_map.125 = (f32[64,128]{1,0:T(8,128)S(1)}, f32[64,128]{1,0:T(8,128)S(1)}, f32[1,2048]{1,0:T(1,128)S(1)}, f32[160,128]{1,0:T(8,128)S(1)}) custom-call(f32[160,128]{1,0:T(8,128)S(1)} %bitcast.9, f32[136,128]{1,0:T(8,128)S(1)} %get-tuple-element.19.fields_ref, s32[16,128]{1,0:T(8,128)S(1)} %get-tuple-element.20.points_ref, s32[2,1024]{1,0:T(2,128)S(1)} %copy-done.4, ...), custom_call_target="tpu_custom_call" | custom-call | tf_op jit(solution)/shard_map/pallas_call | solution.py:571
  41.1 9.3 %all_to_all.23 = f32[32,1,640]{2,1,0:T(1,128)S(1)} all-to-all(f32[32,1,640]{2,1,0:T(1,128)S(1)} %bitcast.13), channel_id=1, replica_groups=mesh['grp'=4,'sub'=8] {'grp','sub'}, dimensions={0} | all-to-all | bytes 163840 | tf_op jit(solution)/shard_map/all_to_all | solution.py:605
  50.4 1.1 %shard_map.126 = (f32[16,512]{1,0:T(8,128)}, f32[16,512]{1,0:T(8,128)}) custom-call(f32[160,128]{1,0:T(8,128)S(1)} %bitcast.10, s32[16,128]{1,0:T(8,128)S(1)} %get-tuple-element.20.points_ref, s32[2,1024]{1,0:T(2,128)S(1)} %copy-done.4, f32[64,128]{1,0:T(8,128)S(1)} %get-tuple-element.22.smoothed_ref.old_ref, f32[64,128]{1,0:T(8,128)S(1)} %get-tuple-element.30.field_ref, ...), custom_call_target="tpu_custom_call" | custom-call | tf_op jit(solution)/shard_map/pallas_call | solution.py:571
Async XLA Ops:
  1.9 15.7 %copy-start = (bf16[256,256]{1,0:T(8,128)(2,1)S(1)}, bf16[256,256]{1,0:T(8,128)(2,1)}, u32[]{:S(2)}) copy-start(bf16[256,256]{1,0:T(8,128)(2,1)} %constant.4.clone.inner_ref) | copy-start | bytes 393220
  1.9 15.7 %copy-start.1 = (f32[16,512]{1,0:T(8,128)S(1)}, f32[16,512]{1,0:T(8,128)}, u32[]{:S(2)}) copy-start(f32[16,512]{1,0:T(8,128)} %helmholtz_ref.7) | copy-start | bytes 98308
  1.9 15.7 %copy-start.2 = (f32[16,1536]{1,0:T(8,128)S(1)}, f32[16,1536]{1,0:T(8,128)}, u32[]{:S(2)}) copy-start(f32[16,1536]{1,0:T(8,128)} %metric_ref.3) | copy-start | bytes 294916
  1.9 15.7 %copy-start.4 = (s32[2,1024]{1,0:T(2,128)S(1)}, s32[2,1024]{1,0:T(2,128)}, u32[]{:S(2)}) copy-start(s32[2,1024]{1,0:T(2,128)} %pair_ref.7) | copy-start | bytes 24580
  2.0 15.7 %copy-start.5 = (f32[64,128]{1,0:T(8,128)S(1)}, f32[64,128]{1,0:T(8,128)}, u32[]{:S(2)}) copy-start(f32[64,128]{1,0:T(8,128)} %constant.5.clone.first_ref) | copy-start | bytes 98308
  19.6 9.8 %copy-start.3 = (f32[16,512]{1,0:T(8,128)S(1)}, f32[16,512]{1,0:T(8,128)}, u32[]{:S(2)}) copy-start(f32[16,512]{1,0:T(8,128)} %jacobi_ref.3) | copy-start | bytes 98308
  19.6 9.8 %copy-start.6 = (f32[1,64,64]{2,1,0:T(8,128)S(1)}, f32[1,64,64]{2,1,0:T(8,128)}, u32[]{:S(2)}) copy-start(f32[1,64,64]{2,1,0:T(8,128)} %inverse_ref.1) | copy-start | bytes 49156

commit v7 on v6

--- a/solution.py
+++ b/solution.py
@@ -10,7 +10,6 @@
 NC = 64
 POINTS = 512
 LANES = 128
-STEP = 256
 FACE_ROWS = 4
 ROWS = 5
 FIRST_ROWS = 10
@@ -91,60 +90,37 @@
     return jnp.where(steps == lane.astype(F32).astype(BF16), one, jnp.zeros_like(one))
 
 
-def gather(field, chunks):
-    high, low = split(field)
-    both = jnp.concatenate([high, low], axis=1)
-    out = []
-    for row, lane in chunks:
-        lanes = lane_hot(lane)
-        picked = jnp.dot(
-            both, jnp.concatenate([lanes, lanes], axis=0), preferred_element_type=F32
-        )
-        out.append(
-            jnp.sum(
-                jnp.where(one_hot(row, field.shape[0]), picked, 0.0), axis=0, keepdims=True
-            )
-        )
+def take(values, lanes):
+    return jnp.take_along_axis(values, lanes, axis=1, mode="promise_in_bounds")
+
+
+def gather(field_ref, points):
+    row, lane = locate(points, field_ref.shape[0] // 4)
+    out = jnp.zeros(points.shape, F32)
+    for h in range(field_ref.shape[0]):
+        spread = jnp.broadcast_to(field_ref[h : h + 1, :], points.shape)
+        out = jnp.where(row == h, take(spread, lane), out)
     return out
 
 
-def scatter(rows, chunks, values):
-    total = jnp.zeros((2 * rows, LANES), F32)
-    for (row, lane), value in zip(chunks, values):
-        steps = lax.broadcasted_iota(jnp.int32, (rows, row.shape[1]), 0).astype(F32).astype(BF16)
+def joined(rows):
+    return [
+        jnp.concatenate([rows[at : at + 1], rows[at + 1 : at + 2]], axis=1)
+        for at in range(0, rows.shape[0], 2)
+    ]
+
+
+def scatter(count, points, values):
+    total = jnp.zeros((2 * count, LANES), F32)
+    rows, lanes = locate(points, count // 4)
+    for row, lane, value in zip(joined(rows), joined(lanes), joined(values)):
+        steps = lax.broadcasted_iota(jnp.int32, (count, row.shape[1]), 0).astype(F32).astype(BF16)
         mine = steps == row.astype(F32).astype(BF16)
         parts = [jnp.where(mine, part, jnp.zeros_like(steps)) for part in split(value)]
         total = total + lax.dot_general(
             jnp.concatenate(parts, axis=0), lane_hot(lane), NT, preferred_element_type=F32
         )
-    return total[:rows] + total[rows:]
-
-
-def chunked(row, lane):
-    return [
-        (row[:, at : at + STEP], lane[:, at : at + STEP]) for at in range(0, row.shape[1], STEP)
-    ]
-
-
-def cut(row):
-    return [row[:, at : at + STEP] for at in range(0, row.shape[1], STEP)]
-
-
-def pair_chunks(pair_ref, elements):
-    row, lane = locate(pair_ref[...], elements)
-    return chunked(row[0:1], lane[0:1]) + chunked(row[1:2], lane[1:2])
-
-
-def joined(rows):
-    return [
-        jnp.concatenate([rows[at : at + 1], rows[at + 1 : at + 2]], axis=1)
-        for at in range(0, rows.shape[0], 2)
-    ]
-
-
-def far_chunks(points, elements):
-    row, lane = locate(points, elements)
-    return list(zip(joined(row), joined(lane)))
+    return total[:count] + total[count:]
 
 
 def halves(wide):
@@ -174,11 +150,6 @@
     sent_ref[pl.ds(at, devices, count), :] = jnp.broadcast_to(row, (devices, LANES))
 
 
-def send_values(sent_ref, count, values, peers):
-    rows = jnp.concatenate([row for pair in values for row in halves(pair)], axis=0)
-    send_rows(sent_ref, count, 0, rows, peers)
-
-
 def get(received_ref, count, at):
     return received_ref[pl.ds(at, received_ref.shape[0] // count, count), :]
 
@@ -204,8 +175,8 @@
 
 
 def swapped(values):
-    count = len(values) // 2
-    return values[count:] + values[:count]
+    count = values.shape[0] // 2
+    return jnp.concatenate([values[count:], values[:count]], axis=0)
 
 
 def along_first(field, table_ref, base):
@@ -265,9 +236,7 @@
 
 def corners(points):
     first, second, third = factors(points)
-    return [
-        first[q >> 2 & 1] * (second[q >> 1 & 1] * third[q & 1]) for q in range(8)
-    ]
+    return [first[q >> 2 & 1] * (second[q >> 1 & 1] * third[q & 1]) for q in range(8)]
 
 
 def own_corners():
@@ -286,7 +255,7 @@
 
 
 def one_vertex(flat):
-    return jnp.where(one_hot(whole(flat), NC), 1.0, 0.0)
+    return jnp.where(one_hot(flat, NC), 1.0, 0.0)
 
 
 def whole(values):
@@ -321,45 +290,37 @@
     return jnp.concatenate([part, jnp.zeros((1, LANES - NC), F32)], axis=1)
 
 
-def column(row):
-    shape = (NC, LANES)
-    keep = lax.broadcasted_iota(jnp.int32, shape, 0) == lax.broadcasted_iota(jnp.int32, shape, 1)
-    return jnp.sum(jnp.where(keep, row, 0.0), axis=1, keepdims=True)
-
-
 def get_solved(received_ref, count, peers):
     rows = get(received_ref, count, TERMS)
     return [
-        column(
-            jnp.sum(
-                jnp.where(own_group(rows.shape[0], peers, away), rows, 0.0), axis=0, keepdims=True
-            )
-        )
+        jnp.sum(jnp.where(own_group(rows.shape[0], peers, away), rows, 0.0), axis=0, keepdims=True)
         for away in (0, -1, 1)
     ]
 
 
-def prolonged(solved, vertices, elements):
-    flat = jnp.sum(vertices * solved, axis=0, keepdims=True)
+def prolonged(solved, flat, elements):
+    shape = (elements, LANES)
+    element = lax.broadcasted_iota(jnp.int32, shape, 0)
+    at_corner = take(jnp.broadcast_to(solved, shape), jnp.broadcast_to(flat, shape))
     out = [None] * 4
     for q, corner in enumerate(own_corners()):
-        value = jnp.sum(jnp.where(own_place(elements, q), flat, 0.0), axis=1, keepdims=True)
+        value = take(at_corner, element + q * elements)
         for c in range(4):
             term = value * corner[:, c * LANES : (c + 1) * LANES]
             out[c] = term if out[c] is None else out[c] + term
     return jnp.concatenate(out, axis=0)
 
 
-def prolong_at(points, vertices, elements):
-    mine = lax.broadcasted_iota(jnp.int32, (elements, points.shape[1]), 0) == points >> 9
-    weights = jnp.concatenate([jnp.where(mine, corner, 0.0) for corner in corners(points)], axis=0)
-    high, low = split(weights)
-    both = jnp.dot(
-        vertices.astype(BF16),
-        jnp.concatenate([high, low], axis=1),
-        preferred_element_type=F32,
-    )
-    return both[:, : points.shape[1]] + both[:, points.shape[1] :]
+def prolonged_far(solved, maps, points, elements):
+    peers = points.shape[0] - 2 * FACE_ROWS
+    counts = (peers, FACE_ROWS, FACE_ROWS)
+    spread = [jnp.broadcast_to(part, (n, LANES)) for part, n in zip(solved, counts)]
+    at_corner = take(jnp.concatenate(spread, axis=0), maps)
+    element = (points >> 9) & (elements - 1)
+    total = jnp.zeros(points.shape, F32)
+    for q, corner in enumerate(corners(points)):
+        total = total + corner * take(at_corner, element + q * elements)
+    return total
 
 
 def total_of(array):
@@ -382,9 +343,9 @@
 
 
 def first_kernel(
-    right_hbm, jacobi_hbm, inverse_hbm, map_hbm, slot_hbm, face_hbm,
-    sent_ref, fields_ref, points_ref,
-    right_ref, jacobi_ref, inverse_ref, map_ref, slot_ref, face_ref, sems,
+    right_hbm, jacobi_hbm, inverse_hbm, map_hbm, slot_hbm, face_hbm, pair_hbm,
+    sent_ref, fields_ref, points_ref, flat_ref,
+    right_ref, jacobi_ref, inverse_ref, map_ref, slot_ref, face_ref, pair_ref, sems,
 ):
     copies = []
     for k, (source, target) in enumerate(
@@ -395,6 +356,7 @@
             (jacobi_hbm, jacobi_ref),
             (map_hbm, map_ref),
             (inverse_hbm, inverse_ref),
+            (pair_hbm, pair_ref),
         )
     ):
         copy = pltpu.make_async_copy(source, target, sems.at[k])
@@ -404,145 +366,129 @@
         copy.wait()
     elements = right_ref.shape[0]
     peers = slot_ref.shape[1]
+    far = peers + 2 * FACE_ROWS
     faces = face_ref[...]
-    faces = jnp.concatenate(halves(faces[0:1]) + halves(faces[1:2]), axis=0)
-    points = jnp.concatenate([slot_ref[0], faces], axis=0)
-    points_ref[...] = points
+    pairs = pair_ref[...]
+    points_ref[0:peers, :] = slot_ref[0]
+    points_ref[peers:far, :] = jnp.concatenate(halves(faces[0:1]) + halves(faces[1:2]), axis=0)
+    points_ref[far:, :] = jnp.concatenate(halves(pairs[0:1]) + halves(pairs[1:2]), axis=0)
+    points = points_ref[0:far, :]
     resid = rows_of(right_ref[...])
     flat = flat_map(map_ref[...])
-    smoothed = rows_of(jacobi_ref[...]) * resid
+    flat_ref[...] = whole(flat)
     fields_ref[0 : 4 * elements, :] = resid
-    fields_ref[4 * elements : 8 * elements, :] = smoothed
-    fields_ref[8 * elements :, :] = jnp.broadcast_to(flat, (8, LANES))
-    part = coarse_part(resid, one_vertex(flat), inverse_ref[0])
-    values = gather(smoothed, far_chunks(points, elements))
-    send_values(sent_ref, FIRST_ROWS, values, peers)
+    fields_ref[4 * elements :, :] = rows_of(jacobi_ref[...]) * resid
+    part = coarse_part(resid, one_vertex(whole(flat)), inverse_ref[0])
+    values = gather(fields_ref.at[4 * elements : 8 * elements], points)
+    send_rows(sent_ref, FIRST_ROWS, 0, values, peers)
     send_same(sent_ref, FIRST_ROWS, TERMS, part)
     send_same(sent_ref, FIRST_ROWS, TERMS + 1, flat)
     send_rows(sent_ref, FIRST_ROWS, TERMS + 2, points.astype(F32), peers)
 
 
-def static_of(received_ref, peers, elements):
+def far_maps(received_ref, peers):
     maps = get(received_ref, FIRST_ROWS, TERMS + 1)
-    own = get_shared(maps, peers)
-    points = whole(get_rows(received_ref, FIRST_ROWS, TERMS + 2, peers))
-    out = [
-        prolong_at(points[b : b + 1], one_vertex(own[b : b + 1]), elements) for b in range(peers)
+    sides = [
+        jnp.broadcast_to(get_row(maps, peers, away), (FACE_ROWS, LANES)) for away in (-1, 1)
     ]
-    for k, pair in enumerate(joined(points[peers:])):
-        away = -1 if 2 * k < FACE_ROWS else 1
-        out.append(prolong_at(pair, one_vertex(get_row(maps, peers, away)), elements))
-    return jnp.concatenate(out, axis=1)
+    return whole(jnp.concatenate([get_shared(maps, peers)] + sides, axis=0))
 
 
 def apply(
-    smoothed, count, received_ref, weights, solved, metric_ref, helmholtz_ref,
-    first_ref, inner_ref, pair_ref, points_ref, dots, back_ref, local_ref, sent_ref,
-):
-    elements = smoothed.shape[0] // 4
-    peers = points_ref.shape[0] - 2 * FACE_ROWS
-    pairs = pair_chunks(pair_ref, elements)
-    far = far_chunks(points_ref[...], elements)
-    ends = [LANES * k for k in (0, peers, peers + FACE_ROWS, peers + 2 * FACE_ROWS)]
-    coarse = []
-    for k in range(3):
-        coarse += halves(
-            jnp.sum(weights[:, ends[k] : ends[k + 1]] * solved[k], axis=0, keepdims=True)
-        )
-    incoming = get_rows(received_ref, count, 0, peers) + jnp.concatenate(coarse, axis=0)
-    values = swapped(gather(smoothed, pairs)) + joined(incoming)
-    summed = smoothed + scatter(smoothed.shape[0], pairs + far, values)
+    smoothed_ref, count, received_ref, maps, far_points, solved, metric_ref, helmholtz_ref,
+    first_ref, inner_ref, points_ref, dots, back_ref, local_ref, sent_ref,
+):
+    elements = smoothed_ref.shape[0] // 4
+    far = far_points.shape[0]
+    peers = far - 2 * FACE_ROWS
+    points = points_ref[...]
+    incoming = get_rows(received_ref, count, 0, peers)
+    incoming = incoming + prolonged_far(solved, maps, far_points, elements)
+    near = swapped(gather(smoothed_ref, points[far:]))
+    smoothed = smoothed_ref[...]
+    summed = smoothed + scatter(
+        4 * elements, points, jnp.concatenate([incoming, near], axis=0)
+    )
     back, energy = stiffness(summed, metric_ref, first_ref, inner_ref)
     energy = energy + rows_of(helmholtz_ref[...]) * smoothed * smoothed
     back_ref[...] = back
-    values = gather(back, pairs + far)
-    near = swapped(values[: len(pairs)])
-    for k, value in enumerate(near):
-        local_ref[0:1, k * STEP : (k + 1) * STEP] = value
-    send_values(sent_ref, ROWS, values[len(pairs) :], peers)
+    values = gather(back_ref, points)
+    local_ref[...] = swapped(values[far:])
+    send_rows(sent_ref, ROWS, 0, values[:far], peers)
     send_same(sent_ref, ROWS, TERMS, packed(dots + [total_of(energy)]))
 
 
-def image_of(
-    field_ref, back_ref, local_ref, received_ref, helmholtz_ref, pair_ref, points_ref
-):
-    elements = field_ref.shape[0] // 4
-    peers = points_ref.shape[0] - 2 * FACE_ROWS
-    chunks = pair_chunks(pair_ref, elements) + far_chunks(points_ref[...], elements)
-    values = cut(local_ref[...]) + joined(get_rows(received_ref, ROWS, 0, peers))
-    summed = back_ref[...] + scatter(field_ref.shape[0], chunks, values)
+def image_of(field_ref, back_ref, local_ref, received_ref, helmholtz_ref, points_ref):
+    peers = points_ref.shape[0] - local_ref.shape[0] - 2 * FACE_ROWS
+    incoming = get_rows(received_ref, ROWS, 0, peers)
+    values = jnp.concatenate([incoming, local_ref[...]], axis=0)
+    summed = back_ref[...] + scatter(field_ref.shape[0], points_ref[...], values)
     return summed + rows_of(helmholtz_ref[...]) * field_ref[...]
 
 
 def start_kernel(
-    received_ref, fields_ref, points_ref, pair_ref, metric_ref, helmholtz_ref,
-    first_ref, inner_ref,
-    smoothed_ref, weights_ref, back_ref, local_ref, sent_ref,
+    received_ref, fields_ref, points_ref, flat_ref, metric_ref, helmholtz_ref, first_ref, inner_ref,
+    smoothed_ref, maps_ref, far_points_ref, back_ref, local_ref, sent_ref,
 ):
     elements = helmholtz_ref.shape[0]
-    peers = points_ref.shape[0] - 2 * FACE_ROWS
+    peers = maps_ref.shape[0] - 2 * FACE_ROWS
     solved = get_solved(received_ref, FIRST_ROWS, peers)
     resid = fields_ref[0 : 4 * elements, :]
-    vertices = one_vertex(fields_ref[8 * elements : 8 * elements + 1, :])
-    smoothed = fields_ref[4 * elements : 8 * elements, :]
-    smoothed = smoothed + prolonged(solved[0], vertices, elements)
+    smoothed = fields_ref[4 * elements :, :] + prolonged(solved[0], flat_ref[...], elements)
     smoothed_ref[...] = smoothed
-    weights = static_of(received_ref, peers, elements)
-    weights_ref[...] = weights
+    maps = far_maps(received_ref, peers)
+    maps_ref[...] = maps
+    far_points = whole(get_rows(received_ref, FIRST_ROWS, TERMS + 2, peers))
+    far_points_ref[...] = far_points
     apply(
-        smoothed, FIRST_ROWS, received_ref, weights, solved, metric_ref,
-        helmholtz_ref, first_ref, inner_ref, pair_ref, points_ref,
+        smoothed_ref, FIRST_ROWS, received_ref, maps, far_points, solved, metric_ref,
+        helmholtz_ref, first_ref, inner_ref, points_ref,
         [total_of(resid * smoothed)], back_ref, local_ref, sent_ref,
     )
 
 
 def middle_kernel(
-    received_ref, fields_ref, points_ref, pair_ref, jacobi_ref, helmholtz_ref,
-    inverse_ref, smoothed_ref, back_ref, local_ref,
-    image_ref, resid_ref, scalars_ref, sent_ref,
+    received_ref, fields_ref, points_ref, flat_ref, jacobi_ref, helmholtz_ref, inverse_ref,
+    smoothed_ref, back_ref, local_ref,
+    image_ref, resid_ref, rough_ref, scalars_ref, sent_ref,
 ):
     elements = helmholtz_ref.shape[0]
-    peers = points_ref.shape[0] - 2 * FACE_ROWS
+    far = points_ref.shape[0] - local_ref.shape[0]
     dots = jnp.sum(get(received_ref, ROWS, TERMS), axis=0, keepdims=True)
     scalars_ref[...] = dots
     values = unpacked(dots, 2)
     alpha = values[0] / values[1]
-    image = image_of(
-        smoothed_ref, back_ref, local_ref, received_ref, helmholtz_ref, pair_ref,
-        points_ref,
-    )
+    image = image_of(smoothed_ref, back_ref, local_ref, received_ref, helmholtz_ref, points_ref)
     image_ref[...] = image
     resid = fields_ref[0 : 4 * elements, :] - alpha * image
     resid_ref[...] = resid
-    vertices = one_vertex(fields_ref[8 * elements : 8 * elements + 1, :])
-    part = coarse_part(resid, vertices, inverse_ref[0])
-    values = gather(rows_of(jacobi_ref[...]) * resid, far_chunks(points_ref[...], elements))
-    send_values(sent_ref, ROWS, values, peers)
+    rough_ref[...] = rows_of(jacobi_ref[...]) * resid
+    part = coarse_part(resid, one_vertex(flat_ref[...]), inverse_ref[0])
+    values = gather(rough_ref, points_ref[0:far, :])
+    send_rows(sent_ref, ROWS, 0, values, far - 2 * FACE_ROWS)
     send_same(sent_ref, ROWS, TERMS, part)
 
 
 def second_kernel(
-    received_ref, fields_ref, points_ref, pair_ref, resid_ref, image_ref,
-    weights_ref, jacobi_ref, metric_ref, helmholtz_ref, first_ref, inner_ref,
+    received_ref, points_ref, flat_ref, maps_ref, far_points_ref, resid_ref, rough_ref, image_ref,
+    metric_ref, helmholtz_ref, first_ref, inner_ref,
     smoothed_ref, back_ref, local_ref, sent_ref,
 ):
     elements = helmholtz_ref.shape[0]
-    peers = points_ref.shape[0] - 2 * FACE_ROWS
-    solved = get_solved(received_ref, ROWS, peers)
+    solved = get_solved(received_ref, ROWS, maps_ref.shape[0] - 2 * FACE_ROWS)
     resid = resid_ref[...]
-    vertices = one_vertex(fields_ref[8 * elements : 8 * elements + 1, :])
-    smoothed = rows_of(jacobi_ref[...]) * resid + prolonged(solved[0], vertices, elements)
+    smoothed = rough_ref[...] + prolonged(solved[0], flat_ref[...], elements)
     smoothed_ref[...] = smoothed
     apply(
-        smoothed, ROWS, received_ref, weights_ref[...], solved, metric_ref,
-        helmholtz_ref, first_ref, inner_ref, pair_ref, points_ref,
+        smoothed_ref, ROWS, received_ref, maps_ref[...], far_points_ref[...], solved, metric_ref,
+        helmholtz_ref, first_ref, inner_ref, points_ref,
         [total_of(resid * smoothed), total_of(image_ref[...] * smoothed)],
         back_ref, local_ref, sent_ref,
     )
 
 
 def final_kernel(
-    received_ref, points_ref, pair_ref, old_ref, field_ref, resid_ref, old_image_ref,
+    received_ref, points_ref, old_ref, field_ref, resid_ref, old_image_ref,
     scalars_ref, back_ref, local_ref, helmholtz_ref,
     solution_ref, residual_ref,
 ):
@@ -555,10 +501,7 @@
     old = old_ref[...]
     direction = field_ref[...] + beta * old
     solution_ref[...] = wide_of(alpha * old + step * direction)
-    image = image_of(
-        field_ref, back_ref, local_ref, received_ref, helmholtz_ref, pair_ref,
-        points_ref,
-    )
+    image = image_of(field_ref, back_ref, local_ref, received_ref, helmholtz_ref, points_ref)
     image = image + beta * old_image_ref[...]
     residual_ref[...] = wide_of(resid_ref[...] - step * image)
 
@@ -596,44 +539,44 @@
     t = {name: jnp.asarray(value) for name, value in tables().items()}
     elements = right_side.shape[0]
     field = (4 * elements, LANES)
-    local = (1, pair_list.shape[0] * pair_list.shape[1])
-    points_shape = (peers + 2 * FACE_ROWS, LANES)
+    far = (peers + face_points.size // LANES, LANES)
+    local = (pair_list.size // LANES, LANES)
     sent_shape = (groups * peers * ROWS, LANES)
 
     def exchange(sent):
         rows = sent.reshape(groups * peers, 1, -1)
         return lax.all_to_all(rows, ("grp", "sub"), 0, 0, tiled=True).reshape(sent.shape)
 
-    sent, fields, points = call(
+    sent, fields, points, flat = call(
         first_kernel,
         [
             (groups * peers * FIRST_ROWS, LANES),
-            (8 * elements + 8, LANES),
-            (points_shape, jnp.int32),
+            (8 * elements, LANES),
+            ((far[0] + local[0], LANES), jnp.int32),
+            ((1, LANES), jnp.int32),
         ],
-        right_side, jacobi, coarse_inverse, coarse_map, shared_slots, face_points, copied=True,
-    )
-    smoothed, weights, back, near, sent = call(
+        right_side, jacobi, coarse_inverse, coarse_map, shared_slots, face_points, pair_list,
+        copied=True,
+    )
+    smoothed, maps, far_points, back, near, sent = call(
         start_kernel,
-        [field, (NC, points_shape[0] * LANES), field, local, sent_shape],
-        exchange(sent), fields, points, pair_list, metric, helmholtz,
-        t["first"], t["inner"],
-    )
-    image, resid, scalars, sent = call(
-        middle_kernel, [field, field, (1, LANES), sent_shape],
-        exchange(sent), fields, points, pair_list, jacobi, helmholtz, coarse_inverse,
+        [field, (far, jnp.int32), (far, jnp.int32), field, local, sent_shape],
+        exchange(sent), fields, points, flat, metric, helmholtz, t["first"], t["inner"],
+    )
+    image, resid, rough, scalars, sent = call(
+        middle_kernel, [field, field, field, (1, LANES), sent_shape],
+        exchange(sent), fields, points, flat, jacobi, helmholtz, coarse_inverse,
         smoothed, back, near,
     )
     second, back, near, sent = call(
         second_kernel, [field, field, local, sent_shape],
-        exchange(sent), fields, points, pair_list, resid, image, weights, jacobi,
+        exchange(sent), points, flat, maps, far_points, resid, rough, image,
         metric, helmholtz, t["first"], t["inner"],
     )
     return tuple(
         call(
             final_kernel, [right_side.shape, right_side.shape],
-            exchange(sent), points, pair_list, smoothed, second, resid, image, scalars,
-            back, near, helmholtz,
+            exchange(sent), points, smoothed, second, resid, image, scalars, back, near, helmholtz,
         )
     )
 

time: 51.8 us -> 52.2 us (level)
  no operation moved by 1% of the time
where the time goes in v7:
time: 52.2 us; the launch traced here: 51.9 us
  blocking collectives  44 us (84%)
  Pallas kernels  7.1 us (14%)
  between operations  0.71 us (1%)
    all_to_all x4, blocking collectives, exchange(): lax.all_to_all(rows, ('grp', 'sub'), 0, 0, tiled=True).reshape(sent.shape)  44 us
    pallas_call x5, Pallas kernels, call(): pl.pallas_call(kernel, out_shape=[jax.ShapeDtypeStruct(*(out if isinstanc...  7.1 us

profile of v7, /device:TPU:0, one launch (start us, length us, event | category | flops | bytes accessed | tf_op | source)
XLA Modules:
  0.0 51.9 jit_solution(15507992739394724401)
XLA Ops:
  0.6 1.4 %shard_map.122 = (f32[320,128]{1,0:T(8,128)S(1)}, f32[128,128]{1,0:T(8,128)S(1)}, s32[32,128]{1,0:T(8,128)S(1)}, s32[1,128]{1,0:T(1,128)S(1)}) custom-call(f32[16,512]{1,0:T(8,128)} %right_hbm.1, f32[16,512]{1,0:T(8,128)} %jacobi_ref.1, f32[1,64,64]{2,1,0:T(8,128)} %inverse_ref.1, s32[8,16]{1,0:T(8,128)} %map_hbm.1, s32[1,8,128]{2,1,0:T(8,128)} %slot_hbm.1, ...), custom_call_target="tpu_custom_call" | custom-call | tf_op jit(solution)/shard_map/pallas_call | solution.py:514
  2.0 0.0 copy-start
  2.0 0.0 copy-start.1
  2.1 0.0 copy-start.2
  2.1 0.0 copy-start.3
  2.1 15.7 %all_to_all.20 = f32[32,1,1280]{2,1,0:T(1,128)S(1)} all-to-all(f32[32,1,1280]{2,1,0:T(1,128)S(1)} %bitcast.12), channel_id=1, replica_groups=mesh['grp'=4,'sub'=8] {'grp','sub'}, dimensions={0} | all-to-all | bytes 327680 | tf_op jit(solution)/shard_map/all_to_all | solution.py:548
  17.8 0.0 copy-done
  17.8 0.0 copy-done.1
  17.8 0.0 copy-done.2
  17.8 0.0 copy-done.3
  17.8 1.9 %shard_map.123 = (f32[64,128]{1,0:T(8,128)S(1)}, s32[16,128]{1,0:T(8,128)S(1)}, s32[16,128]{1,0:T(8,128)S(1)}, f32[64,128]{1,0:T(8,128)S(1)}, f32[16,128]{1,0:T(8,128)S(1)}, /*index=5*/f32[160,128]{1,0:T(8,128)S(1)}) custom-call(f32[320,128]{1,0:T(8,128)S(1)} %bitcast.8, f32[128,128]{1,0:T(8,128)S(1)} %get-tuple-element.22.fields_ref, ...), custom_call_target="tpu_custom_call" | custom-call | tf_op jit(solution)/shard_map/pallas_call | solution.py:514
  19.6 0.0 copy-start.4
  19.6 0.0 copy-start.5
  19.7 9.7 %all_to_all.21 = f32[32,1,640]{2,1,0:T(1,128)S(1)} all-to-all(f32[32,1,640]{2,1,0:T(1,128)S(1)} %bitcast.15), channel_id=1, replica_groups=mesh['grp'=4,'sub'=8] {'grp','sub'}, dimensions={0} | all-to-all | bytes 163840 | tf_op jit(solution)/shard_map/all_to_all | solution.py:548
  29.4 0.0 copy-done.4
  29.4 0.0 copy-done.5
  29.4 0.9 %shard_map.124 = (f32[64,128]{1,0:T(8,128)S(1)}, f32[64,128]{1,0:T(8,128)S(1)}, f32[64,128]{1,0:T(8,128)S(1)}, f32[1,128]{1,0:T(1,128)S(1)}, f32[160,128]{1,0:T(8,128)S(1)}) custom-call(f32[160,128]{1,0:T(8,128)S(1)} %bitcast.11, f32[128,128]{1,0:T(8,128)S(1)} %get-tuple-element.22.fields_ref, s32[32,128]{1,0:T(8,128)S(1)} %get-tuple-element.23.points_ref, ...), custom_call_target="tpu_custom_call" | custom-call | tf_op jit(solution)/shard_map/pallas_call | solution.py:514
  30.3 9.3 %all_to_all.22 = f32[32,1,640]{2,1,0:T(1,128)S(1)} all-to-all(f32[32,1,640]{2,1,0:T(1,128)S(1)} %bitcast.14), channel_id=1, replica_groups=mesh['grp'=4,'sub'=8] {'grp','sub'}, dimensions={0} | all-to-all | bytes 163840 | tf_op jit(solution)/shard_map/all_to_all | solution.py:548
  39.6 1.9 %shard_map.125 = (f32[64,128]{1,0:T(8,128)S(1)}, f32[64,128]{1,0:T(8,128)S(1)}, f32[16,128]{1,0:T(8,128)S(1)}, f32[160,128]{1,0:T(8,128)S(1)}) custom-call(f32[160,128]{1,0:T(8,128)S(1)} %bitcast.9, s32[32,128]{1,0:T(8,128)S(1)} %get-tuple-element.23.points_ref, s32[1,128]{1,0:T(1,128)S(1)} %get-tuple-element.24.flat_ref, ...), custom_call_target="tpu_custom_call" | custom-call | tf_op jit(solution)/shard_map/pallas_call | solution.py:514
  41.5 9.3 %all_to_all.23 = f32[32,1,640]{2,1,0:T(1,128)S(1)} all-to-all(f32[32,1,640]{2,1,0:T(1,128)S(1)} %bitcast.13), channel_id=1, replica_groups=mesh['grp'=4,'sub'=8] {'grp','sub'}, dimensions={0} | all-to-all | bytes 163840 | tf_op jit(solution)/shard_map/all_to_all | solution.py:548
  50.8 1.1 %shard_map.126 = (f32[16,512]{1,0:T(8,128)}, f32[16,512]{1,0:T(8,128)}) custom-call(f32[160,128]{1,0:T(8,128)S(1)} %bitcast.10, s32[32,128]{1,0:T(8,128)S(1)} %get-tuple-element.23.points_ref, f32[64,128]{1,0:T(8,128)S(1)} %get-tuple-element.26.smoothed_ref.old_ref, f32[64,128]{1,0:T(8,128)S(1)} %get-tuple-element.36.field_ref, ...), custom_call_target="tpu_custom_call" | custom-call | tf_op jit(solution)/shard_map/pallas_call | solution.py:514
Async XLA Ops:
  2.0 15.7 %copy-start = (bf16[256,256]{1,0:T(8,128)(2,1)S(1)}, bf16[256,256]{1,0:T(8,128)(2,1)}, u32[]{:S(2)}) copy-start(bf16[256,256]{1,0:T(8,128)(2,1)} %constant.4.clone.inner_ref) | copy-start | bytes 393220
  2.0 15.7 %copy-start.1 = (f32[16,512]{1,0:T(8,128)S(1)}, f32[16,512]{1,0:T(8,128)}, u32[]{:S(2)}) copy-start(f32[16,512]{1,0:T(8,128)} %helmholtz_ref.7) | copy-start | bytes 98308
  2.1 15.7 %copy-start.2 = (f32[16,1536]{1,0:T(8,128)S(1)}, f32[16,1536]{1,0:T(8,128)}, u32[]{:S(2)}) copy-start(f32[16,1536]{1,0:T(8,128)} %metric_ref.3) | copy-start | bytes 294916
  2.1 15.7 %copy-start.3 = (f32[64,128]{1,0:T(8,128)S(1)}, f32[64,128]{1,0:T(8,128)}, u32[]{:S(2)}) copy-start(f32[64,128]{1,0:T(8,128)} %constant.5.clone.first_ref) | copy-start | bytes 98308
  19.6 9.8 %copy-start.4 = (f32[16,512]{1,0:T(8,128)S(1)}, f32[16,512]{1,0:T(8,128)}, u32[]{:S(2)}) copy-start(f32[16,512]{1,0:T(8,128)} %jacobi_ref.1) | copy-start | bytes 98308
  19.6 9.8 %copy-start.5 = (f32[1,64,64]{2,1,0:T(8,128)S(1)}, f32[1,64,64]{2,1,0:T(8,128)}, u32[]{:S(2)}) copy-start(f32[1,64,64]{2,1,0:T(8,128)} %inverse_ref.1) | copy-start | bytes 49156

commit v8 on v7

--- a/solution.py
+++ b/solution.py
@@ -1,3 +1,5 @@
+import functools
+
 import jax
 import jax.numpy as jnp
 import ml_dtypes
@@ -94,26 +96,29 @@
     return jnp.take_along_axis(values, lanes, axis=1, mode="promise_in_bounds")
 
 
-def gather(field_ref, points):
-    row, lane = locate(points, field_ref.shape[0] // 4)
-    out = jnp.zeros(points.shape, F32)
-    for h in range(field_ref.shape[0]):
-        spread = jnp.broadcast_to(field_ref[h : h + 1, :], points.shape)
-        out = jnp.where(row == h, take(spread, lane), out)
-    return out
-
-
-def joined(rows):
+def joined(rows, count):
     return [
-        jnp.concatenate([rows[at : at + 1], rows[at + 1 : at + 2]], axis=1)
-        for at in range(0, rows.shape[0], 2)
+        jnp.concatenate([rows[at + k : at + k + 1] for k in range(count)], axis=1)
+        for at in range(0, rows.shape[0], count)
     ]
+
+
+def gather(field, points):
+    rows, lanes = locate(points, field.shape[0] // 4)
+    both = jnp.concatenate(split(field), axis=1)
+    out = []
+    for row, lane in zip(joined(rows, 2), joined(lanes, 2)):
+        hot = lane_hot(lane)
+        picked = jnp.dot(both, jnp.concatenate([hot, hot], axis=0), preferred_element_type=F32)
+        mine = jnp.where(one_hot(row, field.shape[0]), picked, 0.0)
+        out += halves(jnp.sum(mine, axis=0, keepdims=True))
+    return jnp.concatenate(out, axis=0)
 
 
 def scatter(count, points, values):
     total = jnp.zeros((2 * count, LANES), F32)
     rows, lanes = locate(points, count // 4)
-    for row, lane, value in zip(joined(rows), joined(lanes), joined(values)):
+    for row, lane, value in zip(joined(rows, 4), joined(lanes, 4), joined(values, 4)):
         steps = lax.broadcasted_iota(jnp.int32, (count, row.shape[1]), 0).astype(F32).astype(BF16)
         mine = steps == row.astype(F32).astype(BF16)
         parts = [jnp.where(mine, part, jnp.zeros_like(steps)) for part in split(value)]
@@ -311,11 +316,8 @@
     return jnp.concatenate(out, axis=0)
 
 
-def prolonged_far(solved, maps, points, elements):
-    peers = points.shape[0] - 2 * FACE_ROWS
-    counts = (peers, FACE_ROWS, FACE_ROWS)
-    spread = [jnp.broadcast_to(part, (n, LANES)) for part, n in zip(solved, counts)]
-    at_corner = take(jnp.concatenate(spread, axis=0), maps)
+def prolonged_at(solved, maps, points, elements):
+    at_corner = take(solved, maps)
     element = (points >> 9) & (elements - 1)
     total = jnp.zeros(points.shape, F32)
     for q, corner in enumerate(corners(points)):
@@ -344,7 +346,7 @@
 
 def first_kernel(
     right_hbm, jacobi_hbm, inverse_hbm, map_hbm, slot_hbm, face_hbm, pair_hbm,
-    sent_ref, fields_ref, points_ref, flat_ref,
+    sent_ref, resid_ref, rough_ref, points_ref, flat_ref,
     right_ref, jacobi_ref, inverse_ref, map_ref, slot_ref, face_ref, pair_ref, sems,
 ):
     copies = []
@@ -376,10 +378,11 @@
     resid = rows_of(right_ref[...])
     flat = flat_map(map_ref[...])
     flat_ref[...] = whole(flat)
-    fields_ref[0 : 4 * elements, :] = resid
-    fields_ref[4 * elements :, :] = rows_of(jacobi_ref[...]) * resid
+    resid_ref[...] = resid
+    rough = rows_of(jacobi_ref[...]) * resid
+    rough_ref[...] = rough
     part = coarse_part(resid, one_vertex(whole(flat)), inverse_ref[0])
-    values = gather(fields_ref.at[4 * elements : 8 * elements], points)
+    values = gather(rough, points)
     send_rows(sent_ref, FIRST_ROWS, 0, values, peers)
     send_same(sent_ref, FIRST_ROWS, TERMS, part)
     send_same(sent_ref, FIRST_ROWS, TERMS + 1, flat)
@@ -395,84 +398,98 @@
 
 
 def apply(
-    smoothed_ref, count, received_ref, maps, far_points, solved, metric_ref, helmholtz_ref,
-    first_ref, inner_ref, points_ref, dots, back_ref, local_ref, sent_ref,
+    smoothed, count, received_ref, near, flat, maps, far_points, solved, metric_ref,
+    helmholtz_ref, first_ref, inner_ref, points_ref, dots, back_ref, sent_ref,
 ):
-    elements = smoothed_ref.shape[0] // 4
+    elements = smoothed.shape[0] // 4
     far = far_points.shape[0]
     peers = far - 2 * FACE_ROWS
     points = points_ref[...]
-    incoming = get_rows(received_ref, count, 0, peers)
-    incoming = incoming + prolonged_far(solved, maps, far_points, elements)
-    near = swapped(gather(smoothed_ref, points[far:]))
-    smoothed = smoothed_ref[...]
-    summed = smoothed + scatter(
-        4 * elements, points, jnp.concatenate([incoming, near], axis=0)
-    )
+    counts = (peers, FACE_ROWS, FACE_ROWS, near.shape[0])
+    coarse = prolonged_at(
+        jnp.concatenate(
+            [
+                jnp.broadcast_to(part, (n, LANES))
+                for part, n in zip((*solved, solved[0]), counts)
+            ],
+            axis=0,
+        ),
+        jnp.concatenate([maps, jnp.broadcast_to(flat, near.shape)], axis=0),
+        jnp.concatenate([far_points, swapped(points[far:])], axis=0),
+        elements,
+    )
+    incoming = jnp.concatenate([get_rows(received_ref, count, 0, peers), near], axis=0)
+    summed = smoothed + scatter(4 * elements, points, incoming + coarse)
     back, energy = stiffness(summed, metric_ref, first_ref, inner_ref)
     energy = energy + rows_of(helmholtz_ref[...]) * smoothed * smoothed
     back_ref[...] = back
-    values = gather(back_ref, points)
-    local_ref[...] = swapped(values[far:])
-    send_rows(sent_ref, ROWS, 0, values[:far], peers)
+    send_rows(sent_ref, ROWS, 0, gather(back, points[:far]), peers)
     send_same(sent_ref, ROWS, TERMS, packed(dots + [total_of(energy)]))
 
 
-def image_of(field_ref, back_ref, local_ref, received_ref, helmholtz_ref, points_ref):
-    peers = points_ref.shape[0] - local_ref.shape[0] - 2 * FACE_ROWS
-    incoming = get_rows(received_ref, ROWS, 0, peers)
-    values = jnp.concatenate([incoming, local_ref[...]], axis=0)
-    summed = back_ref[...] + scatter(field_ref.shape[0], points_ref[...], values)
-    return summed + rows_of(helmholtz_ref[...]) * field_ref[...]
+def near_kernel(field_ref, points_ref, near_ref):
+    points = points_ref[points_ref.shape[0] - near_ref.shape[0] :, :]
+    near_ref[...] = swapped(gather(field_ref[...], points))
+
+
+def inside_kernel(field_ref, back_ref, helmholtz_ref, points_ref, inside_ref, *, far):
+    points = points_ref[far:, :]
+    back = back_ref[...]
+    near = scatter(back.shape[0], points, swapped(gather(back, points)))
+    inside_ref[...] = back + near + rows_of(helmholtz_ref[...]) * field_ref[...]
+
+
+def image_of(inside_ref, received_ref, points_ref, far):
+    incoming = get_rows(received_ref, ROWS, 0, far - 2 * FACE_ROWS)
+    return inside_ref[...] + scatter(inside_ref.shape[0], points_ref[0:far, :], incoming)
 
 
 def start_kernel(
-    received_ref, fields_ref, points_ref, flat_ref, metric_ref, helmholtz_ref, first_ref, inner_ref,
-    smoothed_ref, maps_ref, far_points_ref, back_ref, local_ref, sent_ref,
+    received_ref, near_ref, resid_ref, rough_ref, points_ref, flat_ref, metric_ref, helmholtz_ref,
+    first_ref, inner_ref,
+    smoothed_ref, maps_ref, far_points_ref, back_ref, sent_ref,
 ):
     elements = helmholtz_ref.shape[0]
     peers = maps_ref.shape[0] - 2 * FACE_ROWS
     solved = get_solved(received_ref, FIRST_ROWS, peers)
-    resid = fields_ref[0 : 4 * elements, :]
-    smoothed = fields_ref[4 * elements :, :] + prolonged(solved[0], flat_ref[...], elements)
+    resid = resid_ref[...]
+    smoothed = rough_ref[...] + prolonged(solved[0], flat_ref[...], elements)
     smoothed_ref[...] = smoothed
     maps = far_maps(received_ref, peers)
     maps_ref[...] = maps
     far_points = whole(get_rows(received_ref, FIRST_ROWS, TERMS + 2, peers))
     far_points_ref[...] = far_points
     apply(
-        smoothed_ref, FIRST_ROWS, received_ref, maps, far_points, solved, metric_ref,
-        helmholtz_ref, first_ref, inner_ref, points_ref,
-        [total_of(resid * smoothed)], back_ref, local_ref, sent_ref,
+        smoothed, FIRST_ROWS, received_ref, near_ref[...], flat_ref[...], maps, far_points, solved,
+        metric_ref, helmholtz_ref, first_ref, inner_ref, points_ref,
+        [total_of(resid * smoothed)], back_ref, sent_ref,
     )
 
 
 def middle_kernel(
-    received_ref, fields_ref, points_ref, flat_ref, jacobi_ref, helmholtz_ref, inverse_ref,
-    smoothed_ref, back_ref, local_ref,
-    image_ref, resid_ref, rough_ref, scalars_ref, sent_ref,
+    received_ref, inside_ref, right_ref, points_ref, flat_ref, jacobi_ref, inverse_ref,
+    image_ref, resid_ref, rough_ref, scalars_ref, sent_ref, *, far,
 ):
-    elements = helmholtz_ref.shape[0]
-    far = points_ref.shape[0] - local_ref.shape[0]
     dots = jnp.sum(get(received_ref, ROWS, TERMS), axis=0, keepdims=True)
     scalars_ref[...] = dots
     values = unpacked(dots, 2)
     alpha = values[0] / values[1]
-    image = image_of(smoothed_ref, back_ref, local_ref, received_ref, helmholtz_ref, points_ref)
+    image = image_of(inside_ref, received_ref, points_ref, far)
     image_ref[...] = image
-    resid = fields_ref[0 : 4 * elements, :] - alpha * image
+    resid = right_ref[...] - alpha * image
     resid_ref[...] = resid
-    rough_ref[...] = rows_of(jacobi_ref[...]) * resid
+    rough = rows_of(jacobi_ref[...]) * resid
+    rough_ref[...] = rough
     part = coarse_part(resid, one_vertex(flat_ref[...]), inverse_ref[0])
-    values = gather(rough_ref, points_ref[0:far, :])
+    values = gather(rough, points_ref[0:far, :])
     send_rows(sent_ref, ROWS, 0, values, far - 2 * FACE_ROWS)
     send_same(sent_ref, ROWS, TERMS, part)
 
 
 def second_kernel(
-    received_ref, points_ref, flat_ref, maps_ref, far_points_ref, resid_ref, rough_ref, image_ref,
-    metric_ref, helmholtz_ref, first_ref, inner_ref,
-    smoothed_ref, back_ref, local_ref, sent_ref,
+    received_ref, near_ref, points_ref, flat_ref, maps_ref, far_points_ref, resid_ref, rough_ref,
+    image_ref, metric_ref, helmholtz_ref, first_ref, inner_ref,
+    smoothed_ref, back_ref, sent_ref,
 ):
     elements = helmholtz_ref.shape[0]
     solved = get_solved(received_ref, ROWS, maps_ref.shape[0] - 2 * FACE_ROWS)
@@ -480,17 +497,16 @@
     smoothed = rough_ref[...] + prolonged(solved[0], flat_ref[...], elements)
     smoothed_ref[...] = smoothed
     apply(
-        smoothed_ref, ROWS, received_ref, maps_ref[...], far_points_ref[...], solved, metric_ref,
-        helmholtz_ref, first_ref, inner_ref, points_ref,
+        smoothed, ROWS, received_ref, near_ref[...], flat_ref[...], maps_ref[...],
+        far_points_ref[...], solved, metric_ref, helmholtz_ref, first_ref, inner_ref, points_ref,
         [total_of(resid * smoothed), total_of(image_ref[...] * smoothed)],
-        back_ref, local_ref, sent_ref,
+        back_ref, sent_ref,
     )
 
 
 def final_kernel(
-    received_ref, points_ref, old_ref, field_ref, resid_ref, old_image_ref,
-    scalars_ref, back_ref, local_ref, helmholtz_ref,
-    solution_ref, residual_ref,
+    received_ref, inside_ref, points_ref, old_ref, field_ref, resid_ref, old_image_ref, scalars_ref,
+    solution_ref, residual_ref, *, far,
 ):
     before = unpacked(scalars_ref[...], 2)
     now = unpacked(jnp.sum(get(received_ref, ROWS, TERMS), axis=0, keepdims=True), 3)
@@ -501,7 +517,7 @@
     old = old_ref[...]
     direction = field_ref[...] + beta * old
     solution_ref[...] = wide_of(alpha * old + step * direction)
-    image = image_of(field_ref, back_ref, local_ref, received_ref, helmholtz_ref, points_ref)
+    image = image_of(inside_ref, received_ref, points_ref, far)
     image = image + beta * old_image_ref[...]
     residual_ref[...] = wide_of(resid_ref[...] - step * image)
 
@@ -542,41 +558,53 @@
     far = (peers + face_points.size // LANES, LANES)
     local = (pair_list.size // LANES, LANES)
     sent_shape = (groups * peers * ROWS, LANES)
+    inside_part, middle, final = [
+        functools.partial(kernel, far=far[0])
+        for kernel in (inside_kernel, middle_kernel, final_kernel)
+    ]
 
     def exchange(sent):
         rows = sent.reshape(groups * peers, 1, -1)
         return lax.all_to_all(rows, ("grp", "sub"), 0, 0, tiled=True).reshape(sent.shape)
 
-    sent, fields, points, flat = call(
+    sent, resid, rough, points, flat = call(
         first_kernel,
         [
             (groups * peers * FIRST_ROWS, LANES),
-            (8 * elements, LANES),
+            field,
+            field,
             ((far[0] + local[0], LANES), jnp.int32),
             ((1, LANES), jnp.int32),
         ],
         right_side, jacobi, coarse_inverse, coarse_map, shared_slots, face_points, pair_list,
         copied=True,
     )
-    smoothed, maps, far_points, back, near, sent = call(
+    received = exchange(sent)
+    (near,) = call(near_kernel, [local], rough, points)
+    smoothed, maps, far_points, back, sent = call(
         start_kernel,
-        [field, (far, jnp.int32), (far, jnp.int32), field, local, sent_shape],
-        exchange(sent), fields, points, flat, metric, helmholtz, t["first"], t["inner"],
-    )
+        [field, (far, jnp.int32), (far, jnp.int32), field, sent_shape],
+        received, near, resid, rough, points, flat, metric, helmholtz, t["first"], t["inner"],
+    )
+    received = exchange(sent)
+    (inside,) = call(inside_part, [field], smoothed, back, helmholtz, points)
     image, resid, rough, scalars, sent = call(
-        middle_kernel, [field, field, field, (1, LANES), sent_shape],
-        exchange(sent), fields, points, flat, jacobi, helmholtz, coarse_inverse,
-        smoothed, back, near,
-    )
-    second, back, near, sent = call(
-        second_kernel, [field, field, local, sent_shape],
-        exchange(sent), points, flat, maps, far_points, resid, rough, image,
+        middle, [field, field, field, (1, LANES), sent_shape],
+        received, inside, resid, points, flat, jacobi, coarse_inverse,
+    )
+    received = exchange(sent)
+    (near,) = call(near_kernel, [local], rough, points)
+    second, back, sent = call(
+        second_kernel, [field, field, sent_shape],
+        received, near, points, flat, maps, far_points, resid, rough, image,
         metric, helmholtz, t["first"], t["inner"],
     )
+    received = exchange(sent)
+    (inside,) = call(inside_part, [field], second, back, helmholtz, points)
     return tuple(
         call(
-            final_kernel, [right_side.shape, right_side.shape],
-            exchange(sent), points, smoothed, second, resid, image, scalars, back, near, helmholtz,
+            final, [right_side.shape, right_side.shape],
+            received, inside, points, smoothed, second, resid, image, scalars,
         )
     )
 

time: 52.2 us -> 55.5 us (1.063)
  blocking collectives: 44 us -> 0 us
  waiting for transfers between devices: 0 us -> 29.5 us
  starting transfers between devices: 0 us -> 15 us
  Pallas kernels: 7.1 us -> 9.76 us
    all_to_all x4 -> x0, blocking collectives: 44 us -> none  [exchange(): lax.all_to_all(rows, ('grp', 'sub'), 0, 0, tiled=True).reshape(sent.shape)]
    all_to_all x0 -> x4, waiting for transfers between devices: none -> 29.5 us  [exchange(): lax.all_to_all(rows, ('grp', 'sub'), 0, 0, tiled=True).reshape(sent.shape)]
    all_to_all x0 -> x4, starting transfers between devices: none -> 15 us  [exchange(): lax.all_to_all(rows, ('grp', 'sub'), 0, 0, tiled=True).reshape(sent.shape)]
    pallas_call x5 -> x9, Pallas kernels: 7.1 us -> 9.76 us  [call(): pl.pallas_call(kernel, out_shape=[jax.ShapeDtypeStruct(*(out if isinstanc...]
  transfers between devices with their start and end apart: 0 -> 4, of which waited for: 0 -> 4; matrix products, arithmetic and copies ran while one was open for 0% -> 0% of each run, Pallas kernels for 0% -> 3%
where the time goes in v8:
time: 55.5 us; the launch traced here: 55.1 us
  waiting for transfers between devices  29.5 us (53%)
  starting transfers between devices  15 us (27%)
  Pallas kernels  9.76 us (18%)
  between operations  0.76 us (1%)
    all_to_all x4, waiting for transfers between devices, exchange(): lax.all_to_all(rows, ('grp', 'sub'), 0, 0, tiled=True).reshape(sent.shape)  29.5 us
    all_to_all x4, starting transfers between devices, exchange(): lax.all_to_all(rows, ('grp', 'sub'), 0, 0, tiled=True).reshape(sent.shape)  15 us
    pallas_call x9, Pallas kernels, call(): pl.pallas_call(kernel, out_shape=[jax.ShapeDtypeStruct(*(out if isinstanc...  9.76 us
  transfers between devices with their start and end apart: 4, of which 4 were waited for; matrix products, arithmetic and copies ran while one was open for 0% of the time, Pallas kernels for 3%

profile of v8, /device:TPU:0, one launch (start us, length us, event | category | flops | bytes accessed | tf_op | source)
XLA Modules:
  0.0 55.1 jit_solution(12159210689919933917)
XLA Ops:
  0.6 1.9 %shard_map.122 = (f32[320,128]{1,0:T(8,128)}, f32[64,128]{1,0:T(8,128)S(1)}, f32[64,128]{1,0:T(8,128)S(1)}, s32[32,128]{1,0:T(8,128)S(1)}, s32[1,128]{1,0:T(1,128)S(1)}) custom-call(f32[16,512]{1,0:T(8,128)} %right_hbm.1, f32[16,512]{1,0:T(8,128)} %jacobi_ref.1, f32[1,64,64]{2,1,0:T(8,128)} %inverse_ref.1, s32[8,16]{1,0:T(8,128)} %map_hbm.1, ...), custom_call_target="tpu_custom_call" | custom-call | tf_op jit(solution)/shard_map/pallas_call | solution.py:530
  2.6 0.0 copy-start
  2.6 0.0 copy-start.2
  2.6 7.3 %all-to-all-start = ((f32[32,1,1280]{2,1,0:T(1,128)}), f32[32,1,1280]{2,1,0:T(1,128)S(1)}, u32[]{:S(2)}, u32[]{:S(2)}) async-start(f32[32,1,1280]{2,1,0:T(1,128)} %bitcast), calls=%async_computation | async-start | bytes 327680 | tf_op jit(solution)/shard_map/all_to_all | solution.py:568
  9.9 0.0 copy-start.3
  9.9 0.0 copy-start.1
  9.9 0.3 shard_map.123.near_ref
  10.3 8.2 %all-to-all-done = f32[32,1,1280]{2,1,0:T(1,128)S(1)} async-done(((f32[32,1,1280]{2,1,0:T(1,128)}), f32[32,1,1280]{2,1,0:T(1,128)S(1)}, u32[]{:S(2)}, u32[]{:S(2)}) %all-to-all-start) | async-done | bytes 163872 | tf_op jit(solution)/shard_map/all_to_all | solution.py:568
  18.5 0.0 copy-done
  18.5 0.0 copy-done.2
  18.5 0.0 copy-done.3
  18.5 0.0 copy-done.1
  18.5 1.9 %shard_map.124 = (f32[64,128]{1,0:T(8,128)S(1)}, s32[16,128]{1,0:T(8,128)S(1)}, s32[16,128]{1,0:T(8,128)S(1)}, f32[64,128]{1,0:T(8,128)S(1)}, f32[160,128]{1,0:T(8,128)}) custom-call(f32[320,128]{1,0:T(8,128)S(1)} %bitcast.8, f32[16,128]{1,0:T(8,128)S(1)} %shard_map.123.near_ref, f32[64,128]{1,0:T(8,128)S(1)} %get-tuple-element.23.resid_ref.right_ref, ...), custom_call_target="tpu_custom_call" | custom-call | tf_op jit(solution)/shard_map/pallas_call | solution.py:530
  20.4 2.6 %all-to-all-start.1 = ((f32[32,1,640]{2,1,0:T(1,128)}), f32[32,1,640]{2,1,0:T(1,128)S(1)}, u32[]{:S(2)}, u32[]{:S(2)}) async-start(f32[32,1,640]{2,1,0:T(1,128)} %bitcast.2), calls=%async_computation.1 | async-start | bytes 163840 | tf_op jit(solution)/shard_map/all_to_all | solution.py:568
  23.0 0.0 copy-start.4
  23.0 0.0 copy-start.5
  23.0 0.6 %shard_map.125.inside_ref = f32[64,128]{1,0:T(8,128)S(1)} custom-call(f32[64,128]{1,0:T(8,128)S(1)} %get-tuple-element.26.field_ref.old_ref, f32[64,128]{1,0:T(8,128)S(1)} %get-tuple-element.27.back_ref, f32[16,512]{1,0:T(8,128)S(1)} %copy-done.1, s32[32,128]{1,0:T(8,128)S(1)} %get-tuple-element.22.points_ref), custom_call_target="tpu_custom_call" | custom-call | tf_op jit(solution)/shard_map/pallas_call | solution.py:530
  23.6 7.0 %all-to-all-done.1 = f32[32,1,640]{2,1,0:T(1,128)S(1)} async-done(((f32[32,1,640]{2,1,0:T(1,128)}), f32[32,1,640]{2,1,0:T(1,128)S(1)}, u32[]{:S(2)}, u32[]{:S(2)}) %all-to-all-start.1) | async-done | bytes 81952 | tf_op jit(solution)/shard_map/all_to_all | solution.py:568
  30.6 0.0 copy-done.4
  30.6 0.0 copy-done.5
  30.6 1.2 %shard_map.126 = (f32[64,128]{1,0:T(8,128)S(1)}, f32[64,128]{1,0:T(8,128)S(1)}, f32[64,128]{1,0:T(8,128)S(1)}, f32[1,128]{1,0:T(1,128)S(1)}, f32[160,128]{1,0:T(8,128)}) custom-call(f32[160,128]{1,0:T(8,128)S(1)} %bitcast.10, f32[64,128]{1,0:T(8,128)S(1)} %shard_map.125.inside_ref, f32[64,128]{1,0:T(8,128)S(1)} %get-tuple-element.23.resid_ref.right_ref, ...), custom_call_target="tpu_custom_call" | custom-call | tf_op jit(solution)/shard_map/pallas_call | solution.py:530
  31.9 2.6 %all-to-all-start.2 = ((f32[32,1,640]{2,1,0:T(1,128)}), f32[32,1,640]{2,1,0:T(1,128)S(1)}, u32[]{:S(2)}, u32[]{:S(2)}) async-start(f32[32,1,640]{2,1,0:T(1,128)} %bitcast.4), calls=%async_computation.2 | async-start | bytes 163840 | tf_op jit(solution)/shard_map/all_to_all | solution.py:568
  34.4 0.3 shard_map.127.near_ref
  34.8 7.3 %all-to-all-done.2 = f32[32,1,640]{2,1,0:T(1,128)S(1)} async-done(((f32[32,1,640]{2,1,0:T(1,128)}), f32[32,1,640]{2,1,0:T(1,128)S(1)}, u32[]{:S(2)}, u32[]{:S(2)}) %all-to-all-start.2) | async-done | bytes 81952 | tf_op jit(solution)/shard_map/all_to_all | solution.py:568
  42.0 1.9 %shard_map.128 = (f32[64,128]{1,0:T(8,128)S(1)}, f32[64,128]{1,0:T(8,128)S(1)}, f32[160,128]{1,0:T(8,128)}) custom-call(f32[160,128]{1,0:T(8,128)S(1)} %bitcast.9, f32[16,128]{1,0:T(8,128)S(1)} %shard_map.127.near_ref, s32[32,128]{1,0:T(8,128)S(1)} %get-tuple-element.22.points_ref, s32[1,128]{1,0:T(1,128)S(1)} %get-tuple-element.24.flat_ref, ...), custom_call_target="tpu_custom_call" | custom-call | tf_op jit(solution)/shard_map/pallas_call | solution.py:530
  44.0 2.6 %all-to-all-start.3 = ((f32[32,1,640]{2,1,0:T(1,128)}), f32[32,1,640]{2,1,0:T(1,128)S(1)}, u32[]{:S(2)}, u32[]{:S(2)}) async-start(f32[32,1,640]{2,1,0:T(1,128)} %bitcast.6), calls=%async_computation.3 | async-start | bytes 163840 | tf_op jit(solution)/shard_map/all_to_all | solution.py:568
  46.5 0.6 %shard_map.129.inside_ref = f32[64,128]{1,0:T(8,128)S(1)} custom-call(f32[64,128]{1,0:T(8,128)S(1)} %get-tuple-element.35.field_ref, f32[64,128]{1,0:T(8,128)S(1)} %get-tuple-element.36.back_ref, f32[16,512]{1,0:T(8,128)S(1)} %copy-done.1, s32[32,128]{1,0:T(8,128)S(1)} %get-tuple-element.22.points_ref), custom_call_target="tpu_custom_call" | custom-call | tf_op jit(solution)/shard_map/pallas_call | solution.py:530
  47.1 7.0 %all-to-all-done.3 = f32[32,1,640]{2,1,0:T(1,128)S(1)} async-done(((f32[32,1,640]{2,1,0:T(1,128)}), f32[32,1,640]{2,1,0:T(1,128)S(1)}, u32[]{:S(2)}, u32[]{:S(2)}) %all-to-all-start.3) | async-done | bytes 81952 | tf_op jit(solution)/shard_map/all_to_all | solution.py:568
  54.1 0.9 %shard_map.130 = (f32[16,512]{1,0:T(8,128)}, f32[16,512]{1,0:T(8,128)}) custom-call(f32[160,128]{1,0:T(8,128)S(1)} %bitcast.11, f32[64,128]{1,0:T(8,128)S(1)} %shard_map.129.inside_ref, s32[32,128]{1,0:T(8,128)S(1)} %get-tuple-element.22.points_ref, f32[64,128]{1,0:T(8,128)S(1)} %get-tuple-element.26.field_ref.old_ref, ...), custom_call_target="tpu_custom_call" | custom-call | tf_op jit(solution)/shard_map/pallas_call | solution.py:530
Async XLA Ops:
  2.6 15.9 %copy-start = (bf16[256,256]{1,0:T(8,128)(2,1)S(1)}, bf16[256,256]{1,0:T(8,128)(2,1)}, u32[]{:S(2)}) copy-start(bf16[256,256]{1,0:T(8,128)(2,1)} %constant.4.clone.inner_ref) | copy-start | bytes 393220
  2.6 15.9 %copy-start.2 = (f32[16,1536]{1,0:T(8,128)S(1)}, f32[16,1536]{1,0:T(8,128)}, u32[]{:S(2)}) copy-start(f32[16,1536]{1,0:T(8,128)} %metric_ref.3) | copy-start | bytes 294916
  2.6 15.9 %all-to-all-start = ((f32[32,1,1280]{2,1,0:T(1,128)}), f32[32,1,1280]{2,1,0:T(1,128)S(1)}, u32[]{:S(2)}, u32[]{:S(2)}) async-start(f32[32,1,1280]{2,1,0:T(1,128)} %bitcast), calls=%async_computation | async-start | bytes 327680 | tf_op jit(solution)/shard_map/all_to_all | solution.py:568
  9.9 8.6 %copy-start.3 = (f32[64,128]{1,0:T(8,128)S(1)}, f32[64,128]{1,0:T(8,128)}, u32[]{:S(2)}) copy-start(f32[64,128]{1,0:T(8,128)} %constant.5.clone.first_ref) | copy-start | bytes 98308
  9.9 8.6 %copy-start.1 = (f32[16,512]{1,0:T(8,128)S(1)}, f32[16,512]{1,0:T(8,128)}, u32[]{:S(2)}) copy-start(f32[16,512]{1,0:T(8,128)} %helmholtz_ref.7) | copy-start | bytes 98308
  20.4 10.2 %all-to-all-start.1 = ((f32[32,1,640]{2,1,0:T(1,128)}), f32[32,1,640]{2,1,0:T(1,128)S(1)}, u32[]{:S(2)}, u32[]{:S(2)}) async-start(f32[32,1,640]{2,1,0:T(1,128)} %bitcast.2), calls=%async_computation.1 | async-start | bytes 163840 | tf_op jit(solution)/shard_map/all_to_all | solution.py:568
  23.0 7.6 %copy-start.4 = (f32[16,512]{1,0:T(8,128)S(1)}, f32[16,512]{1,0:T(8,128)}, u32[]{:S(2)}) copy-start(f32[16,512]{1,0:T(8,128)} %jacobi_ref.1) | copy-start | bytes 98308
  23.0 7.6 %copy-start.5 = (f32[1,64,64]{2,1,0:T(8,128)S(1)}, f32[1,64,64]{2,1,0:T(8,128)}, u32[]{:S(2)}) copy-start(f32[1,64,64]{2,1,0:T(8,128)} %inverse_ref.1) | copy-start | bytes 49156
  31.9 10.2 %all-to-all-start.2 = ((f32[32,1,640]{2,1,0:T(1,128)}), f32[32,1,640]{2,1,0:T(1,128)S(1)}, u32[]{:S(2)}, u32[]{:S(2)}) async-start(f32[32,1,640]{2,1,0:T(1,128)} %bitcast.4), calls=%async_computation.2 | async-start | bytes 163840 | tf_op jit(solution)/shard_map/all_to_all | solution.py:568
  44.0 10.2 %all-to-all-start.3 = ((f32[32,1,640]{2,1,0:T(1,128)}), f32[32,1,640]{2,1,0:T(1,128)S(1)}, u32[]{:S(2)}, u32[]{:S(2)}) async-start(f32[32,1,640]{2,1,0:T(1,128)} %bitcast.6), calls=%async_computation.3 | async-start | bytes 163840 | tf_op jit(solution)/shard_map/all_to_all | solution.py:568

commit v9 on v6

--- a/solution.py
+++ b/solution.py
@@ -91,20 +91,18 @@
     return jnp.where(steps == lane.astype(F32).astype(BF16), one, jnp.zeros_like(one))
 
 
+def take(values, lanes):
+    return jnp.take_along_axis(values, lanes, axis=1, mode="promise_in_bounds")
+
+
 def gather(field, chunks):
-    high, low = split(field)
-    both = jnp.concatenate([high, low], axis=1)
+    count = field.shape[0]
+    both = jnp.concatenate(split(field), axis=0)
     out = []
     for row, lane in chunks:
-        lanes = lane_hot(lane)
-        picked = jnp.dot(
-            both, jnp.concatenate([lanes, lanes], axis=0), preferred_element_type=F32
-        )
-        out.append(
-            jnp.sum(
-                jnp.where(one_hot(row, field.shape[0]), picked, 0.0), axis=0, keepdims=True
-            )
-        )
+        picked = jnp.dot(both, lane_hot(lane), preferred_element_type=F32)
+        mine = jnp.where(one_hot(row, count), picked[:count] + picked[count:], 0.0)
+        out.append(jnp.sum(mine, axis=0, keepdims=True))
     return out
 
 
@@ -321,45 +319,34 @@
     return jnp.concatenate([part, jnp.zeros((1, LANES - NC), F32)], axis=1)
 
 
-def column(row):
-    shape = (NC, LANES)
-    keep = lax.broadcasted_iota(jnp.int32, shape, 0) == lax.broadcasted_iota(jnp.int32, shape, 1)
-    return jnp.sum(jnp.where(keep, row, 0.0), axis=1, keepdims=True)
-
-
 def get_solved(received_ref, count, peers):
     rows = get(received_ref, count, TERMS)
     return [
-        column(
-            jnp.sum(
-                jnp.where(own_group(rows.shape[0], peers, away), rows, 0.0), axis=0, keepdims=True
-            )
-        )
+        jnp.sum(jnp.where(own_group(rows.shape[0], peers, away), rows, 0.0), axis=0, keepdims=True)
         for away in (0, -1, 1)
     ]
 
 
-def prolonged(solved, vertices, elements):
-    flat = jnp.sum(vertices * solved, axis=0, keepdims=True)
+def prolonged(solved, flat, elements):
+    shape = (elements, LANES)
+    element = lax.broadcasted_iota(jnp.int32, shape, 0)
+    at_corner = take(jnp.broadcast_to(solved, shape), jnp.broadcast_to(flat, shape))
     out = [None] * 4
     for q, corner in enumerate(own_corners()):
-        value = jnp.sum(jnp.where(own_place(elements, q), flat, 0.0), axis=1, keepdims=True)
+        value = take(at_corner, element + q * elements)
         for c in range(4):
             term = value * corner[:, c * LANES : (c + 1) * LANES]
             out[c] = term if out[c] is None else out[c] + term
     return jnp.concatenate(out, axis=0)
 
 
-def prolong_at(points, vertices, elements):
-    mine = lax.broadcasted_iota(jnp.int32, (elements, points.shape[1]), 0) == points >> 9
-    weights = jnp.concatenate([jnp.where(mine, corner, 0.0) for corner in corners(points)], axis=0)
-    high, low = split(weights)
-    both = jnp.dot(
-        vertices.astype(BF16),
-        jnp.concatenate([high, low], axis=1),
-        preferred_element_type=F32,
-    )
-    return both[:, : points.shape[1]] + both[:, points.shape[1] :]
+def prolonged_at(solved, maps, points, elements):
+    at_corner = take(solved, maps)
+    element = (points >> 9) & (elements - 1)
+    total = jnp.zeros(points.shape, F32)
+    for q, corner in enumerate(corners(points)):
+        total = total + corner * take(at_corner, element + q * elements)
+    return total
 
 
 def total_of(array):
@@ -422,34 +409,27 @@
     send_rows(sent_ref, FIRST_ROWS, TERMS + 2, points.astype(F32), peers)
 
 
-def static_of(received_ref, peers, elements):
+def far_maps(received_ref, peers):
     maps = get(received_ref, FIRST_ROWS, TERMS + 1)
-    own = get_shared(maps, peers)
-    points = whole(get_rows(received_ref, FIRST_ROWS, TERMS + 2, peers))
-    out = [
-        prolong_at(points[b : b + 1], one_vertex(own[b : b + 1]), elements) for b in range(peers)
+    sides = [
+        jnp.broadcast_to(get_row(maps, peers, away), (FACE_ROWS, LANES)) for away in (-1, 1)
     ]
-    for k, pair in enumerate(joined(points[peers:])):
-        away = -1 if 2 * k < FACE_ROWS else 1
-        out.append(prolong_at(pair, one_vertex(get_row(maps, peers, away)), elements))
-    return jnp.concatenate(out, axis=1)
+    return whole(jnp.concatenate([get_shared(maps, peers)] + sides, axis=0))
 
 
 def apply(
-    smoothed, count, received_ref, weights, solved, metric_ref, helmholtz_ref,
+    smoothed, count, received_ref, maps, far_points, solved, metric_ref, helmholtz_ref,
     first_ref, inner_ref, pair_ref, points_ref, dots, back_ref, local_ref, sent_ref,
 ):
     elements = smoothed.shape[0] // 4
     peers = points_ref.shape[0] - 2 * FACE_ROWS
     pairs = pair_chunks(pair_ref, elements)
     far = far_chunks(points_ref[...], elements)
-    ends = [LANES * k for k in (0, peers, peers + FACE_ROWS, peers + 2 * FACE_ROWS)]
-    coarse = []
-    for k in range(3):
-        coarse += halves(
-            jnp.sum(weights[:, ends[k] : ends[k + 1]] * solved[k], axis=0, keepdims=True)
-        )
-    incoming = get_rows(received_ref, count, 0, peers) + jnp.concatenate(coarse, axis=0)
+    counts = (peers, FACE_ROWS, FACE_ROWS)
+    spread = [jnp.broadcast_to(part, (n, LANES)) for part, n in zip(solved, counts)]
+    incoming = get_rows(received_ref, count, 0, peers) + prolonged_at(
+        jnp.concatenate(spread, axis=0), maps, far_points, elements
+    )
     values = swapped(gather(smoothed, pairs)) + joined(incoming)
     summed = smoothed + scatter(smoothed.shape[0], pairs + far, values)
     back, energy = stiffness(summed, metric_ref, first_ref, inner_ref)
@@ -477,20 +457,22 @@
 def start_kernel(
     received_ref, fields_ref, points_ref, pair_ref, metric_ref, helmholtz_ref,
     first_ref, inner_ref,
-    smoothed_ref, weights_ref, back_ref, local_ref, sent_ref,
+    smoothed_ref, maps_ref, far_points_ref, back_ref, local_ref, sent_ref,
 ):
     elements = helmholtz_ref.shape[0]
     peers = points_ref.shape[0] - 2 * FACE_ROWS
     solved = get_solved(received_ref, FIRST_ROWS, peers)
     resid = fields_ref[0 : 4 * elements, :]
-    vertices = one_vertex(fields_ref[8 * elements : 8 * elements + 1, :])
+    flat = whole(fields_ref[8 * elements : 8 * elements + 1, :])
     smoothed = fields_ref[4 * elements : 8 * elements, :]
-    smoothed = smoothed + prolonged(solved[0], vertices, elements)
+    smoothed = smoothed + prolonged(solved[0], flat, elements)
     smoothed_ref[...] = smoothed
-    weights = static_of(received_ref, peers, elements)
-    weights_ref[...] = weights
+    maps = far_maps(received_ref, peers)
+    maps_ref[...] = maps
+    far_points = whole(get_rows(received_ref, FIRST_ROWS, TERMS + 2, peers))
+    far_points_ref[...] = far_points
     apply(
-        smoothed, FIRST_ROWS, received_ref, weights, solved, metric_ref,
+        smoothed, FIRST_ROWS, received_ref, maps, far_points, solved, metric_ref,
         helmholtz_ref, first_ref, inner_ref, pair_ref, points_ref,
         [total_of(resid * smoothed)], back_ref, local_ref, sent_ref,
     )
@@ -523,18 +505,18 @@
 
 def second_kernel(
     received_ref, fields_ref, points_ref, pair_ref, resid_ref, image_ref,
-    weights_ref, jacobi_ref, metric_ref, helmholtz_ref, first_ref, inner_ref,
+    maps_ref, far_points_ref, jacobi_ref, metric_ref, helmholtz_ref, first_ref, inner_ref,
     smoothed_ref, back_ref, local_ref, sent_ref,
 ):
     elements = helmholtz_ref.shape[0]
     peers = points_ref.shape[0] - 2 * FACE_ROWS
     solved = get_solved(received_ref, ROWS, peers)
     resid = resid_ref[...]
-    vertices = one_vertex(fields_ref[8 * elements : 8 * elements + 1, :])
-    smoothed = rows_of(jacobi_ref[...]) * resid + prolonged(solved[0], vertices, elements)
+    flat = whole(fields_ref[8 * elements : 8 * elements + 1, :])
+    smoothed = rows_of(jacobi_ref[...]) * resid + prolonged(solved[0], flat, elements)
     smoothed_ref[...] = smoothed
     apply(
-        smoothed, ROWS, received_ref, weights_ref[...], solved, metric_ref,
+        smoothed, ROWS, received_ref, maps_ref[...], far_points_ref[...], solved, metric_ref,
         helmholtz_ref, first_ref, inner_ref, pair_ref, points_ref,
         [total_of(resid * smoothed), total_of(image_ref[...] * smoothed)],
         back_ref, local_ref, sent_ref,
@@ -613,9 +595,9 @@
         ],
         right_side, jacobi, coarse_inverse, coarse_map, shared_slots, face_points, copied=True,
     )
-    smoothed, weights, back, near, sent = call(
+    smoothed, maps, far_points, back, near, sent = call(
         start_kernel,
-        [field, (NC, points_shape[0] * LANES), field, local, sent_shape],
+        [field, (points_shape, jnp.int32), (points_shape, jnp.int32), field, local, sent_shape],
         exchange(sent), fields, points, pair_list, metric, helmholtz,
         t["first"], t["inner"],
     )
@@ -626,7 +608,7 @@
     )
     second, back, near, sent = call(
         second_kernel, [field, field, local, sent_shape],
-        exchange(sent), fields, points, pair_list, resid, image, weights, jacobi,
+        exchange(sent), fields, points, pair_list, resid, image, maps, far_points, jacobi,
         metric, helmholtz, t["first"], t["inner"],
     )
     return tuple(

time: 51.8 us -> 51.4 us (level)
  no operation moved by 1% of the time
where the time goes in v9:
time: 51.4 us; the launch traced here: 51.1 us
  blocking collectives  44 us (86%)
  Pallas kernels  6.33 us (12%)
  between operations  0.74 us (1%)
    all_to_all x4, blocking collectives, exchange(): lax.all_to_all(rows, ('grp', 'sub'), 0, 0, tiled=True).reshape(sent.shape)  44 us
    pallas_call x5, Pallas kernels, call(): pl.pallas_call(kernel, out_shape=[jax.ShapeDtypeStruct(*(out if isinstanc...  6.33 us

profile of v9, /device:TPU:0, one launch (start us, length us, event | category | flops | bytes accessed | tf_op | source)
XLA Modules:
  0.0 51.1 jit_solution(17636285046849334141)
XLA Ops:
  0.6 1.3 %shard_map.122 = (f32[320,128]{1,0:T(8,128)S(1)}, f32[136,128]{1,0:T(8,128)S(1)}, s32[16,128]{1,0:T(8,128)S(1)}) custom-call(f32[16,512]{1,0:T(8,128)} %right_hbm.1, f32[16,512]{1,0:T(8,128)} %jacobi_ref.3, f32[1,64,64]{2,1,0:T(8,128)} %inverse_ref.1, s32[8,16]{1,0:T(8,128)} %map_hbm.1, s32[1,8,128]{2,1,0:T(8,128)} %slot_hbm.1, s32[2,512]{1,0:T(2,128)} %face_hbm.1), custom_call_target="tpu_custom_call" | custom-call | tf_op jit(solution)/shard_map/pallas_call | solution.py:553
  1.9 0.0 copy-start
  1.9 0.0 copy-start.1
  1.9 0.0 copy-start.2
  1.9 0.0 copy-start.4
  2.0 0.0 copy-start.5
  2.0 15.7 %all_to_all.20 = f32[32,1,1280]{2,1,0:T(1,128)S(1)} all-to-all(f32[32,1,1280]{2,1,0:T(1,128)S(1)} %bitcast.12), channel_id=1, replica_groups=mesh['grp'=4,'sub'=8] {'grp','sub'}, dimensions={0} | all-to-all | bytes 327680 | tf_op jit(solution)/shard_map/all_to_all | solution.py:587
  17.6 0.0 copy-done
  17.6 0.0 copy-done.1
  17.7 0.0 copy-done.2
  17.7 0.0 copy-done.4
  17.7 0.0 copy-done.5
  17.7 1.6 %shard_map.123 = (f32[64,128]{1,0:T(8,128)S(1)}, s32[16,128]{1,0:T(8,128)S(1)}, s32[16,128]{1,0:T(8,128)S(1)}, f32[64,128]{1,0:T(8,128)S(1)}, f32[1,2048]{1,0:T(1,128)S(1)}, /*index=5*/f32[160,128]{1,0:T(8,128)S(1)}) custom-call(f32[320,128]{1,0:T(8,128)S(1)} %bitcast.8, f32[136,128]{1,0:T(8,128)S(1)} %get-tuple-element.20.fields_ref, ...), custom_call_target="tpu_custom_call" | custom-call | tf_op jit(solution)/shard_map/pallas_call | solution.py:553
  19.3 0.0 copy-start.3
  19.3 0.0 copy-start.6
  19.3 9.7 %all_to_all.21 = f32[32,1,640]{2,1,0:T(1,128)S(1)} all-to-all(f32[32,1,640]{2,1,0:T(1,128)S(1)} %bitcast.14), channel_id=1, replica_groups=mesh['grp'=4,'sub'=8] {'grp','sub'}, dimensions={0} | all-to-all | bytes 163840 | tf_op jit(solution)/shard_map/all_to_all | solution.py:587
  29.1 0.0 copy-done.3
  29.1 0.0 copy-done.6
  29.1 0.7 %shard_map.124 = (f32[64,128]{1,0:T(8,128)S(1)}, f32[64,128]{1,0:T(8,128)S(1)}, f32[1,128]{1,0:T(1,128)S(1)}, f32[160,128]{1,0:T(8,128)S(1)}) custom-call(f32[160,128]{1,0:T(8,128)S(1)} %bitcast.11, f32[136,128]{1,0:T(8,128)S(1)} %get-tuple-element.20.fields_ref, s32[16,128]{1,0:T(8,128)S(1)} %get-tuple-element.21.points_ref, s32[2,1024]{1,0:T(2,128)S(1)} %copy-done.4, ...), custom_call_target="tpu_custom_call" | custom-call | tf_op jit(solution)/shard_map/pallas_call | solution.py:553
  29.8 9.3 %all_to_all.22 = f32[32,1,640]{2,1,0:T(1,128)S(1)} all-to-all(f32[32,1,640]{2,1,0:T(1,128)S(1)} %bitcast.15), channel_id=1, replica_groups=mesh['grp'=4,'sub'=8] {'grp','sub'}, dimensions={0} | all-to-all | bytes 163840 | tf_op jit(solution)/shard_map/all_to_all | solution.py:587
  39.1 1.6 %shard_map.125 = (f32[64,128]{1,0:T(8,128)S(1)}, f32[64,128]{1,0:T(8,128)S(1)}, f32[1,2048]{1,0:T(1,128)S(1)}, f32[160,128]{1,0:T(8,128)S(1)}) custom-call(f32[160,128]{1,0:T(8,128)S(1)} %bitcast.9, f32[136,128]{1,0:T(8,128)S(1)} %get-tuple-element.20.fields_ref, s32[16,128]{1,0:T(8,128)S(1)} %get-tuple-element.21.points_ref, s32[2,1024]{1,0:T(2,128)S(1)} %copy-done.4, ...), custom_call_target="tpu_custom_call" | custom-call | tf_op jit(solution)/shard_map/pallas_call | solution.py:553
  40.7 9.3 %all_to_all.23 = f32[32,1,640]{2,1,0:T(1,128)S(1)} all-to-all(f32[32,1,640]{2,1,0:T(1,128)S(1)} %bitcast.13), channel_id=1, replica_groups=mesh['grp'=4,'sub'=8] {'grp','sub'}, dimensions={0} | all-to-all | bytes 163840 | tf_op jit(solution)/shard_map/all_to_all | solution.py:587
  50.0 1.1 %shard_map.126 = (f32[16,512]{1,0:T(8,128)}, f32[16,512]{1,0:T(8,128)}) custom-call(f32[160,128]{1,0:T(8,128)S(1)} %bitcast.10, s32[16,128]{1,0:T(8,128)S(1)} %get-tuple-element.21.points_ref, s32[2,1024]{1,0:T(2,128)S(1)} %copy-done.4, f32[64,128]{1,0:T(8,128)S(1)} %get-tuple-element.23.smoothed_ref.old_ref, f32[64,128]{1,0:T(8,128)S(1)} %get-tuple-element.32.field_ref, ...), custom_call_target="tpu_custom_call" | custom-call | tf_op jit(solution)/shard_map/pallas_call | solution.py:553
Async XLA Ops:
  1.9 15.7 %copy-start = (f32[16,512]{1,0:T(8,128)S(1)}, f32[16,512]{1,0:T(8,128)}, u32[]{:S(2)}) copy-start(f32[16,512]{1,0:T(8,128)} %helmholtz_ref.7) | copy-start | bytes 98308
  1.9 15.7 %copy-start.1 = (bf16[256,256]{1,0:T(8,128)(2,1)S(1)}, bf16[256,256]{1,0:T(8,128)(2,1)}, u32[]{:S(2)}) copy-start(bf16[256,256]{1,0:T(8,128)(2,1)} %constant.4.clone.inner_ref) | copy-start | bytes 393220
  1.9 15.7 %copy-start.2 = (f32[16,1536]{1,0:T(8,128)S(1)}, f32[16,1536]{1,0:T(8,128)}, u32[]{:S(2)}) copy-start(f32[16,1536]{1,0:T(8,128)} %metric_ref.3) | copy-start | bytes 294916
  1.9 15.7 %copy-start.4 = (s32[2,1024]{1,0:T(2,128)S(1)}, s32[2,1024]{1,0:T(2,128)}, u32[]{:S(2)}) copy-start(s32[2,1024]{1,0:T(2,128)} %pair_ref.7) | copy-start | bytes 24580
  2.0 15.7 %copy-start.5 = (f32[64,128]{1,0:T(8,128)S(1)}, f32[64,128]{1,0:T(8,128)}, u32[]{:S(2)}) copy-start(f32[64,128]{1,0:T(8,128)} %constant.5.clone.first_ref) | copy-start | bytes 98308
  19.3 9.8 %copy-start.3 = (f32[16,512]{1,0:T(8,128)S(1)}, f32[16,512]{1,0:T(8,128)}, u32[]{:S(2)}) copy-start(f32[16,512]{1,0:T(8,128)} %jacobi_ref.3) | copy-start | bytes 98308
  19.3 9.7 %copy-start.6 = (f32[1,64,64]{2,1,0:T(8,128)S(1)}, f32[1,64,64]{2,1,0:T(8,128)}, u32[]{:S(2)}) copy-start(f32[1,64,64]{2,1,0:T(8,128)} %inverse_ref.1) | copy-start | bytes 49156

commit v10 on v9

--- a/solution.py
+++ b/solution.py
@@ -274,12 +274,13 @@
 
 def flat_map(mapped):
     elements = mapped.shape[1]
-    width = 8 * elements
-    own = own_element(elements, width)
-    place = lax.broadcasted_iota(jnp.int32, (8, width), 1) // elements
-    spread = jnp.where(own, 1.0, 0.0).astype(BF16)
-    wide = jnp.dot(mapped.astype(F32).astype(BF16), spread, preferred_element_type=F32)
-    keep = lax.broadcasted_iota(jnp.int32, (8, width), 0) == place
+    shape = (8, 8 * elements)
+    lane = lax.broadcasted_iota(jnp.int32, shape, 1)
+    padded = jnp.concatenate(
+        [mapped.astype(F32), jnp.zeros((8, shape[1] - elements), F32)], axis=1
+    )
+    wide = take(padded, lane & (elements - 1))
+    keep = lax.broadcasted_iota(jnp.int32, shape, 0) == lane // elements
     return jnp.sum(jnp.where(keep, wide, 0.0), axis=0, keepdims=True)
 
 
@@ -418,19 +419,30 @@
 
 
 def apply(
-    smoothed, count, received_ref, maps, far_points, solved, metric_ref, helmholtz_ref,
+    rough, smoothed, count, received_ref, flat, maps, far_points, solved, metric_ref, helmholtz_ref,
     first_ref, inner_ref, pair_ref, points_ref, dots, back_ref, local_ref, sent_ref,
 ):
     elements = smoothed.shape[0] // 4
     peers = points_ref.shape[0] - 2 * FACE_ROWS
     pairs = pair_chunks(pair_ref, elements)
     far = far_chunks(points_ref[...], elements)
-    counts = (peers, FACE_ROWS, FACE_ROWS)
-    spread = [jnp.broadcast_to(part, (n, LANES)) for part, n in zip(solved, counts)]
-    incoming = get_rows(received_ref, count, 0, peers) + prolonged_at(
-        jnp.concatenate(spread, axis=0), maps, far_points, elements
-    )
-    values = swapped(gather(smoothed, pairs)) + joined(incoming)
+    near = gather(rough, pairs)
+    partners = pair_ref[...]
+    partners = jnp.concatenate(halves(partners[1:2]) + halves(partners[0:1]), axis=0)
+    counts = (peers, FACE_ROWS, FACE_ROWS, partners.shape[0])
+    spread = [
+        jnp.broadcast_to(part, (n, LANES)) for part, n in zip((*solved, solved[0]), counts)
+    ]
+    coarse = prolonged_at(
+        jnp.concatenate(spread, axis=0),
+        jnp.concatenate([maps, jnp.broadcast_to(flat, partners.shape)], axis=0),
+        jnp.concatenate([far_points, partners], axis=0),
+        elements,
+    )
+    split_at = points_ref.shape[0]
+    incoming = get_rows(received_ref, count, 0, peers) + coarse[:split_at]
+    values = [value + more for value, more in zip(swapped(near), joined(coarse[split_at:]))]
+    values = values + joined(incoming)
     summed = smoothed + scatter(smoothed.shape[0], pairs + far, values)
     back, energy = stiffness(summed, metric_ref, first_ref, inner_ref)
     energy = energy + rows_of(helmholtz_ref[...]) * smoothed * smoothed
@@ -464,15 +476,15 @@
     solved = get_solved(received_ref, FIRST_ROWS, peers)
     resid = fields_ref[0 : 4 * elements, :]
     flat = whole(fields_ref[8 * elements : 8 * elements + 1, :])
-    smoothed = fields_ref[4 * elements : 8 * elements, :]
-    smoothed = smoothed + prolonged(solved[0], flat, elements)
+    rough = fields_ref[4 * elements : 8 * elements, :]
+    smoothed = rough + prolonged(solved[0], flat, elements)
     smoothed_ref[...] = smoothed
     maps = far_maps(received_ref, peers)
     maps_ref[...] = maps
     far_points = whole(get_rows(received_ref, FIRST_ROWS, TERMS + 2, peers))
     far_points_ref[...] = far_points
     apply(
-        smoothed, FIRST_ROWS, received_ref, maps, far_points, solved, metric_ref,
+        rough, smoothed, FIRST_ROWS, received_ref, flat, maps, far_points, solved, metric_ref,
         helmholtz_ref, first_ref, inner_ref, pair_ref, points_ref,
         [total_of(resid * smoothed)], back_ref, local_ref, sent_ref,
     )
@@ -513,10 +525,11 @@
     solved = get_solved(received_ref, ROWS, peers)
     resid = resid_ref[...]
     flat = whole(fields_ref[8 * elements : 8 * elements + 1, :])
-    smoothed = rows_of(jacobi_ref[...]) * resid + prolonged(solved[0], flat, elements)
+    rough = rows_of(jacobi_ref[...]) * resid
+    smoothed = rough + prolonged(solved[0], flat, elements)
     smoothed_ref[...] = smoothed
     apply(
-        smoothed, ROWS, received_ref, maps_ref[...], far_points_ref[...], solved, metric_ref,
+        rough, smoothed, ROWS, received_ref, flat, maps_ref[...], far_points_ref[...], solved, metric_ref,
         helmholtz_ref, first_ref, inner_ref, pair_ref, points_ref,
         [total_of(resid * smoothed), total_of(image_ref[...] * smoothed)],
         back_ref, local_ref, sent_ref,

time: 51.4 us -> 51.3 us (level)
  no operation moved by 1% of the time
where the time goes in v10:
time: 51.3 us; the launch traced here: 51 us
  blocking collectives  44 us (86%)
  Pallas kernels  6.16 us (12%)
  between operations  0.74 us (1%)
    all_to_all x4, blocking collectives, exchange(): lax.all_to_all(rows, ('grp', 'sub'), 0, 0, tiled=True).reshape(sent.shape)  44 us
    pallas_call x5, Pallas kernels, call(): pl.pallas_call(kernel, out_shape=[jax.ShapeDtypeStruct(*(out if isinstanc...  6.16 us

profile of v10, /device:TPU:0, one launch (start us, length us, event | category | flops | bytes accessed | tf_op | source)
XLA Modules:
  0.0 51.0 jit_solution(7713511015665230489)
XLA Ops:
  0.6 1.3 %shard_map.122 = (f32[320,128]{1,0:T(8,128)S(1)}, f32[136,128]{1,0:T(8,128)S(1)}, s32[16,128]{1,0:T(8,128)S(1)}) custom-call(f32[16,512]{1,0:T(8,128)} %right_hbm.1, f32[16,512]{1,0:T(8,128)} %jacobi_ref.3, f32[1,64,64]{2,1,0:T(8,128)} %inverse_ref.1, s32[8,16]{1,0:T(8,128)} %map_hbm.1, s32[1,8,128]{2,1,0:T(8,128)} %slot_hbm.1, s32[2,512]{1,0:T(2,128)} %face_hbm.1), custom_call_target="tpu_custom_call" | custom-call | tf_op jit(solution)/shard_map/pallas_call | solution.py:566
  1.9 0.0 copy-start
  1.9 0.0 copy-start.1
  1.9 0.0 copy-start.2
  1.9 0.0 copy-start.4
  2.0 0.0 copy-start.5
  2.0 15.7 %all_to_all.20 = f32[32,1,1280]{2,1,0:T(1,128)S(1)} all-to-all(f32[32,1,1280]{2,1,0:T(1,128)S(1)} %bitcast.12), channel_id=1, replica_groups=mesh['grp'=4,'sub'=8] {'grp','sub'}, dimensions={0} | all-to-all | bytes 327680 | tf_op jit(solution)/shard_map/all_to_all | solution.py:600
  17.6 0.0 copy-done
  17.6 0.0 copy-done.1
  17.6 0.0 copy-done.2
  17.7 0.0 copy-done.4
  17.7 0.0 copy-done.5
  17.7 1.6 %shard_map.123 = (f32[64,128]{1,0:T(8,128)S(1)}, s32[16,128]{1,0:T(8,128)S(1)}, s32[16,128]{1,0:T(8,128)S(1)}, f32[64,128]{1,0:T(8,128)S(1)}, f32[1,2048]{1,0:T(1,128)S(1)}, /*index=5*/f32[160,128]{1,0:T(8,128)S(1)}) custom-call(f32[320,128]{1,0:T(8,128)S(1)} %bitcast.8, f32[136,128]{1,0:T(8,128)S(1)} %get-tuple-element.20.fields_ref, ...), custom_call_target="tpu_custom_call" | custom-call | tf_op jit(solution)/shard_map/pallas_call | solution.py:566
  19.2 0.0 copy-start.3
  19.2 0.0 copy-start.6
  19.3 9.7 %all_to_all.21 = f32[32,1,640]{2,1,0:T(1,128)S(1)} all-to-all(f32[32,1,640]{2,1,0:T(1,128)S(1)} %bitcast.14), channel_id=1, replica_groups=mesh['grp'=4,'sub'=8] {'grp','sub'}, dimensions={0} | all-to-all | bytes 163840 | tf_op jit(solution)/shard_map/all_to_all | solution.py:600
  29.0 0.0 copy-done.3
  29.0 0.0 copy-done.6
  29.0 0.7 %shard_map.124 = (f32[64,128]{1,0:T(8,128)S(1)}, f32[64,128]{1,0:T(8,128)S(1)}, f32[1,128]{1,0:T(1,128)S(1)}, f32[160,128]{1,0:T(8,128)S(1)}) custom-call(f32[160,128]{1,0:T(8,128)S(1)} %bitcast.11, f32[136,128]{1,0:T(8,128)S(1)} %get-tuple-element.20.fields_ref, s32[16,128]{1,0:T(8,128)S(1)} %get-tuple-element.21.points_ref, s32[2,1024]{1,0:T(2,128)S(1)} %copy-done.4, ...), custom_call_target="tpu_custom_call" | custom-call | tf_op jit(solution)/shard_map/pallas_call | solution.py:566
  29.8 9.3 %all_to_all.22 = f32[32,1,640]{2,1,0:T(1,128)S(1)} all-to-all(f32[32,1,640]{2,1,0:T(1,128)S(1)} %bitcast.15), channel_id=1, replica_groups=mesh['grp'=4,'sub'=8] {'grp','sub'}, dimensions={0} | all-to-all | bytes 163840 | tf_op jit(solution)/shard_map/all_to_all | solution.py:600
  39.1 1.5 %shard_map.125 = (f32[64,128]{1,0:T(8,128)S(1)}, f32[64,128]{1,0:T(8,128)S(1)}, f32[1,2048]{1,0:T(1,128)S(1)}, f32[160,128]{1,0:T(8,128)S(1)}) custom-call(f32[160,128]{1,0:T(8,128)S(1)} %bitcast.9, f32[136,128]{1,0:T(8,128)S(1)} %get-tuple-element.20.fields_ref, s32[16,128]{1,0:T(8,128)S(1)} %get-tuple-element.21.points_ref, s32[2,1024]{1,0:T(2,128)S(1)} %copy-done.4, ...), custom_call_target="tpu_custom_call" | custom-call | tf_op jit(solution)/shard_map/pallas_call | solution.py:566
  40.6 9.3 %all_to_all.23 = f32[32,1,640]{2,1,0:T(1,128)S(1)} all-to-all(f32[32,1,640]{2,1,0:T(1,128)S(1)} %bitcast.13), channel_id=1, replica_groups=mesh['grp'=4,'sub'=8] {'grp','sub'}, dimensions={0} | all-to-all | bytes 163840 | tf_op jit(solution)/shard_map/all_to_all | solution.py:600
  49.9 1.1 %shard_map.126 = (f32[16,512]{1,0:T(8,128)}, f32[16,512]{1,0:T(8,128)}) custom-call(f32[160,128]{1,0:T(8,128)S(1)} %bitcast.10, s32[16,128]{1,0:T(8,128)S(1)} %get-tuple-element.21.points_ref, s32[2,1024]{1,0:T(2,128)S(1)} %copy-done.4, f32[64,128]{1,0:T(8,128)S(1)} %get-tuple-element.23.smoothed_ref.old_ref, f32[64,128]{1,0:T(8,128)S(1)} %get-tuple-element.32.field_ref, ...), custom_call_target="tpu_custom_call" | custom-call | tf_op jit(solution)/shard_map/pallas_call | solution.py:566
Async XLA Ops:
  1.9 15.7 %copy-start = (f32[16,512]{1,0:T(8,128)S(1)}, f32[16,512]{1,0:T(8,128)}, u32[]{:S(2)}) copy-start(f32[16,512]{1,0:T(8,128)} %helmholtz_ref.7) | copy-start | bytes 98308
  1.9 15.7 %copy-start.1 = (bf16[256,256]{1,0:T(8,128)(2,1)S(1)}, bf16[256,256]{1,0:T(8,128)(2,1)}, u32[]{:S(2)}) copy-start(bf16[256,256]{1,0:T(8,128)(2,1)} %constant.4.clone.inner_ref) | copy-start | bytes 393220
  1.9 15.7 %copy-start.2 = (f32[16,1536]{1,0:T(8,128)S(1)}, f32[16,1536]{1,0:T(8,128)}, u32[]{:S(2)}) copy-start(f32[16,1536]{1,0:T(8,128)} %metric_ref.3) | copy-start | bytes 294916
  1.9 15.7 %copy-start.4 = (s32[2,1024]{1,0:T(2,128)S(1)}, s32[2,1024]{1,0:T(2,128)}, u32[]{:S(2)}) copy-start(s32[2,1024]{1,0:T(2,128)} %pair_ref.7) | copy-start | bytes 24580
  2.0 15.7 %copy-start.5 = (f32[64,128]{1,0:T(8,128)S(1)}, f32[64,128]{1,0:T(8,128)}, u32[]{:S(2)}) copy-start(f32[64,128]{1,0:T(8,128)} %constant.5.clone.first_ref) | copy-start | bytes 98308
  19.2 9.8 %copy-start.3 = (f32[16,512]{1,0:T(8,128)S(1)}, f32[16,512]{1,0:T(8,128)}, u32[]{:S(2)}) copy-start(f32[16,512]{1,0:T(8,128)} %jacobi_ref.3) | copy-start | bytes 98308
  19.2 9.8 %copy-start.6 = (f32[1,64,64]{2,1,0:T(8,128)S(1)}, f32[1,64,64]{2,1,0:T(8,128)}, u32[]{:S(2)}) copy-start(f32[1,64,64]{2,1,0:T(8,128)} %inverse_ref.1) | copy-start | bytes 49156

commit v11 on v10

--- a/solution.py
+++ b/solution.py
@@ -149,9 +149,17 @@
     return [wide[:, at : at + LANES] for at in range(0, wide.shape[1], LANES)]
 
 
+def owner(devices, peers):
+    place = lax.broadcasted_iota(jnp.int32, (devices, LANES), 0)
+    return lax.rem(place + middle_of(devices // peers) * peers, devices)
+
+
+def middle_of(groups):
+    return groups // 2
+
+
 def own_group(devices, peers, away=0):
-    shape = (devices, LANES)
-    return lax.broadcasted_iota(jnp.int32, shape, 0) // peers - lax.axis_index("grp") == away
+    return owner(devices, peers) // peers - lax.axis_index("grp") == away
 
 
 def send_rows(sent_ref, count, at, rows, peers):
@@ -191,7 +199,7 @@
 
 def get_row(rows, peers, away):
     here = lax.axis_index("grp") * peers + lax.axis_index("sub")
-    source = lax.broadcasted_iota(jnp.int32, rows.shape, 0) - here == away * peers
+    source = owner(rows.shape[0], peers) - here == away * peers
     return jnp.sum(jnp.where(source, rows, 0.0), axis=0, keepdims=True)
 
 
@@ -595,9 +603,15 @@
     points_shape = (peers + 2 * FACE_ROWS, LANES)
     sent_shape = (groups * peers * ROWS, LANES)
 
+    devices = groups * peers
+    order = [(d + middle_of(groups) * peers) % devices for d in range(devices)]
+
     def exchange(sent):
         rows = sent.reshape(groups * peers, 1, -1)
-        return lax.all_to_all(rows, ("grp", "sub"), 0, 0, tiled=True).reshape(sent.shape)
+        received = lax.all_to_all(
+            rows, ("grp", "sub"), 0, 0, axis_index_groups=[order], tiled=True
+        )
+        return received.reshape(sent.shape)
 
     sent, fields, points = call(
         first_kernel,

time: 51.3 us -> 51.3 us (level)
  no operation moved by 1% of the time
where the time goes in v11:
time: 51.3 us; the launch traced here: 51 us
  blocking collectives  44 us (86%)
  Pallas kernels  6.17 us (12%)
  between operations  0.74 us (1%)
    all_to_all x4, blocking collectives, exchange(): lax.all_to_all(rows, ('grp', 'sub'), 0, 0, axis_index_groups=[order], til...  44 us
    pallas_call x5, Pallas kernels, call(): pl.pallas_call(kernel, out_shape=[jax.ShapeDtypeStruct(*(out if isinstanc...  6.17 us

profile of v11, /device:TPU:0, one launch (start us, length us, event | category | flops | bytes accessed | tf_op | source)
XLA Modules:
  0.0 51.0 jit_solution(13934939174703013998)
XLA Ops:
  0.6 1.3 %shard_map.122 = (f32[320,128]{1,0:T(8,128)S(1)}, f32[136,128]{1,0:T(8,128)S(1)}, s32[16,128]{1,0:T(8,128)S(1)}) custom-call(f32[16,512]{1,0:T(8,128)} %right_hbm.1, f32[16,512]{1,0:T(8,128)} %jacobi_ref.3, f32[1,64,64]{2,1,0:T(8,128)} %inverse_ref.1, s32[8,16]{1,0:T(8,128)} %map_hbm.1, s32[1,8,128]{2,1,0:T(8,128)} %slot_hbm.1, s32[2,512]{1,0:T(2,128)} %face_hbm.1), custom_call_target="tpu_custom_call" | custom-call | tf_op jit(solution)/shard_map/pallas_call | solution.py:574
  1.9 0.0 copy-start
  1.9 0.0 copy-start.1
  1.9 0.0 copy-start.2
  1.9 0.0 copy-start.4
  2.0 0.0 copy-start.5
  2.0 15.7 %all_to_all.20 = f32[32,1,1280]{2,1,0:T(1,128)S(1)} all-to-all(f32[32,1,1280]{2,1,0:T(1,128)S(1)} %bitcast.12), channel_id=1, replica_groups={{16,17,18,19,20,21,22,23,24,25,26,27,28,29,30,31,0,1,2,3,4,5,6,7,8,9,10..., dimensions={0} | all-to-all | bytes 327680 | tf_op jit(solution)/shard_map/all_to_all | solution.py:611
  17.6 0.0 copy-done
  17.6 0.0 copy-done.1
  17.6 0.0 copy-done.2
  17.7 0.0 copy-done.4
  17.7 0.0 copy-done.5
  17.7 1.5 %shard_map.123 = (f32[64,128]{1,0:T(8,128)S(1)}, s32[16,128]{1,0:T(8,128)S(1)}, s32[16,128]{1,0:T(8,128)S(1)}, f32[64,128]{1,0:T(8,128)S(1)}, f32[1,2048]{1,0:T(1,128)S(1)}, /*index=5*/f32[160,128]{1,0:T(8,128)S(1)}) custom-call(f32[320,128]{1,0:T(8,128)S(1)} %bitcast.8, f32[136,128]{1,0:T(8,128)S(1)} %get-tuple-element.20.fields_ref, ...), custom_call_target="tpu_custom_call" | custom-call | tf_op jit(solution)/shard_map/pallas_call | solution.py:574
  19.2 0.0 copy-start.3
  19.2 0.0 copy-start.6
  19.3 9.7 %all_to_all.21 = f32[32,1,640]{2,1,0:T(1,128)S(1)} all-to-all(f32[32,1,640]{2,1,0:T(1,128)S(1)} %bitcast.14), channel_id=1, replica_groups={{16,17,18,19,20,21,22,23,24,25,26,27,28,29,30,31,0,1,2,3,4,5,6,7,8,9,10..., dimensions={0} | all-to-all | bytes 163840 | tf_op jit(solution)/shard_map/all_to_all | solution.py:611
  29.0 0.0 copy-done.3
  29.0 0.0 copy-done.6
  29.0 0.7 %shard_map.124 = (f32[64,128]{1,0:T(8,128)S(1)}, f32[64,128]{1,0:T(8,128)S(1)}, f32[1,128]{1,0:T(1,128)S(1)}, f32[160,128]{1,0:T(8,128)S(1)}) custom-call(f32[160,128]{1,0:T(8,128)S(1)} %bitcast.11, f32[136,128]{1,0:T(8,128)S(1)} %get-tuple-element.20.fields_ref, s32[16,128]{1,0:T(8,128)S(1)} %get-tuple-element.21.points_ref, s32[2,1024]{1,0:T(2,128)S(1)} %copy-done.4, ...), custom_call_target="tpu_custom_call" | custom-call | tf_op jit(solution)/shard_map/pallas_call | solution.py:574
  29.7 9.3 %all_to_all.22 = f32[32,1,640]{2,1,0:T(1,128)S(1)} all-to-all(f32[32,1,640]{2,1,0:T(1,128)S(1)} %bitcast.15), channel_id=1, replica_groups={{16,17,18,19,20,21,22,23,24,25,26,27,28,29,30,31,0,1,2,3,4,5,6,7,8,9,10..., dimensions={0} | all-to-all | bytes 163840 | tf_op jit(solution)/shard_map/all_to_all | solution.py:611
  39.0 1.5 %shard_map.125 = (f32[64,128]{1,0:T(8,128)S(1)}, f32[64,128]{1,0:T(8,128)S(1)}, f32[1,2048]{1,0:T(1,128)S(1)}, f32[160,128]{1,0:T(8,128)S(1)}) custom-call(f32[160,128]{1,0:T(8,128)S(1)} %bitcast.9, f32[136,128]{1,0:T(8,128)S(1)} %get-tuple-element.20.fields_ref, s32[16,128]{1,0:T(8,128)S(1)} %get-tuple-element.21.points_ref, s32[2,1024]{1,0:T(2,128)S(1)} %copy-done.4, ...), custom_call_target="tpu_custom_call" | custom-call | tf_op jit(solution)/shard_map/pallas_call | solution.py:574
  40.6 9.3 %all_to_all.23 = f32[32,1,640]{2,1,0:T(1,128)S(1)} all-to-all(f32[32,1,640]{2,1,0:T(1,128)S(1)} %bitcast.13), channel_id=1, replica_groups={{16,17,18,19,20,21,22,23,24,25,26,27,28,29,30,31,0,1,2,3,4,5,6,7,8,9,10..., dimensions={0} | all-to-all | bytes 163840 | tf_op jit(solution)/shard_map/all_to_all | solution.py:611
  49.9 1.1 %shard_map.126 = (f32[16,512]{1,0:T(8,128)}, f32[16,512]{1,0:T(8,128)}) custom-call(f32[160,128]{1,0:T(8,128)S(1)} %bitcast.10, s32[16,128]{1,0:T(8,128)S(1)} %get-tuple-element.21.points_ref, s32[2,1024]{1,0:T(2,128)S(1)} %copy-done.4, f32[64,128]{1,0:T(8,128)S(1)} %get-tuple-element.23.smoothed_ref.old_ref, f32[64,128]{1,0:T(8,128)S(1)} %get-tuple-element.32.field_ref, ...), custom_call_target="tpu_custom_call" | custom-call | tf_op jit(solution)/shard_map/pallas_call | solution.py:574
Async XLA Ops:
  1.9 15.7 %copy-start = (f32[16,512]{1,0:T(8,128)S(1)}, f32[16,512]{1,0:T(8,128)}, u32[]{:S(2)}) copy-start(f32[16,512]{1,0:T(8,128)} %helmholtz_ref.7) | copy-start | bytes 98308
  1.9 15.7 %copy-start.1 = (bf16[256,256]{1,0:T(8,128)(2,1)S(1)}, bf16[256,256]{1,0:T(8,128)(2,1)}, u32[]{:S(2)}) copy-start(bf16[256,256]{1,0:T(8,128)(2,1)} %constant.4.clone.inner_ref) | copy-start | bytes 393220
  1.9 15.7 %copy-start.2 = (f32[16,1536]{1,0:T(8,128)S(1)}, f32[16,1536]{1,0:T(8,128)}, u32[]{:S(2)}) copy-start(f32[16,1536]{1,0:T(8,128)} %metric_ref.3) | copy-start | bytes 294916
  1.9 15.7 %copy-start.4 = (s32[2,1024]{1,0:T(2,128)S(1)}, s32[2,1024]{1,0:T(2,128)}, u32[]{:S(2)}) copy-start(s32[2,1024]{1,0:T(2,128)} %pair_ref.7) | copy-start | bytes 24580
  2.0 15.7 %copy-start.5 = (f32[64,128]{1,0:T(8,128)S(1)}, f32[64,128]{1,0:T(8,128)}, u32[]{:S(2)}) copy-start(f32[64,128]{1,0:T(8,128)} %constant.5.clone.first_ref) | copy-start | bytes 98308
  19.2 9.7 %copy-start.3 = (f32[16,512]{1,0:T(8,128)S(1)}, f32[16,512]{1,0:T(8,128)}, u32[]{:S(2)}) copy-start(f32[16,512]{1,0:T(8,128)} %jacobi_ref.3) | copy-start | bytes 98308
  19.2 9.7 %copy-start.6 = (f32[1,64,64]{2,1,0:T(8,128)S(1)}, f32[1,64,64]{2,1,0:T(8,128)}, u32[]{:S(2)}) copy-start(f32[1,64,64]{2,1,0:T(8,128)} %inverse_ref.1) | copy-start | bytes 49156

commit v12 on v10

--- a/solution.py
+++ b/solution.py
@@ -122,10 +122,6 @@
     return [
         (row[:, at : at + STEP], lane[:, at : at + STEP]) for at in range(0, row.shape[1], STEP)
     ]
-
-
-def cut(row):
-    return [row[:, at : at + STEP] for at in range(0, row.shape[1], STEP)]
 
 
 def pair_chunks(pair_ref, elements):
@@ -420,7 +416,7 @@
 
 def apply(
     rough, smoothed, count, received_ref, flat, maps, far_points, solved, metric_ref, helmholtz_ref,
-    first_ref, inner_ref, pair_ref, points_ref, dots, back_ref, local_ref, sent_ref,
+    first_ref, inner_ref, pair_ref, points_ref, dots, back_ref, sent_ref,
 ):
     elements = smoothed.shape[0] // 4
     peers = points_ref.shape[0] - 2 * FACE_ROWS
@@ -447,29 +443,27 @@
     back, energy = stiffness(summed, metric_ref, first_ref, inner_ref)
     energy = energy + rows_of(helmholtz_ref[...]) * smoothed * smoothed
     back_ref[...] = back
-    values = gather(back, pairs + far)
-    near = swapped(values[: len(pairs)])
-    for k, value in enumerate(near):
-        local_ref[0:1, k * STEP : (k + 1) * STEP] = value
-    send_values(sent_ref, ROWS, values[len(pairs) :], peers)
+    send_values(sent_ref, ROWS, gather(back, far), peers)
     send_same(sent_ref, ROWS, TERMS, packed(dots + [total_of(energy)]))
 
 
 def image_of(
-    field_ref, back_ref, local_ref, received_ref, helmholtz_ref, pair_ref, points_ref
+    field_ref, back_ref, received_ref, helmholtz_ref, pair_ref, points_ref
 ):
     elements = field_ref.shape[0] // 4
     peers = points_ref.shape[0] - 2 * FACE_ROWS
-    chunks = pair_chunks(pair_ref, elements) + far_chunks(points_ref[...], elements)
-    values = cut(local_ref[...]) + joined(get_rows(received_ref, ROWS, 0, peers))
-    summed = back_ref[...] + scatter(field_ref.shape[0], chunks, values)
+    pairs = pair_chunks(pair_ref, elements)
+    back = back_ref[...]
+    values = swapped(gather(back, pairs)) + joined(get_rows(received_ref, ROWS, 0, peers))
+    far = far_chunks(points_ref[...], elements)
+    summed = back + scatter(field_ref.shape[0], pairs + far, values)
     return summed + rows_of(helmholtz_ref[...]) * field_ref[...]
 
 
 def start_kernel(
     received_ref, fields_ref, points_ref, pair_ref, metric_ref, helmholtz_ref,
     first_ref, inner_ref,
-    smoothed_ref, maps_ref, far_points_ref, back_ref, local_ref, sent_ref,
+    smoothed_ref, maps_ref, far_points_ref, back_ref, sent_ref,
 ):
     elements = helmholtz_ref.shape[0]
     peers = points_ref.shape[0] - 2 * FACE_ROWS
@@ -486,13 +480,13 @@
     apply(
         rough, smoothed, FIRST_ROWS, received_ref, flat, maps, far_points, solved, metric_ref,
         helmholtz_ref, first_ref, inner_ref, pair_ref, points_ref,
-        [total_of(resid * smoothed)], back_ref, local_ref, sent_ref,
+        [total_of(resid * smoothed)], back_ref, sent_ref,
     )
 
 
 def middle_kernel(
     received_ref, fields_ref, points_ref, pair_ref, jacobi_ref, helmholtz_ref,
-    inverse_ref, smoothed_ref, back_ref, local_ref,
+    inverse_ref, smoothed_ref, back_ref,
     image_ref, resid_ref, scalars_ref, sent_ref,
 ):
     elements = helmholtz_ref.shape[0]
@@ -502,7 +496,7 @@
     values = unpacked(dots, 2)
     alpha = values[0] / values[1]
     image = image_of(
-        smoothed_ref, back_ref, local_ref, received_ref, helmholtz_ref, pair_ref,
+        smoothed_ref, back_ref, received_ref, helmholtz_ref, pair_ref,
         points_ref,
     )
     image_ref[...] = image
@@ -518,7 +512,7 @@
 def second_kernel(
     received_ref, fields_ref, points_ref, pair_ref, resid_ref, image_ref,
     maps_ref, far_points_ref, jacobi_ref, metric_ref, helmholtz_ref, first_ref, inner_ref,
-    smoothed_ref, back_ref, local_ref, sent_ref,
+    smoothed_ref, back_ref, sent_ref,
 ):
     elements = helmholtz_ref.shape[0]
     peers = points_ref.shape[0] - 2 * FACE_ROWS
@@ -532,13 +526,13 @@
         rough, smoothed, ROWS, received_ref, flat, maps_ref[...], far_points_ref[...], solved, metric_ref,
         helmholtz_ref, first_ref, inner_ref, pair_ref, points_ref,
         [total_of(resid * smoothed), total_of(image_ref[...] * smoothed)],
-        back_ref, local_ref, sent_ref,
+        back_ref, sent_ref,
     )
 
 
 def final_kernel(
     received_ref, points_ref, pair_ref, old_ref, field_ref, resid_ref, old_image_ref,
-    scalars_ref, back_ref, local_ref, helmholtz_ref,
+    scalars_ref, back_ref, helmholtz_ref,
     solution_ref, residual_ref,
 ):
     before = unpacked(scalars_ref[...], 2)
@@ -551,7 +545,7 @@
     direction = field_ref[...] + beta * old
     solution_ref[...] = wide_of(alpha * old + step * direction)
     image = image_of(
-        field_ref, back_ref, local_ref, received_ref, helmholtz_ref, pair_ref,
+        field_ref, back_ref, received_ref, helmholtz_ref, pair_ref,
         points_ref,
     )
     image = image + beta * old_image_ref[...]
@@ -591,7 +585,6 @@
     t = {name: jnp.asarray(value) for name, value in tables().items()}
     elements = right_side.shape[0]
     field = (4 * elements, LANES)
-    local = (1, pair_list.shape[0] * pair_list.shape[1])
     points_shape = (peers + 2 * FACE_ROWS, LANES)
     sent_shape = (groups * peers * ROWS, LANES)
 
@@ -608,19 +601,19 @@
         ],
         right_side, jacobi, coarse_inverse, coarse_map, shared_slots, face_points, copied=True,
     )
-    smoothed, maps, far_points, back, near, sent = call(
+    smoothed, maps, far_points, back, sent = call(
         start_kernel,
-        [field, (points_shape, jnp.int32), (points_shape, jnp.int32), field, local, sent_shape],
+        [field, (points_shape, jnp.int32), (points_shape, jnp.int32), field, sent_shape],
         exchange(sent), fields, points, pair_list, metric, helmholtz,
         t["first"], t["inner"],
     )
     image, resid, scalars, sent = call(
         middle_kernel, [field, field, (1, LANES), sent_shape],
         exchange(sent), fields, points, pair_list, jacobi, helmholtz, coarse_inverse,
-        smoothed, back, near,
-    )
-    second, back, near, sent = call(
-        second_kernel, [field, field, local, sent_shape],
+        smoothed, back,
+    )
+    second, back, sent = call(
+        second_kernel, [field, field, sent_shape],
         exchange(sent), fields, points, pair_list, resid, image, maps, far_points, jacobi,
         metric, helmholtz, t["first"], t["inner"],
     )
@@ -628,7 +621,7 @@
         call(
             final_kernel, [right_side.shape, right_side.shape],
             exchange(sent), points, pair_list, smoothed, second, resid, image, scalars,
-            back, near, helmholtz,
+            back, helmholtz,
         )
     )
 

time: 51.3 us -> 51.4 us (level)
  no operation moved by 1% of the time
where the time goes in v12:
time: 51.4 us; the launch traced here: 51.1 us
  blocking collectives  44 us (86%)
  Pallas kernels  6.28 us (12%)
  between operations  0.74 us (1%)
    all_to_all x4, blocking collectives, exchange(): lax.all_to_all(rows, ('grp', 'sub'), 0, 0, tiled=True).reshape(sent.shape)  44 us
    pallas_call x5, Pallas kernels, call(): pl.pallas_call(kernel, out_shape=[jax.ShapeDtypeStruct(*(out if isinstanc...  6.28 us

profile of v12, /device:TPU:0, one launch (start us, length us, event | category | flops | bytes accessed | tf_op | source)
XLA Modules:
  0.0 51.1 jit_solution(16752291392625808959)
XLA Ops:
  0.6 1.3 %shard_map.122 = (f32[320,128]{1,0:T(8,128)S(1)}, f32[136,128]{1,0:T(8,128)S(1)}, s32[16,128]{1,0:T(8,128)S(1)}) custom-call(f32[16,512]{1,0:T(8,128)} %right_hbm.1, f32[16,512]{1,0:T(8,128)} %jacobi_ref.3, f32[1,64,64]{2,1,0:T(8,128)} %inverse_ref.1, s32[8,16]{1,0:T(8,128)} %map_hbm.1, s32[1,8,128]{2,1,0:T(8,128)} %slot_hbm.1, s32[2,512]{1,0:T(2,128)} %face_hbm.1), custom_call_target="tpu_custom_call" | custom-call | tf_op jit(solution)/shard_map/pallas_call | solution.py:560
  1.9 0.0 copy-start
  1.9 0.0 copy-start.1
  1.9 0.0 copy-start.2
  1.9 0.0 copy-start.4
  2.0 0.0 copy-start.5
  2.0 15.7 %all_to_all.20 = f32[32,1,1280]{2,1,0:T(1,128)S(1)} all-to-all(f32[32,1,1280]{2,1,0:T(1,128)S(1)} %bitcast.12), channel_id=1, replica_groups=mesh['grp'=4,'sub'=8] {'grp','sub'}, dimensions={0} | all-to-all | bytes 327680 | tf_op jit(solution)/shard_map/all_to_all | solution.py:593
  17.6 0.0 copy-done
  17.6 0.0 copy-done.1
  17.6 0.0 copy-done.2
  17.7 0.0 copy-done.4
  17.7 0.0 copy-done.5
  17.7 1.4 %shard_map.123 = (f32[64,128]{1,0:T(8,128)S(1)}, s32[16,128]{1,0:T(8,128)S(1)}, s32[16,128]{1,0:T(8,128)S(1)}, f32[64,128]{1,0:T(8,128)S(1)}, f32[160,128]{1,0:T(8,128)S(1)}) custom-call(f32[320,128]{1,0:T(8,128)S(1)} %bitcast.8, f32[136,128]{1,0:T(8,128)S(1)} %get-tuple-element.18.fields_ref, s32[16,128]{1,0:T(8,128)S(1)} %get-tuple-element.19.points_ref, ...), custom_call_target="tpu_custom_call" | custom-call | tf_op jit(solution)/shard_map/pallas_call | solution.py:560
  19.1 0.0 copy-start.3
  19.1 0.0 copy-start.6
  19.1 9.7 %all_to_all.21 = f32[32,1,640]{2,1,0:T(1,128)S(1)} all-to-all(f32[32,1,640]{2,1,0:T(1,128)S(1)} %bitcast.14), channel_id=1, replica_groups=mesh['grp'=4,'sub'=8] {'grp','sub'}, dimensions={0} | all-to-all | bytes 163840 | tf_op jit(solution)/shard_map/all_to_all | solution.py:593
  28.8 0.0 copy-done.3
  28.8 0.0 copy-done.6
  28.8 1.0 %shard_map.124 = (f32[64,128]{1,0:T(8,128)S(1)}, f32[64,128]{1,0:T(8,128)S(1)}, f32[1,128]{1,0:T(1,128)S(1)}, f32[160,128]{1,0:T(8,128)S(1)}) custom-call(f32[160,128]{1,0:T(8,128)S(1)} %bitcast.11, f32[136,128]{1,0:T(8,128)S(1)} %get-tuple-element.18.fields_ref, s32[16,128]{1,0:T(8,128)S(1)} %get-tuple-element.19.points_ref, s32[2,1024]{1,0:T(2,128)S(1)} %copy-done.4, ...), custom_call_target="tpu_custom_call" | custom-call | tf_op jit(solution)/shard_map/pallas_call | solution.py:560
  29.8 9.3 %all_to_all.22 = f32[32,1,640]{2,1,0:T(1,128)S(1)} all-to-all(f32[32,1,640]{2,1,0:T(1,128)S(1)} %bitcast.15), channel_id=1, replica_groups=mesh['grp'=4,'sub'=8] {'grp','sub'}, dimensions={0} | all-to-all | bytes 163840 | tf_op jit(solution)/shard_map/all_to_all | solution.py:593
  39.1 1.4 %shard_map.125 = (f32[64,128]{1,0:T(8,128)S(1)}, f32[64,128]{1,0:T(8,128)S(1)}, f32[160,128]{1,0:T(8,128)S(1)}) custom-call(f32[160,128]{1,0:T(8,128)S(1)} %bitcast.10, f32[136,128]{1,0:T(8,128)S(1)} %get-tuple-element.18.fields_ref, s32[16,128]{1,0:T(8,128)S(1)} %get-tuple-element.19.points_ref, s32[2,1024]{1,0:T(2,128)S(1)} %copy-done.4, ...), custom_call_target="tpu_custom_call" | custom-call | tf_op jit(solution)/shard_map/pallas_call | solution.py:560
  40.5 9.3 %all_to_all.23 = f32[32,1,640]{2,1,0:T(1,128)S(1)} all-to-all(f32[32,1,640]{2,1,0:T(1,128)S(1)} %bitcast.13), channel_id=1, replica_groups=mesh['grp'=4,'sub'=8] {'grp','sub'}, dimensions={0} | all-to-all | bytes 163840 | tf_op jit(solution)/shard_map/all_to_all | solution.py:593
  49.8 1.3 %shard_map.126 = (f32[16,512]{1,0:T(8,128)}, f32[16,512]{1,0:T(8,128)}) custom-call(f32[160,128]{1,0:T(8,128)S(1)} %bitcast.9, s32[16,128]{1,0:T(8,128)S(1)} %get-tuple-element.19.points_ref, s32[2,1024]{1,0:T(2,128)S(1)} %copy-done.4, f32[64,128]{1,0:T(8,128)S(1)} %get-tuple-element.21.smoothed_ref.old_ref, f32[64,128]{1,0:T(8,128)S(1)} %get-tuple-element.29.field_ref, ...), custom_call_target="tpu_custom_call" | custom-call | tf_op jit(solution)/shard_map/pallas_call | solution.py:560
Async XLA Ops:
  1.9 15.7 %copy-start = (f32[16,512]{1,0:T(8,128)S(1)}, f32[16,512]{1,0:T(8,128)}, u32[]{:S(2)}) copy-start(f32[16,512]{1,0:T(8,128)} %helmholtz_ref.7) | copy-start | bytes 98308
  1.9 15.7 %copy-start.1 = (bf16[256,256]{1,0:T(8,128)(2,1)S(1)}, bf16[256,256]{1,0:T(8,128)(2,1)}, u32[]{:S(2)}) copy-start(bf16[256,256]{1,0:T(8,128)(2,1)} %constant.4.clone.inner_ref) | copy-start | bytes 393220
  1.9 15.7 %copy-start.2 = (f32[16,1536]{1,0:T(8,128)S(1)}, f32[16,1536]{1,0:T(8,128)}, u32[]{:S(2)}) copy-start(f32[16,1536]{1,0:T(8,128)} %metric_ref.3) | copy-start | bytes 294916
  1.9 15.7 %copy-start.4 = (s32[2,1024]{1,0:T(2,128)S(1)}, s32[2,1024]{1,0:T(2,128)}, u32[]{:S(2)}) copy-start(s32[2,1024]{1,0:T(2,128)} %pair_ref.7) | copy-start | bytes 24580
  2.0 15.7 %copy-start.5 = (f32[64,128]{1,0:T(8,128)S(1)}, f32[64,128]{1,0:T(8,128)}, u32[]{:S(2)}) copy-start(f32[64,128]{1,0:T(8,128)} %constant.5.clone.first_ref) | copy-start | bytes 98308
  19.1 9.8 %copy-start.3 = (f32[16,512]{1,0:T(8,128)S(1)}, f32[16,512]{1,0:T(8,128)}, u32[]{:S(2)}) copy-start(f32[16,512]{1,0:T(8,128)} %jacobi_ref.3) | copy-start | bytes 98308
  19.1 9.8 %copy-start.6 = (f32[1,64,64]{2,1,0:T(8,128)S(1)}, f32[1,64,64]{2,1,0:T(8,128)}, u32[]{:S(2)}) copy-start(f32[1,64,64]{2,1,0:T(8,128)} %inverse_ref.1) | copy-start | bytes 49156

commit v13 on v10

--- a/solution.py
+++ b/solution.py
@@ -99,8 +99,8 @@
     count = field.shape[0]
     both = jnp.concatenate(split(field), axis=0)
     out = []
-    for row, lane in chunks:
-        picked = jnp.dot(both, lane_hot(lane), preferred_element_type=F32)
+    for row, hot in chunks:
+        picked = jnp.dot(both, hot, preferred_element_type=F32)
         mine = jnp.where(one_hot(row, count), picked[:count] + picked[count:], 0.0)
         out.append(jnp.sum(mine, axis=0, keepdims=True))
     return out
@@ -108,12 +108,12 @@
 
 def scatter(rows, chunks, values):
     total = jnp.zeros((2 * rows, LANES), F32)
-    for (row, lane), value in zip(chunks, values):
+    for (row, hot), value in zip(chunks, values):
         steps = lax.broadcasted_iota(jnp.int32, (rows, row.shape[1]), 0).astype(F32).astype(BF16)
         mine = steps == row.astype(F32).astype(BF16)
         parts = [jnp.where(mine, part, jnp.zeros_like(steps)) for part in split(value)]
         total = total + lax.dot_general(
-            jnp.concatenate(parts, axis=0), lane_hot(lane), NT, preferred_element_type=F32
+            jnp.concatenate(parts, axis=0), hot, NT, preferred_element_type=F32
         )
     return total[:rows] + total[rows:]
 
@@ -128,7 +128,7 @@
     return [row[:, at : at + STEP] for at in range(0, row.shape[1], STEP)]
 
 
-def pair_chunks(pair_ref, elements):
+def pair_places(pair_ref, elements):
     row, lane = locate(pair_ref[...], elements)
     return chunked(row[0:1], lane[0:1]) + chunked(row[1:2], lane[1:2])
 
@@ -140,9 +140,24 @@
     ]
 
 
-def far_chunks(points, elements):
+def far_places(points, elements):
     row, lane = locate(points, elements)
     return list(zip(joined(row), joined(lane)))
+
+
+def built(places, hot_ref):
+    out = []
+    for k, (row, lane) in enumerate(places):
+        hot = lane_hot(lane)
+        hot_ref[k * LANES : (k + 1) * LANES, :] = hot
+        out.append((row, hot))
+    return out
+
+
+def loaded(places, hot_ref):
+    return [
+        (row, hot_ref[k * LANES : (k + 1) * LANES, :]) for k, (row, lane) in enumerate(places)
+    ]
 
 
 def halves(wide):
@@ -371,7 +386,7 @@
 
 def first_kernel(
     right_hbm, jacobi_hbm, inverse_hbm, map_hbm, slot_hbm, face_hbm,
-    sent_ref, fields_ref, points_ref,
+    sent_ref, fields_ref, points_ref, far_hot_ref,
     right_ref, jacobi_ref, inverse_ref, map_ref, slot_ref, face_ref, sems,
 ):
     copies = []
@@ -403,7 +418,7 @@
     fields_ref[4 * elements : 8 * elements, :] = smoothed
     fields_ref[8 * elements :, :] = jnp.broadcast_to(flat, (8, LANES))
     part = coarse_part(resid, one_vertex(flat), inverse_ref[0])
-    values = gather(smoothed, far_chunks(points, elements))
+    values = gather(smoothed, built(far_places(points, elements), far_hot_ref))
     send_values(sent_ref, FIRST_ROWS, values, peers)
     send_same(sent_ref, FIRST_ROWS, TERMS, part)
     send_same(sent_ref, FIRST_ROWS, TERMS + 1, flat)
@@ -420,12 +435,12 @@
 
 def apply(
     rough, smoothed, count, received_ref, flat, maps, far_points, solved, metric_ref, helmholtz_ref,
-    first_ref, inner_ref, pair_ref, points_ref, dots, back_ref, local_ref, sent_ref,
+    first_ref, inner_ref, pair_ref, pairs, points_ref, far_hot_ref, dots, back_ref, local_ref,
+    sent_ref,
 ):
     elements = smoothed.shape[0] // 4
     peers = points_ref.shape[0] - 2 * FACE_ROWS
-    pairs = pair_chunks(pair_ref, elements)
-    far = far_chunks(points_ref[...], elements)
+    far = loaded(far_places(points_ref[...], elements), far_hot_ref)
     near = gather(rough, pairs)
     partners = pair_ref[...]
     partners = jnp.concatenate(halves(partners[1:2]) + halves(partners[0:1]), axis=0)
@@ -456,20 +471,22 @@
 
 
 def image_of(
-    field_ref, back_ref, local_ref, received_ref, helmholtz_ref, pair_ref, points_ref
+    field_ref, back_ref, local_ref, received_ref, helmholtz_ref, pair_ref, pair_hot_ref, points_ref,
+    far_hot_ref,
 ):
     elements = field_ref.shape[0] // 4
     peers = points_ref.shape[0] - 2 * FACE_ROWS
-    chunks = pair_chunks(pair_ref, elements) + far_chunks(points_ref[...], elements)
+    chunks = loaded(pair_places(pair_ref, elements), pair_hot_ref)
+    chunks = chunks + loaded(far_places(points_ref[...], elements), far_hot_ref)
     values = cut(local_ref[...]) + joined(get_rows(received_ref, ROWS, 0, peers))
     summed = back_ref[...] + scatter(field_ref.shape[0], chunks, values)
     return summed + rows_of(helmholtz_ref[...]) * field_ref[...]
 
 
 def start_kernel(
-    received_ref, fields_ref, points_ref, pair_ref, metric_ref, helmholtz_ref,
+    received_ref, fields_ref, points_ref, far_hot_ref, pair_ref, metric_ref, helmholtz_ref,
     first_ref, inner_ref,
-    smoothed_ref, maps_ref, far_points_ref, back_ref, local_ref, sent_ref,
+    smoothed_ref, maps_ref, far_points_ref, back_ref, local_ref, sent_ref, pair_hot_ref,
 ):
     elements = helmholtz_ref.shape[0]
     peers = points_ref.shape[0] - 2 * FACE_ROWS
@@ -485,13 +502,14 @@
     far_points_ref[...] = far_points
     apply(
         rough, smoothed, FIRST_ROWS, received_ref, flat, maps, far_points, solved, metric_ref,
-        helmholtz_ref, first_ref, inner_ref, pair_ref, points_ref,
+        helmholtz_ref, first_ref, inner_ref, pair_ref,
+        built(pair_places(pair_ref, elements), pair_hot_ref), points_ref, far_hot_ref,
         [total_of(resid * smoothed)], back_ref, local_ref, sent_ref,
     )
 
 
 def middle_kernel(
-    received_ref, fields_ref, points_ref, pair_ref, jacobi_ref, helmholtz_ref,
+    received_ref, fields_ref, points_ref, far_hot_ref, pair_ref, pair_hot_ref, jacobi_ref, helmholtz_ref,
     inverse_ref, smoothed_ref, back_ref, local_ref,
     image_ref, resid_ref, scalars_ref, sent_ref,
 ):
@@ -503,20 +521,22 @@
     alpha = values[0] / values[1]
     image = image_of(
         smoothed_ref, back_ref, local_ref, received_ref, helmholtz_ref, pair_ref,
-        points_ref,
+        pair_hot_ref, points_ref, far_hot_ref,
     )
     image_ref[...] = image
     resid = fields_ref[0 : 4 * elements, :] - alpha * image
     resid_ref[...] = resid
     vertices = one_vertex(fields_ref[8 * elements : 8 * elements + 1, :])
     part = coarse_part(resid, vertices, inverse_ref[0])
-    values = gather(rows_of(jacobi_ref[...]) * resid, far_chunks(points_ref[...], elements))
+    values = gather(
+        rows_of(jacobi_ref[...]) * resid, loaded(far_places(points_ref[...], elements), far_hot_ref),
+    )
     send_values(sent_ref, ROWS, values, peers)
     send_same(sent_ref, ROWS, TERMS, part)
 
 
 def second_kernel(
-    received_ref, fields_ref, points_ref, pair_ref, resid_ref, image_ref,
+    received_ref, fields_ref, points_ref, far_hot_ref, pair_ref, pair_hot_ref, resid_ref, image_ref,
     maps_ref, far_points_ref, jacobi_ref, metric_ref, helmholtz_ref, first_ref, inner_ref,
     smoothed_ref, back_ref, local_ref, sent_ref,
 ):
@@ -530,14 +550,15 @@
     smoothed_ref[...] = smoothed
     apply(
         rough, smoothed, ROWS, received_ref, flat, maps_ref[...], far_points_ref[...], solved, metric_ref,
-        helmholtz_ref, first_ref, inner_ref, pair_ref, points_ref,
+        helmholtz_ref, first_ref, inner_ref, pair_ref,
+        loaded(pair_places(pair_ref, elements), pair_hot_ref), points_ref, far_hot_ref,
         [total_of(resid * smoothed), total_of(image_ref[...] * smoothed)],
         back_ref, local_ref, sent_ref,
     )
 
 
 def final_kernel(
-    received_ref, points_ref, pair_ref, old_ref, field_ref, resid_ref, old_image_ref,
+    received_ref, points_ref, far_hot_ref, pair_ref, pair_hot_ref, old_ref, field_ref, resid_ref, old_image_ref,
     scalars_ref, back_ref, local_ref, helmholtz_ref,
     solution_ref, residual_ref,
 ):
@@ -552,7 +573,7 @@
     solution_ref[...] = wide_of(alpha * old + step * direction)
     image = image_of(
         field_ref, back_ref, local_ref, received_ref, helmholtz_ref, pair_ref,
-        points_ref,
+        pair_hot_ref, points_ref, far_hot_ref,
     )
     image = image + beta * old_image_ref[...]
     residual_ref[...] = wide_of(resid_ref[...] - step * image)
@@ -599,35 +620,40 @@
         rows = sent.reshape(groups * peers, 1, -1)
         return lax.all_to_all(rows, ("grp", "sub"), 0, 0, tiled=True).reshape(sent.shape)
 
-    sent, fields, points = call(
+    far_hot_shape = (points_shape[0] * LANES // 2, STEP)
+    pair_hot_shape = (local[1] * LANES // STEP, STEP)
+
+    sent, fields, points, far_hot = call(
         first_kernel,
         [
             (groups * peers * FIRST_ROWS, LANES),
             (8 * elements + 8, LANES),
             (points_shape, jnp.int32),
+            (far_hot_shape, BF16),
         ],
         right_side, jacobi, coarse_inverse, coarse_map, shared_slots, face_points, copied=True,
     )
-    smoothed, maps, far_points, back, near, sent = call(
+    smoothed, maps, far_points, back, near, sent, pair_hot = call(
         start_kernel,
-        [field, (points_shape, jnp.int32), (points_shape, jnp.int32), field, local, sent_shape],
-        exchange(sent), fields, points, pair_list, metric, helmholtz,
+        [field, (points_shape, jnp.int32), (points_shape, jnp.int32), field, local, sent_shape,
+         (pair_hot_shape, BF16)],
+        exchange(sent), fields, points, far_hot, pair_list, metric, helmholtz,
         t["first"], t["inner"],
     )
     image, resid, scalars, sent = call(
         middle_kernel, [field, field, (1, LANES), sent_shape],
-        exchange(sent), fields, points, pair_list, jacobi, helmholtz, coarse_inverse,
+        exchange(sent), fields, points, far_hot, pair_list, pair_hot, jacobi, helmholtz, coarse_inverse,
         smoothed, back, near,
     )
     second, back, near, sent = call(
         second_kernel, [field, field, local, sent_shape],
-        exchange(sent), fields, points, pair_list, resid, image, maps, far_points, jacobi,
+        exchange(sent), fields, points, far_hot, pair_list, pair_hot, resid, image, maps, far_points, jacobi,
         metric, helmholtz, t["first"], t["inner"],
     )
     return tuple(
         call(
             final_kernel, [right_side.shape, right_side.shape],
-            exchange(sent), points, pair_list, smoothed, second, resid, image, scalars,
+            exchange(sent), points, far_hot, pair_list, pair_hot, smoothed, second, resid, image, scalars,
             back, near, helmholtz,
         )
     )

time: 51.3 us -> 51.3 us (level)
  no operation moved by 1% of the time
where the time goes in v13:
time: 51.3 us; the launch traced here: 50.9 us
  blocking collectives  44 us (86%)
  Pallas kernels  6.16 us (12%)
  between operations  0.74 us (1%)
    all_to_all x4, blocking collectives, exchange(): lax.all_to_all(rows, ('grp', 'sub'), 0, 0, tiled=True).reshape(sent.shape)  44 us
    pallas_call x5, Pallas kernels, call(): pl.pallas_call(kernel, out_shape=[jax.ShapeDtypeStruct(*(out if isinstanc...  6.16 us

profile of v13, /device:TPU:0, one launch (start us, length us, event | category | flops | bytes accessed | tf_op | source)
XLA Modules:
  0.0 50.9 jit_solution(18405720425754328250)
XLA Ops:
  0.6 1.3 %shard_map.122 = (f32[320,128]{1,0:T(8,128)S(1)}, f32[136,128]{1,0:T(8,128)S(1)}, s32[16,128]{1,0:T(8,128)S(1)}, bf16[1024,256]{1,0:T(8,128)(2,1)S(1)}) custom-call(f32[16,512]{1,0:T(8,128)} %right_hbm.1, f32[16,512]{1,0:T(8,128)} %jacobi_ref.3, f32[1,64,64]{2,1,0:T(8,128)} %inverse_ref.1, s32[8,16]{1,0:T(8,128)} %map_hbm.1, s32[1,8,128]{2,1,0:T(8,128)} %slot_hbm.1, ...), custom_call_target="tpu_custom_call" | custom-call | tf_op jit(solution)/shard_map/pallas_call | solution.py:587
  1.9 0.0 copy-start
  1.9 0.0 copy-start.1
  1.9 0.0 copy-start.2
  2.0 0.0 copy-start.4
  2.0 0.0 copy-start.6
  2.0 15.7 %all_to_all.20 = f32[32,1,1280]{2,1,0:T(1,128)S(1)} all-to-all(f32[32,1,1280]{2,1,0:T(1,128)S(1)} %bitcast.12), channel_id=1, replica_groups=mesh['grp'=4,'sub'=8] {'grp','sub'}, dimensions={0} | all-to-all | bytes 327680 | tf_op jit(solution)/shard_map/all_to_all | solution.py:621
  17.7 0.0 copy-done
  17.7 0.0 copy-done.1
  17.7 0.0 copy-done.2
  17.7 0.0 copy-done.4
  17.7 0.0 copy-done.6
  17.7 1.6 %shard_map.123 = (f32[64,128]{1,0:T(8,128)S(1)}, s32[16,128]{1,0:T(8,128)S(1)}, s32[16,128]{1,0:T(8,128)S(1)}, f32[64,128]{1,0:T(8,128)S(1)}, f32[1,2048]{1,0:T(...) custom-call(f32[320,128]{1,0:T(8,128)S(1)} %bitcast.8, f32[136,128]{1,0:T(8,128)S(1)} %get-tuple-element.22.fields_ref, ...), custom_call_target="tpu_custom_call" | custom-call | tf_op jit(solution)/shard_map/pallas_call | solution.py:587
  19.2 0.0 copy-start.3
  19.3 0.0 copy-start.5
  19.3 9.7 %all_to_all.21 = f32[32,1,640]{2,1,0:T(1,128)S(1)} all-to-all(f32[32,1,640]{2,1,0:T(1,128)S(1)} %bitcast.14), channel_id=1, replica_groups=mesh['grp'=4,'sub'=8] {'grp','sub'}, dimensions={0} | all-to-all | bytes 163840 | tf_op jit(solution)/shard_map/all_to_all | solution.py:621
  29.0 0.0 copy-done.3
  29.0 0.0 copy-done.5
  29.0 0.7 %shard_map.124 = (f32[64,128]{1,0:T(8,128)S(1)}, f32[64,128]{1,0:T(8,128)S(1)}, f32[1,128]{1,0:T(1,128)S(1)}, f32[160,128]{1,0:T(8,128)S(1)}) custom-call(f32[160,128]{1,0:T(8,128)S(1)} %bitcast.11, f32[136,128]{1,0:T(8,128)S(1)} %get-tuple-element.22.fields_ref, s32[16,128]{1,0:T(8,128)S(1)} %get-tuple-element.23.points_ref, ...), custom_call_target="tpu_custom_call" | custom-call | tf_op jit(solution)/shard_map/pallas_call | solution.py:587
  29.7 9.3 %all_to_all.22 = f32[32,1,640]{2,1,0:T(1,128)S(1)} all-to-all(f32[32,1,640]{2,1,0:T(1,128)S(1)} %bitcast.15), channel_id=1, replica_groups=mesh['grp'=4,'sub'=8] {'grp','sub'}, dimensions={0} | all-to-all | bytes 163840 | tf_op jit(solution)/shard_map/all_to_all | solution.py:621
  39.0 1.5 %shard_map.125 = (f32[64,128]{1,0:T(8,128)S(1)}, f32[64,128]{1,0:T(8,128)S(1)}, f32[1,2048]{1,0:T(1,128)S(1)}, f32[160,128]{1,0:T(8,128)S(1)}) custom-call(f32[160,128]{1,0:T(8,128)S(1)} %bitcast.10, f32[136,128]{1,0:T(8,128)S(1)} %get-tuple-element.22.fields_ref, s32[16,128]{1,0:T(8,128)S(1)} %get-tuple-element.23.points_ref, ...), custom_call_target="tpu_custom_call" | custom-call | tf_op jit(solution)/shard_map/pallas_call | solution.py:587
  40.6 9.3 %all_to_all.23 = f32[32,1,640]{2,1,0:T(1,128)S(1)} all-to-all(f32[32,1,640]{2,1,0:T(1,128)S(1)} %bitcast.13), channel_id=1, replica_groups=mesh['grp'=4,'sub'=8] {'grp','sub'}, dimensions={0} | all-to-all | bytes 163840 | tf_op jit(solution)/shard_map/all_to_all | solution.py:621
  49.9 1.1 %shard_map.126 = (f32[16,512]{1,0:T(8,128)}, f32[16,512]{1,0:T(8,128)}) custom-call(f32[160,128]{1,0:T(8,128)S(1)} %bitcast.9, s32[16,128]{1,0:T(8,128)S(1)} %get-tuple-element.23.points_ref, bf16[1024,256]{1,0:T(8,128)(2,1)S(1)} %get-tuple-element.24.far_hot_ref, s32[2,1024]{1,0:T(2,128)S(1)} %copy-done.4, ...), custom_call_target="tpu_custom_call" | custom-call | tf_op jit(solution)/shard_map/pallas_call | solution.py:587
Async XLA Ops:
  1.9 15.7 %copy-start = (f32[16,512]{1,0:T(8,128)S(1)}, f32[16,512]{1,0:T(8,128)}, u32[]{:S(2)}) copy-start(f32[16,512]{1,0:T(8,128)} %helmholtz_ref.7) | copy-start | bytes 98308
  1.9 15.7 %copy-start.1 = (bf16[256,256]{1,0:T(8,128)(2,1)S(1)}, bf16[256,256]{1,0:T(8,128)(2,1)}, u32[]{:S(2)}) copy-start(bf16[256,256]{1,0:T(8,128)(2,1)} %constant.4.clone.inner_ref) | copy-start | bytes 393220
  1.9 15.7 %copy-start.2 = (f32[16,1536]{1,0:T(8,128)S(1)}, f32[16,1536]{1,0:T(8,128)}, u32[]{:S(2)}) copy-start(f32[16,1536]{1,0:T(8,128)} %metric_ref.3) | copy-start | bytes 294916
  2.0 15.7 %copy-start.4 = (s32[2,1024]{1,0:T(2,128)S(1)}, s32[2,1024]{1,0:T(2,128)}, u32[]{:S(2)}) copy-start(s32[2,1024]{1,0:T(2,128)} %pair_ref.7) | copy-start | bytes 24580
  2.0 15.7 %copy-start.6 = (f32[64,128]{1,0:T(8,128)S(1)}, f32[64,128]{1,0:T(8,128)}, u32[]{:S(2)}) copy-start(f32[64,128]{1,0:T(8,128)} %constant.5.clone.first_ref) | copy-start | bytes 98308
  19.2 9.8 %copy-start.3 = (f32[16,512]{1,0:T(8,128)S(1)}, f32[16,512]{1,0:T(8,128)}, u32[]{:S(2)}) copy-start(f32[16,512]{1,0:T(8,128)} %jacobi_ref.3) | copy-start | bytes 98308
  19.3 9.7 %copy-start.5 = (f32[1,64,64]{2,1,0:T(8,128)S(1)}, f32[1,64,64]{2,1,0:T(8,128)}, u32[]{:S(2)}) copy-start(f32[1,64,64]{2,1,0:T(8,128)} %inverse_ref.1) | copy-start | bytes 49156

commit v14 on v13

--- a/solution.py
+++ b/solution.py
@@ -10,7 +10,6 @@
 NC = 64
 POINTS = 512
 LANES = 128
-STEP = 256
 FACE_ROWS = 4
 ROWS = 5
 FIRST_ROWS = 10
@@ -95,69 +94,44 @@
     return jnp.take_along_axis(values, lanes, axis=1, mode="promise_in_bounds")
 
 
-def gather(field, chunks):
+def gather(field, points):
+    row, hot = points
     count = field.shape[0]
     both = jnp.concatenate(split(field), axis=0)
-    out = []
-    for row, hot in chunks:
-        picked = jnp.dot(both, hot, preferred_element_type=F32)
-        mine = jnp.where(one_hot(row, count), picked[:count] + picked[count:], 0.0)
-        out.append(jnp.sum(mine, axis=0, keepdims=True))
-    return out
-
-
-def scatter(rows, chunks, values):
-    total = jnp.zeros((2 * rows, LANES), F32)
-    for (row, hot), value in zip(chunks, values):
-        steps = lax.broadcasted_iota(jnp.int32, (rows, row.shape[1]), 0).astype(F32).astype(BF16)
-        mine = steps == row.astype(F32).astype(BF16)
-        parts = [jnp.where(mine, part, jnp.zeros_like(steps)) for part in split(value)]
-        total = total + lax.dot_general(
-            jnp.concatenate(parts, axis=0), hot, NT, preferred_element_type=F32
-        )
-    return total[:rows] + total[rows:]
-
-
-def chunked(row, lane):
-    return [
-        (row[:, at : at + STEP], lane[:, at : at + STEP]) for at in range(0, row.shape[1], STEP)
-    ]
-
-
-def cut(row):
-    return [row[:, at : at + STEP] for at in range(0, row.shape[1], STEP)]
-
-
-def pair_places(pair_ref, elements):
-    row, lane = locate(pair_ref[...], elements)
-    return chunked(row[0:1], lane[0:1]) + chunked(row[1:2], lane[1:2])
-
-
-def joined(rows):
-    return [
-        jnp.concatenate([rows[at : at + 1], rows[at + 1 : at + 2]], axis=1)
-        for at in range(0, rows.shape[0], 2)
-    ]
-
-
-def far_places(points, elements):
+    picked = jnp.dot(both, hot, preferred_element_type=F32)
+    mine = jnp.where(one_hot(row, count), picked[:count] + picked[count:], 0.0)
+    return jnp.sum(mine, axis=0, keepdims=True)
+
+
+def scatter(count, points, values):
+    row, hot = points
+    steps = lax.broadcasted_iota(jnp.int32, (count, row.shape[1]), 0).astype(F32).astype(BF16)
+    mine = steps == row.astype(F32).astype(BF16)
+    parts = [jnp.where(mine, part, jnp.zeros_like(steps)) for part in split(values)]
+    total = lax.dot_general(
+        jnp.concatenate(parts, axis=0), hot, NT, preferred_element_type=F32
+    )
+    return total[:count] + total[count:]
+
+
+def line(rows):
+    return jnp.concatenate([rows[k : k + 1] for k in range(rows.shape[0])], axis=1)
+
+
+def places_of(points, elements):
     row, lane = locate(points, elements)
-    return list(zip(joined(row), joined(lane)))
+    return line(row), line(lane)
 
 
 def built(places, hot_ref):
-    out = []
-    for k, (row, lane) in enumerate(places):
-        hot = lane_hot(lane)
-        hot_ref[k * LANES : (k + 1) * LANES, :] = hot
-        out.append((row, hot))
-    return out
+    row, lane = places
+    hot = lane_hot(lane)
+    hot_ref[...] = hot
+    return row, hot
 
 
 def loaded(places, hot_ref):
-    return [
-        (row, hot_ref[k * LANES : (k + 1) * LANES, :]) for k, (row, lane) in enumerate(places)
-    ]
+    return places[0], hot_ref[...]
 
 
 def halves(wide):
@@ -188,8 +162,7 @@
 
 
 def send_values(sent_ref, count, values, peers):
-    rows = jnp.concatenate([row for pair in values for row in halves(pair)], axis=0)
-    send_rows(sent_ref, count, 0, rows, peers)
+    send_rows(sent_ref, count, 0, jnp.concatenate(halves(values), axis=0), peers)
 
 
 def get(received_ref, count, at):
@@ -217,8 +190,8 @@
 
 
 def swapped(values):
-    count = len(values) // 2
-    return values[count:] + values[:count]
+    count = values.shape[1] // 2
+    return jnp.concatenate([values[:, count:], values[:, :count]], axis=1)
 
 
 def along_first(field, table_ref, base):
@@ -418,7 +391,7 @@
     fields_ref[4 * elements : 8 * elements, :] = smoothed
     fields_ref[8 * elements :, :] = jnp.broadcast_to(flat, (8, LANES))
     part = coarse_part(resid, one_vertex(flat), inverse_ref[0])
-    values = gather(smoothed, built(far_places(points, elements), far_hot_ref))
+    values = gather(smoothed, built(places_of(points, elements), far_hot_ref))
     send_values(sent_ref, FIRST_ROWS, values, peers)
     send_same(sent_ref, FIRST_ROWS, TERMS, part)
     send_same(sent_ref, FIRST_ROWS, TERMS + 1, flat)
@@ -440,7 +413,7 @@
 ):
     elements = smoothed.shape[0] // 4
     peers = points_ref.shape[0] - 2 * FACE_ROWS
-    far = loaded(far_places(points_ref[...], elements), far_hot_ref)
+    far = loaded(places_of(points_ref[...], elements), far_hot_ref)
     near = gather(rough, pairs)
     partners = pair_ref[...]
     partners = jnp.concatenate(halves(partners[1:2]) + halves(partners[0:1]), axis=0)
@@ -456,17 +429,14 @@
     )
     split_at = points_ref.shape[0]
     incoming = get_rows(received_ref, count, 0, peers) + coarse[:split_at]
-    values = [value + more for value, more in zip(swapped(near), joined(coarse[split_at:]))]
-    values = values + joined(incoming)
-    summed = smoothed + scatter(smoothed.shape[0], pairs + far, values)
+    near = swapped(near) + line(coarse[split_at:])
+    count = smoothed.shape[0]
+    summed = smoothed + scatter(count, pairs, near) + scatter(count, far, line(incoming))
     back, energy = stiffness(summed, metric_ref, first_ref, inner_ref)
     energy = energy + rows_of(helmholtz_ref[...]) * smoothed * smoothed
     back_ref[...] = back
-    values = gather(back, pairs + far)
-    near = swapped(values[: len(pairs)])
-    for k, value in enumerate(near):
-        local_ref[0:1, k * STEP : (k + 1) * STEP] = value
-    send_values(sent_ref, ROWS, values[len(pairs) :], peers)
+    local_ref[...] = swapped(gather(back, pairs))
+    send_values(sent_ref, ROWS, gather(back, far), peers)
     send_same(sent_ref, ROWS, TERMS, packed(dots + [total_of(energy)]))
 
 
@@ -476,10 +446,11 @@
 ):
     elements = field_ref.shape[0] // 4
     peers = points_ref.shape[0] - 2 * FACE_ROWS
-    chunks = loaded(pair_places(pair_ref, elements), pair_hot_ref)
-    chunks = chunks + loaded(far_places(points_ref[...], elements), far_hot_ref)
-    values = cut(local_ref[...]) + joined(get_rows(received_ref, ROWS, 0, peers))
-    summed = back_ref[...] + scatter(field_ref.shape[0], chunks, values)
+    pairs = loaded(places_of(pair_ref[...], elements), pair_hot_ref)
+    far = loaded(places_of(points_ref[...], elements), far_hot_ref)
+    incoming = line(get_rows(received_ref, ROWS, 0, peers))
+    count = field_ref.shape[0]
+    summed = back_ref[...] + scatter(count, pairs, local_ref[...]) + scatter(count, far, incoming)
     return summed + rows_of(helmholtz_ref[...]) * field_ref[...]
 
 
@@ -503,7 +474,7 @@
     apply(
         rough, smoothed, FIRST_ROWS, received_ref, flat, maps, far_points, solved, metric_ref,
         helmholtz_ref, first_ref, inner_ref, pair_ref,
-        built(pair_places(pair_ref, elements), pair_hot_ref), points_ref, far_hot_ref,
+        built(places_of(pair_ref[...], elements), pair_hot_ref), points_ref, far_hot_ref,
         [total_of(resid * smoothed)], back_ref, local_ref, sent_ref,
     )
 
@@ -529,7 +500,7 @@
     vertices = one_vertex(fields_ref[8 * elements : 8 * elements + 1, :])
     part = coarse_part(resid, vertices, inverse_ref[0])
     values = gather(
-        rows_of(jacobi_ref[...]) * resid, loaded(far_places(points_ref[...], elements), far_hot_ref),
+        rows_of(jacobi_ref[...]) * resid, loaded(places_of(points_ref[...], elements), far_hot_ref),
     )
     send_values(sent_ref, ROWS, values, peers)
     send_same(sent_ref, ROWS, TERMS, part)
@@ -551,7 +522,7 @@
     apply(
         rough, smoothed, ROWS, received_ref, flat, maps_ref[...], far_points_ref[...], solved, metric_ref,
         helmholtz_ref, first_ref, inner_ref, pair_ref,
-        loaded(pair_places(pair_ref, elements), pair_hot_ref), points_ref, far_hot_ref,
+        loaded(places_of(pair_ref[...], elements), pair_hot_ref), points_ref, far_hot_ref,
         [total_of(resid * smoothed), total_of(image_ref[...] * smoothed)],
         back_ref, local_ref, sent_ref,
     )
@@ -620,8 +591,8 @@
         rows = sent.reshape(groups * peers, 1, -1)
         return lax.all_to_all(rows, ("grp", "sub"), 0, 0, tiled=True).reshape(sent.shape)
 
-    far_hot_shape = (points_shape[0] * LANES // 2, STEP)
-    pair_hot_shape = (local[1] * LANES // STEP, STEP)
+    far_hot_shape = (LANES, points_shape[0] * LANES)
+    pair_hot_shape = (LANES, local[1])
 
     sent, fields, points, far_hot = call(
         first_kernel,

time: 51.3 us -> 52.1 us (1.016)
  Pallas kernels: 6.16 us -> 6.96 us
    pallas_call x5, Pallas kernels: 6.16 us -> 6.96 us  [call(): pl.pallas_call(kernel, out_shape=[jax.ShapeDtypeStruct(*(out if isinstanc...]
where the time goes in v14:
time: 52.1 us; the launch traced here: 51.7 us
  blocking collectives  44 us (84%)
  Pallas kernels  6.96 us (13%)
  between operations  0.74 us (1%)
    all_to_all x4, blocking collectives, exchange(): lax.all_to_all(rows, ('grp', 'sub'), 0, 0, tiled=True).reshape(sent.shape)  44 us
    pallas_call x5, Pallas kernels, call(): pl.pallas_call(kernel, out_shape=[jax.ShapeDtypeStruct(*(out if isinstanc...  6.96 us

profile of v14, /device:TPU:0, one launch (start us, length us, event | category | flops | bytes accessed | tf_op | source)
XLA Modules:
  0.0 51.7 jit_solution(7541159184439692661)
XLA Ops:
  0.6 1.3 %shard_map.122 = (f32[320,128]{1,0:T(8,128)S(1)}, f32[136,128]{1,0:T(8,128)S(1)}, s32[16,128]{1,0:T(8,128)S(1)}, bf16[128,2048]{1,0:T(8,128)(2,1)S(1)}) custom-call(f32[16,512]{1,0:T(8,128)} %right_hbm.1, f32[16,512]{1,0:T(8,128)} %jacobi_ref.3, f32[1,64,64]{2,1,0:T(8,128)} %inverse_ref.1, s32[8,16]{1,0:T(8,128)} %map_hbm.1, s32[1,8,128]{2,1,0:T(8,128)} %slot_hbm.1, ...), custom_call_target="tpu_custom_call" | custom-call | tf_op jit(solution)/shard_map/pallas_call | solution.py:558
  1.9 0.0 copy-start
  1.9 0.0 copy-start.1
  1.9 0.0 copy-start.2
  1.9 0.0 copy-start.4
  2.0 0.0 copy-start.6
  2.0 15.7 %all_to_all.20 = f32[32,1,1280]{2,1,0:T(1,128)S(1)} all-to-all(f32[32,1,1280]{2,1,0:T(1,128)S(1)} %bitcast.12), channel_id=1, replica_groups=mesh['grp'=4,'sub'=8] {'grp','sub'}, dimensions={0} | all-to-all | bytes 327680 | tf_op jit(solution)/shard_map/all_to_all | solution.py:592
  17.6 0.0 copy-done
  17.7 0.0 copy-done.1
  17.7 0.0 copy-done.2
  17.7 0.0 copy-done.4
  17.7 0.0 copy-done.6
  17.7 2.0 %shard_map.123 = (f32[64,128]{1,0:T(8,128)S(1)}, s32[16,128]{1,0:T(8,128)S(1)}, s32[16,128]{1,0:T(8,128)S(1)}, f32[64,128]{1,0:T(8,128)S(1)}, f32[1,2048]{1,0:T(...) custom-call(f32[320,128]{1,0:T(8,128)S(1)} %bitcast.8, f32[136,128]{1,0:T(8,128)S(1)} %get-tuple-element.22.fields_ref, ...), custom_call_target="tpu_custom_call" | custom-call | tf_op jit(solution)/shard_map/pallas_call | solution.py:558
  19.6 0.0 copy-start.3
  19.7 0.0 copy-start.5
  19.7 9.7 %all_to_all.21 = f32[32,1,640]{2,1,0:T(1,128)S(1)} all-to-all(f32[32,1,640]{2,1,0:T(1,128)S(1)} %bitcast.14), channel_id=1, replica_groups=mesh['grp'=4,'sub'=8] {'grp','sub'}, dimensions={0} | all-to-all | bytes 163840 | tf_op jit(solution)/shard_map/all_to_all | solution.py:592
  29.4 0.0 copy-done.3
  29.4 0.0 copy-done.5
  29.4 0.7 %shard_map.124 = (f32[64,128]{1,0:T(8,128)S(1)}, f32[64,128]{1,0:T(8,128)S(1)}, f32[1,128]{1,0:T(1,128)S(1)}, f32[160,128]{1,0:T(8,128)S(1)}) custom-call(f32[160,128]{1,0:T(8,128)S(1)} %bitcast.11, f32[136,128]{1,0:T(8,128)S(1)} %get-tuple-element.22.fields_ref, s32[16,128]{1,0:T(8,128)S(1)} %get-tuple-element.23.points_ref, ...), custom_call_target="tpu_custom_call" | custom-call | tf_op jit(solution)/shard_map/pallas_call | solution.py:558
  30.2 9.3 %all_to_all.22 = f32[32,1,640]{2,1,0:T(1,128)S(1)} all-to-all(f32[32,1,640]{2,1,0:T(1,128)S(1)} %bitcast.15), channel_id=1, replica_groups=mesh['grp'=4,'sub'=8] {'grp','sub'}, dimensions={0} | all-to-all | bytes 163840 | tf_op jit(solution)/shard_map/all_to_all | solution.py:592
  39.5 1.9 %shard_map.125 = (f32[64,128]{1,0:T(8,128)S(1)}, f32[64,128]{1,0:T(8,128)S(1)}, f32[1,2048]{1,0:T(1,128)S(1)}, f32[160,128]{1,0:T(8,128)S(1)}) custom-call(f32[160,128]{1,0:T(8,128)S(1)} %bitcast.10, f32[136,128]{1,0:T(8,128)S(1)} %get-tuple-element.22.fields_ref, s32[16,128]{1,0:T(8,128)S(1)} %get-tuple-element.23.points_ref, ...), custom_call_target="tpu_custom_call" | custom-call | tf_op jit(solution)/shard_map/pallas_call | solution.py:558
  41.4 9.3 %all_to_all.23 = f32[32,1,640]{2,1,0:T(1,128)S(1)} all-to-all(f32[32,1,640]{2,1,0:T(1,128)S(1)} %bitcast.13), channel_id=1, replica_groups=mesh['grp'=4,'sub'=8] {'grp','sub'}, dimensions={0} | all-to-all | bytes 163840 | tf_op jit(solution)/shard_map/all_to_all | solution.py:592
  50.7 1.1 %shard_map.126 = (f32[16,512]{1,0:T(8,128)}, f32[16,512]{1,0:T(8,128)}) custom-call(f32[160,128]{1,0:T(8,128)S(1)} %bitcast.9, s32[16,128]{1,0:T(8,128)S(1)} %get-tuple-element.23.points_ref, bf16[128,2048]{1,0:T(8,128)(2,1)S(1)} %get-tuple-element.24.far_hot_ref, s32[2,1024]{1,0:T(2,128)S(1)} %copy-done.4, ...), custom_call_target="tpu_custom_call" | custom-call | tf_op jit(solution)/shard_map/pallas_call | solution.py:558
Async XLA Ops:
  1.9 15.7 %copy-start = (f32[16,512]{1,0:T(8,128)S(1)}, f32[16,512]{1,0:T(8,128)}, u32[]{:S(2)}) copy-start(f32[16,512]{1,0:T(8,128)} %helmholtz_ref.7) | copy-start | bytes 98308
  1.9 15.7 %copy-start.1 = (bf16[256,256]{1,0:T(8,128)(2,1)S(1)}, bf16[256,256]{1,0:T(8,128)(2,1)}, u32[]{:S(2)}) copy-start(bf16[256,256]{1,0:T(8,128)(2,1)} %constant.4.clone.inner_ref) | copy-start | bytes 393220
  1.9 15.7 %copy-start.2 = (f32[16,1536]{1,0:T(8,128)S(1)}, f32[16,1536]{1,0:T(8,128)}, u32[]{:S(2)}) copy-start(f32[16,1536]{1,0:T(8,128)} %metric_ref.3) | copy-start | bytes 294916
  1.9 15.7 %copy-start.4 = (s32[2,1024]{1,0:T(2,128)S(1)}, s32[2,1024]{1,0:T(2,128)}, u32[]{:S(2)}) copy-start(s32[2,1024]{1,0:T(2,128)} %pair_ref.7) | copy-start | bytes 24580
  2.0 15.7 %copy-start.6 = (f32[64,128]{1,0:T(8,128)S(1)}, f32[64,128]{1,0:T(8,128)}, u32[]{:S(2)}) copy-start(f32[64,128]{1,0:T(8,128)} %constant.5.clone.first_ref) | copy-start | bytes 98308
  19.6 9.8 %copy-start.3 = (f32[16,512]{1,0:T(8,128)S(1)}, f32[16,512]{1,0:T(8,128)}, u32[]{:S(2)}) copy-start(f32[16,512]{1,0:T(8,128)} %jacobi_ref.3) | copy-start | bytes 98308
  19.7 9.7 %copy-start.5 = (f32[1,64,64]{2,1,0:T(8,128)S(1)}, f32[1,64,64]{2,1,0:T(8,128)}, u32[]{:S(2)}) copy-start(f32[1,64,64]{2,1,0:T(8,128)} %inverse_ref.1) | copy-start | bytes 49156

commit v15 on v13

--- a/solution.py
+++ b/solution.py
@@ -112,8 +112,8 @@
         steps = lax.broadcasted_iota(jnp.int32, (rows, row.shape[1]), 0).astype(F32).astype(BF16)
         mine = steps == row.astype(F32).astype(BF16)
         parts = [jnp.where(mine, part, jnp.zeros_like(steps)) for part in split(value)]
-        total = total + lax.dot_general(
-            jnp.concatenate(parts, axis=0), hot, NT, preferred_element_type=F32
+        total = total + jnp.dot(
+            jnp.concatenate(parts, axis=0), hot, preferred_element_type=F32
         )
     return total[:rows] + total[rows:]
 
@@ -152,6 +152,21 @@
         hot_ref[k * LANES : (k + 1) * LANES, :] = hot
         out.append((row, hot))
     return out
+
+
+def turned(places, hot_ref):
+    out = []
+    for k, (row, hot) in enumerate(places):
+        hot = hot.astype(F32).T.astype(BF16)
+        hot_ref[k * STEP : (k + 1) * STEP, :] = hot
+        out.append((row, hot))
+    return out
+
+
+def loaded_turned(places, hot_ref):
+    return [
+        (row, hot_ref[k * STEP : (k + 1) * STEP, :]) for k, (row, lane) in enumerate(places)
+    ]
 
 
 def loaded(places, hot_ref):
@@ -435,12 +450,11 @@
 
 def apply(
     rough, smoothed, count, received_ref, flat, maps, far_points, solved, metric_ref, helmholtz_ref,
-    first_ref, inner_ref, pair_ref, pairs, points_ref, far_hot_ref, dots, back_ref, local_ref,
-    sent_ref,
+    first_ref, inner_ref, pair_ref, pairs, points_ref, far, turned_places, dots, back_ref,
+    local_ref, sent_ref,
 ):
     elements = smoothed.shape[0] // 4
     peers = points_ref.shape[0] - 2 * FACE_ROWS
-    far = loaded(far_places(points_ref[...], elements), far_hot_ref)
     near = gather(rough, pairs)
     partners = pair_ref[...]
     partners = jnp.concatenate(halves(partners[1:2]) + halves(partners[0:1]), axis=0)
@@ -458,7 +472,7 @@
     incoming = get_rows(received_ref, count, 0, peers) + coarse[:split_at]
     values = [value + more for value, more in zip(swapped(near), joined(coarse[split_at:]))]
     values = values + joined(incoming)
-    summed = smoothed + scatter(smoothed.shape[0], pairs + far, values)
+    summed = smoothed + scatter(smoothed.shape[0], turned_places, values)
     back, energy = stiffness(summed, metric_ref, first_ref, inner_ref)
     energy = energy + rows_of(helmholtz_ref[...]) * smoothed * smoothed
     back_ref[...] = back
@@ -471,13 +485,12 @@
 
 
 def image_of(
-    field_ref, back_ref, local_ref, received_ref, helmholtz_ref, pair_ref, pair_hot_ref, points_ref,
-    far_hot_ref,
+    field_ref, back_ref, local_ref, received_ref, helmholtz_ref, pair_ref, points_ref, turned_ref,
 ):
     elements = field_ref.shape[0] // 4
     peers = points_ref.shape[0] - 2 * FACE_ROWS
-    chunks = loaded(pair_places(pair_ref, elements), pair_hot_ref)
-    chunks = chunks + loaded(far_places(points_ref[...], elements), far_hot_ref)
+    chunks = pair_places(pair_ref, elements) + far_places(points_ref[...], elements)
+    chunks = loaded_turned(chunks, turned_ref)
     values = cut(local_ref[...]) + joined(get_rows(received_ref, ROWS, 0, peers))
     summed = back_ref[...] + scatter(field_ref.shape[0], chunks, values)
     return summed + rows_of(helmholtz_ref[...]) * field_ref[...]
@@ -486,7 +499,7 @@
 def start_kernel(
     received_ref, fields_ref, points_ref, far_hot_ref, pair_ref, metric_ref, helmholtz_ref,
     first_ref, inner_ref,
-    smoothed_ref, maps_ref, far_points_ref, back_ref, local_ref, sent_ref, pair_hot_ref,
+    smoothed_ref, maps_ref, far_points_ref, back_ref, local_ref, sent_ref, pair_hot_ref, turned_ref,
 ):
     elements = helmholtz_ref.shape[0]
     peers = points_ref.shape[0] - 2 * FACE_ROWS
@@ -500,16 +513,18 @@
     maps_ref[...] = maps
     far_points = whole(get_rows(received_ref, FIRST_ROWS, TERMS + 2, peers))
     far_points_ref[...] = far_points
+    pairs = built(pair_places(pair_ref, elements), pair_hot_ref)
+    far = loaded(far_places(points_ref[...], elements), far_hot_ref)
     apply(
         rough, smoothed, FIRST_ROWS, received_ref, flat, maps, far_points, solved, metric_ref,
         helmholtz_ref, first_ref, inner_ref, pair_ref,
-        built(pair_places(pair_ref, elements), pair_hot_ref), points_ref, far_hot_ref,
+        pairs, points_ref, far, turned(pairs + far, turned_ref),
         [total_of(resid * smoothed)], back_ref, local_ref, sent_ref,
     )
 
 
 def middle_kernel(
-    received_ref, fields_ref, points_ref, far_hot_ref, pair_ref, pair_hot_ref, jacobi_ref, helmholtz_ref,
+    received_ref, fields_ref, points_ref, far_hot_ref, pair_ref, turned_ref, jacobi_ref, helmholtz_ref,
     inverse_ref, smoothed_ref, back_ref, local_ref,
     image_ref, resid_ref, scalars_ref, sent_ref,
 ):
@@ -521,7 +536,7 @@
     alpha = values[0] / values[1]
     image = image_of(
         smoothed_ref, back_ref, local_ref, received_ref, helmholtz_ref, pair_ref,
-        pair_hot_ref, points_ref, far_hot_ref,
+        points_ref, turned_ref,
     )
     image_ref[...] = image
     resid = fields_ref[0 : 4 * elements, :] - alpha * image
@@ -536,7 +551,7 @@
 
 
 def second_kernel(
-    received_ref, fields_ref, points_ref, far_hot_ref, pair_ref, pair_hot_ref, resid_ref, image_ref,
+    received_ref, fields_ref, points_ref, far_hot_ref, pair_ref, pair_hot_ref, turned_ref, resid_ref, image_ref,
     maps_ref, far_points_ref, jacobi_ref, metric_ref, helmholtz_ref, first_ref, inner_ref,
     smoothed_ref, back_ref, local_ref, sent_ref,
 ):
@@ -548,17 +563,19 @@
     rough = rows_of(jacobi_ref[...]) * resid
     smoothed = rough + prolonged(solved[0], flat, elements)
     smoothed_ref[...] = smoothed
+    pairs = loaded(pair_places(pair_ref, elements), pair_hot_ref)
+    far = loaded(far_places(points_ref[...], elements), far_hot_ref)
     apply(
         rough, smoothed, ROWS, received_ref, flat, maps_ref[...], far_points_ref[...], solved, metric_ref,
         helmholtz_ref, first_ref, inner_ref, pair_ref,
-        loaded(pair_places(pair_ref, elements), pair_hot_ref), points_ref, far_hot_ref,
+        pairs, points_ref, far, loaded_turned(pairs + far, turned_ref),
         [total_of(resid * smoothed), total_of(image_ref[...] * smoothed)],
         back_ref, local_ref, sent_ref,
     )
 
 
 def final_kernel(
-    received_ref, points_ref, far_hot_ref, pair_ref, pair_hot_ref, old_ref, field_ref, resid_ref, old_image_ref,
+    received_ref, points_ref, pair_ref, turned_ref, old_ref, field_ref, resid_ref, old_image_ref,
     scalars_ref, back_ref, local_ref, helmholtz_ref,
     solution_ref, residual_ref,
 ):
@@ -573,7 +590,7 @@
     solution_ref[...] = wide_of(alpha * old + step * direction)
     image = image_of(
         field_ref, back_ref, local_ref, received_ref, helmholtz_ref, pair_ref,
-        pair_hot_ref, points_ref, far_hot_ref,
+        points_ref, turned_ref,
     )
     image = image + beta * old_image_ref[...]
     residual_ref[...] = wide_of(resid_ref[...] - step * image)
@@ -622,6 +639,7 @@
 
     far_hot_shape = (points_shape[0] * LANES // 2, STEP)
     pair_hot_shape = (local[1] * LANES // STEP, STEP)
+    turned_shape = (local[1] + points_shape[0] * LANES, LANES)
 
     sent, fields, points, far_hot = call(
         first_kernel,
@@ -633,27 +651,27 @@
         ],
         right_side, jacobi, coarse_inverse, coarse_map, shared_slots, face_points, copied=True,
     )
-    smoothed, maps, far_points, back, near, sent, pair_hot = call(
+    smoothed, maps, far_points, back, near, sent, pair_hot, turned_hot = call(
         start_kernel,
         [field, (points_shape, jnp.int32), (points_shape, jnp.int32), field, local, sent_shape,
-         (pair_hot_shape, BF16)],
+         (pair_hot_shape, BF16), (turned_shape, BF16)],
         exchange(sent), fields, points, far_hot, pair_list, metric, helmholtz,
         t["first"], t["inner"],
     )
     image, resid, scalars, sent = call(
         middle_kernel, [field, field, (1, LANES), sent_shape],
-        exchange(sent), fields, points, far_hot, pair_list, pair_hot, jacobi, helmholtz, coarse_inverse,
+        exchange(sent), fields, points, far_hot, pair_list, turned_hot, jacobi, helmholtz, coarse_inverse,
         smoothed, back, near,
     )
     second, back, near, sent = call(
         second_kernel, [field, field, local, sent_shape],
-        exchange(sent), fields, points, far_hot, pair_list, pair_hot, resid, image, maps, far_points, jacobi,
+        exchange(sent), fields, points, far_hot, pair_list, pair_hot, turned_hot, resid, image, maps, far_points, jacobi,
         metric, helmholtz, t["first"], t["inner"],
     )
     return tuple(
         call(
             final_kernel, [right_side.shape, right_side.shape],
-            exchange(sent), points, far_hot, pair_list, pair_hot, smoothed, second, resid, image, scalars,
+            exchange(sent), points, pair_list, turned_hot, smoothed, second, resid, image, scalars,
             back, near, helmholtz,
         )
     )

time: 51.3 us -> 51.4 us (level)
  no operation moved by 1% of the time
where the time goes in v15:
time: 51.4 us; the launch traced here: 51.1 us
  blocking collectives  44 us (86%)
  Pallas kernels  6.29 us (12%)
  between operations  0.74 us (1%)
    all_to_all x4, blocking collectives, exchange(): lax.all_to_all(rows, ('grp', 'sub'), 0, 0, tiled=True).reshape(sent.shape)  44 us
    pallas_call x5, Pallas kernels, call(): pl.pallas_call(kernel, out_shape=[jax.ShapeDtypeStruct(*(out if isinstanc...  6.29 us

profile of v15, /device:TPU:0, one launch (start us, length us, event | category | flops | bytes accessed | tf_op | source)
XLA Modules:
  0.0 51.1 jit_solution(15461477744781696077)
XLA Ops:
  0.6 1.3 %shard_map.122 = (f32[320,128]{1,0:T(8,128)S(1)}, f32[136,128]{1,0:T(8,128)S(1)}, s32[16,128]{1,0:T(8,128)S(1)}, bf16[1024,256]{1,0:T(8,128)(2,1)S(1)}) custom-call(f32[16,512]{1,0:T(8,128)} %right_hbm.1, f32[16,512]{1,0:T(8,128)} %jacobi_ref.3, f32[1,64,64]{2,1,0:T(8,128)} %inverse_ref.1, s32[8,16]{1,0:T(8,128)} %map_hbm.1, s32[1,8,128]{2,1,0:T(8,128)} %slot_hbm.1, ...), custom_call_target="tpu_custom_call" | custom-call | tf_op jit(solution)/shard_map/pallas_call | solution.py:604
  1.9 0.0 copy-start
  1.9 0.0 copy-start.1
  1.9 0.0 copy-start.2
  2.0 0.0 copy-start.4
  2.0 0.0 copy-start.6
  2.0 15.7 %all_to_all.20 = f32[32,1,1280]{2,1,0:T(1,128)S(1)} all-to-all(f32[32,1,1280]{2,1,0:T(1,128)S(1)} %bitcast.12), channel_id=1, replica_groups=mesh['grp'=4,'sub'=8] {'grp','sub'}, dimensions={0} | all-to-all | bytes 327680 | tf_op jit(solution)/shard_map/all_to_all | solution.py:638
  17.7 0.0 copy-done
  17.7 0.0 copy-done.1
  17.7 0.0 copy-done.2
  17.7 0.0 copy-done.4
  17.7 0.0 copy-done.6
  17.7 1.7 %shard_map.123 = (f32[64,128]{1,0:T(8,128)S(1)}, s32[16,128]{1,0:T(8,128)S(1)}, s32[16,128]{1,0:T(8,128)S(1)}, f32[64,128]{1,0:T(8,128)S(1)}, f32[1,2048]{1,0:T(...) custom-call(f32[320,128]{1,0:T(8,128)S(1)} %bitcast.8, ...), custom_call_target="tpu_custom_call" | custom-call | tf_op jit(solution)/shard_map/pallas_call | solution.py:604
  19.4 0.0 copy-start.3
  19.4 0.0 copy-start.5
  19.4 9.7 %all_to_all.21 = f32[32,1,640]{2,1,0:T(1,128)S(1)} all-to-all(f32[32,1,640]{2,1,0:T(1,128)S(1)} %bitcast.14), channel_id=1, replica_groups=mesh['grp'=4,'sub'=8] {'grp','sub'}, dimensions={0} | all-to-all | bytes 163840 | tf_op jit(solution)/shard_map/all_to_all | solution.py:638
  29.2 0.0 copy-done.3
  29.2 0.0 copy-done.5
  29.2 0.7 %shard_map.124 = (f32[64,128]{1,0:T(8,128)S(1)}, f32[64,128]{1,0:T(8,128)S(1)}, f32[1,128]{1,0:T(1,128)S(1)}, f32[160,128]{1,0:T(8,128)S(1)}) custom-call(f32[160,128]{1,0:T(8,128)S(1)} %bitcast.11, f32[136,128]{1,0:T(8,128)S(1)} %get-tuple-element.23.fields_ref, s32[16,128]{1,0:T(8,128)S(1)} %get-tuple-element.24.points_ref, ...), custom_call_target="tpu_custom_call" | custom-call | tf_op jit(solution)/shard_map/pallas_call | solution.py:604
  29.9 9.3 %all_to_all.22 = f32[32,1,640]{2,1,0:T(1,128)S(1)} all-to-all(f32[32,1,640]{2,1,0:T(1,128)S(1)} %bitcast.15), channel_id=1, replica_groups=mesh['grp'=4,'sub'=8] {'grp','sub'}, dimensions={0} | all-to-all | bytes 163840 | tf_op jit(solution)/shard_map/all_to_all | solution.py:638
  39.2 1.5 %shard_map.125 = (f32[64,128]{1,0:T(8,128)S(1)}, f32[64,128]{1,0:T(8,128)S(1)}, f32[1,2048]{1,0:T(1,128)S(1)}, f32[160,128]{1,0:T(8,128)S(1)}) custom-call(f32[160,128]{1,0:T(8,128)S(1)} %bitcast.10, f32[136,128]{1,0:T(8,128)S(1)} %get-tuple-element.23.fields_ref, s32[16,128]{1,0:T(8,128)S(1)} %get-tuple-element.24.points_ref, ...), custom_call_target="tpu_custom_call" | custom-call | tf_op jit(solution)/shard_map/pallas_call | solution.py:604
  40.7 9.3 %all_to_all.23 = f32[32,1,640]{2,1,0:T(1,128)S(1)} all-to-all(f32[32,1,640]{2,1,0:T(1,128)S(1)} %bitcast.13), channel_id=1, replica_groups=mesh['grp'=4,'sub'=8] {'grp','sub'}, dimensions={0} | all-to-all | bytes 163840 | tf_op jit(solution)/shard_map/all_to_all | solution.py:638
  50.0 1.1 %shard_map.126 = (f32[16,512]{1,0:T(8,128)}, f32[16,512]{1,0:T(8,128)}) custom-call(f32[160,128]{1,0:T(8,128)S(1)} %bitcast.9, s32[16,128]{1,0:T(8,128)S(1)} %get-tuple-element.24.points_ref, s32[2,1024]{1,0:T(2,128)S(1)} %copy-done.4, bf16[4096,128]{1,0:T(8,128)(2,1)S(1)} %get-tuple-element.27.turned_ref, ...), custom_call_target="tpu_custom_call" | custom-call | tf_op jit(solution)/shard_map/pallas_call | solution.py:604
Async XLA Ops:
  1.9 15.7 %copy-start = (bf16[256,256]{1,0:T(8,128)(2,1)S(1)}, bf16[256,256]{1,0:T(8,128)(2,1)}, u32[]{:S(2)}) copy-start(bf16[256,256]{1,0:T(8,128)(2,1)} %constant.4.clone.inner_ref) | copy-start | bytes 393220
  1.9 15.7 %copy-start.1 = (f32[16,512]{1,0:T(8,128)S(1)}, f32[16,512]{1,0:T(8,128)}, u32[]{:S(2)}) copy-start(f32[16,512]{1,0:T(8,128)} %helmholtz_ref.7) | copy-start | bytes 98308
  1.9 15.7 %copy-start.2 = (f32[16,1536]{1,0:T(8,128)S(1)}, f32[16,1536]{1,0:T(8,128)}, u32[]{:S(2)}) copy-start(f32[16,1536]{1,0:T(8,128)} %metric_ref.3) | copy-start | bytes 294916
  2.0 15.7 %copy-start.4 = (s32[2,1024]{1,0:T(2,128)S(1)}, s32[2,1024]{1,0:T(2,128)}, u32[]{:S(2)}) copy-start(s32[2,1024]{1,0:T(2,128)} %pair_ref.7) | copy-start | bytes 24580
  2.0 15.7 %copy-start.6 = (f32[64,128]{1,0:T(8,128)S(1)}, f32[64,128]{1,0:T(8,128)}, u32[]{:S(2)}) copy-start(f32[64,128]{1,0:T(8,128)} %constant.5.clone.first_ref) | copy-start | bytes 98308
  19.4 9.8 %copy-start.3 = (f32[16,512]{1,0:T(8,128)S(1)}, f32[16,512]{1,0:T(8,128)}, u32[]{:S(2)}) copy-start(f32[16,512]{1,0:T(8,128)} %jacobi_ref.3) | copy-start | bytes 98308
  19.4 9.7 %copy-start.5 = (f32[1,64,64]{2,1,0:T(8,128)S(1)}, f32[1,64,64]{2,1,0:T(8,128)}, u32[]{:S(2)}) copy-start(f32[1,64,64]{2,1,0:T(8,128)} %inverse_ref.1) | copy-start | bytes 49156

commit v16 on v13

--- a/solution.py
+++ b/solution.py
@@ -196,24 +196,27 @@
     return received_ref[pl.ds(at, received_ref.shape[0] // count, count), :]
 
 
-def get_shared(rows, peers):
-    mine = jnp.where(own_group(rows.shape[0], peers), rows, 0.0)
-    shared = mine[:peers]
-    for g in range(1, rows.shape[0] // peers):
-        shared = shared + mine[g * peers : (g + 1) * peers]
-    return shared
-
-
-def get_row(rows, peers, away):
-    here = lax.axis_index("grp") * peers + lax.axis_index("sub")
-    source = lax.broadcasted_iota(jnp.int32, rows.shape, 0) - here == away * peers
-    return jnp.sum(jnp.where(source, rows, 0.0), axis=0, keepdims=True)
+def inside(received_ref, count, peers, away):
+    groups = received_ref.shape[0] // (count * peers)
+    group = lax.axis_index("grp") + away
+    kept = jnp.clip(group, 0, groups - 1)
+    return kept, jnp.where(group == kept, 1.0, 0.0)
+
+
+def get_group(received_ref, count, at, peers, away=0):
+    group, kept = inside(received_ref, count, peers, away)
+    return received_ref[pl.ds(group * (peers * count) + at, peers, count), :] * kept
+
+
+def get_side(received_ref, count, at, rows, peers, away):
+    group, kept = inside(received_ref, count, peers, away)
+    place = group * peers + lax.axis_index("sub")
+    return received_ref[pl.ds(place * count + at, rows), :] * kept
 
 
 def get_rows(received_ref, count, at, peers):
-    rows = [get(received_ref, count, at + r) for r in range(FACE_ROWS)]
-    faces = [get_row(part, peers, away) for away in (-1, 1) for part in rows]
-    return jnp.concatenate([get_shared(rows[0], peers)] + faces, axis=0)
+    sides = [get_side(received_ref, count, at, FACE_ROWS, peers, away) for away in (-1, 1)]
+    return jnp.concatenate([get_group(received_ref, count, at, peers)] + sides, axis=0)
 
 
 def swapped(values):
@@ -336,9 +339,8 @@
 
 
 def get_solved(received_ref, count, peers):
-    rows = get(received_ref, count, TERMS)
     return [
-        jnp.sum(jnp.where(own_group(rows.shape[0], peers, away), rows, 0.0), axis=0, keepdims=True)
+        jnp.sum(get_group(received_ref, count, TERMS, peers, away), axis=0, keepdims=True)
         for away in (0, -1, 1)
     ]
 
@@ -403,14 +405,18 @@
         copy = pltpu.make_async_copy(source, target, sems.at[k])
         copy.start()
         copies.append(copy)
-    for copy in copies:
-        copy.wait()
     elements = right_ref.shape[0]
     peers = slot_ref.shape[1]
+    for copy in copies[:2]:
+        copy.wait()
     faces = face_ref[...]
     faces = jnp.concatenate(halves(faces[0:1]) + halves(faces[1:2]), axis=0)
     points = jnp.concatenate([slot_ref[0], faces], axis=0)
     points_ref[...] = points
+    places = built(far_places(points, elements), far_hot_ref)
+    send_rows(sent_ref, FIRST_ROWS, TERMS + 2, points.astype(F32), peers)
+    for copy in copies[2:]:
+        copy.wait()
     resid = rows_of(right_ref[...])
     flat = flat_map(map_ref[...])
     smoothed = rows_of(jacobi_ref[...]) * resid
@@ -418,19 +424,21 @@
     fields_ref[4 * elements : 8 * elements, :] = smoothed
     fields_ref[8 * elements :, :] = jnp.broadcast_to(flat, (8, LANES))
     part = coarse_part(resid, one_vertex(flat), inverse_ref[0])
-    values = gather(smoothed, built(far_places(points, elements), far_hot_ref))
+    values = gather(smoothed, places)
     send_values(sent_ref, FIRST_ROWS, values, peers)
     send_same(sent_ref, FIRST_ROWS, TERMS, part)
     send_same(sent_ref, FIRST_ROWS, TERMS + 1, flat)
-    send_rows(sent_ref, FIRST_ROWS, TERMS + 2, points.astype(F32), peers)
 
 
 def far_maps(received_ref, peers):
-    maps = get(received_ref, FIRST_ROWS, TERMS + 1)
+    own = get_group(received_ref, FIRST_ROWS, TERMS + 1, peers)
     sides = [
-        jnp.broadcast_to(get_row(maps, peers, away), (FACE_ROWS, LANES)) for away in (-1, 1)
-    ]
-    return whole(jnp.concatenate([get_shared(maps, peers)] + sides, axis=0))
+        jnp.broadcast_to(
+            get_side(received_ref, FIRST_ROWS, TERMS + 1, 1, peers, away), (FACE_ROWS, LANES)
+        )
+        for away in (-1, 1)
+    ]
+    return whole(jnp.concatenate([own] + sides, axis=0))
 
 
 def apply(

time: 51.3 us -> 51.1 us (level)
  no operation moved by 1% of the time
where the time goes in v16:
time: 51.1 us; the launch traced here: 50.8 us
  blocking collectives  44 us (86%)
  Pallas kernels  6 us (12%)
  between operations  0.74 us (1%)
    all_to_all x4, blocking collectives, exchange(): lax.all_to_all(rows, ('grp', 'sub'), 0, 0, tiled=True).reshape(sent.shape)  44 us
    pallas_call x5, Pallas kernels, call(): pl.pallas_call(kernel, out_shape=[jax.ShapeDtypeStruct(*(out if isinstanc...  6 us

profile of v16, /device:TPU:0, one launch (start us, length us, event | category | flops | bytes accessed | tf_op | source)
XLA Modules:
  0.0 50.8 jit_solution(10715359931090619337)
XLA Ops:
  0.6 1.2 %shard_map.122 = (f32[320,128]{1,0:T(8,128)S(1)}, f32[136,128]{1,0:T(8,128)S(1)}, s32[16,128]{1,0:T(8,128)S(1)}, bf16[1024,256]{1,0:T(8,128)(2,1)S(1)}) custom-call(f32[16,512]{1,0:T(8,128)} %right_hbm.1, f32[16,512]{1,0:T(8,128)} %jacobi_ref.3, f32[1,64,64]{2,1,0:T(8,128)} %inverse_ref.1, s32[8,16]{1,0:T(8,128)} %map_hbm.1, s32[1,8,128]{2,1,0:T(8,128)} %slot_hbm.1, ...), custom_call_target="tpu_custom_call" | custom-call | tf_op jit(solution)/shard_map/pallas_call | solution.py:595
  1.9 0.0 copy-start
  1.9 0.0 copy-start.1
  1.9 0.0 copy-start.2
  1.9 0.0 copy-start.4
  1.9 0.0 copy-start.6
  1.9 15.7 %all_to_all.20 = f32[32,1,1280]{2,1,0:T(1,128)S(1)} all-to-all(f32[32,1,1280]{2,1,0:T(1,128)S(1)} %bitcast.12), channel_id=1, replica_groups=mesh['grp'=4,'sub'=8] {'grp','sub'}, dimensions={0} | all-to-all | bytes 327680 | tf_op jit(solution)/shard_map/all_to_all | solution.py:629
  17.6 0.0 copy-done
  17.6 0.0 copy-done.1
  17.6 0.0 copy-done.2
  17.6 0.0 copy-done.4
  17.6 0.0 copy-done.6
  17.6 1.5 %shard_map.123 = (f32[64,128]{1,0:T(8,128)S(1)}, s32[16,128]{1,0:T(8,128)S(1)}, s32[16,128]{1,0:T(8,128)S(1)}, f32[64,128]{1,0:T(8,128)S(1)}, f32[1,2048]{1,0:T(...) custom-call(f32[320,128]{1,0:T(8,128)S(1)} %bitcast.8, f32[136,128]{1,0:T(8,128)S(1)} %get-tuple-element.22.fields_ref, ...), custom_call_target="tpu_custom_call" | custom-call | tf_op jit(solution)/shard_map/pallas_call | solution.py:595
  19.1 0.0 copy-start.3
  19.2 0.0 copy-start.5
  19.2 9.7 %all_to_all.21 = f32[32,1,640]{2,1,0:T(1,128)S(1)} all-to-all(f32[32,1,640]{2,1,0:T(1,128)S(1)} %bitcast.14), channel_id=1, replica_groups=mesh['grp'=4,'sub'=8] {'grp','sub'}, dimensions={0} | all-to-all | bytes 163840 | tf_op jit(solution)/shard_map/all_to_all | solution.py:629
  28.9 0.0 copy-done.3
  28.9 0.0 copy-done.5
  28.9 0.7 %shard_map.124 = (f32[64,128]{1,0:T(8,128)S(1)}, f32[64,128]{1,0:T(8,128)S(1)}, f32[1,128]{1,0:T(1,128)S(1)}, f32[160,128]{1,0:T(8,128)S(1)}) custom-call(f32[160,128]{1,0:T(8,128)S(1)} %bitcast.11, f32[136,128]{1,0:T(8,128)S(1)} %get-tuple-element.22.fields_ref, s32[16,128]{1,0:T(8,128)S(1)} %get-tuple-element.23.points_ref, ...), custom_call_target="tpu_custom_call" | custom-call | tf_op jit(solution)/shard_map/pallas_call | solution.py:595
  29.6 9.3 %all_to_all.22 = f32[32,1,640]{2,1,0:T(1,128)S(1)} all-to-all(f32[32,1,640]{2,1,0:T(1,128)S(1)} %bitcast.15), channel_id=1, replica_groups=mesh['grp'=4,'sub'=8] {'grp','sub'}, dimensions={0} | all-to-all | bytes 163840 | tf_op jit(solution)/shard_map/all_to_all | solution.py:629
  38.9 1.5 %shard_map.125 = (f32[64,128]{1,0:T(8,128)S(1)}, f32[64,128]{1,0:T(8,128)S(1)}, f32[1,2048]{1,0:T(1,128)S(1)}, f32[160,128]{1,0:T(8,128)S(1)}) custom-call(f32[160,128]{1,0:T(8,128)S(1)} %bitcast.10, f32[136,128]{1,0:T(8,128)S(1)} %get-tuple-element.22.fields_ref, s32[16,128]{1,0:T(8,128)S(1)} %get-tuple-element.23.points_ref, ...), custom_call_target="tpu_custom_call" | custom-call | tf_op jit(solution)/shard_map/pallas_call | solution.py:595
  40.4 9.3 %all_to_all.23 = f32[32,1,640]{2,1,0:T(1,128)S(1)} all-to-all(f32[32,1,640]{2,1,0:T(1,128)S(1)} %bitcast.13), channel_id=1, replica_groups=mesh['grp'=4,'sub'=8] {'grp','sub'}, dimensions={0} | all-to-all | bytes 163840 | tf_op jit(solution)/shard_map/all_to_all | solution.py:629
  49.7 1.1 %shard_map.126 = (f32[16,512]{1,0:T(8,128)}, f32[16,512]{1,0:T(8,128)}) custom-call(f32[160,128]{1,0:T(8,128)S(1)} %bitcast.9, s32[16,128]{1,0:T(8,128)S(1)} %get-tuple-element.23.points_ref, bf16[1024,256]{1,0:T(8,128)(2,1)S(1)} %get-tuple-element.24.far_hot_ref, s32[2,1024]{1,0:T(2,128)S(1)} %copy-done.4, ...), custom_call_target="tpu_custom_call" | custom-call | tf_op jit(solution)/shard_map/pallas_call | solution.py:595
Async XLA Ops:
  1.9 15.7 %copy-start = (f32[16,512]{1,0:T(8,128)S(1)}, f32[16,512]{1,0:T(8,128)}, u32[]{:S(2)}) copy-start(f32[16,512]{1,0:T(8,128)} %helmholtz_ref.7) | copy-start | bytes 98308
  1.9 15.7 %copy-start.1 = (bf16[256,256]{1,0:T(8,128)(2,1)S(1)}, bf16[256,256]{1,0:T(8,128)(2,1)}, u32[]{:S(2)}) copy-start(bf16[256,256]{1,0:T(8,128)(2,1)} %constant.4.clone.inner_ref) | copy-start | bytes 393220
  1.9 15.7 %copy-start.2 = (f32[16,1536]{1,0:T(8,128)S(1)}, f32[16,1536]{1,0:T(8,128)}, u32[]{:S(2)}) copy-start(f32[16,1536]{1,0:T(8,128)} %metric_ref.3) | copy-start | bytes 294916
  1.9 15.7 %copy-start.4 = (s32[2,1024]{1,0:T(2,128)S(1)}, s32[2,1024]{1,0:T(2,128)}, u32[]{:S(2)}) copy-start(s32[2,1024]{1,0:T(2,128)} %pair_ref.7) | copy-start | bytes 24580
  1.9 15.7 %copy-start.6 = (f32[64,128]{1,0:T(8,128)S(1)}, f32[64,128]{1,0:T(8,128)}, u32[]{:S(2)}) copy-start(f32[64,128]{1,0:T(8,128)} %constant.5.clone.first_ref) | copy-start | bytes 98308
  19.1 9.8 %copy-start.3 = (f32[16,512]{1,0:T(8,128)S(1)}, f32[16,512]{1,0:T(8,128)}, u32[]{:S(2)}) copy-start(f32[16,512]{1,0:T(8,128)} %jacobi_ref.3) | copy-start | bytes 98308
  19.2 9.8 %copy-start.5 = (f32[1,64,64]{2,1,0:T(8,128)S(1)}, f32[1,64,64]{2,1,0:T(8,128)}, u32[]{:S(2)}) copy-start(f32[1,64,64]{2,1,0:T(8,128)} %inverse_ref.1) | copy-start | bytes 49156

commit v17 on v16

--- a/solution.py
+++ b/solution.py
@@ -164,43 +164,37 @@
     return [wide[:, at : at + LANES] for at in range(0, wide.shape[1], LANES)]
 
 
-def own_group(devices, peers, away=0):
-    shape = (devices, LANES)
-    return lax.broadcasted_iota(jnp.int32, shape, 0) // peers - lax.axis_index("grp") == away
-
-
-def send_rows(sent_ref, count, at, rows, peers):
-    devices = sent_ref.shape[0] // count
-    above = own_group(devices, peers, 1)
-    shared = jnp.concatenate([rows[:peers]] * (devices // peers), axis=0)
-    for r in range(FACE_ROWS):
-        down = rows[peers + r : peers + r + 1]
-        up = rows[peers + FACE_ROWS + r : peers + FACE_ROWS + r + 1]
-        out = jnp.where(above, up, down)
-        if r == 0:
-            out = jnp.where(own_group(devices, peers), shared, out)
-        sent_ref[pl.ds(at + r, devices, count), :] = out
-
-
-def send_same(sent_ref, count, at, row):
-    devices = sent_ref.shape[0] // count
-    sent_ref[pl.ds(at, devices, count), :] = jnp.broadcast_to(row, (devices, LANES))
-
-
-def send_values(sent_ref, count, values, peers):
-    rows = jnp.concatenate([row for pair in values for row in halves(pair)], axis=0)
-    send_rows(sent_ref, count, 0, rows, peers)
-
-
-def get(received_ref, count, at):
-    return received_ref[pl.ds(at, received_ref.shape[0] // count, count), :]
-
-
 def inside(received_ref, count, peers, away):
     groups = received_ref.shape[0] // (count * peers)
     group = lax.axis_index("grp") + away
     kept = jnp.clip(group, 0, groups - 1)
     return kept, jnp.where(group == kept, 1.0, 0.0)
+
+
+def send_rows(sent_ref, count, at, rows, peers):
+    group = lax.axis_index("grp")
+    for b in range(peers):
+        sent_ref[pl.ds((group * peers + b) * count + at, 1), :] = rows[b : b + 1]
+    for side, away in enumerate((-1, 1)):
+        kept, _ = inside(sent_ref, count, peers, away)
+        place = kept * peers + lax.axis_index("sub")
+        for r in range(FACE_ROWS):
+            k = peers + side * FACE_ROWS + r
+            sent_ref[pl.ds(place * count + at + r, 1), :] = rows[k : k + 1]
+
+
+def send_same(sent_ref, count, at, row):
+    devices = sent_ref.shape[0] // count
+    sent_ref[pl.ds(at, devices, count), :] = jnp.broadcast_to(row, (devices, LANES))
+
+
+def send_values(sent_ref, count, values, peers):
+    rows = jnp.concatenate([row for pair in values for row in halves(pair)], axis=0)
+    send_rows(sent_ref, count, 0, rows, peers)
+
+
+def get(received_ref, count, at):
+    return received_ref[pl.ds(at, received_ref.shape[0] // count, count), :]
 
 
 def get_group(received_ref, count, at, peers, away=0):

time: 51.1 us -> 51.1 us (level)
  no operation moved by 1% of the time
where the time goes in v17:
time: 51.1 us; the launch traced here: 50.8 us
  blocking collectives  44 us (86%)
  Pallas kernels  5.98 us (12%)
  between operations  0.74 us (1%)
    all_to_all x4, blocking collectives, exchange(): lax.all_to_all(rows, ('grp', 'sub'), 0, 0, tiled=True).reshape(sent.shape)  44 us
    pallas_call x5, Pallas kernels, call(): pl.pallas_call(kernel, out_shape=[jax.ShapeDtypeStruct(*(out if isinstanc...  5.98 us

profile of v17, /device:TPU:0, one launch (start us, length us, event | category | flops | bytes accessed | tf_op | source)
XLA Modules:
  0.0 50.8 jit_solution(9246997637012950943)
XLA Ops:
  0.6 1.2 %shard_map.122 = (f32[320,128]{1,0:T(8,128)S(1)}, f32[136,128]{1,0:T(8,128)S(1)}, s32[16,128]{1,0:T(8,128)S(1)}, bf16[1024,256]{1,0:T(8,128)(2,1)S(1)}) custom-call(f32[16,512]{1,0:T(8,128)} %right_hbm.1, f32[16,512]{1,0:T(8,128)} %jacobi_ref.3, f32[1,64,64]{2,1,0:T(8,128)} %inverse_ref.1, s32[8,16]{1,0:T(8,128)} %map_hbm.1, s32[1,8,128]{2,1,0:T(8,128)} %slot_hbm.1, ...), custom_call_target="tpu_custom_call" | custom-call | tf_op jit(solution)/shard_map/pallas_call | solution.py:589
  1.9 0.0 copy-start
  1.9 0.0 copy-start.1
  1.9 0.0 copy-start.2
  1.9 0.0 copy-start.4
  1.9 0.0 copy-start.6
  1.9 15.7 %all_to_all.20 = f32[32,1,1280]{2,1,0:T(1,128)S(1)} all-to-all(f32[32,1,1280]{2,1,0:T(1,128)S(1)} %bitcast.12), channel_id=1, replica_groups=mesh['grp'=4,'sub'=8] {'grp','sub'}, dimensions={0} | all-to-all | bytes 327680 | tf_op jit(solution)/shard_map/all_to_all | solution.py:623
  17.6 0.0 copy-done
  17.6 0.0 copy-done.1
  17.6 0.0 copy-done.2
  17.6 0.0 copy-done.4
  17.6 0.0 copy-done.6
  17.6 1.5 %shard_map.123 = (f32[64,128]{1,0:T(8,128)S(1)}, s32[16,128]{1,0:T(8,128)S(1)}, s32[16,128]{1,0:T(8,128)S(1)}, f32[64,128]{1,0:T(8,128)S(1)}, f32[1,2048]{1,0:T(...) custom-call(f32[320,128]{1,0:T(8,128)S(1)} %bitcast.8, f32[136,128]{1,0:T(8,128)S(1)} %get-tuple-element.22.fields_ref, ...), custom_call_target="tpu_custom_call" | custom-call | tf_op jit(solution)/shard_map/pallas_call | solution.py:589
  19.1 0.0 copy-start.3
  19.2 0.0 copy-start.5
  19.2 9.7 %all_to_all.21 = f32[32,1,640]{2,1,0:T(1,128)S(1)} all-to-all(f32[32,1,640]{2,1,0:T(1,128)S(1)} %bitcast.14), channel_id=1, replica_groups=mesh['grp'=4,'sub'=8] {'grp','sub'}, dimensions={0} | all-to-all | bytes 163840 | tf_op jit(solution)/shard_map/all_to_all | solution.py:623
  28.9 0.0 copy-done.3
  28.9 0.0 copy-done.5
  28.9 0.7 %shard_map.124 = (f32[64,128]{1,0:T(8,128)S(1)}, f32[64,128]{1,0:T(8,128)S(1)}, f32[1,128]{1,0:T(1,128)S(1)}, f32[160,128]{1,0:T(8,128)S(1)}) custom-call(f32[160,128]{1,0:T(8,128)S(1)} %bitcast.11, f32[136,128]{1,0:T(8,128)S(1)} %get-tuple-element.22.fields_ref, s32[16,128]{1,0:T(8,128)S(1)} %get-tuple-element.23.points_ref, ...), custom_call_target="tpu_custom_call" | custom-call | tf_op jit(solution)/shard_map/pallas_call | solution.py:589
  29.6 9.3 %all_to_all.22 = f32[32,1,640]{2,1,0:T(1,128)S(1)} all-to-all(f32[32,1,640]{2,1,0:T(1,128)S(1)} %bitcast.15), channel_id=1, replica_groups=mesh['grp'=4,'sub'=8] {'grp','sub'}, dimensions={0} | all-to-all | bytes 163840 | tf_op jit(solution)/shard_map/all_to_all | solution.py:623
  38.9 1.5 %shard_map.125 = (f32[64,128]{1,0:T(8,128)S(1)}, f32[64,128]{1,0:T(8,128)S(1)}, f32[1,2048]{1,0:T(1,128)S(1)}, f32[160,128]{1,0:T(8,128)S(1)}) custom-call(f32[160,128]{1,0:T(8,128)S(1)} %bitcast.10, f32[136,128]{1,0:T(8,128)S(1)} %get-tuple-element.22.fields_ref, s32[16,128]{1,0:T(8,128)S(1)} %get-tuple-element.23.points_ref, ...), custom_call_target="tpu_custom_call" | custom-call | tf_op jit(solution)/shard_map/pallas_call | solution.py:589
  40.4 9.3 %all_to_all.23 = f32[32,1,640]{2,1,0:T(1,128)S(1)} all-to-all(f32[32,1,640]{2,1,0:T(1,128)S(1)} %bitcast.13), channel_id=1, replica_groups=mesh['grp'=4,'sub'=8] {'grp','sub'}, dimensions={0} | all-to-all | bytes 163840 | tf_op jit(solution)/shard_map/all_to_all | solution.py:623
  49.7 1.1 %shard_map.126 = (f32[16,512]{1,0:T(8,128)}, f32[16,512]{1,0:T(8,128)}) custom-call(f32[160,128]{1,0:T(8,128)S(1)} %bitcast.9, s32[16,128]{1,0:T(8,128)S(1)} %get-tuple-element.23.points_ref, bf16[1024,256]{1,0:T(8,128)(2,1)S(1)} %get-tuple-element.24.far_hot_ref, s32[2,1024]{1,0:T(2,128)S(1)} %copy-done.4, ...), custom_call_target="tpu_custom_call" | custom-call | tf_op jit(solution)/shard_map/pallas_call | solution.py:589
Async XLA Ops:
  1.9 15.7 %copy-start = (f32[16,512]{1,0:T(8,128)S(1)}, f32[16,512]{1,0:T(8,128)}, u32[]{:S(2)}) copy-start(f32[16,512]{1,0:T(8,128)} %helmholtz_ref.7) | copy-start | bytes 98308
  1.9 15.7 %copy-start.1 = (bf16[256,256]{1,0:T(8,128)(2,1)S(1)}, bf16[256,256]{1,0:T(8,128)(2,1)}, u32[]{:S(2)}) copy-start(bf16[256,256]{1,0:T(8,128)(2,1)} %constant.4.clone.inner_ref) | copy-start | bytes 393220
  1.9 15.7 %copy-start.2 = (f32[16,1536]{1,0:T(8,128)S(1)}, f32[16,1536]{1,0:T(8,128)}, u32[]{:S(2)}) copy-start(f32[16,1536]{1,0:T(8,128)} %metric_ref.3) | copy-start | bytes 294916
  1.9 15.7 %copy-start.4 = (s32[2,1024]{1,0:T(2,128)S(1)}, s32[2,1024]{1,0:T(2,128)}, u32[]{:S(2)}) copy-start(s32[2,1024]{1,0:T(2,128)} %pair_ref.7) | copy-start | bytes 24580
  1.9 15.7 %copy-start.6 = (f32[64,128]{1,0:T(8,128)S(1)}, f32[64,128]{1,0:T(8,128)}, u32[]{:S(2)}) copy-start(f32[64,128]{1,0:T(8,128)} %constant.5.clone.first_ref) | copy-start | bytes 98308
  19.1 9.8 %copy-start.3 = (f32[16,512]{1,0:T(8,128)S(1)}, f32[16,512]{1,0:T(8,128)}, u32[]{:S(2)}) copy-start(f32[16,512]{1,0:T(8,128)} %jacobi_ref.3) | copy-start | bytes 98308
  19.2 9.7 %copy-start.5 = (f32[1,64,64]{2,1,0:T(8,128)S(1)}, f32[1,64,64]{2,1,0:T(8,128)}, u32[]{:S(2)}) copy-start(f32[1,64,64]{2,1,0:T(8,128)} %inverse_ref.1) | copy-start | bytes 49156

commit v18 on v16

--- a/solution.py
+++ b/solution.py
@@ -388,7 +388,7 @@
 
 def first_kernel(
     right_hbm, jacobi_hbm, inverse_hbm, map_hbm, slot_hbm, face_hbm,
-    sent_ref, fields_ref, points_ref, far_hot_ref,
+    sent_ref, fields_ref, points_ref, far_hot_ref, smoother_ref, solver_ref,
     right_ref, jacobi_ref, inverse_ref, map_ref, slot_ref, face_ref, sems,
 ):
     copies = []
@@ -419,7 +419,10 @@
         copy.wait()
     resid = rows_of(right_ref[...])
     flat = flat_map(map_ref[...])
-    smoothed = rows_of(jacobi_ref[...]) * resid
+    smoother = rows_of(jacobi_ref[...])
+    smoother_ref[...] = smoother
+    solver_ref[...] = inverse_ref[0]
+    smoothed = smoother * resid
     fields_ref[0 : 4 * elements, :] = resid
     fields_ref[4 * elements : 8 * elements, :] = smoothed
     fields_ref[8 * elements :, :] = jnp.broadcast_to(flat, (8, LANES))
@@ -517,8 +520,8 @@
 
 
 def middle_kernel(
-    received_ref, fields_ref, points_ref, far_hot_ref, pair_ref, pair_hot_ref, jacobi_ref, helmholtz_ref,
-    inverse_ref, smoothed_ref, back_ref, local_ref,
+    received_ref, fields_ref, points_ref, far_hot_ref, pair_ref, pair_hot_ref, smoother_ref, helmholtz_ref,
+    solver_ref, smoothed_ref, back_ref, local_ref,
     image_ref, resid_ref, scalars_ref, sent_ref,
 ):
     elements = helmholtz_ref.shape[0]
@@ -535,9 +538,9 @@
     resid = fields_ref[0 : 4 * elements, :] - alpha * image
     resid_ref[...] = resid
     vertices = one_vertex(fields_ref[8 * elements : 8 * elements + 1, :])
-    part = coarse_part(resid, vertices, inverse_ref[0])
+    part = coarse_part(resid, vertices, solver_ref[...])
     values = gather(
-        rows_of(jacobi_ref[...]) * resid, loaded(far_places(points_ref[...], elements), far_hot_ref),
+        smoother_ref[...] * resid, loaded(far_places(points_ref[...], elements), far_hot_ref),
     )
     send_values(sent_ref, ROWS, values, peers)
     send_same(sent_ref, ROWS, TERMS, part)
@@ -545,7 +548,7 @@
 
 def second_kernel(
     received_ref, fields_ref, points_ref, far_hot_ref, pair_ref, pair_hot_ref, resid_ref, image_ref,
-    maps_ref, far_points_ref, jacobi_ref, metric_ref, helmholtz_ref, first_ref, inner_ref,
+    maps_ref, far_points_ref, smoother_ref, metric_ref, helmholtz_ref, first_ref, inner_ref,
     smoothed_ref, back_ref, local_ref, sent_ref,
 ):
     elements = helmholtz_ref.shape[0]
@@ -553,7 +556,7 @@
     solved = get_solved(received_ref, ROWS, peers)
     resid = resid_ref[...]
     flat = whole(fields_ref[8 * elements : 8 * elements + 1, :])
-    rough = rows_of(jacobi_ref[...]) * resid
+    rough = smoother_ref[...] * resid
     smoothed = rough + prolonged(solved[0], flat, elements)
     smoothed_ref[...] = smoothed
     apply(
@@ -631,13 +634,15 @@
     far_hot_shape = (points_shape[0] * LANES // 2, STEP)
     pair_hot_shape = (local[1] * LANES // STEP, STEP)
 
-    sent, fields, points, far_hot = call(
+    sent, fields, points, far_hot, smoother, solver = call(
         first_kernel,
         [
             (groups * peers * FIRST_ROWS, LANES),
             (8 * elements + 8, LANES),
             (points_shape, jnp.int32),
             (far_hot_shape, BF16),
+            field,
+            (NC, NC),
         ],
         right_side, jacobi, coarse_inverse, coarse_map, shared_slots, face_points, copied=True,
     )
@@ -650,12 +655,12 @@
     )
     image, resid, scalars, sent = call(
         middle_kernel, [field, field, (1, LANES), sent_shape],
-        exchange(sent), fields, points, far_hot, pair_list, pair_hot, jacobi, helmholtz, coarse_inverse,
+        exchange(sent), fields, points, far_hot, pair_list, pair_hot, smoother, helmholtz, solver,
         smoothed, back, near,
     )
     second, back, near, sent = call(
         second_kernel, [field, field, local, sent_shape],
-        exchange(sent), fields, points, far_hot, pair_list, pair_hot, resid, image, maps, far_points, jacobi,
+        exchange(sent), fields, points, far_hot, pair_list, pair_hot, resid, image, maps, far_points, smoother,
         metric, helmholtz, t["first"], t["inner"],
     )
     return tuple(

time: 51.1 us -> 51 us (level)
  no operation moved by 1% of the time
where the time goes in v18:
time: 51 us; the launch traced here: 50.8 us
  blocking collectives  44 us (86%)
  Pallas kernels  6 us (12%)
  between operations  0.72 us (1%)
    all_to_all x4, blocking collectives, exchange(): lax.all_to_all(rows, ('grp', 'sub'), 0, 0, tiled=True).reshape(sent.shape)  44 us
    pallas_call x5, Pallas kernels, call(): pl.pallas_call(kernel, out_shape=[jax.ShapeDtypeStruct(*(out if isinstanc...  6 us

profile of v18, /device:TPU:0, one launch (start us, length us, event | category | flops | bytes accessed | tf_op | source)
XLA Modules:
  0.0 50.8 jit_solution(18041252253377809809)
XLA Ops:
  0.6 1.2 %shard_map.122 = (f32[320,128]{1,0:T(8,128)S(1)}, f32[136,128]{1,0:T(8,128)S(1)}, s32[16,128]{1,0:T(8,128)S(1)}, bf16[1024,256]{1,0:T(8,128)(2,1)S(1)}, f32[64,128]{1,0:T(8,128)S(1)}, /*index=5*/f32[64,64]{1,0:T(8,128)S(1)}) custom-call(f32[16,512]{1,0:T(8,128)} %right_hbm.1, f32[16,512]{1,0:T(8,128)} %jacobi_hbm.1, f32[1,64,64]{2,1,0:T(8,128)} %inverse_hbm.1, ...), custom_call_target="tpu_custom_call" | custom-call | tf_op jit(solution)/shard_map/pallas_call | solution.py:598
  1.9 0.0 copy-start
  1.9 0.0 copy-start.1
  1.9 0.0 copy-start.2
  1.9 0.0 copy-start.3
  1.9 0.0 copy-start.4
  1.9 15.7 %all_to_all.20 = f32[32,1,1280]{2,1,0:T(1,128)S(1)} all-to-all(f32[32,1,1280]{2,1,0:T(1,128)S(1)} %bitcast.12), channel_id=1, replica_groups=mesh['grp'=4,'sub'=8] {'grp','sub'}, dimensions={0} | all-to-all | bytes 327680 | tf_op jit(solution)/shard_map/all_to_all | solution.py:632
  17.6 0.0 copy-done
  17.6 0.0 copy-done.1
  17.6 0.0 copy-done.2
  17.6 0.0 copy-done.3
  17.6 0.0 copy-done.4
  17.6 1.5 %shard_map.123 = (f32[64,128]{1,0:T(8,128)S(1)}, s32[16,128]{1,0:T(8,128)S(1)}, s32[16,128]{1,0:T(8,128)S(1)}, f32[64,128]{1,0:T(8,128)S(1)}, f32[1,2048]{1,0:T(...) custom-call(f32[320,128]{1,0:T(8,128)S(1)} %bitcast.8, f32[136,128]{1,0:T(8,128)S(1)} %get-tuple-element.24.fields_ref, ...), custom_call_target="tpu_custom_call" | custom-call | tf_op jit(solution)/shard_map/pallas_call | solution.py:598
  19.1 9.7 %all_to_all.21 = f32[32,1,640]{2,1,0:T(1,128)S(1)} all-to-all(f32[32,1,640]{2,1,0:T(1,128)S(1)} %bitcast.14), channel_id=1, replica_groups=mesh['grp'=4,'sub'=8] {'grp','sub'}, dimensions={0} | all-to-all | bytes 163840 | tf_op jit(solution)/shard_map/all_to_all | solution.py:632
  28.9 0.7 %shard_map.124 = (f32[64,128]{1,0:T(8,128)S(1)}, f32[64,128]{1,0:T(8,128)S(1)}, f32[1,128]{1,0:T(1,128)S(1)}, f32[160,128]{1,0:T(8,128)S(1)}) custom-call(f32[160,128]{1,0:T(8,128)S(1)} %bitcast.11, f32[136,128]{1,0:T(8,128)S(1)} %get-tuple-element.24.fields_ref, s32[16,128]{1,0:T(8,128)S(1)} %get-tuple-element.25.points_ref, ...), custom_call_target="tpu_custom_call" | custom-call | tf_op jit(solution)/shard_map/pallas_call | solution.py:598
  29.6 9.3 %all_to_all.22 = f32[32,1,640]{2,1,0:T(1,128)S(1)} all-to-all(f32[32,1,640]{2,1,0:T(1,128)S(1)} %bitcast.15), channel_id=1, replica_groups=mesh['grp'=4,'sub'=8] {'grp','sub'}, dimensions={0} | all-to-all | bytes 163840 | tf_op jit(solution)/shard_map/all_to_all | solution.py:632
  38.9 1.5 %shard_map.125 = (f32[64,128]{1,0:T(8,128)S(1)}, f32[64,128]{1,0:T(8,128)S(1)}, f32[1,2048]{1,0:T(1,128)S(1)}, f32[160,128]{1,0:T(8,128)S(1)}) custom-call(f32[160,128]{1,0:T(8,128)S(1)} %bitcast.10, f32[136,128]{1,0:T(8,128)S(1)} %get-tuple-element.24.fields_ref, s32[16,128]{1,0:T(8,128)S(1)} %get-tuple-element.25.points_ref, ...), custom_call_target="tpu_custom_call" | custom-call | tf_op jit(solution)/shard_map/pallas_call | solution.py:598
  40.4 9.3 %all_to_all.23 = f32[32,1,640]{2,1,0:T(1,128)S(1)} all-to-all(f32[32,1,640]{2,1,0:T(1,128)S(1)} %bitcast.13), channel_id=1, replica_groups=mesh['grp'=4,'sub'=8] {'grp','sub'}, dimensions={0} | all-to-all | bytes 163840 | tf_op jit(solution)/shard_map/all_to_all | solution.py:632
  49.7 1.1 %shard_map.126 = (f32[16,512]{1,0:T(8,128)}, f32[16,512]{1,0:T(8,128)}) custom-call(f32[160,128]{1,0:T(8,128)S(1)} %bitcast.9, s32[16,128]{1,0:T(8,128)S(1)} %get-tuple-element.25.points_ref, bf16[1024,256]{1,0:T(8,128)(2,1)S(1)} %get-tuple-element.26.far_hot_ref, s32[2,1024]{1,0:T(2,128)S(1)} %copy-done.3, ...), custom_call_target="tpu_custom_call" | custom-call | tf_op jit(solution)/shard_map/pallas_call | solution.py:598
Async XLA Ops:
  1.9 15.7 %copy-start = (f32[16,512]{1,0:T(8,128)S(1)}, f32[16,512]{1,0:T(8,128)}, u32[]{:S(2)}) copy-start(f32[16,512]{1,0:T(8,128)} %helmholtz_ref.7) | copy-start | bytes 98308
  1.9 15.7 %copy-start.1 = (bf16[256,256]{1,0:T(8,128)(2,1)S(1)}, bf16[256,256]{1,0:T(8,128)(2,1)}, u32[]{:S(2)}) copy-start(bf16[256,256]{1,0:T(8,128)(2,1)} %constant.4.clone.inner_ref) | copy-start | bytes 393220
  1.9 15.7 %copy-start.2 = (f32[16,1536]{1,0:T(8,128)S(1)}, f32[16,1536]{1,0:T(8,128)}, u32[]{:S(2)}) copy-start(f32[16,1536]{1,0:T(8,128)} %metric_ref.3) | copy-start | bytes 294916
  1.9 15.7 %copy-start.3 = (s32[2,1024]{1,0:T(2,128)S(1)}, s32[2,1024]{1,0:T(2,128)}, u32[]{:S(2)}) copy-start(s32[2,1024]{1,0:T(2,128)} %pair_ref.7) | copy-start | bytes 24580
  1.9 15.7 %copy-start.4 = (f32[64,128]{1,0:T(8,128)S(1)}, f32[64,128]{1,0:T(8,128)}, u32[]{:S(2)}) copy-start(f32[64,128]{1,0:T(8,128)} %constant.5.clone.first_ref) | copy-start | bytes 98308

commit v19 on v16

--- a/solution.py
+++ b/solution.py
@@ -267,15 +267,15 @@
 
 def factors(points):
     nodes = 0.5 * (1.0 + np.cos(np.pi * np.arange(8) / 7.0))
+    lane = lax.broadcasted_iota(jnp.int32, (1, LANES), 1)
+    table = jnp.full(lane.shape, nodes[7], F32)
+    for m in range(7):
+        table = jnp.where(lane == m, float(nodes[m]), table)
+    table = jnp.broadcast_to(table, points.shape)
     out = []
     for shift in (6, 3, 0):
-        index = (points >> shift) & 7
-        near = jnp.full(points.shape, nodes[7], F32)
-        far = jnp.full(points.shape, nodes[0], F32)
-        for m in range(7):
-            near = jnp.where(index == m, float(nodes[m]), near)
-            far = jnp.where(index == m, float(nodes[7 - m]), far)
-        out.append((near, far))
+        near = take(table, (points >> shift) & 7)
+        out.append((near, 1.0 - near))
     return out
 
 
@@ -287,7 +287,9 @@
 
 
 def own_corners():
-    return corners(lax.broadcasted_iota(jnp.int32, (1, POINTS), 1))
+    shape = (8, LANES)
+    chunk = lax.broadcasted_iota(jnp.int32, shape, 0) & 3
+    return corners(chunk * LANES + lax.broadcasted_iota(jnp.int32, shape, 1))
 
 
 def flat_map(mapped):
@@ -329,7 +331,7 @@
     for q, corner in enumerate(own_corners()):
         inner = None
         for c in range(4):
-            term = field[c * elements : (c + 1) * elements] * corner[:, c * LANES : (c + 1) * LANES]
+            term = field[c * elements : (c + 1) * elements] * corner[c : c + 1]
             inner = term if inner is None else inner + term
         flat = jnp.where(own_place(elements, q), jnp.sum(inner, axis=1, keepdims=True), flat)
     flat = jnp.sum(flat, axis=0, keepdims=True)
@@ -353,7 +355,7 @@
     for q, corner in enumerate(own_corners()):
         value = take(at_corner, element + q * elements)
         for c in range(4):
-            term = value * corner[:, c * LANES : (c + 1) * LANES]
+            term = value * corner[c : c + 1]
             out[c] = term if out[c] is None else out[c] + term
     return jnp.concatenate(out, axis=0)
 

time: 51.1 us -> 51 us (level)
  no operation moved by 1% of the time
where the time goes in v19:
time: 51 us; the launch traced here: 50.7 us
  blocking collectives  44 us (86%)
  Pallas kernels  5.91 us (12%)
  between operations  0.74 us (1%)
    all_to_all x4, blocking collectives, exchange(): lax.all_to_all(rows, ('grp', 'sub'), 0, 0, tiled=True).reshape(sent.shape)  44 us
    pallas_call x5, Pallas kernels, call(): pl.pallas_call(kernel, out_shape=[jax.ShapeDtypeStruct(*(out if isinstanc...  5.91 us

profile of v19, /device:TPU:0, one launch (start us, length us, event | category | flops | bytes accessed | tf_op | source)
XLA Modules:
  0.0 50.7 jit_solution(3443669173971765213)
XLA Ops:
  0.6 1.2 %shard_map.122 = (f32[320,128]{1,0:T(8,128)S(1)}, f32[136,128]{1,0:T(8,128)S(1)}, s32[16,128]{1,0:T(8,128)S(1)}, bf16[1024,256]{1,0:T(8,128)(2,1)S(1)}) custom-call(f32[16,512]{1,0:T(8,128)} %right_hbm.1, f32[16,512]{1,0:T(8,128)} %jacobi_ref.3, f32[1,64,64]{2,1,0:T(8,128)} %inverse_ref.1, s32[8,16]{1,0:T(8,128)} %map_hbm.1, s32[1,8,128]{2,1,0:T(8,128)} %slot_hbm.1, ...), custom_call_target="tpu_custom_call" | custom-call | tf_op jit(solution)/shard_map/pallas_call | solution.py:597
  1.8 0.0 copy-start
  1.9 0.0 copy-start.1
  1.9 0.0 copy-start.2
  1.9 0.0 copy-start.4
  1.9 0.0 copy-start.6
  1.9 15.7 %all_to_all.20 = f32[32,1,1280]{2,1,0:T(1,128)S(1)} all-to-all(f32[32,1,1280]{2,1,0:T(1,128)S(1)} %bitcast.12), channel_id=1, replica_groups=mesh['grp'=4,'sub'=8] {'grp','sub'}, dimensions={0} | all-to-all | bytes 327680 | tf_op jit(solution)/shard_map/all_to_all | solution.py:631
  17.6 0.0 copy-done
  17.6 0.0 copy-done.1
  17.6 0.0 copy-done.2
  17.6 0.0 copy-done.4
  17.6 0.0 copy-done.6
  17.6 1.5 %shard_map.123 = (f32[64,128]{1,0:T(8,128)S(1)}, s32[16,128]{1,0:T(8,128)S(1)}, s32[16,128]{1,0:T(8,128)S(1)}, f32[64,128]{1,0:T(8,128)S(1)}, f32[1,2048]{1,0:T(...) custom-call(f32[320,128]{1,0:T(8,128)S(1)} %bitcast.8, f32[136,128]{1,0:T(8,128)S(1)} %get-tuple-element.22.fields_ref, ...), custom_call_target="tpu_custom_call" | custom-call | tf_op jit(solution)/shard_map/pallas_call | solution.py:597
  19.1 0.0 copy-start.3
  19.1 0.0 copy-start.5
  19.1 9.7 %all_to_all.21 = f32[32,1,640]{2,1,0:T(1,128)S(1)} all-to-all(f32[32,1,640]{2,1,0:T(1,128)S(1)} %bitcast.14), channel_id=1, replica_groups=mesh['grp'=4,'sub'=8] {'grp','sub'}, dimensions={0} | all-to-all | bytes 163840 | tf_op jit(solution)/shard_map/all_to_all | solution.py:631
  28.8 0.0 copy-done.3
  28.8 0.0 copy-done.5
  28.8 0.7 %shard_map.124 = (f32[64,128]{1,0:T(8,128)S(1)}, f32[64,128]{1,0:T(8,128)S(1)}, f32[1,128]{1,0:T(1,128)S(1)}, f32[160,128]{1,0:T(8,128)S(1)}) custom-call(f32[160,128]{1,0:T(8,128)S(1)} %bitcast.11, f32[136,128]{1,0:T(8,128)S(1)} %get-tuple-element.22.fields_ref, s32[16,128]{1,0:T(8,128)S(1)} %get-tuple-element.23.points_ref, ...), custom_call_target="tpu_custom_call" | custom-call | tf_op jit(solution)/shard_map/pallas_call | solution.py:597
  29.6 9.3 %all_to_all.22 = f32[32,1,640]{2,1,0:T(1,128)S(1)} all-to-all(f32[32,1,640]{2,1,0:T(1,128)S(1)} %bitcast.15), channel_id=1, replica_groups=mesh['grp'=4,'sub'=8] {'grp','sub'}, dimensions={0} | all-to-all | bytes 163840 | tf_op jit(solution)/shard_map/all_to_all | solution.py:631
  38.9 1.5 %shard_map.125 = (f32[64,128]{1,0:T(8,128)S(1)}, f32[64,128]{1,0:T(8,128)S(1)}, f32[1,2048]{1,0:T(1,128)S(1)}, f32[160,128]{1,0:T(8,128)S(1)}) custom-call(f32[160,128]{1,0:T(8,128)S(1)} %bitcast.10, f32[136,128]{1,0:T(8,128)S(1)} %get-tuple-element.22.fields_ref, s32[16,128]{1,0:T(8,128)S(1)} %get-tuple-element.23.points_ref, ...), custom_call_target="tpu_custom_call" | custom-call | tf_op jit(solution)/shard_map/pallas_call | solution.py:597
  40.3 9.3 %all_to_all.23 = f32[32,1,640]{2,1,0:T(1,128)S(1)} all-to-all(f32[32,1,640]{2,1,0:T(1,128)S(1)} %bitcast.13), channel_id=1, replica_groups=mesh['grp'=4,'sub'=8] {'grp','sub'}, dimensions={0} | all-to-all | bytes 163840 | tf_op jit(solution)/shard_map/all_to_all | solution.py:631
  49.6 1.1 %shard_map.126 = (f32[16,512]{1,0:T(8,128)}, f32[16,512]{1,0:T(8,128)}) custom-call(f32[160,128]{1,0:T(8,128)S(1)} %bitcast.9, s32[16,128]{1,0:T(8,128)S(1)} %get-tuple-element.23.points_ref, bf16[1024,256]{1,0:T(8,128)(2,1)S(1)} %get-tuple-element.24.far_hot_ref, s32[2,1024]{1,0:T(2,128)S(1)} %copy-done.4, ...), custom_call_target="tpu_custom_call" | custom-call | tf_op jit(solution)/shard_map/pallas_call | solution.py:597
Async XLA Ops:
  1.8 15.7 %copy-start = (f32[16,512]{1,0:T(8,128)S(1)}, f32[16,512]{1,0:T(8,128)}, u32[]{:S(2)}) copy-start(f32[16,512]{1,0:T(8,128)} %helmholtz_ref.7) | copy-start | bytes 98308
  1.9 15.7 %copy-start.1 = (bf16[256,256]{1,0:T(8,128)(2,1)S(1)}, bf16[256,256]{1,0:T(8,128)(2,1)}, u32[]{:S(2)}) copy-start(bf16[256,256]{1,0:T(8,128)(2,1)} %constant.4.clone.inner_ref) | copy-start | bytes 393220
  1.9 15.7 %copy-start.2 = (f32[16,1536]{1,0:T(8,128)S(1)}, f32[16,1536]{1,0:T(8,128)}, u32[]{:S(2)}) copy-start(f32[16,1536]{1,0:T(8,128)} %metric_ref.3) | copy-start | bytes 294916
  1.9 15.7 %copy-start.4 = (s32[2,1024]{1,0:T(2,128)S(1)}, s32[2,1024]{1,0:T(2,128)}, u32[]{:S(2)}) copy-start(s32[2,1024]{1,0:T(2,128)} %pair_ref.7) | copy-start | bytes 24580
  1.9 15.7 %copy-start.6 = (f32[64,128]{1,0:T(8,128)S(1)}, f32[64,128]{1,0:T(8,128)}, u32[]{:S(2)}) copy-start(f32[64,128]{1,0:T(8,128)} %constant.5.clone.first_ref) | copy-start | bytes 98308
  19.1 9.8 %copy-start.3 = (f32[16,512]{1,0:T(8,128)S(1)}, f32[16,512]{1,0:T(8,128)}, u32[]{:S(2)}) copy-start(f32[16,512]{1,0:T(8,128)} %jacobi_ref.3) | copy-start | bytes 98308
  19.1 9.7 %copy-start.5 = (f32[1,64,64]{2,1,0:T(8,128)S(1)}, f32[1,64,64]{2,1,0:T(8,128)}, u32[]{:S(2)}) copy-start(f32[1,64,64]{2,1,0:T(8,128)} %inverse_ref.1) | copy-start | bytes 49156

commit v20 on v19

--- a/solution.py
+++ b/solution.py
@@ -108,12 +108,19 @@
 
 def scatter(rows, chunks, values):
     total = jnp.zeros((2 * rows, LANES), F32)
-    for (row, hot), value in zip(chunks, values):
-        steps = lax.broadcasted_iota(jnp.int32, (rows, row.shape[1]), 0).astype(F32).astype(BF16)
-        mine = steps == row.astype(F32).astype(BF16)
-        parts = [jnp.where(mine, part, jnp.zeros_like(steps)) for part in split(value)]
+    for at in range(0, len(chunks), 2):
+        left, right = [], []
+        for (row, hot), value in zip(chunks[at : at + 2], values[at : at + 2]):
+            steps = lax.broadcasted_iota(jnp.int32, (rows, STEP), 0).astype(F32).astype(BF16)
+            mine = steps == row.astype(F32).astype(BF16)
+            parts = [jnp.where(mine, part, jnp.zeros_like(steps)) for part in split(value)]
+            left.append(jnp.concatenate(parts, axis=0))
+            right.append(hot)
         total = total + lax.dot_general(
-            jnp.concatenate(parts, axis=0), hot, NT, preferred_element_type=F32
+            jnp.concatenate(left, axis=1),
+            jnp.concatenate(right, axis=1),
+            NT,
+            preferred_element_type=F32,
         )
     return total[:rows] + total[rows:]
 

time: 51 us -> 51.1 us (level)
  no operation moved by 1% of the time
where the time goes in v20:
time: 51.1 us; the launch traced here: 50.7 us
  blocking collectives  44 us (86%)
  Pallas kernels  5.94 us (12%)
  between operations  0.74 us (1%)
    all_to_all x4, blocking collectives, exchange(): lax.all_to_all(rows, ('grp', 'sub'), 0, 0, tiled=True).reshape(sent.shape)  44 us
    pallas_call x5, Pallas kernels, call(): pl.pallas_call(kernel, out_shape=[jax.ShapeDtypeStruct(*(out if isinstanc...  5.94 us

profile of v20, /device:TPU:0, one launch (start us, length us, event | category | flops | bytes accessed | tf_op | source)
XLA Modules:
  0.0 50.7 jit_solution(9959630205830730195)
XLA Ops:
  0.6 1.2 %shard_map.122 = (f32[320,128]{1,0:T(8,128)S(1)}, f32[136,128]{1,0:T(8,128)S(1)}, s32[16,128]{1,0:T(8,128)S(1)}, bf16[1024,256]{1,0:T(8,128)(2,1)S(1)}) custom-call(f32[16,512]{1,0:T(8,128)} %right_hbm.1, f32[16,512]{1,0:T(8,128)} %jacobi_ref.3, f32[1,64,64]{2,1,0:T(8,128)} %inverse_ref.1, s32[8,16]{1,0:T(8,128)} %map_hbm.1, s32[1,8,128]{2,1,0:T(8,128)} %slot_hbm.1, ...), custom_call_target="tpu_custom_call" | custom-call | tf_op jit(solution)/shard_map/pallas_call | solution.py:604
  1.8 0.0 copy-start
  1.9 0.0 copy-start.1
  1.9 0.0 copy-start.2
  1.9 0.0 copy-start.4
  1.9 0.0 copy-start.6
  1.9 15.7 %all_to_all.20 = f32[32,1,1280]{2,1,0:T(1,128)S(1)} all-to-all(f32[32,1,1280]{2,1,0:T(1,128)S(1)} %bitcast.12), channel_id=1, replica_groups=mesh['grp'=4,'sub'=8] {'grp','sub'}, dimensions={0} | all-to-all | bytes 327680 | tf_op jit(solution)/shard_map/all_to_all | solution.py:638
  17.6 0.0 copy-done
  17.6 0.0 copy-done.1
  17.6 0.0 copy-done.2
  17.6 0.0 copy-done.4
  17.6 0.0 copy-done.6
  17.6 1.5 %shard_map.123 = (f32[64,128]{1,0:T(8,128)S(1)}, s32[16,128]{1,0:T(8,128)S(1)}, s32[16,128]{1,0:T(8,128)S(1)}, f32[64,128]{1,0:T(8,128)S(1)}, f32[1,2048]{1,0:T(...) custom-call(f32[320,128]{1,0:T(8,128)S(1)} %bitcast.8, f32[136,128]{1,0:T(8,128)S(1)} %get-tuple-element.22.fields_ref, ...), custom_call_target="tpu_custom_call" | custom-call | tf_op jit(solution)/shard_map/pallas_call | solution.py:604
  19.1 0.0 copy-start.3
  19.1 0.0 copy-start.5
  19.1 9.7 %all_to_all.21 = f32[32,1,640]{2,1,0:T(1,128)S(1)} all-to-all(f32[32,1,640]{2,1,0:T(1,128)S(1)} %bitcast.14), channel_id=1, replica_groups=mesh['grp'=4,'sub'=8] {'grp','sub'}, dimensions={0} | all-to-all | bytes 163840 | tf_op jit(solution)/shard_map/all_to_all | solution.py:638
  28.9 0.0 copy-done.3
  28.9 0.0 copy-done.5
  28.9 0.7 %shard_map.124 = (f32[64,128]{1,0:T(8,128)S(1)}, f32[64,128]{1,0:T(8,128)S(1)}, f32[1,128]{1,0:T(1,128)S(1)}, f32[160,128]{1,0:T(8,128)S(1)}) custom-call(f32[160,128]{1,0:T(8,128)S(1)} %bitcast.11, f32[136,128]{1,0:T(8,128)S(1)} %get-tuple-element.22.fields_ref, s32[16,128]{1,0:T(8,128)S(1)} %get-tuple-element.23.points_ref, ...), custom_call_target="tpu_custom_call" | custom-call | tf_op jit(solution)/shard_map/pallas_call | solution.py:604
  29.6 9.3 %all_to_all.22 = f32[32,1,640]{2,1,0:T(1,128)S(1)} all-to-all(f32[32,1,640]{2,1,0:T(1,128)S(1)} %bitcast.15), channel_id=1, replica_groups=mesh['grp'=4,'sub'=8] {'grp','sub'}, dimensions={0} | all-to-all | bytes 163840 | tf_op jit(solution)/shard_map/all_to_all | solution.py:638
  38.9 1.5 %shard_map.125 = (f32[64,128]{1,0:T(8,128)S(1)}, f32[64,128]{1,0:T(8,128)S(1)}, f32[1,2048]{1,0:T(1,128)S(1)}, f32[160,128]{1,0:T(8,128)S(1)}) custom-call(f32[160,128]{1,0:T(8,128)S(1)} %bitcast.10, f32[136,128]{1,0:T(8,128)S(1)} %get-tuple-element.22.fields_ref, s32[16,128]{1,0:T(8,128)S(1)} %get-tuple-element.23.points_ref, ...), custom_call_target="tpu_custom_call" | custom-call | tf_op jit(solution)/shard_map/pallas_call | solution.py:604
  40.4 9.3 %all_to_all.23 = f32[32,1,640]{2,1,0:T(1,128)S(1)} all-to-all(f32[32,1,640]{2,1,0:T(1,128)S(1)} %bitcast.13), channel_id=1, replica_groups=mesh['grp'=4,'sub'=8] {'grp','sub'}, dimensions={0} | all-to-all | bytes 163840 | tf_op jit(solution)/shard_map/all_to_all | solution.py:638
  49.7 1.1 %shard_map.126 = (f32[16,512]{1,0:T(8,128)}, f32[16,512]{1,0:T(8,128)}) custom-call(f32[160,128]{1,0:T(8,128)S(1)} %bitcast.9, s32[16,128]{1,0:T(8,128)S(1)} %get-tuple-element.23.points_ref, bf16[1024,256]{1,0:T(8,128)(2,1)S(1)} %get-tuple-element.24.far_hot_ref, s32[2,1024]{1,0:T(2,128)S(1)} %copy-done.4, ...), custom_call_target="tpu_custom_call" | custom-call | tf_op jit(solution)/shard_map/pallas_call | solution.py:604
Async XLA Ops:
  1.8 15.7 %copy-start = (f32[16,512]{1,0:T(8,128)S(1)}, f32[16,512]{1,0:T(8,128)}, u32[]{:S(2)}) copy-start(f32[16,512]{1,0:T(8,128)} %helmholtz_ref.7) | copy-start | bytes 98308
  1.9 15.7 %copy-start.1 = (bf16[256,256]{1,0:T(8,128)(2,1)S(1)}, bf16[256,256]{1,0:T(8,128)(2,1)}, u32[]{:S(2)}) copy-start(bf16[256,256]{1,0:T(8,128)(2,1)} %constant.4.clone.inner_ref) | copy-start | bytes 393220
  1.9 15.7 %copy-start.2 = (f32[16,1536]{1,0:T(8,128)S(1)}, f32[16,1536]{1,0:T(8,128)}, u32[]{:S(2)}) copy-start(f32[16,1536]{1,0:T(8,128)} %metric_ref.3) | copy-start | bytes 294916
  1.9 15.7 %copy-start.4 = (s32[2,1024]{1,0:T(2,128)S(1)}, s32[2,1024]{1,0:T(2,128)}, u32[]{:S(2)}) copy-start(s32[2,1024]{1,0:T(2,128)} %pair_ref.7) | copy-start | bytes 24580
  1.9 15.7 %copy-start.6 = (f32[64,128]{1,0:T(8,128)S(1)}, f32[64,128]{1,0:T(8,128)}, u32[]{:S(2)}) copy-start(f32[64,128]{1,0:T(8,128)} %constant.5.clone.first_ref) | copy-start | bytes 98308
  19.1 9.8 %copy-start.3 = (f32[16,512]{1,0:T(8,128)S(1)}, f32[16,512]{1,0:T(8,128)}, u32[]{:S(2)}) copy-start(f32[16,512]{1,0:T(8,128)} %jacobi_ref.3) | copy-start | bytes 98308
  19.1 9.8 %copy-start.5 = (f32[1,64,64]{2,1,0:T(8,128)S(1)}, f32[1,64,64]{2,1,0:T(8,128)}, u32[]{:S(2)}) copy-start(f32[1,64,64]{2,1,0:T(8,128)} %inverse_ref.1) | copy-start | bytes 49156

commit v21 on v20

--- a/solution.py
+++ b/solution.py
@@ -397,7 +397,7 @@
 
 def first_kernel(
     right_hbm, jacobi_hbm, inverse_hbm, map_hbm, slot_hbm, face_hbm,
-    sent_ref, fields_ref, points_ref, far_hot_ref,
+    sent_ref, fields_ref, points_ref, far_hot_ref, smoother_ref, solver_ref,
     right_ref, jacobi_ref, inverse_ref, map_ref, slot_ref, face_ref, sems,
 ):
     copies = []
@@ -428,7 +428,10 @@
         copy.wait()
     resid = rows_of(right_ref[...])
     flat = flat_map(map_ref[...])
-    smoothed = rows_of(jacobi_ref[...]) * resid
+    smoother = rows_of(jacobi_ref[...])
+    smoother_ref[...] = smoother
+    solver_ref[...] = inverse_ref[0]
+    smoothed = smoother * resid
     fields_ref[0 : 4 * elements, :] = resid
     fields_ref[4 * elements : 8 * elements, :] = smoothed
     fields_ref[8 * elements :, :] = jnp.broadcast_to(flat, (8, LANES))
@@ -526,8 +529,8 @@
 
 
 def middle_kernel(
-    received_ref, fields_ref, points_ref, far_hot_ref, pair_ref, pair_hot_ref, jacobi_ref, helmholtz_ref,
-    inverse_ref, smoothed_ref, back_ref, local_ref,
+    received_ref, fields_ref, points_ref, far_hot_ref, pair_ref, pair_hot_ref, smoother_ref, helmholtz_ref,
+    solver_ref, smoothed_ref, back_ref, local_ref,
     image_ref, resid_ref, scalars_ref, sent_ref,
 ):
     elements = helmholtz_ref.shape[0]
@@ -544,9 +547,9 @@
     resid = fields_ref[0 : 4 * elements, :] - alpha * image
     resid_ref[...] = resid
     vertices = one_vertex(fields_ref[8 * elements : 8 * elements + 1, :])
-    part = coarse_part(resid, vertices, inverse_ref[0])
+    part = coarse_part(resid, vertices, solver_ref[...])
     values = gather(
-        rows_of(jacobi_ref[...]) * resid, loaded(far_places(points_ref[...], elements), far_hot_ref),
+        smoother_ref[...] * resid, loaded(far_places(points_ref[...], elements), far_hot_ref),
     )
     send_values(sent_ref, ROWS, values, peers)
     send_same(sent_ref, ROWS, TERMS, part)
@@ -554,7 +557,7 @@
 
 def second_kernel(
     received_ref, fields_ref, points_ref, far_hot_ref, pair_ref, pair_hot_ref, resid_ref, image_ref,
-    maps_ref, far_points_ref, jacobi_ref, metric_ref, helmholtz_ref, first_ref, inner_ref,
+    maps_ref, far_points_ref, smoother_ref, metric_ref, helmholtz_ref, first_ref, inner_ref,
     smoothed_ref, back_ref, local_ref, sent_ref,
 ):
     elements = helmholtz_ref.shape[0]
@@ -562,7 +565,7 @@
     solved = get_solved(received_ref, ROWS, peers)
     resid = resid_ref[...]
     flat = whole(fields_ref[8 * elements : 8 * elements + 1, :])
-    rough = rows_of(jacobi_ref[...]) * resid
+    rough = smoother_ref[...] * resid
     smoothed = rough + prolonged(solved[0], flat, elements)
     smoothed_ref[...] = smoothed
     apply(
@@ -640,13 +643,15 @@
     far_hot_shape = (points_shape[0] * LANES // 2, STEP)
     pair_hot_shape = (local[1] * LANES // STEP, STEP)
 
-    sent, fields, points, far_hot = call(
+    sent, fields, points, far_hot, smoother, solver = call(
         first_kernel,
         [
             (groups * peers * FIRST_ROWS, LANES),
             (8 * elements + 8, LANES),
             (points_shape, jnp.int32),
             (far_hot_shape, BF16),
+            field,
+            (NC, NC),
         ],
         right_side, jacobi, coarse_inverse, coarse_map, shared_slots, face_points, copied=True,
     )
@@ -659,12 +664,12 @@
     )
     image, resid, scalars, sent = call(
         middle_kernel, [field, field, (1, LANES), sent_shape],
-        exchange(sent), fields, points, far_hot, pair_list, pair_hot, jacobi, helmholtz, coarse_inverse,
+        exchange(sent), fields, points, far_hot, pair_list, pair_hot, smoother, helmholtz, solver,
         smoothed, back, near,
     )
     second, back, near, sent = call(
         second_kernel, [field, field, local, sent_shape],
-        exchange(sent), fields, points, far_hot, pair_list, pair_hot, resid, image, maps, far_points, jacobi,
+        exchange(sent), fields, points, far_hot, pair_list, pair_hot, resid, image, maps, far_points, smoother,
         metric, helmholtz, t["first"], t["inner"],
     )
     return tuple(

time: 51.1 us -> 51 us (level)
  no operation moved by 1% of the time
where the time goes in v21:
time: 51 us; the launch traced here: 50.7 us
  blocking collectives  44 us (86%)
  Pallas kernels  5.94 us (12%)
  between operations  0.72 us (1%)
    all_to_all x4, blocking collectives, exchange(): lax.all_to_all(rows, ('grp', 'sub'), 0, 0, tiled=True).reshape(sent.shape)  44 us
    pallas_call x5, Pallas kernels, call(): pl.pallas_call(kernel, out_shape=[jax.ShapeDtypeStruct(*(out if isinstanc...  5.94 us

profile of v21, /device:TPU:0, one launch (start us, length us, event | category | flops | bytes accessed | tf_op | source)
XLA Modules:
  0.0 50.7 jit_solution(14299023461928981364)
XLA Ops:
  0.6 1.2 %shard_map.122 = (f32[320,128]{1,0:T(8,128)S(1)}, f32[136,128]{1,0:T(8,128)S(1)}, s32[16,128]{1,0:T(8,128)S(1)}, bf16[1024,256]{1,0:T(8,128)(2,1)S(1)}, f32[64,128]{1,0:T(8,128)S(1)}, /*index=5*/f32[64,64]{1,0:T(8,128)S(1)}) custom-call(f32[16,512]{1,0:T(8,128)} %right_hbm.1, f32[16,512]{1,0:T(8,128)} %jacobi_hbm.1, f32[1,64,64]{2,1,0:T(8,128)} %inverse_hbm.1, ...), custom_call_target="tpu_custom_call" | custom-call | tf_op jit(solution)/shard_map/pallas_call | solution.py:607
  1.8 0.0 copy-start
  1.9 0.0 copy-start.1
  1.9 0.0 copy-start.2
  1.9 0.0 copy-start.3
  1.9 0.0 copy-start.4
  1.9 15.7 %all_to_all.20 = f32[32,1,1280]{2,1,0:T(1,128)S(1)} all-to-all(f32[32,1,1280]{2,1,0:T(1,128)S(1)} %bitcast.12), channel_id=1, replica_groups=mesh['grp'=4,'sub'=8] {'grp','sub'}, dimensions={0} | all-to-all | bytes 327680 | tf_op jit(solution)/shard_map/all_to_all | solution.py:641
  17.6 0.0 copy-done
  17.6 0.0 copy-done.1
  17.6 0.0 copy-done.2
  17.6 0.0 copy-done.3
  17.6 0.0 copy-done.4
  17.6 1.5 %shard_map.123 = (f32[64,128]{1,0:T(8,128)S(1)}, s32[16,128]{1,0:T(8,128)S(1)}, s32[16,128]{1,0:T(8,128)S(1)}, f32[64,128]{1,0:T(8,128)S(1)}, f32[1,2048]{1,0:T(...) custom-call(f32[320,128]{1,0:T(8,128)S(1)} %bitcast.8, f32[136,128]{1,0:T(8,128)S(1)} %get-tuple-element.24.fields_ref, ...), custom_call_target="tpu_custom_call" | custom-call | tf_op jit(solution)/shard_map/pallas_call | solution.py:607
  19.1 9.7 %all_to_all.21 = f32[32,1,640]{2,1,0:T(1,128)S(1)} all-to-all(f32[32,1,640]{2,1,0:T(1,128)S(1)} %bitcast.14), channel_id=1, replica_groups=mesh['grp'=4,'sub'=8] {'grp','sub'}, dimensions={0} | all-to-all | bytes 163840 | tf_op jit(solution)/shard_map/all_to_all | solution.py:641
  28.8 0.7 %shard_map.124 = (f32[64,128]{1,0:T(8,128)S(1)}, f32[64,128]{1,0:T(8,128)S(1)}, f32[1,128]{1,0:T(1,128)S(1)}, f32[160,128]{1,0:T(8,128)S(1)}) custom-call(f32[160,128]{1,0:T(8,128)S(1)} %bitcast.11, f32[136,128]{1,0:T(8,128)S(1)} %get-tuple-element.24.fields_ref, s32[16,128]{1,0:T(8,128)S(1)} %get-tuple-element.25.points_ref, ...), custom_call_target="tpu_custom_call" | custom-call | tf_op jit(solution)/shard_map/pallas_call | solution.py:607
  29.6 9.3 %all_to_all.22 = f32[32,1,640]{2,1,0:T(1,128)S(1)} all-to-all(f32[32,1,640]{2,1,0:T(1,128)S(1)} %bitcast.15), channel_id=1, replica_groups=mesh['grp'=4,'sub'=8] {'grp','sub'}, dimensions={0} | all-to-all | bytes 163840 | tf_op jit(solution)/shard_map/all_to_all | solution.py:641
  38.9 1.5 %shard_map.125 = (f32[64,128]{1,0:T(8,128)S(1)}, f32[64,128]{1,0:T(8,128)S(1)}, f32[1,2048]{1,0:T(1,128)S(1)}, f32[160,128]{1,0:T(8,128)S(1)}) custom-call(f32[160,128]{1,0:T(8,128)S(1)} %bitcast.10, f32[136,128]{1,0:T(8,128)S(1)} %get-tuple-element.24.fields_ref, s32[16,128]{1,0:T(8,128)S(1)} %get-tuple-element.25.points_ref, ...), custom_call_target="tpu_custom_call" | custom-call | tf_op jit(solution)/shard_map/pallas_call | solution.py:607
  40.3 9.3 %all_to_all.23 = f32[32,1,640]{2,1,0:T(1,128)S(1)} all-to-all(f32[32,1,640]{2,1,0:T(1,128)S(1)} %bitcast.13), channel_id=1, replica_groups=mesh['grp'=4,'sub'=8] {'grp','sub'}, dimensions={0} | all-to-all | bytes 163840 | tf_op jit(solution)/shard_map/all_to_all | solution.py:641
  49.6 1.1 %shard_map.126 = (f32[16,512]{1,0:T(8,128)}, f32[16,512]{1,0:T(8,128)}) custom-call(f32[160,128]{1,0:T(8,128)S(1)} %bitcast.9, s32[16,128]{1,0:T(8,128)S(1)} %get-tuple-element.25.points_ref, bf16[1024,256]{1,0:T(8,128)(2,1)S(1)} %get-tuple-element.26.far_hot_ref, s32[2,1024]{1,0:T(2,128)S(1)} %copy-done.3, ...), custom_call_target="tpu_custom_call" | custom-call | tf_op jit(solution)/shard_map/pallas_call | solution.py:607
Async XLA Ops:
  1.8 15.7 %copy-start = (f32[16,512]{1,0:T(8,128)S(1)}, f32[16,512]{1,0:T(8,128)}, u32[]{:S(2)}) copy-start(f32[16,512]{1,0:T(8,128)} %helmholtz_ref.7) | copy-start | bytes 98308
  1.9 15.7 %copy-start.1 = (bf16[256,256]{1,0:T(8,128)(2,1)S(1)}, bf16[256,256]{1,0:T(8,128)(2,1)}, u32[]{:S(2)}) copy-start(bf16[256,256]{1,0:T(8,128)(2,1)} %constant.4.clone.inner_ref) | copy-start | bytes 393220
  1.9 15.7 %copy-start.2 = (f32[16,1536]{1,0:T(8,128)S(1)}, f32[16,1536]{1,0:T(8,128)}, u32[]{:S(2)}) copy-start(f32[16,1536]{1,0:T(8,128)} %metric_ref.3) | copy-start | bytes 294916
  1.9 15.7 %copy-start.3 = (s32[2,1024]{1,0:T(2,128)S(1)}, s32[2,1024]{1,0:T(2,128)}, u32[]{:S(2)}) copy-start(s32[2,1024]{1,0:T(2,128)} %pair_ref.7) | copy-start | bytes 24580
  1.9 15.7 %copy-start.4 = (f32[64,128]{1,0:T(8,128)S(1)}, f32[64,128]{1,0:T(8,128)}, u32[]{:S(2)}) copy-start(f32[64,128]{1,0:T(8,128)} %constant.5.clone.first_ref) | copy-start | bytes 98308
